TPU v7x, 32 devices: a whole 2x2x4 slice. The times are simulated.
32 devices in a mesh: section: 4 (over y, x), batch: 8 (over z, core).
Axes of the slice: x: 2, y: 2, z: 4, core: 2. Of those that a mesh axis runs over, the one named last changes fastest.
Arguments:
- frames_in: bfloat16 [4096, 1024], P('batch'), may hold values from -6 to 6
- cotangent: bfloat16 [4096, 1024], P('batch'), may hold values from -6 to 6
- qkv_weight: bfloat16 [4, 1024, 3072], P('section'), may hold values from -0.1875 to 0.1875
- out_weight: bfloat16 [4, 1024, 1024], P('section'), may hold values from -1 to 1
- up_weight: bfloat16 [4, 1024, 4096], P('section'), may hold values from -0.1875 to 0.1875
- down_weight: bfloat16 [4, 4096, 1024], P('section'), may hold values from -0.09375 to 0.09375
- norm_table: float32 [4, 32, 1024], P('section'), may hold values from -0.5 to 0.5
- lengths: int32 [32], P('batch'), may hold values from 75 to 128, as said below
- codebooks: int32 [32], P('batch'), may hold values from 1 to 7
Outputs:
- layer_outputs: bfloat16 [4, 4096, 1024], P('section', 'batch')
- input_grads: bfloat16 [4, 4096, 1024], P('section', 'batch')
- grad_qkv: float32 [4, 1024, 3072], P('section', 'batch')
- grad_out: float32 [4, 1024, 1024], P('section', 'batch')
- grad_up: float32 [4, 1024, 4096], P('section', 'batch')
- grad_down: float32 [4, 4096, 1024], P('section', None, 'batch')
- grad_norms: float32 [4, 32, 1024], P('section', None, 'batch')
Inputs may be any that keep to these rules, and one draw needn't show every extreme that they name: `lengths`: every utterance has at least 75 live frames; in every draw some utterance has all 128. `codebooks`: the codebook section that the NAR layers are conditioned on.
All inputs are finite; a program needn't handle non-finite values.
Results may differ from a plain program's by a relative error of at most 0.017.
Values may be sent and summed in bfloat16 or wider, within the bound.
No kernel may reach another device: no remote copies, remote signals or barrier semaphores. Data moves between devices by JAX's collectives and lax.ppermute only.
A program may use at most 320 MiB of HBM per device.

v0:
```python
import jax
import jax.numpy as jnp
from jax import lax
from jax.sharding import PartitionSpec as P

HEADS = 16


epsilon = 1e-05
masked_score = -1e30


def passed_along(x, axis, by):
    size = lax.axis_size(axis)
    pairs = [(i, i + by) for i in range(size) if 0 <= i + by < size]
    return lax.ppermute(x, axis, pairs)


def normalize(values):
    centre = values - jnp.mean(values, axis=-1, keepdims=True)
    reciprocal = lax.rsqrt(jnp.mean(centre * centre, axis=-1, keepdims=True) + epsilon)
    return (centre * reciprocal, reciprocal)


def normalize_back(gradient, normal_part, reciprocal, gain_row):
    scaled = gradient * (1.0 + gain_row)
    centred = scaled - jnp.mean(scaled, axis=-1, keepdims=True)
    return reciprocal * (
        centred - normal_part * jnp.mean(scaled * normal_part, axis=-1, keepdims=True)
    )


def key_mask(frames, length, is_nar):
    query_ids = lax.broadcasted_iota(jnp.int32, (frames, frames), 0)
    key_ids = lax.broadcasted_iota(jnp.int32, (frames, frames), 1)
    return (key_ids < length) & (is_nar | (key_ids <= query_ids))


def table_rows(tables, codebook):
    row_count = tables.shape[0] // 4
    chosen = lax.broadcasted_iota(jnp.int32, (row_count,), 0) == codebook
    blocks = tables.reshape(row_count, 4, tables.shape[1])
    return (jnp.sum(jnp.where(chosen[:, None, None], blocks, 0.0), axis=0), chosen)


def split_heads(packed, frames, features):
    heads_split = packed.reshape(frames, 3, HEADS, features // HEADS)
    return (heads_split[:, 0], heads_split[:, 1], heads_split[:, 2])


def contract_last(left_side, right_side):
    return lax.dot_general(
        left_side, right_side, (((1,), (1,)), ((), ())), preferred_element_type=jnp.float32
    )


def contract_rows(left_side, right_side):
    return lax.dot_general(
        left_side, right_side, (((0,), (0,)), ((), ())), preferred_element_type=jnp.float32
    )


def empty_kept(frames, features, hidden_units):
    return (
        jnp.zeros((frames, features), jnp.bfloat16),
        jnp.zeros((frames, 3 * features), jnp.bfloat16),
        jnp.zeros((HEADS, frames), jnp.float32),
        jnp.zeros((frames, features), jnp.bfloat16),
        jnp.zeros((frames, features), jnp.float32),
        jnp.zeros((frames, features), jnp.bfloat16),
        jnp.zeros((frames, hidden_units), jnp.float32),
        jnp.zeros((frames, hidden_units), jnp.bfloat16),
    )


def empty_pieces(frames, features, hidden_units):
    return (
        jnp.zeros((frames, features), jnp.bfloat16),
        jnp.zeros((frames, 3 * features), jnp.bfloat16),
        jnp.zeros((frames, features), jnp.bfloat16),
        jnp.zeros((frames, features), jnp.bfloat16),
        jnp.zeros((frames, features), jnp.bfloat16),
        jnp.zeros((frames, hidden_units), jnp.bfloat16),
        jnp.zeros((frames, hidden_units), jnp.bfloat16),
        jnp.zeros((frames, features), jnp.bfloat16),
    )


def store_slot(buffer, new_value, micro_slot, active):
    old_value = lax.dynamic_index_in_dim(buffer, micro_slot, 0, keepdims=False)
    return lax.dynamic_update_index_in_dim(
        buffer, jnp.where(active, new_value, old_value), micro_slot, 0
    )


def layer_forward(inputs, weights, length, codebook, is_nar):
    qkv_weight, out_weight, up_weight, down_weight, tables = weights
    frames, features = inputs.shape
    norm_rows, chosen = table_rows(tables, codebook)
    residual = inputs.astype(jnp.float32)
    normal_one, recip_one = normalize(residual)
    normed_one = (normal_one * (1.0 + norm_rows[0]) + norm_rows[1]).astype(jnp.bfloat16)
    packed = jnp.dot(normed_one, qkv_weight, preferred_element_type=jnp.float32).astype(
        jnp.bfloat16
    )
    query_heads, key_heads, value_heads = split_heads(packed, frames, features)
    inv_root = (features // HEADS) ** (-0.5)
    allowed = key_mask(frames, length, is_nar)
    scores = (
        jnp.einsum("qhd,khd->hqk", query_heads, key_heads, preferred_element_type=jnp.float32)
        * inv_root
    )
    scores = jnp.where(allowed[None], scores, masked_score)
    row_max = jnp.max(scores, axis=-1, keepdims=True)
    exp_scores = jnp.exp(scores - row_max)
    row_total = jnp.sum(exp_scores, axis=-1, keepdims=True)
    attn_probs = (exp_scores / row_total).astype(jnp.bfloat16)
    logsum = (row_max + jnp.log(row_total))[..., 0]
    attn_mixed = jnp.einsum(
        "hqk,khd->qhd", attn_probs, value_heads, preferred_element_type=jnp.float32
    )
    attended = attn_mixed.reshape(frames, features).astype(jnp.bfloat16)
    hidden = residual + jnp.dot(attended, out_weight, preferred_element_type=jnp.float32)
    normal_two, recip_two = normalize(hidden)
    normed_two = (normal_two * (1.0 + norm_rows[2]) + norm_rows[3]).astype(jnp.bfloat16)
    upward = jnp.dot(normed_two, up_weight, preferred_element_type=jnp.float32)
    activated = jax.nn.gelu(upward).astype(jnp.bfloat16)
    output = hidden + jnp.dot(activated, down_weight, preferred_element_type=jnp.float32)
    kept_parts = (normed_one, packed, logsum, attended, hidden, normed_two, upward, activated)
    return (output.astype(jnp.bfloat16), kept_parts)


def layer_backward(inputs, kept_parts, grad_out, weights, length, codebook, is_nar):
    qkv_weight, out_weight, up_weight, down_weight, tables = weights
    normed_one, packed, logsum, attended, hidden, normed_two, upward, activated = kept_parts
    frames, features = inputs.shape
    norm_rows, chosen = table_rows(tables, codebook)
    normal_one, recip_one = normalize(inputs.astype(jnp.float32))
    normal_two, recip_two = normalize(hidden)
    grad_act = contract_last(grad_out, down_weight)
    unused_value, gelu_back = jax.vjp(jax.nn.gelu, upward)
    grad_upward = gelu_back(grad_act)[0].astype(jnp.bfloat16)
    grad_two = contract_last(grad_upward, up_weight)
    grad_hidden = grad_out.astype(jnp.float32) + normalize_back(
        grad_two, normal_two, recip_two, norm_rows[2]
    )
    grad_attn = grad_hidden.astype(jnp.bfloat16)
    grad_mixed = (
        contract_last(grad_attn, out_weight)
        .astype(jnp.bfloat16)
        .reshape(frames, HEADS, features // HEADS)
    )
    query_heads, key_heads, value_heads = split_heads(packed, frames, features)
    inv_root = (features // HEADS) ** (-0.5)
    allowed = key_mask(frames, length, is_nar)
    scores = (
        jnp.einsum("qhd,khd->hqk", query_heads, key_heads, preferred_element_type=jnp.float32)
        * inv_root
    )
    probs_full = jnp.where(allowed[None], jnp.exp(scores - logsum[..., None]), 0.0)
    grad_vals = jnp.einsum(
        "hqk,qhd->khd",
        probs_full.astype(jnp.bfloat16),
        grad_mixed,
        preferred_element_type=jnp.float32,
    )
    grad_probs = jnp.einsum(
        "qhd,khd->hqk", grad_mixed, value_heads, preferred_element_type=jnp.float32
    )
    grad_scores = probs_full * (
        grad_probs - jnp.sum(probs_full * grad_probs, axis=-1, keepdims=True)
    )
    grad_scores = grad_scores.astype(jnp.bfloat16)
    grad_query = (
        jnp.einsum("hqk,khd->qhd", grad_scores, key_heads, preferred_element_type=jnp.float32)
        * inv_root
    )
    grad_keys = (
        jnp.einsum("hqk,qhd->khd", grad_scores, query_heads, preferred_element_type=jnp.float32)
        * inv_root
    )
    grad_packed = jnp.concatenate(
        [
            grad_query.reshape(frames, features),
            grad_keys.reshape(frames, features),
            grad_vals.reshape(frames, features),
        ],
        axis=1,
    ).astype(jnp.bfloat16)
    grad_one = contract_last(grad_packed, qkv_weight)
    grad_in = grad_hidden + normalize_back(grad_one, normal_one, recip_one, norm_rows[0])
    row_grads = jnp.stack(
        [
            jnp.sum(grad_one * normal_one, axis=0),
            jnp.sum(grad_one, axis=0),
            jnp.sum(grad_two * normal_two, axis=0),
            jnp.sum(grad_two, axis=0),
        ]
    )
    table_grad = jnp.where(chosen[:, None, None], row_grads[None], 0.0).reshape(tables.shape)
    pieces = (
        normed_one,
        grad_packed,
        attended,
        grad_attn,
        normed_two,
        grad_upward,
        activated,
        grad_out,
    )
    return (grad_in.astype(jnp.bfloat16), pieces, table_grad)


def weight_terms(pieces):
    normed_one, grad_packed, attended, grad_attn, normed_two, grad_upward, activated, grad_out = (
        pieces
    )
    return (
        contract_rows(normed_one, grad_packed),
        contract_rows(attended, grad_attn),
        contract_rows(normed_two, grad_upward),
        contract_rows(grad_out, activated),
    )


def per_device(
    frames_in,
    cotangent,
    qkv_weight,
    out_weight,
    up_weight,
    down_weight,
    norm_table,
    lengths,
    codebooks,
):
    sections = lax.axis_size("section")
    section_id = lax.axis_index("section")
    micro_count = lengths.shape[0]
    features = frames_in.shape[1]
    frames = frames_in.shape[0] // micro_count
    hidden_units = up_weight.shape[2]
    is_nar = section_id % 2 == 1
    weights = (qkv_weight[0], out_weight[0], up_weight[0], down_weight[0], norm_table[0])
    inputs_all = frames_in.reshape(micro_count, frames, features)
    cot_all = cotangent.reshape(micro_count, frames, features)
    layer_in = jnp.zeros_like(inputs_all)
    layer_out = jnp.zeros_like(inputs_all)
    kept_all = jax.tree.map(
        lambda leaf: jnp.zeros((micro_count,) + leaf.shape, leaf.dtype),
        empty_kept(frames, features, hidden_units),
    )
    incoming = jnp.zeros((frames, features), jnp.bfloat16)
    tick_count = micro_count + sections - 1
    for moment in range(tick_count):
        micro_id = moment - section_id
        active = (micro_id >= 0) & (micro_id < micro_count)
        micro_slot = jnp.clip(micro_id, 0, micro_count - 1)
        length = lengths[micro_slot]
        codebook = jnp.where(is_nar, codebooks[micro_slot], 0)
        own_input = lax.dynamic_index_in_dim(inputs_all, micro_slot, 0, keepdims=False)
        layer_entry = jnp.where(section_id == 0, own_input, incoming)
        output, kept_parts = lax.cond(
            active,
            lambda: layer_forward(layer_entry, weights, length, codebook, is_nar),
            lambda: (
                jnp.zeros((frames, features), jnp.bfloat16),
                empty_kept(frames, features, hidden_units),
            ),
        )
        layer_in = store_slot(layer_in, layer_entry, micro_slot, active)
        layer_out = store_slot(layer_out, output, micro_slot, active)
        kept_all = jax.tree.map(
            lambda buffer, new_value: store_slot(buffer, new_value, micro_slot, active),
            kept_all,
            kept_parts,
        )
        if moment + 1 < tick_count:
            incoming = passed_along(output, "section", 1)
    grad_in_all = jnp.zeros_like(inputs_all)
    table_acc = jnp.zeros(norm_table.shape[1:], jnp.float32)
    weight_acc = (
        jnp.zeros((features, 3 * features), jnp.float32),
        jnp.zeros((features, features), jnp.float32),
        jnp.zeros((features, hidden_units), jnp.float32),
        jnp.zeros((features, hidden_units), jnp.float32),
    )
    arriving = jnp.zeros((frames, features), jnp.bfloat16)
    positions = lax.broadcasted_iota(jnp.int32, (frames, 1), 0)
    for moment in range(tick_count):
        micro_id = moment - (sections - 1 - section_id)
        active = (micro_id >= 0) & (micro_id < micro_count)
        micro_slot = jnp.clip(micro_id, 0, micro_count - 1)
        length = lengths[micro_slot]
        codebook = jnp.where(is_nar, codebooks[micro_slot], 0)
        own_cot = lax.dynamic_index_in_dim(cot_all, micro_slot, 0, keepdims=False)
        masked_cot = jnp.where(positions < length, own_cot, jnp.zeros_like(own_cot))
        grad_out = jnp.where(section_id == sections - 1, masked_cot, arriving)
        layer_entry = lax.dynamic_index_in_dim(layer_in, micro_slot, 0, keepdims=False)
        kept_parts = jax.tree.map(
            lambda buffer: lax.dynamic_index_in_dim(buffer, micro_slot, 0, keepdims=False), kept_all
        )

        def run_back():
            return layer_backward(
                layer_entry, kept_parts, grad_out, weights, length, codebook, is_nar
            )

        def skip_back():
            return (
                jnp.zeros((frames, features), jnp.bfloat16),
                empty_pieces(frames, features, hidden_units),
                jnp.zeros(norm_table.shape[1:], jnp.float32),
            )

        grad_in, pieces, table_grad = lax.cond(active, run_back, skip_back)
        grad_in_all = store_slot(grad_in_all, grad_in, micro_slot, active)
        table_acc = table_acc + table_grad

        def add_terms():
            return tuple(
                (running + fresh for running, fresh in zip(weight_acc, weight_terms(pieces)))
            )

        weight_acc = lax.cond(active, add_terms, lambda: weight_acc)
        if moment + 1 < tick_count:
            arriving = passed_along(grad_in, "section", -1)
    summed_qkv, summed_out, summed_up, summed_down, summed_table = (
        lax.psum_scatter(weight_acc[0], "batch", scatter_dimension=0, tiled=True),
        lax.psum_scatter(weight_acc[1], "batch", scatter_dimension=0, tiled=True),
        lax.psum_scatter(weight_acc[2], "batch", scatter_dimension=0, tiled=True),
        lax.psum_scatter(weight_acc[3], "batch", scatter_dimension=0, tiled=True),
        lax.psum_scatter(table_acc, "batch", scatter_dimension=1, tiled=True),
    )
    tokens_dev = micro_count * frames
    return (
        layer_out.reshape(1, tokens_dev, features),
        grad_in_all.reshape(1, tokens_dev, features),
        summed_qkv[None],
        summed_out[None],
        summed_up[None],
        summed_down.T[None],
        summed_table[None],
    )


def solution(mesh):
    in_specs = (
        P("batch", None),
        P("batch", None),
        P("section", None, None),
        P("section", None, None),
        P("section", None, None),
        P("section", None, None),
        P("section", None, None),
        P("batch"),
        P("batch"),
    )
    out_specs = (
        P("section", "batch", None),
        P("section", "batch", None),
        P("section", "batch", None),
        P("section", "batch", None),
        P("section", "batch", None),
        P("section", None, "batch"),
        P("section", None, "batch"),
    )
    return jax.shard_map(
        per_device, mesh=mesh, in_specs=in_specs, out_specs=out_specs, check_vma=False
    )
```

profile of v0, /device:TPU:0, one launch (start us, length us, event | category | flops | bytes accessed | tf_op | source)
XLA Modules:
  0.0 1654.1 jit_solution(13214404132514010461)
XLA Ops:
  10.7 35.3 %conditional.21 = (bf16[128,1024]{1,0:T(8,128)(2,1)}, bf16[128,1024]{1,0:T(8,128)(2,1)}, f32[16,128]{1,0:T(8,128)S(1)}, f32[128,1024]{1,0:T(8,128)}, bf16[128,10...) conditional(s32[]{:T(128)} %convert_element_type.637, ...), branch_computations={%region_0.1_spmd, %region_1.9_spmd} | conditional | flops 3299193344 | bytes 69641712 | solution.py:263
  88.8 36.7 %conditional.22 = (bf16[128,1024]{1,0:T(8,128)(2,1)}, bf16[128,1024]{1,0:T(8,128)(2,1)}, f32[16,128]{1,0:T(8,128)S(1)}, f32[128,1024]{1,0:T(8,128)}, bf16[128,10...) conditional(s32[]{:T(128)} %convert_element_type.638, ...), branch_computations={%region_9.10_spmd, %region_10.18_spmd} | conditional | flops 3299062272 | bytes 66891216 | solution.py:263
  158.9 36.4 %conditional.23 = (bf16[128,1024]{1,0:T(8,128)(2,1)}, bf16[128,1024]{1,0:T(8,128)(2,1)}, f32[16,128]{1,0:T(8,128)S(1)}, f32[128,1024]{1,0:T(8,128)}, bf16[128,10...) conditional(s32[]{:T(128)} %convert_element_type.639, ...), branch_computations={%region_18.19_spmd, %region_19.27_spmd} | conditional | flops 3299062272 | bytes 66891216 | solution.py:263
  229.9 36.3 %conditional.24 = (bf16[128,1024]{1,0:T(8,128)(2,1)}, bf16[128,1024]{1,0:T(8,128)(2,1)}, f32[16,128]{1,0:T(8,128)S(1)}, f32[128,1024]{1,0:T(8,128)}, bf16[128,10...) conditional(s32[]{:T(128)} %convert_element_type.640, ...), branch_computations={%region_27.28_spmd, %region_28.36_spmd} | conditional | flops 3299062272 | bytes 66891216 | solution.py:263
  315.3 16.3 collective-permute-start.4
  366.1 8.1 collective-permute-start.5
  393.4 7.9 conditional.27
  412.0 8.4 conditional.28
  421.7 20.7 %collective-permute-done.6 = bf16[128,1024]{1,0:T(8,128)(2,1)} collective-permute-done((bf16[128,1024]{1,0:T(8,128)(2,1)}, bf16[128,1024]{1,0:T(8,128)(2,1)}, u32[]{:S(2)}, u32[]{:S(2)}) %collective-permute-start.6) | collective-permute-done | bytes 262176 | tf_op jit(solution)/shard_map/ppermute | solution.py:16
  442.4 8.5 conditional.29
  452.3 12.5 collective-permute-done.7
  464.8 8.6 conditional.30
  473.4 8.0 collective-permute-start.8
  481.5 173.1 %collective-permute-done.8 = bf16[128,1024]{1,0:T(8,128)(2,1)} collective-permute-done((bf16[128,1024]{1,0:T(8,128)(2,1)}, bf16[128,1024]{1,0:T(8,128)(2,1)}, u32[]{:S(2)}, u32[]{:S(2)}) %collective-permute-start.8) | collective-permute-done | bytes 262176 | tf_op jit(solution)/shard_map/ppermute | solution.py:16
  654.6 60.9 %conditional.31 = (bf16[128,1024]{1,0:T(8,128)(2,1)}, bf16[128,1024]{1,0:T(8,128)(2,1)}, bf16[128,3072]{0,1:T(8,128)(2,1)}, bf16[128,1024]{1,0:T(8,128)(2,1)}, b...) conditional(s32[]{:T(128)} %convert_element_type.647, ...), branch_computations={%region_111.112_spmd, %region_112.127_spmd} | conditional | flops 3411825152 | bytes 83501976 | solution.py:316
  660.4 8.6 fusion.238
  716.8 8.2 collective-permute-done.9
  725.0 61.1 %conditional.32 = (bf16[128,1024]{1,0:T(8,128)(2,1)}, bf16[128,1024]{1,0:T(8,128)(2,1)}, bf16[128,3072]{0,1:T(8,128)(2,1)}, bf16[128,1024]{1,0:T(8,128)(2,1)}, b...) conditional(s32[]{:T(128)} %convert_element_type.648, ...), branch_computations={%region_127.128_spmd, %region_128.143_spmd} | conditional | flops 3411825152 | bytes 83501976 | solution.py:316
  730.9 8.6 fusion.271
  787.3 8.2 collective-permute-done.10
  795.5 61.3 %conditional.33 = (bf16[128,1024]{1,0:T(8,128)(2,1)}, bf16[128,1024]{1,0:T(8,128)(2,1)}, bf16[128,3072]{0,1:T(8,128)(2,1)}, bf16[128,1024]{1,0:T(8,128)(2,1)}, b...) conditional(s32[]{:T(128)} %convert_element_type.649, ...), branch_computations={%region_143.144_spmd, %region_144.159_spmd} | conditional | flops 3411825152 | bytes 83501976 | solution.py:316
  801.6 8.7 fusion.304
  858.1 8.2 collective-permute-done.11
  866.3 46.8 %conditional.34 = (bf16[128,1024]{1,0:T(8,128)(2,1)S(1)}, bf16[128,1024]{1,0:T(8,128)(2,1)S(1)}, bf16[128,3072]{0,1:T(8,128)(2,1)}, bf16[128,1024]{1,0:T(8,128)(...) conditional(s32[]{:T(128)} %convert_element_type.650, ...), branch_computations={%region_159.160_spmd, %region_160.175_spmd} | conditional | flops 3411825152 | bytes 94974584 | solution.py:316
  871.5 8.6 fusion.337
  915.4 24.4 %conditional.35 = (f32[1024,3072]{1,0:T(8,128)}, f32[1024,1024]{1,0:T(8,128)}, f32[1024,4096]{1,0:T(8,128)}, f32[1024,4096]{1,0:T(8,128)}) conditional(s32[]{:T(128)} %convert_element_type.644, () %tuple.242, (bf16[128,1024]{1,0:T(8,128)(2,1)}, bf16[128,3072]{0,1:T(8,128)(2,1)}, bf16[128,1024]{1,0:T(8,128)(2,1)}, bf16[128,1024]{1,0:T(8,128)(2,1)}, ...), branch_computations={%region_175.176_spmd, %region_176.177_spmd} | conditional | flops 3221225472 | bytes 54525984 | solution.py:325
  940.0 10.5 conditional.37
  950.6 44.8 %conditional.38 = ((f32[1024,3072]{1,0:T(8,128)}, f32[1024,1024]{1,0:T(8,128)}, f32[1024,4096]{1,0:T(8,128)}, f32[1024,4096]{1,0:T(8,128)})) conditional(s32[]{:T(128)} %convert_element_type.647, (f32[1024,3072]{1,0:T(8,128)}, f32[1024,1024]{1,0:T(8,128)}, f32[1024,4096]{1,0:T(8,128)}, f32[1024,4096]{1,0:T(8,128)}) %get-tuple-element.3645, ...), branch_computations={%region_181.182_spmd, %region_182.183_spmd} | conditional | flops 3233808384 | bytes 104857640 | solution.py:325
  950.6 14.2 convolution_add_fusion.22
  969.9 11.2 convolution_add_fusion.24
  981.1 14.3 convolution_add_fusion.23
  995.3 45.0 %conditional.39 = ((f32[1024,3072]{1,0:T(8,128)}, f32[1024,1024]{1,0:T(8,128)}, f32[1024,4096]{1,0:T(8,128)}, f32[1024,4096]{1,0:T(8,128)})) conditional(s32[]{:T(128)} %convert_element_type.648, (f32[1024,3072]{1,0:T(8,128)}, f32[1024,1024]{1,0:T(8,128)}, f32[1024,4096]{1,0:T(8,128)}, f32[1024,4096]{1,0:T(8,128)}) %get-tuple-element.3646, ...), branch_computations={%region_183.184_spmd, %region_184.185_spmd} | conditional | flops 3233808384 | bytes 104857640 | solution.py:325
  995.5 14.3 convolution_add_fusion.26
  1014.8 11.2 convolution_add_fusion.28
  1026.0 14.3 convolution_add_fusion.27
  1040.3 45.2 %conditional.40 = ((f32[1024,3072]{1,0:T(8,128)}, f32[1024,1024]{1,0:T(8,128)}, f32[1024,4096]{1,0:T(8,128)}, f32[1024,4096]{1,0:T(8,128)})) conditional(s32[]{:T(128)} %convert_element_type.649, (f32[1024,3072]{1,0:T(8,128)}, f32[1024,1024]{1,0:T(8,128)}, f32[1024,4096]{1,0:T(8,128)}, f32[1024,4096]{1,0:T(8,128)}) %get-tuple-element.3647, ...), branch_computations={%region_185.186_spmd, %region_186.187_spmd} | conditional | flops 3233808384 | bytes 104857640 | solution.py:325
  1040.6 14.4 convolution_add_fusion.30
  1060.0 11.2 convolution_add_fusion.32
  1071.2 14.3 convolution_add_fusion.31
  1085.5 43.9 %conditional.41 = ((f32[1024,3072]{1,0:T(8,128)}, f32[1024,1024]{1,0:T(8,128)}, f32[1024,4096]{1,0:T(8,128)}, f32[1024,4096]{1,0:T(8,128)})) conditional(s32[]{:T(128)} %convert_element_type.650, (f32[1024,3072]{1,0:T(8,128)}, f32[1024,1024]{1,0:T(8,128)}, f32[1024,4096]{1,0:T(8,128)}, f32[1024,4096]{1,0:T(8,128)}) %get-tuple-element.3648, ...), branch_computations={%region_187.188_spmd, %region_188.189_spmd} | conditional | flops 3233808384 | bytes 108003448 | solution.py:325
  1085.8 13.9 convolution_add_fusion.34
  1104.6 10.9 convolution_add_fusion.36
  1115.5 13.8 convolution_add_fusion.35
  1130.8 17.6 %copy.178 = f32[1024,4096]{0,1:T(8,128)} copy(f32[1024,4096]{1,0:T(8,128)} %get-tuple-element.2784) | data formatting | bytes 33554432 | tf_op jit(solution)/shard_map/cond | solution.py:325
  1156.1 21.6 %reduce-scatter.8.cloned.1.call-done = f32[128,1024]{1,0:T(8,128)} async-done(((f32[1024,1024]{1,0:T(8,128)}), f32[128,1024]{1,0:T(8,128)}) %reduce-scatter.8.cloned.1.call-update) | async-done | bytes 524304 | tf_op jit(solution)/shard_map/reduce_scatter | solution.py:330
  1177.6 130.4 %reduce-scatter.6.cloned.1.call-done = f32[128,3072]{1,0:T(8,128)} async-done(((f32[1024,3072]{1,0:T(8,128)}), f32[128,3072]{1,0:T(8,128)}) %reduce-scatter.6.cloned.1.call-update) | async-done | bytes 1572880 | tf_op jit(solution)/shard_map/reduce_scatter | solution.py:329
  1308.0 169.5 %reduce-scatter.10.cloned.1.call-done = f32[128,4096]{1,0:T(8,128)} async-done(((f32[1024,4096]{1,0:T(8,128)}), f32[128,4096]{1,0:T(8,128)}) %reduce-scatter.10.cloned.1.call-update) | async-done | bytes 2097168 | tf_op jit(solution)/shard_map/reduce_scatter | solution.py:331
  1477.5 169.5 %reduce-scatter.12.cloned.1.call-done = f32[128,4096]{0,1:T(8,128)} async-done(((f32[1024,4096]{0,1:T(8,128)}), f32[128,4096]{0,1:T(8,128)}) %reduce-scatter.12.cloned.1.call-update) | async-done | bytes 2097168 | tf_op jit(solution)/shard_map/reduce_scatter | solution.py:332
  (841 shorter events, 668.7 us)
Async XLA Ops:
  7.2 1148.8 %reduce-scatter.14.cloned.1.call-start = ((), (), s32[]{:S(2)}) async-start(), calls=%async_computation.9 | async-start | bytes 147456 | tf_op jit(solution)/shard_map/reduce_scatter | solution.py:333
  33.5 9.1 slice-start.14
  46.0 41.6 %collective-permute-start = (bf16[128,1024]{1,0:T(8,128)(2,1)}, bf16[128,1024]{1,0:T(8,128)(2,1)}, u32[]{:S(2)}, u32[]{:S(2)}) collective-permute-start(bf16[128,1024]{1,0:T(8,128)(2,1)} %get-tuple-element.2631), channel_id=1, source_target_pairs={{0,8},{8,16},{16,24},{1,9},{9,17},{17,25},{2,10},{10,18},{18,26},{... | collective-permute-start | bytes 786440 | tf_op jit(solution)/shard_map/ppermute | solution.py:16
  49.1 37.1 %copy-start.17 = (bf16[4,128,1024]{2,1,0:T(8,128)(2,1)}, bf16[4,128,1024]{2,1,0:T(8,128)(2,1)S(1)}, u32[]{:S(2)}) copy-start(bf16[4,128,1024]{2,1,0:T(8,128)(2,1)S(1)} %bitcast_dynamic-update-slice_fusion.68) | copy-start | bytes 3145732
  74.5 8.6 copy-start.1
  112.9 9.1 slice-start.16
  125.5 31.5 %collective-permute-start.1 = (bf16[128,1024]{1,0:T(8,128)(2,1)}, bf16[128,1024]{1,0:T(8,128)(2,1)S(1)}, u32[]{:S(2)}, u32[]{:S(2)}) collective-permute-start(bf16[128,1024]{1,0:T(8,128)(2,1)} %get-tuple-element.2632), channel_id=1, source_target_pairs={{0,8},{8,16},{16,24},{1,9},{9,17},{17,25},{2,10},{10,18},{18,26},{... | collective-permute-start | bytes 786440 | tf_op jit(solution)/shard_map/ppermute | solution.py:16
  126.9 7.7 copy-start.61
  130.9 7.6 copy-start.38
  182.7 9.1 slice-start.18
  195.2 8.6 copy-start.63
  198.8 8.9 copy-start.39
  202.3 25.7 %collective-permute-start.2 = (bf16[128,1024]{1,0:T(8,128)(2,1)}, bf16[128,1024]{1,0:T(8,128)(2,1)S(1)}, u32[]{:S(2)}, u32[]{:S(2)}) collective-permute-start(bf16[128,1024]{1,0:T(8,128)(2,1)} %get-tuple-element.2633), channel_id=1, source_target_pairs={{0,8},{8,16},{16,24},{1,9},{9,17},{17,25},{2,10},{10,18},{18,26},{... | collective-permute-start | bytes 786440 | tf_op jit(solution)/shard_map/ppermute | solution.py:16
  220.1 7.9 copy-start.84
  253.7 9.1 slice-start.20
  266.2 8.4 copy-start.64
  269.8 8.7 copy-start.40
  273.3 25.5 %collective-permute-start.3 = (bf16[128,1024]{1,0:T(8,128)(2,1)}, bf16[128,1024]{1,0:T(8,128)(2,1)S(1)}, u32[]{:S(2)}, u32[]{:S(2)}) collective-permute-start(bf16[128,1024]{1,0:T(8,128)(2,1)} %get-tuple-element.2634), channel_id=1, source_target_pairs={{0,8},{8,16},{16,24},{1,9},{9,17},{17,25},{2,10},{10,18},{18,26},{... | collective-permute-start | bytes 786440 | tf_op jit(solution)/shard_map/ppermute | solution.py:16
  291.0 7.9 copy-start.85
  308.3 23.3 %copy-start.65 = (f32[1,128,1024]{2,1,0:T(8,128)S(1)}, f32[1,128,1024]{2,1,0:T(8,128)}, u32[]{:S(2)}) copy-start(f32[1,128,1024]{2,1,0:T(8,128)} %constant_dynamic-slice_fusion.63) | copy-start | bytes 1572868
  311.8 22.6 %copy-start.41 = (bf16[1,128,3072]{1,2,0:T(8,128)(2,1)S(1)}, bf16[1,128,3072]{1,2,0:T(8,128)(2,1)}, u32[]{:S(2)}) copy-start(bf16[1,128,3072]{1,2,0:T(8,128)(2,1)} %constant_dynamic-slice_fusion.45) | copy-start | bytes 2359300
  315.3 34.4 %collective-permute-start.4 = (bf16[128,1024]{1,0:T(8,128)(2,1)}, bf16[128,1024]{1,0:T(8,128)(2,1)S(1)}, u32[]{:S(2)}, u32[]{:S(2)}) collective-permute-start(bf16[128,1024]{1,0:T(8,128)(2,1)} %get-tuple-element.2635), channel_id=1, source_target_pairs={{0,8},{8,16},{16,24},{1,9},{9,17},{17,25},{2,10},{10,18},{18,26},{... | collective-permute-start | bytes 786440 | tf_op jit(solution)/shard_map/ppermute | solution.py:16
  359.2 15.1 copy-start.66
  362.7 14.4 copy-start.42
  366.1 26.2 %collective-permute-start.5 = (bf16[128,1024]{1,0:T(8,128)(2,1)}, bf16[128,1024]{1,0:T(8,128)(2,1)S(1)}, u32[]{:S(2)}, u32[]{:S(2)}) collective-permute-start(bf16[128,1024]{1,0:T(8,128)(2,1)} %get-tuple-element.2636), channel_id=1, source_target_pairs={{0,8},{8,16},{16,24},{1,9},{9,17},{17,25},{2,10},{10,18},{18,26},{... | collective-permute-start | bytes 786440 | tf_op jit(solution)/shard_map/ppermute | solution.py:16
  412.0 30.4 %copy-start.5 = (bf16[128,1024]{1,0:T(8,128)(2,1)S(1)}, bf16[128,1024]{1,0:T(8,128)(2,1)}, u32[]{:S(2)}) copy-start(bf16[128,1024]{1,0:T(8,128)(2,1)} %copy-done.4) | copy-start | bytes 786436
  420.4 22.0 %collective-permute-start.6 = (bf16[128,1024]{1,0:T(8,128)(2,1)}, bf16[128,1024]{1,0:T(8,128)(2,1)}, u32[]{:S(2)}, u32[]{:S(2)}) collective-permute-start(bf16[128,1024]{1,0:T(8,128)(2,1)} %get-tuple-element.2694), channel_id=1, source_target_pairs={{8,0},{16,8},{24,16},{9,1},{17,9},{25,17},{10,2},{18,10},{26,18},{... | collective-permute-start | bytes 786440 | tf_op jit(solution)/shard_map/ppermute | solution.py:16
  451.0 13.9 collective-permute-start.7
  473.4 181.2 %collective-permute-start.8 = (bf16[128,1024]{1,0:T(8,128)(2,1)}, bf16[128,1024]{1,0:T(8,128)(2,1)}, u32[]{:S(2)}, u32[]{:S(2)}) collective-permute-start(bf16[128,1024]{1,0:T(8,128)(2,1)} %get-tuple-element.2696), channel_id=1, source_target_pairs={{8,0},{16,8},{24,16},{9,1},{17,9},{25,17},{10,2},{18,10},{26,18},{... | collective-permute-start | bytes 786440 | tf_op jit(solution)/shard_map/ppermute | solution.py:16
  656.5 13.6 copy-start.157
  715.5 9.5 collective-permute-start.9
  727.1 13.6 copy-start.158
  786.0 9.5 collective-permute-start.10
  797.8 13.7 copy-start.159
  856.8 9.5 collective-permute-start.11
  871.4 8.6 copy-start.35
  915.3 262.3 %reduce-scatter.8.cloned.1.call-start = ((), (), s32[]{:S(2)}) async-start(), calls=%async_computation.6 | async-start | bytes 4718592 | tf_op jit(solution)/shard_map/reduce_scatter | solution.py:330
  1040.3 45.2 %copy-start.7 = (bf16[128,4096]{1,0:T(8,128)(2,1)S(1)}, bf16[128,4096]{1,0:T(8,128)(2,1)}, u32[]{:S(2)}) copy-start(bf16[128,4096]{1,0:T(8,128)(2,1)} %get-tuple-element.2776) | copy-start | bytes 3145732
  1040.3 45.2 %copy-start.15 = (bf16[128,3072]{0,1:T(8,128)(2,1)S(1)}, bf16[128,3072]{0,1:T(8,128)(2,1)}, u32[]{:S(2)}) copy-start(bf16[128,3072]{0,1:T(8,128)(2,1)} %get-tuple-element.2770) | copy-start | bytes 2359300
  1040.3 45.2 %copy-start.27 = (bf16[128,4096]{1,0:T(8,128)(2,1)S(1)}, bf16[128,4096]{1,0:T(8,128)(2,1)}, u32[]{:S(2)}) copy-start(bf16[128,4096]{1,0:T(8,128)(2,1)} %get-tuple-element.2779) | copy-start | bytes 3145732
  1040.3 45.2 %copy-start.37 = (bf16[128,1024]{1,0:T(8,128)(2,1)S(1)}, bf16[128,1024]{1,0:T(8,128)(2,1)}, u32[]{:S(2)}) copy-start(bf16[128,1024]{1,0:T(8,128)(2,1)} %get-tuple-element.2778) | copy-start | bytes 786436
  1040.3 45.2 %copy-start.47 = (bf16[128,1024]{1,0:T(8,128)(2,1)S(1)}, bf16[128,1024]{1,0:T(8,128)(2,1)}, u32[]{:S(2)}) copy-start(bf16[128,1024]{1,0:T(8,128)(2,1)} %copy-done.46) | copy-start | bytes 786436
  1085.8 13.9 copy-start.71
  1104.6 10.9 copy-start.67
  1129.4 178.6 %reduce-scatter.6.cloned.1.call-start = ((), (), s32[]{:S(2)}) async-start(), calls=%async_computation.5 | async-start | bytes 14155776 | tf_op jit(solution)/shard_map/reduce_scatter | solution.py:329
  1130.2 347.4 %reduce-scatter.10.cloned.1.call-start = ((), (), s32[]{:S(2)}) async-start(), calls=%async_computation.7 | async-start | bytes 18874368 | tf_op jit(solution)/shard_map/reduce_scatter | solution.py:331
  1130.7 516.3 %reduce-scatter.12.cloned.1.call-start = ((), (), s32[]{:S(2)}) async-start(), calls=%async_computation.8 | async-start | bytes 18874368 | tf_op jit(solution)/shard_map/reduce_scatter | solution.py:332
  1156.0 491.0 %copy-start.16 = (bf16[4,128,1024]{2,1,0:T(8,128)(2,1)}, bf16[4,128,1024]{2,1,0:T(8,128)(2,1)S(1)}, u32[]{:S(2)}) copy-start(bf16[4,128,1024]{2,1,0:T(8,128)(2,1)S(1)} %bitcast_dynamic-update-slice_fusion.28) | copy-start | bytes 3145732
  (116 other events, 427.2 us)
Sparse Core Ops, SparseCore 0:
  915.5 28.1 reduce-scatter.13
  1129.5 48.0 reduce-scatter.7
  1180.6 127.3 reduce-scatter.5
  1310.9 166.5 reduce-scatter.9
  1480.4 166.6 reduce-scatter.11
where the time goes:
time: 1670 us; the launch traced here: 1650 us
  waiting for transfers between devices  723 us (43%)
  matrix products  363 us (22%)
  local copies, waits for them, and re-layouts  286 us (17%)
  other arithmetic  200 us (12%)
  starting transfers between devices  45.3 us (3%)
  loops' own time  21.2 us (1%)
    ppermute x12, waiting for transfers between devices, passed_along(): return lax.ppermute(x, axis, pairs)  231 us
    dot_general x16, matrix products, contract_rows(): lax.dot_general(left_side, right_side, (((0,), (0,)), ((), ())), preferre...  178 us
    reduce_scatter x1, waiting for transfers between devices, per_device(): lax.psum_scatter(weight_acc[3], 'batch', scatter_dimension=0, tiled=True)  170 us
    reduce_scatter x1, waiting for transfers between devices, per_device(): lax.psum_scatter(weight_acc[2], 'batch', scatter_dimension=0, tiled=True)  170 us
    reduce_scatter x1, waiting for transfers between devices, per_device(): lax.psum_scatter(weight_acc[0], 'batch', scatter_dimension=0, tiled=True)  130 us
    dynamic_update_slice x75, other arithmetic, store_slot(): lax.dynamic_update_index_in_dim(buffer, jnp.where(active, new_value, old_...  109 us
    dynamic_slice x60, local copies, waits for them, and re-layouts, store_slot(): old_value = lax.dynamic_index_in_dim(buffer, micro_slot, 0, keepdims=False)  89.5 us
    dot_general x16, matrix products, contract_last(): lax.dot_general(left_side, right_side, (((1,), (1,)), ((), ())), preferre...  85.3 us
  transfers between devices with their start and end apart: 17, of which 10 were waited for; matrix products, arithmetic and copies ran while one was open for 23% of the time, Pallas kernels for 0%

commit v1 on v0

v1 whole, which is shorter than its diff:
```python
import functools
from typing import Any, NamedTuple

import jax
import jax.numpy as jnp
from jax import lax
from jax.experimental import pallas as pl
from jax.experimental.pallas import tpu as pltpu
from jax.sharding import PartitionSpec as P

HEADS = 16
GROUP = 4
BLOCK = 512
LANES = 128
CORES = 2
LINE = 4

epsilon = 1e-05
masked_score = -1e30
BF16 = jnp.bfloat16
F32 = jnp.float32

in_vmem = pl.BlockSpec(memory_space=pltpu.VMEM)
in_smem = pl.BlockSpec(memory_space=pltpu.SMEM)
anywhere = pl.BlockSpec(memory_space=pl.ANY)


class Weights(NamedTuple):
    qkv: Any
    out: Any
    up: Any
    down: Any


class Reread(NamedTuple):
    entry: Any
    packed: Any
    probs: Any
    hidden: Any
    slope: Any


class Kept(NamedTuple):
    layer_out: Any
    left_keep: Any
    left_send: Any
    act_keep: Any
    act_send: Any


class Back(NamedTuple):
    grad_in: Any
    grad_y: Any
    grad_up: Any
    grad_attn: Any
    grad_packed: Any
    row_grads: Any


def product(left, right):
    return lax.dot_general(left, right, (((1,), (0,)), ((), ())), preferred_element_type=F32)


def product_last(left, right):
    return lax.dot_general(left, right, (((1,), (1,)), ((), ())), preferred_element_type=F32)


def product_first(left, right):
    return lax.dot_general(left, right, (((0,), (0,)), ((), ())), preferred_element_type=F32)


def normalize(values):
    centre = values - jnp.mean(values, axis=-1, keepdims=True)
    reciprocal = lax.rsqrt(jnp.mean(centre * centre, axis=-1, keepdims=True) + epsilon)
    return centre * reciprocal, reciprocal


def normalize_back(gradient, normal_part, reciprocal, gain_row):
    scaled = gradient * (1.0 + gain_row)
    centred = scaled - jnp.mean(scaled, axis=-1, keepdims=True)
    return reciprocal * (
        centred - normal_part * jnp.mean(scaled * normal_part, axis=-1, keepdims=True)
    )


def gelu_and_slope(u):
    root = 0.7978845608028654
    square = u * u
    bent = jnp.tanh(root * u * (1.0 + 0.044715 * square))
    half = 0.5 * (1.0 + bent)
    slope = half + 0.5 * u * (1.0 - bent * bent) * (root * (1.0 + 3 * 0.044715 * square))
    return u * half, slope


def stacked_heads(block, head_size):
    owner = lax.broadcasted_iota(jnp.int32, block.shape, 1) // head_size
    zero = jnp.zeros_like(block)
    return jnp.concatenate([jnp.where(owner == h, block, zero) for h in range(GROUP)], axis=0)


def beside(stack, frames):
    return jnp.concatenate([stack[h * frames : (h + 1) * frames] for h in range(GROUP)], axis=1)


def table_rows(table, code):
    pair = table[pl.ds(pl.multiple_of((code // 2) * 8, 8), 8), :]
    return jnp.where(code % 2 == 1, pair[4:8], pair[0:4])


class Saver:
    def __init__(self, sems, base):
        self.sems, self.base, self.pending = sems, base, []

    def __call__(self, source, target):
        copy = pltpu.make_async_copy(source, target, self.sems.at[self.base + len(self.pending)])
        copy.start()
        self.pending.append(copy)

    def wait(self):
        for copy in self.pending:
            copy.wait()


def turn(source, target, row0, col0, side_by, strips, sems, base):
    side = 256
    ones = (
        lax.broadcasted_iota(jnp.int32, (side, side), 0)
        == lax.broadcasted_iota(jnp.int32, (side, side), 1)
    ).astype(BF16)

    slots = strips.shape[0]
    count = side_by // side

    def strip(i):
        r = pl.multiple_of(row0 + i * side, side)
        return pltpu.make_async_copy(
            strips.at[i % slots],
            target.at[pl.ds(col0, side_by), pl.ds(r, side)],
            sems.at[base + i % slots],
        )

    def one_strip(i, carry):
        @pl.when(i >= slots)
        def slot_is_free():
            strip(i - slots).wait()

        r = pl.multiple_of(row0 + i * side, side)
        for c in range(0, side_by, side):
            strips[i % slots, c : c + side, :] = product_last(
                ones, source[pl.ds(r, side), col0 + c : col0 + c + side]
            ).astype(BF16)
        strip(i).start()
        return carry

    lax.fori_loop(0, count, one_strip, 0)
    for i in range(count - slots, count):
        strip(i).wait()


class Plan(NamedTuple):
    sections: int
    micros: int
    frames: int
    features: int
    hidden_units: int
    rows: int

    def fwd_ticks(self):
        return self.micros + self.sections - 1

    def ticks(self):
        return self.micros + 2 * (self.sections - 1)

    def fwd_id(self, tick, section):
        return tick - section

    def bwd_id(self, tick, section):
        return tick - 2 * (self.sections - 1) + section


def forward_kernel(plan, tick, has_incoming, loads_weights, *refs):
    refs = list(refs)
    take = lambda n: [refs.pop(0) for _ in range(n)]
    if loads_weights:
        lengths, codebooks, given_table = take(3)
        given = Weights(*take(4))
    else:
        info, table = take(2)
        weight = Weights(*take(4))
        take(4)
    incoming = take(1)[0] if has_incoming else None
    (frames_in,) = take(1)
    if loads_weights:
        info, table = take(2)
        weight = Weights(*take(4))
    else:
        take(len(Reread._fields) + len(Kept._fields))
    turned = Weights(*take(4))
    reread = Reread(*take(5))
    kept = Kept(*take(5))
    (outgoing,) = take(1)
    entry, packed, probs, hidden, slope, normed, left, attended, act, strips, sems = refs

    micros, frames, features, hidden_units, rows_kept = plan[1:]
    head_size = features // HEADS
    group_width = GROUP * head_size
    section = lax.axis_index("section")
    core = lax.axis_index("batch") % CORES
    is_nar = section % 2
    micro = plan.fwd_id(tick, section)
    active = (micro >= 0) & (micro < micros)
    slot = jnp.clip(micro, 0, micros - 1)

    loads = []
    if loads_weights:
        for i in range(micros):
            info[i] = lengths[i]
            info[micros + i] = codebooks[i]
        pairs = [(given_table, table)] + list(zip(given, weight))
        for i, (source, target) in enumerate(pairs):
            loads.append(pltpu.make_async_copy(source, target, sems.at[i]))
            loads[i].start()
    base = len(loads)

    def ready(i):
        if loads_weights:
            loads[i].wait()

    @pl.when(active)
    def forward():
        save = Saver(sems, base)
        length = info[slot]
        code = info[micros + slot] * is_nar

        def own_input():
            pltpu.sync_copy(frames_in.at[slot], entry)

        if has_incoming:
            pl.when(section == 0)(own_input)

            @pl.when(section != 0)
            def passed_input():
                entry[...] = incoming[...]

        else:
            own_input()

        save(entry, reread.entry.at[slot])
        share = features // CORES

        def share_columns(source, first):
            for b in range(features // rows_kept):
                at = first + (b // CORES) * rows_kept
                left[b % CORES, :, at : at + rows_kept] = source[
                    :, b * rows_kept : (b + 1) * rows_kept
                ]

        ready(0)
        rows = table_rows(table, code)
        residual = entry[...].astype(F32)
        normal_one, _ = normalize(residual)
        normed[...] = (normal_one * (1.0 + rows[0:1]) + rows[1:2]).astype(BF16)
        share_columns(normed, 0)
        ready(1)
        for j in range(0, 3 * features, BLOCK):
            packed[:, j : j + BLOCK] = product(normed[...], weight.qkv[:, j : j + BLOCK]).astype(
                BF16
            )
        save(packed, reread.packed.at[slot])
        tall = (GROUP * frames, frames)
        query_ids = lax.rem(lax.broadcasted_iota(jnp.int32, tall, 0), frames)
        key_ids = lax.broadcasted_iota(jnp.int32, tall, 1)
        allowed = (key_ids < length) & (key_ids <= query_ids + is_nar * frames)
        inv_root = head_size ** (-0.5)
        for g in range(HEADS // GROUP):
            lo, hi = g * group_width, (g + 1) * group_width
            queries = stacked_heads(packed[:, lo:hi], head_size)
            keys = packed[:, features + lo : features + hi]
            values = stacked_heads(packed[:, 2 * features + lo : 2 * features + hi], head_size)
            scores = jnp.where(allowed, product_last(queries, keys) * inv_root, masked_score)
            exp_scores = jnp.exp(scores - jnp.max(scores, axis=-1, keepdims=True))
            total = jnp.sum(exp_scores, axis=-1, keepdims=True)
            group_probs = (exp_scores / total).astype(BF16)
            probs[g * GROUP * frames : (g + 1) * GROUP * frames, :] = group_probs
            attended[:, lo:hi] = product(beside(group_probs, frames), values).astype(BF16)
        save(probs, reread.probs.at[slot])
        share_columns(attended, share)
        ready(2)
        for j in range(0, features, BLOCK):
            hidden[:, j : j + BLOCK] = residual[:, j : j + BLOCK] + product(
                attended[...], weight.out[:, j : j + BLOCK]
            )
        save(hidden, reread.hidden.at[slot])
        normal_two, _ = normalize(hidden[...])
        normed[...] = (normal_two * (1.0 + rows[2:3]) + rows[3:4]).astype(BF16)
        share_columns(normed, 2 * share)
        save(left.at[core], kept.left_keep.at[slot])
        save(left.at[1 - core], kept.left_send.at[slot])
        ready(3)
        half = hidden_units // CORES
        for j in range(0, hidden_units, BLOCK):
            value, gradient = gelu_and_slope(product(normed[...], weight.up[:, j : j + BLOCK]))
            act[j // half, :, j % half : j % half + BLOCK] = value.astype(BF16)
            slope[:, j : j + BLOCK] = gradient.astype(BF16)
        save(slope, reread.slope.at[slot])
        save(act.at[core], kept.act_keep.at[slot])
        save(act.at[1 - core], kept.act_send.at[slot])
        ready(4)
        for j in range(0, features, BLOCK):
            added = hidden[:, j : j + BLOCK]
            for c in range(CORES):
                added += product(act[c], weight.down[c * half : (c + 1) * half, j : j + BLOCK])
            outgoing[:, j : j + BLOCK] = added.astype(BF16)
        save(outgoing, kept.layer_out.at[slot])
        save.wait()

    units = []
    for source, target in zip(weight, turned):
        total_rows, total_cols = source.shape
        for r in range(0, total_rows, features):
            for c in range(0, total_cols, features):
                units.append((source, target, r, c))
    pieces = 2
    piece = jnp.where(micro < 0, tick, micro - micros + section)

    @pl.when(jnp.logical_not(active))
    def wait_for_weights():
        for i in range(base):
            ready(i)

    for k in range(pieces):

        @pl.when(jnp.logical_not(active) & (piece == k))
        def one_piece(k=k):
            for source, target, r, c in units[k::pieces]:
                turn(source, target, r, c, features, strips, sems, base)


def backward_kernel(plan, tick, has_arriving, first, *refs):
    refs = list(refs)
    take = lambda n: [refs.pop(0) for _ in range(n)]
    info, table = take(2)
    turned = Weights(*take(4))
    take(4)
    arriving = take(1)[0] if has_arriving else None
    (cotangent,) = take(1)
    take(len(Reread._fields))
    if not first:
        take(len(Back._fields))
    reread = Reread(*take(5))
    back = Back(*take(6))
    (returning,) = take(1)
    (entry, packed, probs, hidden, slope, grad_y, grad_up, wide, grad_hidden, grad_attn, mixed,
     grad_packed, row_grads, sems) = refs

    micros, frames, features, hidden_units, _ = plan[1:]
    head_size = features // HEADS
    group_width = GROUP * head_size
    section = lax.axis_index("section")
    is_nar = section % 2
    micro = plan.bwd_id(tick, section)
    active = (micro >= 0) & (micro < micros)
    slot = jnp.clip(micro, 0, micros - 1)

    @pl.when(active)
    def backward():
        length = info[slot]
        code = info[micros + slot] * is_nar
        fetches = []
        for i, target in enumerate((entry, packed, probs, hidden, slope)):
            fetches.append(pltpu.make_async_copy(reread[i].at[slot], target, sems.at[i]))
        for i in (4, 3, 1, 2, 0):
            fetches[i].start()
        save = Saver(sems, len(fetches))

        def own_cotangent():
            pltpu.sync_copy(cotangent.at[slot], grad_y)
            live = lax.broadcasted_iota(jnp.int32, (frames, features), 0) < length
            grad_y[...] = jnp.where(live, grad_y[...], jnp.zeros((frames, features), BF16))

        if has_arriving:
            pl.when(section == plan.sections - 1)(own_cotangent)

            @pl.when(section != plan.sections - 1)
            def passed_gradient():
                grad_y[...] = arriving[...]

        else:
            own_cotangent()

        save(grad_y, back.grad_y.at[slot])
        rows = table_rows(table, code)
        fetches[4].wait()
        for j in range(0, hidden_units, BLOCK):
            grad_act = product(grad_y[...], turned.down[:, j : j + BLOCK])
            grad_up[:, j : j + BLOCK] = (
                grad_act * slope[:, j : j + BLOCK].astype(F32)
            ).astype(BF16)
        save(grad_up, back.grad_up.at[slot])
        for j in range(0, features, BLOCK):
            wide[:, j : j + BLOCK] = product(grad_up[...], turned.up[:, j : j + BLOCK])
        fetches[3].wait()
        normal_two, recip_two = normalize(hidden[...])
        grad_two = wide[...]
        row_grads[2:3, :] = jnp.sum(grad_two * normal_two, axis=0, keepdims=True)
        row_grads[3:4, :] = jnp.sum(grad_two, axis=0, keepdims=True)
        grad_hidden[...] = grad_y[...].astype(F32) + normalize_back(
            grad_two, normal_two, recip_two, rows[2:3]
        )
        grad_attn[...] = grad_hidden[...].astype(BF16)
        save(grad_attn, back.grad_attn.at[slot])
        for j in range(0, features, BLOCK):
            mixed[:, j : j + BLOCK] = product(
                grad_attn[...], turned.out[:, j : j + BLOCK]
            ).astype(BF16)
        fetches[1].wait()
        fetches[2].wait()
        inv_root = head_size ** (-0.5)
        for g in range(HEADS // GROUP):
            lo, hi = g * group_width, (g + 1) * group_width
            queries = stacked_heads(packed[:, lo:hi], head_size)
            keys = stacked_heads(packed[:, features + lo : features + hi], head_size)
            values = packed[:, 2 * features + lo : 2 * features + hi]
            group_mixed = stacked_heads(mixed[:, lo:hi], head_size)
            group_probs = probs[g * GROUP * frames : (g + 1) * GROUP * frames, :]
            wide_probs = group_probs.astype(F32)
            grad_probs = product_last(group_mixed, values)
            inner = jnp.sum(wide_probs * grad_probs, axis=-1, keepdims=True)
            grad_scores = (wide_probs * (grad_probs - inner)).astype(BF16)
            grad_packed[:, lo:hi] = (
                product(beside(grad_scores, frames), keys) * inv_root
            ).astype(BF16)
            grad_packed[:, features + lo : features + hi] = (
                product_first(grad_scores, queries) * inv_root
            ).astype(BF16)
            grad_packed[:, 2 * features + lo : 2 * features + hi] = product_first(
                group_probs, group_mixed
            ).astype(BF16)
        save(grad_packed, back.grad_packed.at[slot])
        for j in range(0, features, BLOCK):
            wide[:, j : j + BLOCK] = product(grad_packed[...], turned.qkv[:, j : j + BLOCK])
        fetches[0].wait()
        normal_one, recip_one = normalize(entry[...].astype(F32))
        grad_one = wide[...]
        row_grads[0:1, :] = jnp.sum(grad_one * normal_one, axis=0, keepdims=True)
        row_grads[1:2, :] = jnp.sum(grad_one, axis=0, keepdims=True)
        save(row_grads, back.row_grads.at[slot])
        returning[...] = (
            grad_hidden[...] + normalize_back(grad_one, normal_one, recip_one, rows[0:1])
        ).astype(BF16)
        save(returning, back.grad_in.at[slot])
        save.wait()


def shapes_of(plan):
    micros, frames, features, hidden_units, _ = plan[1:]
    own = (micros, frames)
    reread = Reread(
        entry=(own + (features,), BF16),
        packed=(own + (3 * features,), BF16),
        probs=((micros, HEADS * frames, frames), BF16),
        hidden=(own + (features,), F32),
        slope=(own + (hidden_units,), BF16),
    )
    share = (own + (3 * features // CORES,), BF16)
    half = (own + (hidden_units // CORES,), BF16)
    kept = Kept((own + (features,), BF16), share, share, half, half)
    wide = (own + (features,), BF16)
    back = Back(
        grad_in=wide,
        grad_y=wide,
        grad_up=(own + (hidden_units,), BF16),
        grad_attn=wide,
        grad_packed=(own + (3 * features,), BF16),
        row_grads=((micros, 4, features), F32),
    )
    return reread, kept, back


def scratch_of(shapes):
    return [pltpu.VMEM(shape[1:], dtype) for shape, dtype in shapes]


class Call:
    def __init__(self):
        self.args, self.in_specs, self.out_shape, self.out_specs = [], [], [], []
        self.aliases = {}

    def take(self, values, spec, space=None):
        for value in values:
            if space is not None:
                value = pltpu.with_memory_space_constraint(value, space)
            self.args.append(value)
            self.in_specs.append(spec)

    def give(self, shapes, spec, space, updates=None):
        for i, (shape, dtype) in enumerate(shapes):
            if updates is not None:
                self.aliases[updates + i] = len(self.out_shape)
            self.out_shape.append(space(shape, dtype))
            self.out_specs.append(spec)

    def run(self, body, scratch, flops):
        return list(
            pl.pallas_call(
                body,
                out_shape=self.out_shape,
                in_specs=self.in_specs,
                out_specs=self.out_specs,
                scratch_shapes=scratch,
                input_output_aliases=self.aliases,
                compiler_params=pltpu.CompilerParams(vmem_limit_bytes=10 * 2**20),
                cost_estimate=pl.CostEstimate(
                    flops=flops, bytes_accessed=2**22, transcendentals=0
                ),
            )(*self.args)
        )


def like(arrays):
    return [(x.shape, x.dtype) for x in arrays]


class State(NamedTuple):
    numbers: Any
    info: Any
    table: Any
    weights: Any
    turned: Any = None
    reread: Any = None
    kept: Any = None
    back: Any = None


def run_forward(plan, tick, state, incoming, frames_in):
    reread_shapes, kept_shapes, _ = shapes_of(plan)
    first = state.turned is None
    at_turned = at_kept = None
    call = Call()
    if first:
        call.take(state.numbers, in_smem)
        call.take([state.table], anywhere)
        call.take(state.weights, anywhere)
    else:
        call.take([state.info], in_smem, pltpu.SMEM)
        call.take([state.table], in_vmem, pltpu.VMEM)
        call.take(state.weights, in_vmem, pltpu.VMEM)
        at_turned = len(call.args)
        call.take(state.turned, anywhere, pltpu.VMEM)
    if incoming is not None:
        call.take([incoming], in_vmem, pltpu.VMEM)
    call.take([frames_in], anywhere)
    if first:
        call.give([((2 * plan.micros,), jnp.int32)], in_smem, pltpu.SMEM)
        call.give(like([state.table]), in_vmem, pltpu.VMEM)
        call.give(like(state.weights), in_vmem, pltpu.VMEM)
    else:
        at_kept = len(call.args)
        call.take(state.reread + state.kept, anywhere, pltpu.HBM)
    call.give([(w.shape[::-1], BF16) for w in state.weights], anywhere, pltpu.VMEM, at_turned)
    call.give(reread_shapes + kept_shapes, anywhere, pltpu.HBM, at_kept)
    call.give([((plan.frames, plan.features), BF16)], in_vmem, pltpu.VMEM)
    scratch = scratch_of(reread_shapes) + [
        pltpu.VMEM((plan.frames, plan.features), BF16),
        pltpu.VMEM((CORES, plan.frames, 3 * plan.features // CORES), BF16),
        pltpu.VMEM((plan.frames, plan.features), BF16),
        pltpu.VMEM((CORES, plan.frames, plan.hidden_units // CORES), BF16),
        pltpu.VMEM((2, plan.features, 256), BF16),
        pltpu.SemaphoreType.DMA((24,)),
    ]
    flops = 2 * plan.frames * sum(w.size for w in state.weights)
    body = functools.partial(forward_kernel, plan, tick, incoming is not None, first)
    got = call.run(body, scratch, flops)
    if first:
        state = state._replace(info=got[0], table=got[1], weights=Weights(*got[2:6]))
        got = got[6:]
    state = state._replace(
        turned=Weights(*got[:4]), reread=Reread(*got[4:9]), kept=Kept(*got[9:14])
    )
    return state, got[14]


def run_backward(plan, tick, state, arriving, cotangent):
    reread_shapes, _, back_shapes = shapes_of(plan)
    first = state.back is None
    call = Call()
    call.take([state.info], in_smem, pltpu.SMEM)
    call.take([state.table], in_vmem, pltpu.VMEM)
    call.take(state.turned, in_vmem, pltpu.VMEM)
    call.take(state.weights, anywhere, pltpu.VMEM)
    if arriving is not None:
        call.take([arriving], in_vmem, pltpu.VMEM)
    call.take([cotangent], anywhere)
    at_reread = len(call.args)
    call.take(state.reread, anywhere, pltpu.HBM)
    at_back = None
    if not first:
        at_back = len(call.args)
        call.take(state.back, anywhere, pltpu.HBM)
    call.give(reread_shapes, anywhere, pltpu.HBM, at_reread)
    call.give(back_shapes, anywhere, pltpu.HBM, at_back)
    call.give([((plan.frames, plan.features), BF16)], in_vmem, pltpu.VMEM)
    narrow = pltpu.VMEM((plan.frames, plan.features), BF16)
    full = pltpu.VMEM((plan.frames, plan.features), F32)
    scratch = scratch_of(reread_shapes) + [
        narrow,
        pltpu.VMEM((plan.frames, plan.hidden_units), BF16),
        full,
        full,
        narrow,
        narrow,
        pltpu.VMEM((plan.frames, 3 * plan.features), BF16),
        pltpu.VMEM((4, plan.features), F32),
        pltpu.SemaphoreType.DMA((16,)),
    ]
    flops = 2 * plan.frames * sum(w.size for w in state.turned)
    body = functools.partial(backward_kernel, plan, tick, arriving is not None, first)
    got = call.run(body, scratch, flops)
    return state._replace(reread=Reread(*got[:5]), back=Back(*got[5:11])), got[11]


def weight_grad_kernel(count, first_column, width, *refs):
    lefts, rights, out = refs[:count], refs[count : 2 * count], refs[2 * count]
    stage, turned, sems = refs[2 * count + 1 :]
    micros, frames, step = rights[0].shape

    @pl.when(pl.program_id(0) == 0)
    def turn_lefts():
        copies = []
        for i, left in enumerate(lefts):
            part = left.at[:, :, pl.ds(first_column, width)]
            copies.append(pltpu.make_async_copy(part, stage.at[i], sems.at[i]))
            copies[i].start()
        for i in range(count):
            copies[i].wait()
            for m in range(micros):
                turned[i, :, m * frames : (m + 1) * frames] = stage[i, m].T

    total = None
    for i in range(count):
        term = product(turned[i], rights[i][...].reshape(micros * frames, step))
        total = term if total is None else total + term
    out[...] = total.astype(BF16)


def weight_grad(lefts, rights, first_column, width):
    count = len(lefts)
    micros, frames, columns = rights[0].shape
    step = min(columns, BLOCK)
    return pl.pallas_call(
        functools.partial(weight_grad_kernel, count, first_column, width),
        grid=(columns // step,),
        out_shape=jax.ShapeDtypeStruct((width, columns), BF16),
        in_specs=[anywhere] * count
        + [pl.BlockSpec((micros, frames, step), lambda j: (0, 0, j))] * count,
        out_specs=pl.BlockSpec((width, step), lambda j: (0, j)),
        scratch_shapes=[
            pltpu.VMEM((count, micros, frames, width), BF16),
            pltpu.VMEM((count, width, micros * frames), BF16),
            pltpu.SemaphoreType.DMA((count,)),
        ],
        compiler_params=pltpu.CompilerParams(vmem_limit_bytes=12 * 2**20),
        cost_estimate=pl.CostEstimate(
            flops=2 * count * micros * frames * width * columns,
            bytes_accessed=2 * width * columns,
            transcendentals=0,
        ),
    )(*lefts, *rights)


def pick(parts, index):
    return lax.dynamic_index_in_dim(parts, index, 0, keepdims=False)


def line_sum(parts, chip, chips):
    def hop(value, sends, by):
        pairs = []
        for z in range(chips):
            if 0 <= z + by < chips and sends(z):
                pairs += [(CORES * z + c, CORES * (z + by) + c) for c in range(CORES)]
        return lax.ppermute(value, "batch", pairs)

    last = chips - 1
    up = pick(parts, jnp.minimum(chip + last, last))
    down = pick(parts, jnp.maximum(chip - last, 0))
    for k in range(1, chips):
        came_up = hop(up, lambda z: z < k, 1).astype(F32)
        came_down = hop(down, lambda z: z > last - k, -1).astype(F32)
        if k < last:
            here_up = pick(parts, jnp.minimum(chip + last - k, last)).astype(F32)
            here_down = pick(parts, jnp.maximum(chip - last + k, 0)).astype(F32)
            up = (here_up + came_up).astype(BF16)
            down = (here_down + came_down).astype(BF16)
    return pick(parts, chip).astype(F32) + came_up + came_down


def table_gradient(row_grads, codes, blocks):
    chosen = lax.broadcasted_iota(jnp.int32, (blocks, codes.shape[0]), 0) == codes
    return jnp.sum(jnp.where(chosen[:, :, None, None], row_grads[None], 0.0), axis=1)


def sums_by_hops(plan, kept, back, table_grad, batch, index):
    chips = batch // CORES
    core, chip = index % CORES, index // CORES
    features, hidden_units = plan.features, plan.hidden_units
    share = features // CORES
    rows = plan.rows
    swap = lambda x: lax.ppermute(x, "batch", [(b, b ^ 1) for b in range(batch)])

    left_peer = swap(kept.left_send)
    act_peer = swap(kept.act_send)
    y_peer = swap(back.grad_y)
    up_peer = swap(back.grad_up)
    attn_peer = swap(back.grad_attn)
    packed_peer = swap(back.grad_packed)

    lefts = [kept.left_keep, left_peer]
    down = weight_grad([back.grad_y, y_peer], [kept.act_keep, act_peer], 0, features)
    up = weight_grad(lefts, [back.grad_up, up_peer], 2 * share, share)
    out = weight_grad(lefts, [back.grad_attn, attn_peer], share, share)
    qkv = weight_grad(lefts, [back.grad_packed, packed_peer], 0, share)

    norms = table_grad.reshape(-1, chips, CORES, rows).transpose(2, 1, 0, 3)
    norms = pick(norms, core) + swap(pick(norms, 1 - core))

    down = line_sum(down.reshape(chips, CORES * rows, hidden_units // CORES), chip, chips)
    up = line_sum(up.reshape(chips, rows, hidden_units), chip, chips)
    qkv = line_sum(qkv.reshape(chips, rows, 3 * features), chip, chips)
    out = line_sum(out.reshape(chips, rows, features), chip, chips)
    norms = line_sum(norms, chip, chips)

    own_rows = lax.dynamic_slice_in_dim(down, core * rows, rows, 0)
    peer_rows = swap(lax.dynamic_slice_in_dim(down, (1 - core) * rows, rows, 0).astype(BF16))
    peer_rows = peer_rows.astype(F32)
    first = jnp.where(core == 0, own_rows, peer_rows)
    second = jnp.where(core == 0, peer_rows, own_rows)
    down = jnp.concatenate([first, second], axis=1).T
    return qkv, out, up, down, norms


def sums_by_scatter(plan, kept, back, table_grad, index):
    features = plan.features
    share = features // CORES
    core = index % CORES

    def local(right, column):
        mine = weight_grad([kept.left_keep], [right], column, share)
        other = weight_grad([kept.left_send], [right], column, share)
        even, odd = jnp.where(core == 0, mine, other), jnp.where(core == 0, other, mine)
        blocks = [x.reshape(-1, 1, plan.rows, x.shape[1]) for x in (even, odd)]
        return jnp.concatenate(blocks, axis=1).reshape(features, -1)

    def scattered(x, dimension):
        return lax.psum_scatter(
            x, "batch", scatter_dimension=dimension, tiled=True
        ).astype(F32)

    mine = weight_grad([back.grad_y], [kept.act_keep], 0, features)
    other = weight_grad([back.grad_y], [kept.act_send], 0, features)
    even, odd = jnp.where(core == 0, mine, other), jnp.where(core == 0, other, mine)
    down = jnp.concatenate([even, odd], axis=1)
    return (
        scattered(local(back.grad_packed, 0), 0),
        scattered(local(back.grad_attn, share), 0),
        scattered(local(back.grad_up, 2 * share), 0),
        scattered(down, 0).T,
        scattered(table_grad, 1),
    )


def per_device(
    frames_in, cotangent, qkv_weight, out_weight, up_weight, down_weight, norm_table, lengths,
    codebooks,
):
    sections = lax.axis_size("section")
    batch = lax.axis_size("batch")
    section = lax.axis_index("section")
    micros = lengths.shape[0]
    tokens, features = frames_in.shape
    frames = tokens // micros
    plan = Plan(
        sections, micros, frames, features, up_weight.shape[2], max(features // batch, LANES)
    )
    frames_all = frames_in.reshape(micros, frames, features)
    cot_all = cotangent.reshape(micros, frames, features)

    state = State(
        numbers=[lengths, codebooks],
        info=None,
        table=norm_table[0],
        weights=Weights(qkv_weight[0], out_weight[0], up_weight[0], down_weight[0]),
    )
    incoming = arriving = None
    working = lambda micro: 0 <= micro < micros
    for tick in range(plan.ticks()):
        sent = returned = None
        if tick < plan.fwd_ticks():
            state, output = run_forward(plan, tick, state, incoming, frames_all)
            onward = [
                (s, s + 1) for s in range(sections - 1) if working(plan.fwd_id(tick, s))
            ]
            if onward:
                sent = lax.ppermute(output, "section", onward)
        if tick >= sections - 1:
            state, output = run_backward(plan, tick, state, arriving, cot_all)
            backward = [
                (s, s - 1) for s in range(1, sections) if working(plan.bwd_id(tick, s))
            ]
            if backward:
                returned = lax.ppermute(output, "section", backward)
        incoming, arriving = sent, returned

    blocks = norm_table.shape[1] // 4
    codes = codebooks * (section % 2)
    table_grad = table_gradient(state.back.row_grads, codes, blocks).reshape(norm_table.shape[1:])
    index = lax.axis_index("batch")
    if batch % CORES == 0 and CORES < batch <= CORES * LINE:
        sums = sums_by_hops(plan, state.kept, state.back, table_grad, batch, index)
    else:
        sums = sums_by_scatter(plan, state.kept, state.back, table_grad, index)
    return (
        state.kept.layer_out.reshape(1, tokens, features),
        state.back.grad_in.reshape(1, tokens, features),
    ) + tuple(x[None] for x in sums)


def solution(mesh):
    section, batch = mesh.axis_names
    over_batch = P(batch)
    over_section = P(section)
    both = P(section, batch, None)
    columns = P(section, None, batch)
    in_specs = (over_batch,) * 2 + (over_section,) * 5 + (over_batch,) * 2
    out_specs = (both,) * 5 + (columns,) * 2
    return jax.shard_map(
        per_device, mesh=mesh, in_specs=in_specs, out_specs=out_specs, check_vma=False
    )
```

time: 1670 us -> 505 us (0.30)
  the two profiles are of different devices: /device:TPU:0 before, /device:TPU:8 now
where the time goes in v1:
time: 505 us; the launch traced here: 496 us
  waiting for transfers between devices  200 us (40%)
  Pallas kernels  146 us (29%)
  starting transfers between devices  101 us (20%)
  local copies, waits for them, and re-layouts  27.1 us (5%)
  other arithmetic  20 us (4%)
    ppermute x30, waiting for transfers between devices, hop(): return lax.ppermute(value, 'batch', pairs)  146 us
    pallas_call x14, Pallas kernels, run(): pl.pallas_call(body, out_shape=self.out_shape, in_specs=self.in_specs, ou...  120 us
    ppermute x30, starting transfers between devices, hop(): return lax.ppermute(value, 'batch', pairs)  73.8 us
    ppermute x6, waiting for transfers between devices, per_device(): returned = lax.ppermute(output, 'section', backward)  36.2 us
    pallas_call x4, Pallas kernels, weight_grad(): pl.pallas_call(functools.partial(weight_grad_kernel, count, first_column,...  25.7 us
    unnamed x41, local copies, waits for them, and re-layouts  18.7 us
    ppermute x6, starting transfers between devices, per_device(): sent = lax.ppermute(output, 'section', onward)  18.4 us
    ppermute x6, waiting for transfers between devices, per_device(): sent = lax.ppermute(output, 'section', onward)  17.6 us
  transfers between devices with their start and end apart: 50, of which 20 were waited for; matrix products, arithmetic and copies ran while one was open for 8% of the time, Pallas kernels for 15%

profile of v1, /device:TPU:8, one launch (start us, length us, event | category | flops | bytes accessed | tf_op | source)
XLA Modules:
  0.0 495.9 jit_solution(15270529946026383444)
XLA Ops:
  0.6 17.2 %shard_map.144 = (s32[8]{0:T(128)S(4)}, f32[32,1024]{1,0:T(8,128)S(1)}, bf16[1024,3072]{1,0:T(8,128)(2,1)S(1)}, bf16[1024,1024]{1,0:T(8,128)(2,1)S(1)}, bf16[102...) custom-call(s32[4]{0:T(128)} %refs_0_.1, ...), custom_call_target="tpu_custom_call" | custom-call | flops 3221225472 | bytes 4194304 | tf_op jit(solution)/shard_map/pallas_call | solution.py:505
  17.9 5.3 %collective-permute-start = (bf16[128,1024]{1,0:T(8,128)(2,1)S(1)}, bf16[128,1024]{1,0:T(8,128)(2,1)S(1)}, u32[]{:S(2)}, u32[]{:S(2)}) collective-permute-start(bf16[128,1024]{1,0:T(8,128)(2,1)S(1)} %get-tuple-element.205), channel_id=1, source_target_pairs={{0,8},{1,9},{2,10},{3,11},{4,12},{5,13},{6,14},{7,15}} | collective-permute-start | bytes 786440 | tf_op jit(solution)/shard_map/ppermute | solution.py:803
  23.2 5.5 %collective-permute-done.refs_10_ = bf16[128,1024]{1,0:T(8,128)(2,1)S(1)} collective-permute-done((bf16[128,1024]{1,0:T(8,128)(2,1)S(1)}, bf16[128,1024]{1,0:T(8,128)(2,1)S(1)}, u32[]{:S(2)}, u32[]{:S(2)}) %collective-permute-start) | collective-permute-done | bytes 262176 | tf_op jit(solution)/shard_map/ppermute | solution.py:803
  28.7 9.6 %shard_map.145 = (bf16[3072,1024]{1,0:T(8,128)(2,1)S(1)}, bf16[1024,1024]{1,0:T(8,128)(2,1)S(1)}, bf16[4096,1024]{1,0:T(8,128)(2,1)S(1)}, bf16[1024,4096]{1,0:T(...) custom-call(s32[8]{0:T(128)S(4)} %get-tuple-element.195.refs_0_, ...), custom_call_target="tpu_custom_call", output_to_operand_aliasing={{0}: (6, {}), {1}: (7, {}), {2}: (8, {}), {3}: (9, {}), {4}... | custom-call | flops 3221225472 | bytes 4194304 | tf_op jit(solution)/shard_map/pallas_call | solution.py:505
  38.4 3.5 collective-permute-start.1
  41.9 4.7 collective-permute-done.1.refs_10_
  46.5 8.9 %shard_map.146 = (bf16[3072,1024]{1,0:T(8,128)(2,1)S(1)}, bf16[1024,1024]{1,0:T(8,128)(2,1)S(1)}, bf16[4096,1024]{1,0:T(8,128)(2,1)S(1)}, bf16[1024,4096]{1,0:T(...) custom-call(s32[8]{0:T(128)S(4)} %get-tuple-element.195.refs_0_, ...), custom_call_target="tpu_custom_call", output_to_operand_aliasing={{0}: (6, {}), {1}: (7, {}), {2}: (8, {}), {3}: (9, {}), {4}... | custom-call | flops 3221225472 | bytes 4194304 | tf_op jit(solution)/shard_map/pallas_call | solution.py:505
  55.4 3.9 collective-permute-start.2
  59.3 4.7 collective-permute-done.2.refs_10_
  64.0 10.2 %shard_map.147 = (bf16[3072,1024]{1,0:T(8,128)(2,1)S(1)}, bf16[1024,1024]{1,0:T(8,128)(2,1)S(1)}, bf16[4096,1024]{1,0:T(8,128)(2,1)S(1)}, bf16[1024,4096]{1,0:T(...) custom-call(s32[8]{0:T(128)S(4)} %get-tuple-element.195.refs_0_, ...), custom_call_target="tpu_custom_call", output_to_operand_aliasing={{0}: (6, {}), {1}: (7, {}), {2}: (8, {}), {3}: (9, {}), {4}... | custom-call | flops 3221225472 | bytes 4194304 | tf_op jit(solution)/shard_map/pallas_call | solution.py:505
  74.2 4.4 collective-permute-start.3
  79.6 2.8 collective-permute-done.3.refs_10_
  82.4 12.4 %shard_map.149 = (bf16[3072,1024]{1,0:T(8,128)(2,1)S(1)}, bf16[1024,1024]{1,0:T(8,128)(2,1)S(1)}, bf16[4096,1024]{1,0:T(8,128)(2,1)S(1)}, bf16[1024,4096]{1,0:T(...) custom-call(s32[8]{0:T(128)S(4)} %get-tuple-element.195.refs_0_, ...), custom_call_target="tpu_custom_call", output_to_operand_aliasing={{0}: (6, {}), {1}: (7, {}), {2}: (8, {}), {3}: (9, {}), {4}... | custom-call | flops 3221225472 | bytes 4194304 | tf_op jit(solution)/shard_map/pallas_call | solution.py:505
  96.4 16.3 %shard_map.151 = (bf16[3072,1024]{1,0:T(8,128)(2,1)S(1)}, bf16[1024,1024]{1,0:T(8,128)(2,1)S(1)}, bf16[4096,1024]{1,0:T(8,128)(2,1)S(1)}, bf16[1024,4096]{1,0:T(...) custom-call(s32[8]{0:T(128)S(4)} %get-tuple-element.195.refs_0_, ...), custom_call_target="tpu_custom_call", output_to_operand_aliasing={{0}: (6, {}), {1}: (7, {}), {2}: (8, {}), {3}: (9, {}), {4}... | custom-call | flops 3221225472 | bytes 4194304 | tf_op jit(solution)/shard_map/pallas_call | solution.py:505
  115.0 9.8 %shard_map.153 = (bf16[3072,1024]{1,0:T(8,128)(2,1)S(1)}, bf16[1024,1024]{1,0:T(8,128)(2,1)S(1)}, bf16[4096,1024]{1,0:T(8,128)(2,1)S(1)}, bf16[1024,4096]{1,0:T(...) custom-call(s32[8]{0:T(128)S(4)} %get-tuple-element.195.refs_0_, ...), custom_call_target="tpu_custom_call", output_to_operand_aliasing={{0}: (6, {}), {1}: (7, {}), {2}: (8, {}), {3}: (9, {}), {4}... | custom-call | flops 3221225472 | bytes 4194304 | tf_op jit(solution)/shard_map/pallas_call | solution.py:505
  124.8 10.0 %collective-permute-done.8.refs_10_ = bf16[128,1024]{1,0:T(8,128)(2,1)S(1)} collective-permute-done((bf16[128,1024]{1,0:T(8,128)(2,1)S(1)}, bf16[128,1024]{1,0:T(8,128)(2,1)S(1)}, u32[]{:S(2)}, u32[]{:S(2)}) %collective-permute-start.8) | collective-permute-done | bytes 262176 | tf_op jit(solution)/shard_map/ppermute | solution.py:810
  134.8 8.5 %shard_map.154 = (bf16[4,128,1024]{2,1,0:T(8,128)(2,1)}, bf16[4,128,3072]{2,1,0:T(8,128)(2,1)}, bf16[4,2048,128]{2,1,0:T(8,128)(2,1)}, f32[4,128,1024]{2,1,0:T(8...) custom-call(s32[8]{0:T(128)S(4)} %get-tuple-element.195.refs_0_, ...), custom_call_target="tpu_custom_call", output_to_operand_aliasing={{0}: (12, {}), {1}: (13, {}), {2}: (14, {}), {3}: (15, {}),... | custom-call | flops 3221225472 | bytes 4194304 | tf_op jit(solution)/shard_map/pallas_call | solution.py:505
  144.5 10.5 %collective-permute-done.9.refs_10_ = bf16[128,1024]{1,0:T(8,128)(2,1)S(1)} collective-permute-done((bf16[128,1024]{1,0:T(8,128)(2,1)S(1)}, bf16[128,1024]{1,0:T(8,128)(2,1)S(1)}, u32[]{:S(2)}, u32[]{:S(2)}) %collective-permute-start.9) | collective-permute-done | bytes 262176 | tf_op jit(solution)/shard_map/ppermute | solution.py:810
  155.0 8.5 %shard_map.155 = (bf16[4,128,1024]{2,1,0:T(8,128)(2,1)}, bf16[4,128,3072]{2,1,0:T(8,128)(2,1)}, bf16[4,2048,128]{2,1,0:T(8,128)(2,1)}, f32[4,128,1024]{2,1,0:T(8...) custom-call(s32[8]{0:T(128)S(4)} %get-tuple-element.195.refs_0_, ...), custom_call_target="tpu_custom_call", output_to_operand_aliasing={{0}: (12, {}), {1}: (13, {}), {2}: (14, {}), {3}: (15, {}),... | custom-call | flops 3221225472 | bytes 4194304 | tf_op jit(solution)/shard_map/pallas_call | solution.py:505
  165.0 9.1 %collective-permute-done.10.refs_10_ = bf16[128,1024]{1,0:T(8,128)(2,1)S(1)} collective-permute-done((bf16[128,1024]{1,0:T(8,128)(2,1)S(1)}, bf16[128,1024]{1,0:T(8,128)(2,1)S(1)}, u32[]{:S(2)}, u32[]{:S(2)}) %collective-permute-start.10) | collective-permute-done | bytes 262176 | tf_op jit(solution)/shard_map/ppermute | solution.py:810
  174.0 8.5 %shard_map.156 = (bf16[4,128,1024]{2,1,0:T(8,128)(2,1)}, bf16[4,128,3072]{2,1,0:T(8,128)(2,1)}, bf16[4,2048,128]{2,1,0:T(8,128)(2,1)}, f32[4,128,1024]{2,1,0:T(8...) custom-call(s32[8]{0:T(128)S(4)} %get-tuple-element.195.refs_0_, ...), custom_call_target="tpu_custom_call", output_to_operand_aliasing={{0}: (12, {}), {1}: (13, {}), {2}: (14, {}), {3}: (15, {}),... | custom-call | flops 3221225472 | bytes 4194304 | tf_op jit(solution)/shard_map/pallas_call | solution.py:505
  184.4 6.7 %collective-permute-done.11.refs_10_ = bf16[128,1024]{1,0:T(8,128)(2,1)S(1)} collective-permute-done((bf16[128,1024]{1,0:T(8,128)(2,1)S(1)}, bf16[128,1024]{1,0:T(8,128)(2,1)S(1)}, u32[]{:S(2)}, u32[]{:S(2)}) %collective-permute-start.11) | collective-permute-done | bytes 262176 | tf_op jit(solution)/shard_map/ppermute | solution.py:810
  191.0 9.4 %shard_map.157 = (bf16[4,128,1024]{2,1,0:T(8,128)(2,1)}, bf16[4,128,3072]{2,1,0:T(8,128)(2,1)}, bf16[4,2048,128]{2,1,0:T(8,128)(2,1)}, f32[4,128,1024]{2,1,0:T(8...) custom-call(s32[8]{0:T(128)S(4)} %get-tuple-element.195.refs_0_, ...), custom_call_target="tpu_custom_call", output_to_operand_aliasing={{0}: (12, {}), {1}: (13, {}), {2}: (14, {}), {3}: (15, {}),... | custom-call | flops 3221225472 | bytes 4194304 | tf_op jit(solution)/shard_map/pallas_call | solution.py:505
  217.0 8.7 %collective-permute-done.21 = bf16[128,1024]{1,0:T(8,128)(2,1)S(1)} collective-permute-done((bf16[128,1024]{1,0:T(8,128)(2,1)S(1)}, bf16[128,1024]{1,0:T(8,128)(2,1)S(1)}, u32[]{:S(2)}, u32[]{:S(2)}) %collective-permute-start.21) | collective-permute-done | bytes 262176 | tf_op jit(solution)/shard_map/ppermute | solution.py:681
  231.7 8.1 %shard_map.161 = bf16[1024,2048]{1,0:T(8,128)(2,1)S(1)} custom-call(bf16[4,128,1024]{2,1,0:T(8,128)(2,1)S(1)} %copy-done.6, bf16[4,128,1024]{2,1,0:T(8,128)(2,1)} %collective-permute-done.34.refs_1_, bf16[4,128,2048]{2,1,0:T(8,128)(2,1)S(1)} %copy-done.4, bf16[4,128,2048]{2,1,0:T(8,128)(2,1)} %collective-permute-done.35.refs_3_), custom_call_target="tpu_custom_call" | custom-call | flops 4294967296 | bytes 4194304 | tf_op jit(solution)/shard_map/pallas_call | solution.py:650
  239.8 3.0 constant_dynamic-slice_fusion.15
  242.8 2.3 copy.189
  251.2 5.5 %collective-permute-start.46 = (bf16[32,128]{1,0:T(8,128)(2,1)S(1)}, bf16[32,128]{1,0:T(8,128)(2,1)S(1)}, u32[]{:S(2)}, u32[]{:S(2)}) collective-permute-start(bf16[32,128]{1,0:T(8,128)(2,1)S(1)} %add_convert_fusion.2), channel_id=1, source_target_pairs={{0,2},{1,3},{2,4},{3,5},{4,6},{5,7},{8,10},{9,11},{10,12},{11,13},... | collective-permute-start | bytes 24584 | tf_op jit(solution)/shard_map/ppermute | solution.py:681
  256.8 16.3 %collective-permute-done.46 = bf16[32,128]{1,0:T(8,128)(2,1)S(1)} collective-permute-done((bf16[32,128]{1,0:T(8,128)(2,1)S(1)}, bf16[32,128]{1,0:T(8,128)(2,1)S(1)}, u32[]{:S(2)}, u32[]{:S(2)}) %collective-permute-start.46) | collective-permute-done | bytes 8224 | tf_op jit(solution)/shard_map/ppermute | solution.py:681
  275.0 3.6 collective-permute-done.49
  287.1 3.1 collective-permute-start.26
  290.8 2.3 copy.197
  293.1 2.3 copy.196
  297.6 2.3 copy.198
  306.0 13.0 %collective-permute-start.37 = (bf16[256,2048]{0,1:T(8,128)(2,1)S(1)}, bf16[256,2048]{0,1:T(8,128)(2,1)S(1)}, u32[]{:S(2)}, u32[]{:S(2)}) collective-permute-start(bf16[256,2048]{0,1:T(8,128)(2,1)S(1)} %fusion.2), channel_id=1, source_target_pairs={{0,2},{1,3},{2,4},{3,5},{8,10},{9,11},{10,12},{11,13},{16,18},{17,... | collective-permute-start | bytes 3145736 | tf_op jit(solution)/shard_map/ppermute | solution.py:681
  321.9 6.8 %shard_map.158 = bf16[512,3072]{1,0:T(8,128)(2,1)S(1)} custom-call(bf16[4,128,1536]{2,1,0:T(8,128)(2,1)S(1)} %copy-done.3, bf16[4,128,1536]{2,1,0:T(8,128)(2,1)S(1)} %copy-done.10, bf16[4,128,3072]{2,1,0:T(8,128)(2,1)S(1)} %copy-done, bf16[4,128,3072]{2,1,0:T(8,128)(2,1)} %collective-permute-done.13.refs_3_), custom_call_target="tpu_custom_call" | custom-call | flops 3221225472 | bytes 3145728 | tf_op jit(solution)/shard_map/pallas_call | solution.py:650
  331.1 7.2 %collective-permute-done.37 = bf16[256,2048]{0,1:T(8,128)(2,1)S(1)} collective-permute-done((bf16[256,2048]{0,1:T(8,128)(2,1)S(1)}, bf16[256,2048]{0,1:T(8,128)(2,1)S(1)}, u32[]{:S(2)}, u32[]{:S(2)}) %collective-permute-start.37) | collective-permute-done | bytes 1048608 | tf_op jit(solution)/shard_map/ppermute | solution.py:681
  338.6 4.4 collective-permute-start.38
  343.0 8.7 %shard_map.160 = bf16[512,4096]{1,0:T(8,128)(2,1)S(1)} custom-call(bf16[4,128,1536]{2,1,0:T(8,128)(2,1)S(1)} %copy-done.3, bf16[4,128,1536]{2,1,0:T(8,128)(2,1)S(1)} %copy-done.10, bf16[4,128,4096]{2,1,0:T(8,128)(2,1)S(1)} %copy-done.1, bf16[4,128,4096]{2,1,0:T(8,128)(2,1)} %collective-permute-done.27.refs_3_), custom_call_target="tpu_custom_call" | custom-call | flops 4294967296 | bytes 4194304 | tf_op jit(solution)/shard_map/pallas_call | solution.py:650
  353.6 4.6 collective-permute-start.41
  360.5 35.9 %collective-permute-done.28 = bf16[128,4096]{1,0:T(8,128)(2,1)S(1)} collective-permute-done((bf16[128,4096]{1,0:T(8,128)(2,1)S(1)}, bf16[128,4096]{1,0:T(8,128)(2,1)S(1)}, u32[]{:S(2)}, u32[]{:S(2)}) %collective-permute-start.28) | collective-permute-done | bytes 1048608 | tf_op jit(solution)/shard_map/ppermute | solution.py:681
  400.2 13.0 %collective-permute-done.15 = bf16[128,3072]{1,0:T(8,128)(2,1)S(1)} collective-permute-done((bf16[128,3072]{1,0:T(8,128)(2,1)S(1)}, bf16[128,3072]{1,0:T(8,128)(2,1)S(1)}, u32[]{:S(2)}, u32[]{:S(2)}) %collective-permute-start.15) | collective-permute-done | bytes 786464 | tf_op jit(solution)/shard_map/ppermute | solution.py:681
  415.2 4.6 collective-permute-start.16
  419.7 16.0 %collective-permute-done.29 = bf16[128,4096]{1,0:T(8,128)(2,1)S(1)} collective-permute-done((bf16[128,4096]{1,0:T(8,128)(2,1)S(1)}, bf16[128,4096]{1,0:T(8,128)(2,1)S(1)}, u32[]{:S(2)}, u32[]{:S(2)}) %collective-permute-start.29) | collective-permute-done | bytes 1048608 | tf_op jit(solution)/shard_map/ppermute | solution.py:681
  440.1 4.6 collective-permute-start.30
  444.7 19.8 %collective-permute-done.32 = bf16[128,4096]{1,0:T(8,128)(2,1)S(1)} collective-permute-done((bf16[128,4096]{1,0:T(8,128)(2,1)S(1)}, bf16[128,4096]{1,0:T(8,128)(2,1)S(1)}, u32[]{:S(2)}, u32[]{:S(2)}) %collective-permute-start.32) | collective-permute-done | bytes 1048608 | tf_op jit(solution)/shard_map/ppermute | solution.py:681
  468.2 13.2 %collective-permute-done.19 = bf16[128,3072]{1,0:T(8,128)(2,1)S(1)} collective-permute-done((bf16[128,3072]{1,0:T(8,128)(2,1)S(1)}, bf16[128,3072]{1,0:T(8,128)(2,1)S(1)}, u32[]{:S(2)}, u32[]{:S(2)}) %collective-permute-start.19) | collective-permute-done | bytes 786464 | tf_op jit(solution)/shard_map/ppermute | solution.py:681
  482.8 10.9 %collective-permute-done.33 = bf16[128,4096]{1,0:T(8,128)(2,1)S(1)} collective-permute-done((bf16[128,4096]{1,0:T(8,128)(2,1)S(1)}, bf16[128,4096]{1,0:T(8,128)(2,1)S(1)}, u32[]{:S(2)}, u32[]{:S(2)}) %collective-permute-start.33) | collective-permute-done | bytes 1048608 | tf_op jit(solution)/shard_map/ppermute | solution.py:681
  (150 shorter events, 83.6 us)
Async XLA Ops:
  17.9 10.8 %collective-permute-start = (bf16[128,1024]{1,0:T(8,128)(2,1)S(1)}, bf16[128,1024]{1,0:T(8,128)(2,1)S(1)}, u32[]{:S(2)}, u32[]{:S(2)}) collective-permute-start(bf16[128,1024]{1,0:T(8,128)(2,1)S(1)} %get-tuple-element.205), channel_id=1, source_target_pairs={{0,8},{1,9},{2,10},{3,11},{4,12},{5,13},{6,14},{7,15}} | collective-permute-start | bytes 786440 | tf_op jit(solution)/shard_map/ppermute | solution.py:803
  38.4 8.2 %collective-permute-start.1 = (bf16[128,1024]{1,0:T(8,128)(2,1)S(1)}, bf16[128,1024]{1,0:T(8,128)(2,1)S(1)}, u32[]{:S(2)}, u32[]{:S(2)}) collective-permute-start(bf16[128,1024]{1,0:T(8,128)(2,1)S(1)} %get-tuple-element.220), channel_id=1, source_target_pairs={{0,8},{8,16},{1,9},{9,17},{2,10},{10,18},{3,11},{11,19},{4,12},{12... | collective-permute-start | bytes 786440 | tf_op jit(solution)/shard_map/ppermute | solution.py:803
  55.4 8.5 %collective-permute-start.2 = (bf16[128,1024]{1,0:T(8,128)(2,1)S(1)}, bf16[128,1024]{1,0:T(8,128)(2,1)S(1)}, u32[]{:S(2)}, u32[]{:S(2)}) collective-permute-start(bf16[128,1024]{1,0:T(8,128)(2,1)S(1)} %get-tuple-element.235), channel_id=1, source_target_pairs={{0,8},{8,16},{16,24},{1,9},{9,17},{17,25},{2,10},{10,18},{18,26},{... | collective-permute-start | bytes 786440 | tf_op jit(solution)/shard_map/ppermute | solution.py:803
  74.2 8.2 %collective-permute-start.3 = (bf16[128,1024]{1,0:T(8,128)(2,1)S(1)}, bf16[128,1024]{1,0:T(8,128)(2,1)S(1)}, u32[]{:S(2)}, u32[]{:S(2)}) collective-permute-start(bf16[128,1024]{1,0:T(8,128)(2,1)S(1)} %get-tuple-element.250), channel_id=1, source_target_pairs={{0,8},{8,16},{16,24},{1,9},{9,17},{17,25},{2,10},{10,18},{18,26},{... | collective-permute-start | bytes 786440 | tf_op jit(solution)/shard_map/ppermute | solution.py:803
  78.9 16.6 %collective-permute-start.5 = (bf16[128,1024]{1,0:T(8,128)(2,1)S(1)}, bf16[128,1024]{1,0:T(8,128)(2,1)S(1)}, u32[]{:S(2)}, u32[]{:S(2)}) collective-permute-start(bf16[128,1024]{1,0:T(8,128)(2,1)S(1)} %get-tuple-element.271), channel_id=1, source_target_pairs={{24,16},{25,17},{26,18},{27,19},{28,20},{29,21},{30,22},{31,23}} | collective-permute-start | bytes 786440 | tf_op jit(solution)/shard_map/ppermute | solution.py:810
  95.7 17.7 %collective-permute-start.7 = (bf16[128,1024]{1,0:T(8,128)(2,1)S(1)}, bf16[128,1024]{1,0:T(8,128)(2,1)S(1)}, u32[]{:S(2)}, u32[]{:S(2)}) collective-permute-start(bf16[128,1024]{1,0:T(8,128)(2,1)S(1)} %get-tuple-element.298), channel_id=1, source_target_pairs={{16,8},{24,16},{17,9},{25,17},{18,10},{26,18},{19,11},{27,19},{20,... | collective-permute-start | bytes 786440 | tf_op jit(solution)/shard_map/ppermute | solution.py:810
  112.8 2.2 collective-permute-start.6
  113.7 21.1 %collective-permute-start.8 = (bf16[128,1024]{1,0:T(8,128)(2,1)S(1)}, bf16[128,1024]{1,0:T(8,128)(2,1)S(1)}, u32[]{:S(2)}, u32[]{:S(2)}) collective-permute-start(bf16[128,1024]{1,0:T(8,128)(2,1)S(1)} %get-tuple-element.325), channel_id=1, source_target_pairs={{8,0},{16,8},{24,16},{9,1},{17,9},{25,17},{10,2},{18,10},{26,18},{... | collective-permute-start | bytes 786440 | tf_op jit(solution)/shard_map/ppermute | solution.py:810
  143.2 11.8 %collective-permute-start.9 = (bf16[128,1024]{1,0:T(8,128)(2,1)S(1)}, bf16[128,1024]{1,0:T(8,128)(2,1)S(1)}, u32[]{:S(2)}, u32[]{:S(2)}) collective-permute-start(bf16[128,1024]{1,0:T(8,128)(2,1)S(1)} %get-tuple-element.337), channel_id=1, source_target_pairs={{8,0},{16,8},{24,16},{9,1},{17,9},{25,17},{10,2},{18,10},{26,18},{... | collective-permute-start | bytes 786440 | tf_op jit(solution)/shard_map/ppermute | solution.py:810
  163.5 10.5 %collective-permute-start.10 = (bf16[128,1024]{1,0:T(8,128)(2,1)S(1)}, bf16[128,1024]{1,0:T(8,128)(2,1)S(1)}, u32[]{:S(2)}, u32[]{:S(2)}) collective-permute-start(bf16[128,1024]{1,0:T(8,128)(2,1)S(1)} %get-tuple-element.349), channel_id=1, source_target_pairs={{8,0},{16,8},{9,1},{17,9},{10,2},{18,10},{11,3},{19,11},{12,4},{20... | collective-permute-start | bytes 786440 | tf_op jit(solution)/shard_map/ppermute | solution.py:810
  182.5 8.5 %collective-permute-start.11 = (bf16[128,1024]{1,0:T(8,128)(2,1)S(1)}, bf16[128,1024]{1,0:T(8,128)(2,1)S(1)}, u32[]{:S(2)}, u32[]{:S(2)}) collective-permute-start(bf16[128,1024]{1,0:T(8,128)(2,1)S(1)} %get-tuple-element.361), channel_id=1, source_target_pairs={{8,0},{9,1},{10,2},{11,3},{12,4},{13,5},{14,6},{15,7}} | collective-permute-start | bytes 786440 | tf_op jit(solution)/shard_map/ppermute | solution.py:810
  183.8 20.0 %collective-permute-start.12 = (bf16[4,128,1536]{2,1,0:T(8,128)(2,1)}, bf16[4,128,1536]{2,1,0:T(8,128)(2,1)S(1)}, u32[]{:S(2)}, u32[]{:S(2)}) collective-permute-start(bf16[4,128,1536]{2,1,0:T(8,128)(2,1)} %get-tuple-element.375), channel_id=1, source_target_pairs={{0,1},{1,0},{2,3},{3,2},{4,5},{5,4},{6,7},{7,6},{8,9},{9,8},{10,11... | collective-permute-start | bytes 4718600 | tf_op jit(solution)/shard_map/ppermute | solution.py:708
  183.9 45.9 %collective-permute-start.35 = (bf16[4,128,2048]{2,1,0:T(8,128)(2,1)}, bf16[4,128,2048]{2,1,0:T(8,128)(2,1)}, u32[]{:S(2)}, u32[]{:S(2)}) collective-permute-start(bf16[4,128,2048]{2,1,0:T(8,128)(2,1)} %get-tuple-element.381), channel_id=1, source_target_pairs={{0,1},{1,0},{2,3},{3,2},{4,5},{5,4},{6,7},{7,6},{8,9},{9,8},{10,11... | collective-permute-start | bytes 6291464 | tf_op jit(solution)/shard_map/ppermute | solution.py:708
  200.4 5.9 %collective-permute-start.20 = (bf16[4,128,1024]{2,1,0:T(8,128)(2,1)}, bf16[4,128,1024]{2,1,0:T(8,128)(2,1)S(1)}, u32[]{:S(2)}, u32[]{:S(2)}) collective-permute-start(bf16[4,128,1024]{2,1,0:T(8,128)(2,1)} %get-tuple-element.377.refs_2_), channel_id=1, source_target_pairs={{0,1},{1,0},{2,3},{3,2},{4,5},{5,4},{6,7},{7,6},{8,9},{9,8},{10,11... | collective-permute-start | bytes 3145736 | tf_op jit(solution)/shard_map/ppermute | solution.py:708
  202.5 25.9 %collective-permute-start.34 = (bf16[4,128,1024]{2,1,0:T(8,128)(2,1)}, bf16[4,128,1024]{2,1,0:T(8,128)(2,1)}, u32[]{:S(2)}, u32[]{:S(2)}) collective-permute-start(bf16[4,128,1024]{2,1,0:T(8,128)(2,1)} %get-tuple-element.379.refs_0_), channel_id=1, source_target_pairs={{0,1},{1,0},{2,3},{3,2},{4,5},{5,4},{6,7},{7,6},{8,9},{9,8},{10,11... | collective-permute-start | bytes 3145736 | tf_op jit(solution)/shard_map/ppermute | solution.py:708
  203.4 139.6 %collective-permute-start.27 = (bf16[4,128,4096]{2,1,0:T(8,128)(2,1)}, bf16[4,128,4096]{2,1,0:T(8,128)(2,1)}, u32[]{:S(2)}, u32[]{:S(2)}) collective-permute-start(bf16[4,128,4096]{2,1,0:T(8,128)(2,1)} %get-tuple-element.378.refs_2_), channel_id=1, source_target_pairs={{0,1},{1,0},{2,3},{3,2},{4,5},{5,4},{6,7},{7,6},{8,9},{9,8},{10,11... | collective-permute-start | bytes 12582920 | tf_op jit(solution)/shard_map/ppermute | solution.py:708
  205.0 10.4 %collective-permute-start.44 = (f32[32,128]{1,0:T(8,128)S(1)}, f32[32,128]{1,0:T(8,128)S(1)}, u32[]{:S(2)}, u32[]{:S(2)}) collective-permute-start(f32[32,128]{1,0:T(8,128)S(1)} %bitcast.161), channel_id=1, source_target_pairs={{0,2},{1,3},{8,10},{9,11},{16,18},{17,19},{24,26},{25,27}} | collective-permute-start | bytes 49160 | tf_op jit(solution)/shard_map/ppermute | solution.py:681
  207.3 9.5 %collective-permute-start.47 = (f32[32,128]{1,0:T(8,128)S(1)}, f32[32,128]{1,0:T(8,128)S(1)}, u32[]{:S(2)}, u32[]{:S(2)}) collective-permute-start(f32[32,128]{1,0:T(8,128)S(1)} %bitcast.160), channel_id=1, source_target_pairs={{6,4},{7,5},{14,12},{15,13},{22,20},{23,21},{30,28},{31,29}} | collective-permute-start | bytes 49160 | tf_op jit(solution)/shard_map/ppermute | solution.py:681
  215.4 10.3 %collective-permute-start.21 = (bf16[128,1024]{1,0:T(8,128)(2,1)S(1)}, bf16[128,1024]{1,0:T(8,128)(2,1)S(1)}, u32[]{:S(2)}, u32[]{:S(2)}) collective-permute-start(bf16[128,1024]{1,0:T(8,128)(2,1)S(1)} %get-tuple-element.402), channel_id=1, source_target_pairs={{0,2},{1,3},{8,10},{9,11},{16,18},{17,19},{24,26},{25,27}} | collective-permute-start | bytes 786440 | tf_op jit(solution)/shard_map/ppermute | solution.py:681
  216.7 105.1 %collective-permute-start.13 = (bf16[4,128,3072]{2,1,0:T(8,128)(2,1)S(1)}, bf16[4,128,3072]{2,1,0:T(8,128)(2,1)}, u32[]{:S(2)}, u32[]{:S(2)}) collective-permute-start(bf16[4,128,3072]{2,1,0:T(8,128)(2,1)S(1)} %copy-done), channel_id=1, source_target_pairs={{0,1},{1,0},{2,3},{3,2},{4,5},{5,4},{6,7},{7,6},{8,9},{9,8},{10,11... | collective-permute-start | bytes 9437192 | tf_op jit(solution)/shard_map/ppermute | solution.py:708
  225.7 24.2 %collective-permute-start.45 = (bf16[32,128]{1,0:T(8,128)(2,1)S(1)}, bf16[32,128]{1,0:T(8,128)(2,1)S(1)}, u32[]{:S(2)}, u32[]{:S(2)}) collective-permute-start(bf16[32,128]{1,0:T(8,128)(2,1)S(1)} %add_convert_fusion.3), channel_id=1, source_target_pairs={{0,2},{1,3},{2,4},{3,5},{8,10},{9,11},{10,12},{11,13},{16,18},{17,... | collective-permute-start | bytes 24584 | tf_op jit(solution)/shard_map/ppermute | solution.py:681
  228.4 16.7 %collective-permute-start.24 = (bf16[128,1024]{1,0:T(8,128)(2,1)S(1)}, bf16[128,1024]{1,0:T(8,128)(2,1)}, u32[]{:S(2)}, u32[]{:S(2)}) collective-permute-start(bf16[128,1024]{1,0:T(8,128)(2,1)S(1)} %get-tuple-element.403), channel_id=1, source_target_pairs={{6,4},{7,5},{14,12},{15,13},{22,20},{23,21},{30,28},{31,29}} | collective-permute-start | bytes 786440 | tf_op jit(solution)/shard_map/ppermute | solution.py:681
  229.7 16.7 %collective-permute-start.22 = (bf16[128,1024]{1,0:T(8,128)(2,1)}, bf16[128,1024]{1,0:T(8,128)(2,1)}, u32[]{:S(2)}, u32[]{:S(2)}) collective-permute-start(bf16[128,1024]{1,0:T(8,128)(2,1)} %fusion.19), channel_id=1, source_target_pairs={{0,2},{1,3},{2,4},{3,5},{8,10},{9,11},{10,12},{11,13},{16,18},{17,... | collective-permute-start | bytes 786440 | tf_op jit(solution)/shard_map/ppermute | solution.py:681
  245.1 6.1 %collective-permute-start.48 = (bf16[32,128]{1,0:T(8,128)(2,1)S(1)}, bf16[32,128]{1,0:T(8,128)(2,1)S(1)}, u32[]{:S(2)}, u32[]{:S(2)}) collective-permute-start(bf16[32,128]{1,0:T(8,128)(2,1)S(1)} %add_convert_fusion.1), channel_id=1, source_target_pairs={{4,2},{5,3},{6,4},{7,5},{12,10},{13,11},{14,12},{15,13},{20,18},{2... | collective-permute-start | bytes 24584 | tf_op jit(solution)/shard_map/ppermute | solution.py:681
  246.4 57.7 %collective-permute-start.36 = (bf16[256,2048]{0,1:T(8,128)(2,1)}, bf16[256,2048]{0,1:T(8,128)(2,1)}, u32[]{:S(2)}, u32[]{:S(2)}) collective-permute-start(bf16[256,2048]{0,1:T(8,128)(2,1)} %bitcast.150), channel_id=1, source_target_pairs={{0,2},{1,3},{8,10},{9,11},{16,18},{17,19},{24,26},{25,27}} | collective-permute-start | bytes 3145736 | tf_op jit(solution)/shard_map/ppermute | solution.py:681
  249.9 32.9 %collective-permute-start.25 = (bf16[128,1024]{1,0:T(8,128)(2,1)}, bf16[128,1024]{1,0:T(8,128)(2,1)}, u32[]{:S(2)}, u32[]{:S(2)}) collective-permute-start(bf16[128,1024]{1,0:T(8,128)(2,1)} %get-tuple-element.401), channel_id=1, source_target_pairs={{4,2},{5,3},{6,4},{7,5},{12,10},{13,11},{14,12},{15,13},{20,18},{2... | collective-permute-start | bytes 786440 | tf_op jit(solution)/shard_map/ppermute | solution.py:681
  251.2 21.9 %collective-permute-start.46 = (bf16[32,128]{1,0:T(8,128)(2,1)S(1)}, bf16[32,128]{1,0:T(8,128)(2,1)S(1)}, u32[]{:S(2)}, u32[]{:S(2)}) collective-permute-start(bf16[32,128]{1,0:T(8,128)(2,1)S(1)} %add_convert_fusion.2), channel_id=1, source_target_pairs={{0,2},{1,3},{2,4},{3,5},{4,6},{5,7},{8,10},{9,11},{10,12},{11,13},... | collective-permute-start | bytes 24584 | tf_op jit(solution)/shard_map/ppermute | solution.py:681
  273.1 5.5 %collective-permute-start.49 = (bf16[32,128]{1,0:T(8,128)(2,1)S(1)}, bf16[32,128]{1,0:T(8,128)(2,1)S(1)}, u32[]{:S(2)}, u32[]{:S(2)}) collective-permute-start(bf16[32,128]{1,0:T(8,128)(2,1)S(1)} %add_convert_fusion), channel_id=1, source_target_pairs={{2,0},{3,1},{4,2},{5,3},{6,4},{7,5},{10,8},{11,9},{12,10},{13,11},... | collective-permute-start | bytes 24584 | tf_op jit(solution)/shard_map/ppermute | solution.py:681
  278.6 8.5 %collective-permute-start.23 = (bf16[128,1024]{1,0:T(8,128)(2,1)}, bf16[128,1024]{1,0:T(8,128)(2,1)S(1)}, u32[]{:S(2)}, u32[]{:S(2)}) collective-permute-start(bf16[128,1024]{1,0:T(8,128)(2,1)} %get-tuple-element.400), channel_id=1, source_target_pairs={{0,2},{1,3},{2,4},{3,5},{4,6},{5,7},{8,10},{9,11},{10,12},{11,13},... | collective-permute-start | bytes 786440 | tf_op jit(solution)/shard_map/ppermute | solution.py:681
  282.8 36.2 %collective-permute-start.39 = (bf16[256,2048]{0,1:T(8,128)(2,1)}, bf16[256,2048]{0,1:T(8,128)(2,1)}, u32[]{:S(2)}, u32[]{:S(2)}) collective-permute-start(bf16[256,2048]{0,1:T(8,128)(2,1)} %bitcast.151), channel_id=1, source_target_pairs={{6,4},{7,5},{14,12},{15,13},{22,20},{23,21},{30,28},{31,29}} | collective-permute-start | bytes 3145736 | tf_op jit(solution)/shard_map/ppermute | solution.py:681
  287.1 15.0 %collective-permute-start.26 = (bf16[128,1024]{1,0:T(8,128)(2,1)}, bf16[128,1024]{1,0:T(8,128)(2,1)}, u32[]{:S(2)}, u32[]{:S(2)}) collective-permute-start(bf16[128,1024]{1,0:T(8,128)(2,1)} %fusion.18), channel_id=1, source_target_pairs={{2,0},{3,1},{4,2},{5,3},{6,4},{7,5},{10,8},{11,9},{12,10},{13,11},... | collective-permute-start | bytes 786440 | tf_op jit(solution)/shard_map/ppermute | solution.py:681
  306.0 32.3 %collective-permute-start.37 = (bf16[256,2048]{0,1:T(8,128)(2,1)S(1)}, bf16[256,2048]{0,1:T(8,128)(2,1)S(1)}, u32[]{:S(2)}, u32[]{:S(2)}) collective-permute-start(bf16[256,2048]{0,1:T(8,128)(2,1)S(1)} %fusion.2), channel_id=1, source_target_pairs={{0,2},{1,3},{2,4},{3,5},{8,10},{9,11},{10,12},{11,13},{16,18},{17,... | collective-permute-start | bytes 3145736 | tf_op jit(solution)/shard_map/ppermute | solution.py:681
  320.6 32.7 %collective-permute-start.40 = (bf16[256,2048]{0,1:T(8,128)(2,1)S(1)}, bf16[256,2048]{0,1:T(8,128)(2,1)S(1)}, u32[]{:S(2)}, u32[]{:S(2)}) collective-permute-start(bf16[256,2048]{0,1:T(8,128)(2,1)S(1)} %fusion), channel_id=1, source_target_pairs={{4,2},{5,3},{6,4},{7,5},{12,10},{13,11},{14,12},{15,13},{20,18},{2... | collective-permute-start | bytes 3145736 | tf_op jit(solution)/shard_map/ppermute | solution.py:681
  328.8 29.4 %collective-permute-start.14 = (bf16[128,3072]{1,0:T(8,128)(2,1)S(1)}, bf16[128,3072]{1,0:T(8,128)(2,1)S(1)}, u32[]{:S(2)}, u32[]{:S(2)}) collective-permute-start(bf16[128,3072]{1,0:T(8,128)(2,1)S(1)} %get-tuple-element.396), channel_id=1, source_target_pairs={{0,2},{1,3},{8,10},{9,11},{16,18},{17,19},{24,26},{25,27}} | collective-permute-start | bytes 2359304 | tf_op jit(solution)/shard_map/ppermute | solution.py:681
  330.4 69.8 %collective-permute-start.17 = (bf16[128,3072]{1,0:T(8,128)(2,1)S(1)}, bf16[128,3072]{1,0:T(8,128)(2,1)S(1)}, u32[]{:S(2)}, u32[]{:S(2)}) collective-permute-start(bf16[128,3072]{1,0:T(8,128)(2,1)S(1)} %get-tuple-element.397), channel_id=1, source_target_pairs={{6,4},{7,5},{14,12},{15,13},{22,20},{23,21},{30,28},{31,29}} | collective-permute-start | bytes 2359304 | tf_op jit(solution)/shard_map/ppermute | solution.py:681
  338.6 59.1 %collective-permute-start.38 = (bf16[256,2048]{0,1:T(8,128)(2,1)S(1)}, bf16[256,2048]{0,1:T(8,128)(2,1)S(1)}, u32[]{:S(2)}, u32[]{:S(2)}) collective-permute-start(bf16[256,2048]{0,1:T(8,128)(2,1)S(1)} %fusion.3), channel_id=1, source_target_pairs={{0,2},{1,3},{2,4},{3,5},{4,6},{5,7},{8,10},{9,11},{10,12},{11,13},... | collective-permute-start | bytes 3145736 | tf_op jit(solution)/shard_map/ppermute | solution.py:681
  351.9 44.5 %collective-permute-start.28 = (bf16[128,4096]{1,0:T(8,128)(2,1)S(1)}, bf16[128,4096]{1,0:T(8,128)(2,1)S(1)}, u32[]{:S(2)}, u32[]{:S(2)}) collective-permute-start(bf16[128,4096]{1,0:T(8,128)(2,1)S(1)} %get-tuple-element.392), channel_id=1, source_target_pairs={{0,2},{1,3},{8,10},{9,11},{16,18},{17,19},{24,26},{25,27}} | collective-permute-start | bytes 3145736 | tf_op jit(solution)/shard_map/ppermute | solution.py:681
  353.6 45.9 %collective-permute-start.41 = (bf16[256,2048]{0,1:T(8,128)(2,1)S(1)}, bf16[256,2048]{0,1:T(8,128)(2,1)S(1)}, u32[]{:S(2)}, u32[]{:S(2)}) collective-permute-start(bf16[256,2048]{0,1:T(8,128)(2,1)S(1)} %fusion.1), channel_id=1, source_target_pairs={{2,0},{3,1},{4,2},{5,3},{6,4},{7,5},{10,8},{11,9},{12,10},{13,11},... | collective-permute-start | bytes 3145736 | tf_op jit(solution)/shard_map/ppermute | solution.py:681
  358.5 54.8 %collective-permute-start.15 = (bf16[128,3072]{1,0:T(8,128)(2,1)S(1)}, bf16[128,3072]{1,0:T(8,128)(2,1)S(1)}, u32[]{:S(2)}, u32[]{:S(2)}) collective-permute-start(bf16[128,3072]{1,0:T(8,128)(2,1)S(1)} %fusion.13), channel_id=1, source_target_pairs={{0,2},{1,3},{2,4},{3,5},{8,10},{9,11},{10,12},{11,13},{16,18},{17,... | collective-permute-start | bytes 2359304 | tf_op jit(solution)/shard_map/ppermute | solution.py:681
  396.4 23.3 %collective-permute-start.31 = (bf16[128,4096]{1,0:T(8,128)(2,1)S(1)}, bf16[128,4096]{1,0:T(8,128)(2,1)S(1)}, u32[]{:S(2)}, u32[]{:S(2)}) collective-permute-start(bf16[128,4096]{1,0:T(8,128)(2,1)S(1)} %get-tuple-element.393), channel_id=1, source_target_pairs={{6,4},{7,5},{14,12},{15,13},{22,20},{23,21},{30,28},{31,29}} | collective-permute-start | bytes 3145736 | tf_op jit(solution)/shard_map/ppermute | solution.py:681
  397.7 38.1 %collective-permute-start.29 = (bf16[128,4096]{1,0:T(8,128)(2,1)S(1)}, bf16[128,4096]{1,0:T(8,128)(2,1)S(1)}, u32[]{:S(2)}, u32[]{:S(2)}) collective-permute-start(bf16[128,4096]{1,0:T(8,128)(2,1)S(1)} %fusion.7), channel_id=1, source_target_pairs={{0,2},{1,3},{2,4},{3,5},{8,10},{9,11},{10,12},{11,13},{16,18},{17,... | collective-permute-start | bytes 3145736 | tf_op jit(solution)/shard_map/ppermute | solution.py:681
  400.2 37.7 %collective-permute-start.42 = (bf16[128,2048]{0,1:T(8,128)(2,1)S(1)}, bf16[128,2048]{0,1:T(8,128)(2,1)S(1)}, u32[]{:S(2)}, u32[]{:S(2)}) collective-permute-start(bf16[128,2048]{0,1:T(8,128)(2,1)S(1)} %dynamic-slice_convert_fusion), channel_id=1, source_target_pairs={{0,1},{1,0},{2,3},{3,2},{4,5},{5,4},{6,7},{7,6},{8,9},{9,8},{10,11... | collective-permute-start | bytes 1572872 | tf_op jit(solution)/shard_map/ppermute | solution.py:708
  413.9 24.1 %collective-permute-start.18 = (bf16[128,3072]{1,0:T(8,128)(2,1)S(1)}, bf16[128,3072]{1,0:T(8,128)(2,1)S(1)}, u32[]{:S(2)}, u32[]{:S(2)}) collective-permute-start(bf16[128,3072]{1,0:T(8,128)(2,1)S(1)} %get-tuple-element.395), channel_id=1, source_target_pairs={{4,2},{5,3},{6,4},{7,5},{12,10},{13,11},{14,12},{15,13},{20,18},{2... | collective-permute-start | bytes 2359304 | tf_op jit(solution)/shard_map/ppermute | solution.py:681
  415.2 53.0 %collective-permute-start.16 = (bf16[128,3072]{1,0:T(8,128)(2,1)S(1)}, bf16[128,3072]{1,0:T(8,128)(2,1)S(1)}, u32[]{:S(2)}, u32[]{:S(2)}) collective-permute-start(bf16[128,3072]{1,0:T(8,128)(2,1)S(1)} %get-tuple-element.394), channel_id=1, source_target_pairs={{0,2},{1,3},{2,4},{3,5},{4,6},{5,7},{8,10},{9,11},{10,12},{11,13},... | collective-permute-start | bytes 2359304 | tf_op jit(solution)/shard_map/ppermute | solution.py:681
  436.5 28.0 %collective-permute-start.32 = (bf16[128,4096]{1,0:T(8,128)(2,1)S(1)}, bf16[128,4096]{1,0:T(8,128)(2,1)S(1)}, u32[]{:S(2)}, u32[]{:S(2)}) collective-permute-start(bf16[128,4096]{1,0:T(8,128)(2,1)S(1)} %get-tuple-element.391), channel_id=1, source_target_pairs={{4,2},{5,3},{6,4},{7,5},{12,10},{13,11},{14,12},{15,13},{20,18},{2... | collective-permute-start | bytes 3145736 | tf_op jit(solution)/shard_map/ppermute | solution.py:681
  438.2 43.2 %collective-permute-start.19 = (bf16[128,3072]{1,0:T(8,128)(2,1)S(1)}, bf16[128,3072]{1,0:T(8,128)(2,1)S(1)}, u32[]{:S(2)}, u32[]{:S(2)}) collective-permute-start(bf16[128,3072]{1,0:T(8,128)(2,1)S(1)} %fusion.12), channel_id=1, source_target_pairs={{2,0},{3,1},{4,2},{5,3},{6,4},{7,5},{10,8},{11,9},{12,10},{13,11},... | collective-permute-start | bytes 2359304 | tf_op jit(solution)/shard_map/ppermute | solution.py:681
  440.1 42.7 %collective-permute-start.30 = (bf16[128,4096]{1,0:T(8,128)(2,1)S(1)}, bf16[128,4096]{1,0:T(8,128)(2,1)S(1)}, u32[]{:S(2)}, u32[]{:S(2)}) collective-permute-start(bf16[128,4096]{1,0:T(8,128)(2,1)S(1)} %get-tuple-element.390), channel_id=1, source_target_pairs={{0,2},{1,3},{2,4},{3,5},{4,6},{5,7},{8,10},{9,11},{10,12},{11,13},... | collective-permute-start | bytes 3145736 | tf_op jit(solution)/shard_map/ppermute | solution.py:681
  464.8 28.9 %collective-permute-start.33 = (bf16[128,4096]{1,0:T(8,128)(2,1)S(1)}, bf16[128,4096]{1,0:T(8,128)(2,1)S(1)}, u32[]{:S(2)}, u32[]{:S(2)}) collective-permute-start(bf16[128,4096]{1,0:T(8,128)(2,1)S(1)} %fusion.6), channel_id=1, source_target_pairs={{2,0},{3,1},{4,2},{5,3},{6,4},{7,5},{10,8},{11,9},{12,10},{13,11},... | collective-permute-start | bytes 3145736 | tf_op jit(solution)/shard_map/ppermute | solution.py:681
  (20 other events, 200.2 us)

commit v2 on v1

--- a/solution.py
+++ b/solution.py
@@ -42,15 +42,16 @@
 
 class Kept(NamedTuple):
     layer_out: Any
-    left_keep: Any
-    left_send: Any
-    act_keep: Any
-    act_send: Any
+    left: Any
+    act_early: Any
+    act_late: Any
 
 
 class Back(NamedTuple):
     grad_in: Any
-    grad_y: Any
+    y_early: Any
+    y_late: Any
+    y_last: Any
     grad_up: Any
     grad_attn: Any
     grad_packed: Any
@@ -116,6 +117,17 @@
         copy.start()
         self.pending.append(copy)
 
+    def spread(self, source, buffers, spans, slot):
+        sem = self.sems.at[self.base + len(self.pending)]
+        copies = []
+        for buffer, (first, end) in zip(buffers, spans):
+            if buffer is None:
+                continue
+            place = jnp.clip(slot - first, 0, end - first - 1)
+            copies.append(pltpu.make_async_copy(source, buffer.at[place], sem))
+            pl.when((slot >= first) & (slot < end))(copies[-1].start)
+        self.pending.append(copies[0])
+
     def wait(self):
         for copy in self.pending:
             copy.wait()
@@ -157,6 +169,28 @@
         strip(i).wait()
 
 
+def split_columns(plan, core, source, target):
+    width = plan.rows
+    for b in range(plan.features // width):
+        at = (b // CORES) * width
+        which = jnp.where(core == b % CORES, 0, 1)
+        target[which, :, at : at + width] = source[:, b * width : (b + 1) * width]
+
+
+def last_y_kernel(plan, arriving, stored, _, y_last, sem):
+    at_start = lax.axis_index("section") == 0
+
+    @pl.when(at_start)
+    def split():
+        split_columns(plan, lax.axis_index("batch") % CORES, arriving, y_last.at[:, 0])
+
+    @pl.when(jnp.logical_not(at_start))
+    def fetch():
+        copy = pltpu.make_async_copy(stored, y_last, sem)
+        copy.start()
+        copy.wait()
+
+
 class Plan(NamedTuple):
     sections: int
     micros: int
@@ -170,6 +204,23 @@
 
     def ticks(self):
         return self.micros + 2 * (self.sections - 1)
+
+    def act_spans(self):
+        half = self.micros // 2
+        return (0, half), (half, self.micros)
+
+    def y_spans(self):
+        half = self.micros // 2
+        return (0, half), (half, self.micros - 1), (self.micros - 1, self.micros)
+
+    def fwd_reaches(self, tick):
+        low, high = tick - (self.sections - 1), tick
+        return tuple(low < end and high >= first for first, end in self.act_spans())
+
+    def bwd_reaches(self, tick):
+        low, high = tick - 2 * (self.sections - 1), tick - (self.sections - 1)
+        last = tick == self.ticks() - 1
+        return tuple(low < end and high >= first and not last for first, end in self.y_spans())
 
     def fwd_id(self, tick, section):
         return tick - section
@@ -190,14 +241,16 @@
         take(4)
     incoming = take(1)[0] if has_incoming else None
     (frames_in,) = take(1)
+    reaches = plan.fwd_reaches(tick)
     if loads_weights:
         info, table = take(2)
         weight = Weights(*take(4))
     else:
-        take(len(Reread._fields) + len(Kept._fields))
+        take(len(Reread._fields) + 2)
+        take(sum(now and had for now, had in zip(reaches, plan.fwd_reaches(tick - 1))))
     turned = Weights(*take(4))
     reread = Reread(*take(5))
-    kept = Kept(*take(5))
+    kept = Kept(*take(2), *[take(1)[0] if on else None for on in reaches])
     (outgoing,) = take(1)
     entry, packed, probs, hidden, slope, normed, left, attended, act, strips, sems = refs
 
@@ -294,23 +347,20 @@
         normal_two, _ = normalize(hidden[...])
         normed[...] = (normal_two * (1.0 + rows[2:3]) + rows[3:4]).astype(BF16)
         share_columns(normed, 2 * share)
-        save(left.at[core], kept.left_keep.at[slot])
-        save(left.at[1 - core], kept.left_send.at[slot])
+        save(left.at[core], kept.left.at[0, slot])
+        save(left.at[1 - core], kept.left.at[1, slot])
         ready(3)
-        half = hidden_units // CORES
         for j in range(0, hidden_units, BLOCK):
             value, gradient = gelu_and_slope(product(normed[...], weight.up[:, j : j + BLOCK]))
-            act[j // half, :, j % half : j % half + BLOCK] = value.astype(BF16)
+            act[:, j : j + BLOCK] = value.astype(BF16)
             slope[:, j : j + BLOCK] = gradient.astype(BF16)
         save(slope, reread.slope.at[slot])
-        save(act.at[core], kept.act_keep.at[slot])
-        save(act.at[1 - core], kept.act_send.at[slot])
+        save.spread(act, (kept.act_early, kept.act_late), plan.act_spans(), slot)
         ready(4)
         for j in range(0, features, BLOCK):
-            added = hidden[:, j : j + BLOCK]
-            for c in range(CORES):
-                added += product(act[c], weight.down[c * half : (c + 1) * half, j : j + BLOCK])
-            outgoing[:, j : j + BLOCK] = added.astype(BF16)
+            outgoing[:, j : j + BLOCK] = (
+                hidden[:, j : j + BLOCK] + product(act[...], weight.down[:, j : j + BLOCK])
+            ).astype(BF16)
         save(outgoing, kept.layer_out.at[slot])
         save.wait()
 
@@ -336,27 +386,31 @@
                 turn(source, target, r, c, features, strips, sems, base)
 
 
-def backward_kernel(plan, tick, has_arriving, first, *refs):
+def backward_kernel(plan, tick, has_arriving, first, unread, *refs):
     refs = list(refs)
     take = lambda n: [refs.pop(0) for _ in range(n)]
     info, table = take(2)
     turned = Weights(*take(4))
-    take(4)
+    take(unread)
     arriving = take(1)[0] if has_arriving else None
     (cotangent,) = take(1)
     take(len(Reread._fields))
+    reaches = plan.bwd_reaches(tick)
+    used = (True,) + reaches + (True,) * 4
     if not first:
-        take(len(Back._fields))
+        had = (True,) + plan.bwd_reaches(tick - 1) + (True,) * 4
+        take(sum(u and h for u, h in zip(used, had)))
     reread = Reread(*take(5))
-    back = Back(*take(6))
+    back = Back(*[take(1)[0] if u else None for u in used])
     (returning,) = take(1)
-    (entry, packed, probs, hidden, slope, grad_y, grad_up, wide, grad_hidden, grad_attn, mixed,
-     grad_packed, row_grads, sems) = refs
+    (entry, packed, probs, hidden, slope, grad_y, y_split, grad_up, wide, grad_hidden, grad_attn,
+     mixed, grad_packed, row_grads, sems) = refs
 
     micros, frames, features, hidden_units, _ = plan[1:]
     head_size = features // HEADS
     group_width = GROUP * head_size
     section = lax.axis_index("section")
+    core = lax.axis_index("batch") % CORES
     is_nar = section % 2
     micro = plan.bwd_id(tick, section)
     active = (micro >= 0) & (micro < micros)
@@ -388,7 +442,11 @@
         else:
             own_cotangent()
 
-        save(grad_y, back.grad_y.at[slot])
+        if any(reaches):
+            split_columns(plan, core, grad_y, y_split)
+            for c in range(CORES):
+                places = [None if b is None else b.at[c] for b in back[1:4]]
+                save.spread(y_split.at[c], places, plan.y_spans(), slot)
         rows = table_rows(table, code)
         fetches[4].wait()
         for j in range(0, hidden_units, BLOCK):
@@ -462,13 +520,15 @@
         hidden=(own + (features,), F32),
         slope=(own + (hidden_units,), BF16),
     )
-    share = (own + (3 * features // CORES,), BF16)
-    half = (own + (hidden_units // CORES,), BF16)
-    kept = Kept((own + (features,), BF16), share, share, half, half)
+    def buffers(spans, before, columns):
+        return [(before + (end - first, frames, columns), BF16) for first, end in spans]
+
+    left = ((CORES,) + own + (3 * features // CORES,), BF16)
+    kept = Kept((own + (features,), BF16), left, *buffers(plan.act_spans(), (), hidden_units))
     wide = (own + (features,), BF16)
     back = Back(
-        grad_in=wide,
-        grad_y=wide,
+        wide,
+        *buffers(plan.y_spans(), (CORES,), features // CORES),
         grad_up=(own + (hidden_units,), BF16),
         grad_attn=wide,
         grad_packed=(own + (3 * features,), BF16),
@@ -499,6 +559,15 @@
                 self.aliases[updates + i] = len(self.out_shape)
             self.out_shape.append(space(shape, dtype))
             self.out_specs.append(spec)
+
+    def update(self, arrays, shapes, used):
+        arrays = arrays or (None,) * len(shapes)
+        for array, shape, use in zip(arrays, shapes, used):
+            if use and array is not None:
+                self.take([array], anywhere, pltpu.HBM)
+                self.give([shape], anywhere, pltpu.HBM, len(self.args) - 1)
+            elif use:
+                self.give([shape], anywhere, pltpu.HBM)
 
     def run(self, body, scratch, flops):
         return list(
@@ -515,6 +584,12 @@
                 ),
             )(*self.args)
         )
+
+
+def updated(old, used, new):
+    new = list(new)
+    old = old or (None,) * len(used)
+    return [new.pop(0) if u else o for o, u in zip(old, used)]
 
 
 def like(arrays):
@@ -556,15 +631,17 @@
         call.give(like(state.weights), in_vmem, pltpu.VMEM)
     else:
         at_kept = len(call.args)
-        call.take(state.reread + state.kept, anywhere, pltpu.HBM)
+        call.take(state.reread, anywhere, pltpu.HBM)
     call.give([(w.shape[::-1], BF16) for w in state.weights], anywhere, pltpu.VMEM, at_turned)
-    call.give(reread_shapes + kept_shapes, anywhere, pltpu.HBM, at_kept)
+    call.give(reread_shapes, anywhere, pltpu.HBM, at_kept)
+    used = (True, True) + plan.fwd_reaches(tick)
+    call.update(state.kept, kept_shapes, used)
     call.give([((plan.frames, plan.features), BF16)], in_vmem, pltpu.VMEM)
     scratch = scratch_of(reread_shapes) + [
         pltpu.VMEM((plan.frames, plan.features), BF16),
         pltpu.VMEM((CORES, plan.frames, 3 * plan.features // CORES), BF16),
         pltpu.VMEM((plan.frames, plan.features), BF16),
-        pltpu.VMEM((CORES, plan.frames, plan.hidden_units // CORES), BF16),
+        pltpu.VMEM((plan.frames, plan.hidden_units), BF16),
         pltpu.VMEM((2, plan.features, 256), BF16),
         pltpu.SemaphoreType.DMA((24,)),
     ]
@@ -574,36 +651,35 @@
     if first:
         state = state._replace(info=got[0], table=got[1], weights=Weights(*got[2:6]))
         got = got[6:]
-    state = state._replace(
-        turned=Weights(*got[:4]), reread=Reread(*got[4:9]), kept=Kept(*got[9:14])
-    )
-    return state, got[14]
-
-
-def run_backward(plan, tick, state, arriving, cotangent):
+    kept = Kept(*updated(state.kept, used, got[9:-1]))
+    return state._replace(turned=Weights(*got[:4]), reread=Reread(*got[4:9]), kept=kept), got[-1]
+
+
+def run_backward(plan, tick, state, arriving, cotangent, after):
     reread_shapes, _, back_shapes = shapes_of(plan)
     first = state.back is None
     call = Call()
     call.take([state.info], in_smem, pltpu.SMEM)
     call.take([state.table], in_vmem, pltpu.VMEM)
     call.take(state.turned, in_vmem, pltpu.VMEM)
-    call.take(state.weights, anywhere, pltpu.VMEM)
+    staying = state.weights if tick < plan.ticks() - 1 else ()
+    call.take(staying, anywhere, pltpu.VMEM)
+    call.take(after, anywhere)
+    unread = len(staying) + len(after)
     if arriving is not None:
         call.take([arriving], in_vmem, pltpu.VMEM)
     call.take([cotangent], anywhere)
     at_reread = len(call.args)
     call.take(state.reread, anywhere, pltpu.HBM)
-    at_back = None
-    if not first:
-        at_back = len(call.args)
-        call.take(state.back, anywhere, pltpu.HBM)
     call.give(reread_shapes, anywhere, pltpu.HBM, at_reread)
-    call.give(back_shapes, anywhere, pltpu.HBM, at_back)
+    used = (True,) + plan.bwd_reaches(tick) + (True,) * 4
+    call.update(state.back, back_shapes, used)
     call.give([((plan.frames, plan.features), BF16)], in_vmem, pltpu.VMEM)
     narrow = pltpu.VMEM((plan.frames, plan.features), BF16)
     full = pltpu.VMEM((plan.frames, plan.features), F32)
     scratch = scratch_of(reread_shapes) + [
         narrow,
+        pltpu.VMEM((CORES, plan.frames, plan.features // CORES), BF16),
         pltpu.VMEM((plan.frames, plan.hidden_units), BF16),
         full,
         full,
@@ -614,21 +690,49 @@
         pltpu.SemaphoreType.DMA((16,)),
     ]
     flops = 2 * plan.frames * sum(w.size for w in state.turned)
-    body = functools.partial(backward_kernel, plan, tick, arriving is not None, first)
+    body = functools.partial(backward_kernel, plan, tick, arriving is not None, first, unread)
     got = call.run(body, scratch, flops)
-    return state._replace(reread=Reread(*got[:5]), back=Back(*got[5:11])), got[11]
-
-
-def weight_grad_kernel(count, first_column, width, *refs):
-    lefts, rights, out = refs[:count], refs[count : 2 * count], refs[2 * count]
-    stage, turned, sems = refs[2 * count + 1 :]
+    back = Back(*updated(state.back, used, got[5:-1]))
+    return state._replace(reread=Reread(*got[:5]), back=back), got[-1]
+
+
+def last_y(plan, state, arriving, before):
+    stored = state.back.y_last
+    return pl.pallas_call(
+        functools.partial(last_y_kernel, plan),
+        out_shape=pltpu.VMEM(stored.shape, BF16),
+        in_specs=[in_vmem, anywhere, anywhere],
+        out_specs=in_vmem,
+        scratch_shapes=[pltpu.SemaphoreType.DMA],
+    )(pltpu.with_memory_space_constraint(arriving, pltpu.VMEM), in_hbm(stored), before)
+
+
+def in_hbm(x):
+    return pltpu.with_memory_space_constraint(x, pltpu.HBM)
+
+
+class Pair(NamedTuple):
+    left: Any
+    share: int
+    right: Any
+    first: int = 0
+
+
+def weight_grad_kernel(shares, first_column, width, has_start, skip_ends, *refs):
+    count = len(shares)
+    lefts, rights = refs[:count], refs[count : 2 * count]
+    start = refs[2 * count] if has_start else None
+    out, stage, turned, sems = refs[-4:]
     micros, frames, step = rights[0].shape
-
-    @pl.when(pl.program_id(0) == 0)
+    chip = lax.axis_index("batch") // CORES
+    chips = lax.axis_size("batch") // CORES
+    works = (chip > 0) & (chip < chips - 1) if skip_ends else chip >= 0
+
+    @pl.when(works & (pl.program_id(0) == 0))
     def turn_lefts():
         copies = []
         for i, left in enumerate(lefts):
-            part = left.at[:, :, pl.ds(first_column, width)]
+            part = left.at[shares[i], :, :, pl.ds(first_column, width)]
             copies.append(pltpu.make_async_copy(part, stage.at[i], sems.at[i]))
             copies[i].start()
         for i in range(count):
@@ -636,62 +740,203 @@
             for m in range(micros):
                 turned[i, :, m * frames : (m + 1) * frames] = stage[i, m].T
 
-    total = None
-    for i in range(count):
-        term = product(turned[i], rights[i][...].reshape(micros * frames, step))
-        total = term if total is None else total + term
-    out[...] = total.astype(BF16)
-
-
-def weight_grad(lefts, rights, first_column, width):
-    count = len(lefts)
-    micros, frames, columns = rights[0].shape
+    @pl.when(works)
+    def add_up():
+        total = start[...].astype(F32) if has_start else None
+        for i in range(count):
+            term = product(turned[i], rights[i][...].reshape(micros * frames, step))
+            total = term if total is None else total + term
+        out[...] = total.astype(BF16)
+
+    if skip_ends:
+
+        @pl.when(jnp.logical_not(works))
+        def nothing():
+            out[...] = jnp.zeros(out.shape, BF16)
+
+
+def weight_grad(pairs, first_column, width, start=None, skip_ends=False, after=()):
+    count = len(pairs)
+    _, micros, frames, _ = pairs[0].left.shape
+    columns = pairs[0].right.shape[2]
     step = min(columns, BLOCK)
+    right_specs = [
+        pl.BlockSpec((micros, frames, step), lambda j, at=p.first // micros: (at, 0, j))
+        for p in pairs
+    ]
+    block = pl.BlockSpec((width, step), lambda j: (0, j))
+    starts = [] if start is None else [start]
+    shares = [p.share for p in pairs]
     return pl.pallas_call(
-        functools.partial(weight_grad_kernel, count, first_column, width),
+        functools.partial(
+            weight_grad_kernel, shares, first_column, width, start is not None, skip_ends
+        ),
         grid=(columns // step,),
-        out_shape=jax.ShapeDtypeStruct((width, columns), BF16),
+        out_shape=pltpu.HBM((width, columns), BF16),
         in_specs=[anywhere] * count
-        + [pl.BlockSpec((micros, frames, step), lambda j: (0, 0, j))] * count,
-        out_specs=pl.BlockSpec((width, step), lambda j: (0, j)),
+        + right_specs
+        + [block] * len(starts)
+        + [anywhere] * len(after),
+        out_specs=block,
         scratch_shapes=[
             pltpu.VMEM((count, micros, frames, width), BF16),
             pltpu.VMEM((count, width, micros * frames), BF16),
             pltpu.SemaphoreType.DMA((count,)),
         ],
-        compiler_params=pltpu.CompilerParams(vmem_limit_bytes=12 * 2**20),
+        compiler_params=pltpu.CompilerParams(vmem_limit_bytes=10 * 2**20),
         cost_estimate=pl.CostEstimate(
             flops=2 * count * micros * frames * width * columns,
             bytes_accessed=2 * width * columns,
             transcendentals=0,
         ),
-    )(*lefts, *rights)
-
-
-def pick(parts, index):
-    return lax.dynamic_index_in_dim(parts, index, 0, keepdims=False)
-
-
-def line_sum(parts, chip, chips):
-    def hop(value, sends, by):
-        pairs = []
-        for z in range(chips):
-            if 0 <= z + by < chips and sends(z):
-                pairs += [(CORES * z + c, CORES * (z + by) + c) for c in range(CORES)]
+    )(
+        *[p.left for p in pairs],
+        *[p.right for p in pairs],
+        *[in_hbm(x) for x in starts],
+        *after,
+    )
+
+
+class Part(NamedTuple):
+    grad: Any
+    column: int
+    width: int
+    result: int
+    place: int
+    tall: bool
+
+
+def fetch_parts(parts, grads, rows, index, target, sems):
+    copies, at = [], 0
+    first_row = pl.multiple_of(index * rows, rows)
+    for i, part in enumerate(parts):
+        source = grads[i].at[pl.ds(first_row, rows), pl.ds(part.column, part.width)]
+        copies.append(
+            pltpu.make_async_copy(source, target.at[:, pl.ds(at, part.width)], sems.at[i])
+        )
+        copies[i].start()
+        at += part.width
+    return copies
+
+
+def send_kernel(parts, rows, hop, adds, *refs):
+    grads, refs = refs[: len(parts)], refs[len(parts) :]
+    came = refs[:2] if adds else None
+    up, down, here, sems = refs[-4:]
+    chip = lax.axis_index("batch") // CORES
+    last = lax.axis_size("batch") // CORES - 1
+    places = (jnp.minimum(chip + last - (hop - 1), last), jnp.maximum(chip - last + (hop - 1), 0))
+    targets = (here.at[0], here.at[1]) if adds else (up, down)
+    copies = []
+    for d in range(2):
+        copies += fetch_parts(parts, grads, rows, places[d], targets[d], sems.at[d])
+    for copy in copies:
+        copy.wait()
+    if adds:
+        up[...] = (here[0].astype(F32) + came[0][...].astype(F32)).astype(BF16)
+        down[...] = (here[1].astype(F32) + came[1][...].astype(F32)).astype(BF16)
+
+
+def finish_kernel(parts, rows, result_count, *refs):
+    grads, refs = refs[: len(parts)], refs[len(parts) :]
+    came = refs[:2]
+    here, total, turned, sems = refs[-4:]
+    results = refs[-5 - result_count : -5]
+    refs[-5][...] = jnp.zeros(refs[-5].shape, F32)
+    chip = lax.axis_index("batch") // CORES
+    for copy in fetch_parts(parts, grads, rows, chip, here, sems):
+        copy.wait()
+    total[...] = here[...].astype(F32) + came[0][...].astype(F32) + came[1][...].astype(F32)
+    copies, at = [], 0
+    for i, part in enumerate(parts):
+        result = results[part.result]
+        if part.tall:
+            turned[...] = total[:, at : at + part.width].T
+            source, target = turned, result.at[pl.ds(part.place, part.width), :]
+        else:
+            source = total.at[pl.ds(0, result.shape[0]), pl.ds(at, part.width)]
+            target = result.at[:, pl.ds(part.place, part.width)]
+        copies.append(pltpu.make_async_copy(source, target, sems.at[i]))
+        copies[i].start()
+        at += part.width
+    for copy in copies:
+        copy.wait()
+
+
+class Piece:
+    def __init__(self, parts, first_hop):
+        self.parts, self.hop, self.first_hop = parts, first_hop - 1, first_hop
+        self.came = None
+        self.width = sum(p.width for p in parts)
+
+
+class Line:
+    def __init__(self, exchange, rows, results, before):
+        self.chips, self.rows, self.before = exchange.chips, rows, before
+        self.results = {}
+        self.shapes = results
+
+    def step(self, piece):
+        if piece.hop == self.chips - 1:
+            self.finish(piece)
+        else:
+            self.send(piece)
+
+    def send(self, piece):
+        adds = piece.came is not None
+        piece.hop += 1
+        shape = (self.rows, piece.width)
+        call = Call()
+        call.take([p.grad for p in piece.parts], anywhere, pltpu.HBM)
+        if adds:
+            call.take(piece.came, in_vmem, pltpu.VMEM)
+        call.take([self.before], anywhere)
+        call.give([(shape, BF16)] * 2, in_vmem, pltpu.VMEM)
+        count = len(piece.parts)
+        scratch = [pltpu.VMEM((2,) + shape, BF16), pltpu.SemaphoreType.DMA((2, count))]
+        parts = [p._replace(grad=None) for p in piece.parts]
+        up, down = call.run(
+            functools.partial(send_kernel, parts, self.rows, piece.hop, adds), scratch, 2**20
+        )
+        self.before = up
+        edge = piece.first_hop - 1
+        last = self.chips - 1
+        piece.came = [
+            self.moved(up, [z for z in range(last) if edge <= z < piece.hop], 1),
+            self.moved(down, [z for z in range(1, last + 1) if edge <= last - z < piece.hop], -1),
+        ]
+
+    def moved(self, value, senders, by):
+        pairs = [(CORES * z + c, CORES * (z + by) + c) for z in senders for c in range(CORES)]
         return lax.ppermute(value, "batch", pairs)
 
-    last = chips - 1
-    up = pick(parts, jnp.minimum(chip + last, last))
-    down = pick(parts, jnp.maximum(chip - last, 0))
-    for k in range(1, chips):
-        came_up = hop(up, lambda z: z < k, 1).astype(F32)
-        came_down = hop(down, lambda z: z > last - k, -1).astype(F32)
-        if k < last:
-            here_up = pick(parts, jnp.minimum(chip + last - k, last)).astype(F32)
-            here_down = pick(parts, jnp.maximum(chip - last + k, 0)).astype(F32)
-            up = (here_up + came_up).astype(BF16)
-            down = (here_down + came_down).astype(BF16)
-    return pick(parts, chip).astype(F32) + came_up + came_down
+    def finish(self, piece):
+        names = sorted({p.result for p in piece.parts})
+        parts = [p._replace(grad=None, result=names.index(p.result)) for p in piece.parts]
+        call = Call()
+        call.take([p.grad for p in piece.parts], anywhere, pltpu.HBM)
+        call.take(piece.came, in_vmem, pltpu.VMEM)
+        call.update(
+            [self.results.get(n) for n in names],
+            [(self.shapes[n], F32) for n in names],
+            [True] * len(names),
+        )
+        call.take([self.before], anywhere)
+        call.give([((8, LANES), F32)], in_vmem, pltpu.VMEM)
+        shape = (self.rows, piece.width)
+        tall = max([p.width for p in parts if p.tall], default=8)
+        scratch = [
+            pltpu.VMEM(shape, BF16),
+            pltpu.VMEM(shape, F32),
+            pltpu.VMEM((tall, self.rows), F32),
+            pltpu.SemaphoreType.DMA((len(parts),)),
+        ]
+        done = call.run(
+            functools.partial(finish_kernel, parts, self.rows, len(names)), scratch, 2**20
+        )
+        self.results.update(zip(names, done))
+        piece.hop = self.chips
+        self.before = done[-1]
 
 
 def table_gradient(row_grads, codes, blocks):
@@ -699,53 +944,106 @@
     return jnp.sum(jnp.where(chosen[:, :, None, None], row_grads[None], 0.0), axis=1)
 
 
-def sums_by_hops(plan, kept, back, table_grad, batch, index):
-    chips = batch // CORES
-    core, chip = index % CORES, index // CORES
+class Exchange:
+    def __init__(self, batch):
+        self.batch = batch
+        self.chips = batch // CORES
+        self.by_hops = batch % CORES == 0 and 2 <= self.chips <= LINE
+        self.ends_hand_over = self.by_hops and self.chips == LINE
+
+    def swap(self, x):
+        if not self.by_hops:
+            return None
+        return lax.ppermute(x, "batch", [(b, b ^ 1) for b in range(self.batch)])
+
+    def inward(self, x):
+        if not self.ends_hand_over:
+            return None
+        top = self.batch - CORES
+        pairs = [(c, CORES + c) for c in range(CORES)]
+        pairs += [(top + c, top - CORES + c) for c in range(CORES)]
+        return lax.ppermute(x, "batch", pairs)
+
+    def sources(self, x):
+        if not self.ends_hand_over:
+            return [x, self.swap(x)]
+        came = self.inward(x)
+        return [x, self.swap(x), came, self.swap(came)]
+
+
+def sums_by_hops(plan, exchange, kept, back, grad_down, lefts, table_grad, before):
+    chips, rows = exchange.chips, plan.rows
     features, hidden_units = plan.features, plan.hidden_units
+    core = lax.axis_index("batch") % CORES
     share = features // CORES
-    rows = plan.rows
-    swap = lambda x: lax.ppermute(x, "batch", [(b, b ^ 1) for b in range(batch)])
-
-    left_peer = swap(kept.left_send)
-    act_peer = swap(kept.act_send)
-    y_peer = swap(back.grad_y)
-    up_peer = swap(back.grad_up)
-    attn_peer = swap(back.grad_attn)
-    packed_peer = swap(back.grad_packed)
-
-    lefts = [kept.left_keep, left_peer]
-    down = weight_grad([back.grad_y, y_peer], [kept.act_keep, act_peer], 0, features)
-    up = weight_grad(lefts, [back.grad_up, up_peer], 2 * share, share)
-    out = weight_grad(lefts, [back.grad_attn, attn_peer], share, share)
-    qkv = weight_grad(lefts, [back.grad_packed, packed_peer], 0, share)
-
-    norms = table_grad.reshape(-1, chips, CORES, rows).transpose(2, 1, 0, 3)
-    norms = pick(norms, core) + swap(pick(norms, 1 - core))
-
-    down = line_sum(down.reshape(chips, CORES * rows, hidden_units // CORES), chip, chips)
-    up = line_sum(up.reshape(chips, rows, hidden_units), chip, chips)
-    qkv = line_sum(qkv.reshape(chips, rows, 3 * features), chip, chips)
-    out = line_sum(out.reshape(chips, rows, features), chip, chips)
-    norms = line_sum(norms, chip, chips)
-
-    own_rows = lax.dynamic_slice_in_dim(down, core * rows, rows, 0)
-    peer_rows = swap(lax.dynamic_slice_in_dim(down, (1 - core) * rows, rows, 0).astype(BF16))
-    peer_rows = peer_rows.astype(F32)
-    first = jnp.where(core == 0, own_rows, peer_rows)
-    second = jnp.where(core == 0, peer_rows, own_rows)
-    down = jnp.concatenate([first, second], axis=1).T
-    return qkv, out, up, down, norms
-
-
-def sums_by_scatter(plan, kept, back, table_grad, index):
+    swap = exchange.swap
+    table_size = table_grad.shape[0]
+    results = [
+        (rows, 3 * features),
+        (rows, features),
+        (rows, hidden_units),
+        (hidden_units, rows),
+        (table_size, rows),
+    ]
+    line = Line(exchange, rows, results, before)
+
+    def of(right, first_column):
+        pairs = [Pair(left, i, r) for i, (left, r) in enumerate(zip(lefts, (right, swap(right))))]
+        grad = weight_grad(pairs, first_column, share, after=[line.before])
+        line.before = grad
+        return grad
+
+    half = hidden_units // 2
+    down = grad_down(before)
+    line.before = down
+    first = 2 if exchange.ends_hand_over else 1
+    downs = [Piece([Part(down, c, half, 3, c, True)], first) for c in (0, half)]
+    for piece in downs:
+        line.step(piece)
+    up = of(back.grad_up, 2 * share)
+    ups = [Piece([Part(up, c, half, 2, c, False)], 1) for c in (0, half)]
+    for piece in ups + downs:
+        line.step(piece)
+    qkv = of(back.grad_packed, 0)
+    for piece in ups:
+        line.step(piece)
+    out = of(back.grad_attn, share)
+    norms = table_grad + swap(table_grad)
+    norms = norms.reshape(table_size, chips, CORES, rows)
+    norms = lax.dynamic_index_in_dim(norms, core, 2, keepdims=False).transpose(1, 0, 2)
+    norms = jnp.pad(norms.astype(BF16), ((0, 0), (0, rows - table_size), (0, 0)))
+    norms = norms.reshape(chips * rows, rows)
+    cut = 2 * features
+    others = [
+        Piece([Part(qkv, 0, cut, 0, 0, False)], 1),
+        Piece(
+            [
+                Part(qkv, cut, features, 0, cut, False),
+                Part(out, 0, features, 1, 0, False),
+                Part(norms, 0, rows, 4, 0, False),
+            ],
+            1,
+        ),
+    ]
+    order = [downs, ups, others, ups, others, others, others]
+    for pieces in order:
+        for piece in pieces:
+            if piece.hop < chips:
+                line.step(piece)
+    return [line.results[i] for i in range(len(results))]
+
+
+def sums_by_scatter(plan, kept, back, table_grad):
     features = plan.features
     share = features // CORES
-    core = index % CORES
-
-    def local(right, column):
-        mine = weight_grad([kept.left_keep], [right], column, share)
-        other = weight_grad([kept.left_send], [right], column, share)
+    core = lax.axis_index("batch") % CORES
+
+    def local(lefts, rights, column):
+        start = [None, None]
+        for left, right in zip(lefts, rights):
+            for i in range(CORES):
+                start[i] = weight_grad([Pair(left, i, right)], column, share, start[i])
+        mine, other = start
         even, odd = jnp.where(core == 0, mine, other), jnp.where(core == 0, other, mine)
         blocks = [x.reshape(-1, 1, plan.rows, x.shape[1]) for x in (even, odd)]
         return jnp.concatenate(blocks, axis=1).reshape(features, -1)
@@ -755,14 +1053,12 @@
             x, "batch", scatter_dimension=dimension, tiled=True
         ).astype(F32)
 
-    mine = weight_grad([back.grad_y], [kept.act_keep], 0, features)
-    other = weight_grad([back.grad_y], [kept.act_send], 0, features)
-    even, odd = jnp.where(core == 0, mine, other), jnp.where(core == 0, other, mine)
-    down = jnp.concatenate([even, odd], axis=1)
+    grad_y = [back.y_early, jnp.concatenate([back.y_late, back.y_last], axis=1)]
+    down = local(grad_y, [kept.act_early, kept.act_late], 0)
     return (
-        scattered(local(back.grad_packed, 0), 0),
-        scattered(local(back.grad_attn, share), 0),
-        scattered(local(back.grad_up, 2 * share), 0),
+        scattered(local([kept.left], [back.grad_packed], 0), 0),
+        scattered(local([kept.left], [back.grad_attn], share), 0),
+        scattered(local([kept.left], [back.grad_up], 2 * share), 0),
         scattered(down, 0).T,
         scattered(table_grad, 1),
     )
@@ -790,10 +1086,27 @@
         table=norm_table[0],
         weights=Weights(qkv_weight[0], out_weight[0], up_weight[0], down_weight[0]),
     )
+    exchange = Exchange(batch)
+
+    def down_pairs(grad_y, act, first=0):
+        return [Pair(y, i % CORES, a, first) for i, (y, a) in enumerate(zip(grad_y, act))]
+
+    def down_grad(pairs, start, before):
+        share = features // CORES
+        return weight_grad(pairs, 0, share, start, exchange.ends_hand_over, [before])
+
+    after = ()
     incoming = arriving = None
     working = lambda micro: 0 <= micro < micros
     for tick in range(plan.ticks()):
         sent = returned = None
+        if tick == plan.ticks() - 1 and exchange.by_hops:
+            down = down_grad(down_pairs(y_early, act_early), None, state.back.grad_in)
+            y_last = exchange.sources(last_y(plan, state, arriving, down))
+            after = act_late[1:3] + y_last[:1]
+        elif tick == plan.ticks() - 1:
+            y_last = last_y(plan, state, arriving, state.back.grad_in)
+            state = state._replace(back=state.back._replace(y_last=y_last))
         if tick < plan.fwd_ticks():
             state, output = run_forward(plan, tick, state, incoming, frames_all)
             onward = [
@@ -802,22 +1115,37 @@
             if onward:
                 sent = lax.ppermute(output, "section", onward)
         if tick >= sections - 1:
-            state, output = run_backward(plan, tick, state, arriving, cot_all)
+            state, output = run_backward(plan, tick, state, arriving, cot_all, after)
+            after = ()
             backward = [
                 (s, s - 1) for s in range(1, sections) if working(plan.bwd_id(tick, s))
             ]
             if backward:
                 returned = lax.ppermute(output, "section", backward)
         incoming, arriving = sent, returned
+        if exchange.by_hops:
+            if tick == plan.act_spans()[0][1] + sections - 2:
+                act_early = exchange.sources(state.kept.act_early)
+            if tick == plan.fwd_ticks() - 1:
+                act_late = exchange.sources(state.kept.act_late)
+                lefts = [state.kept.left, exchange.swap(state.kept.left)]
+                after = act_early[1:3]
+            if tick == plan.y_spans()[0][1] + 2 * sections - 3:
+                y_early = exchange.sources(state.back.y_early)
+            if tick == plan.ticks() - 2:
+                y_late = exchange.sources(state.back.y_late)
 
     blocks = norm_table.shape[1] // 4
     codes = codebooks * (section % 2)
     table_grad = table_gradient(state.back.row_grads, codes, blocks).reshape(norm_table.shape[1:])
-    index = lax.axis_index("batch")
-    if batch % CORES == 0 and CORES < batch <= CORES * LINE:
-        sums = sums_by_hops(plan, state.kept, state.back, table_grad, batch, index)
+    if exchange.by_hops:
+        late_pairs = down_pairs(y_late, act_late) + down_pairs(y_last, act_late, micros // 2 - 1)
+        sums = sums_by_hops(
+            plan, exchange, state.kept, state.back,
+            lambda before: down_grad(late_pairs, down, before), lefts, table_grad, output,
+        )
     else:
-        sums = sums_by_scatter(plan, state.kept, state.back, table_grad, index)
+        sums = sums_by_scatter(plan, state.kept, state.back, table_grad)
     return (
         state.kept.layer_out.reshape(1, tokens, features),
         state.back.grad_in.reshape(1, tokens, features),

time: 505 us -> 545 us (1.079)
  the two profiles are of different devices: /device:TPU:8 before, /device:TPU:0 now
where the time goes in v2:
time: 545 us; the launch traced here: 535 us
  Pallas kernels  192 us (35%)
  starting transfers between devices  177 us (32%)
  waiting for transfers between devices  136 us (25%)
  local copies, waits for them, and re-layouts  28.1 us (5%)
    pallas_call x36, Pallas kernels, run(): pl.pallas_call(body, out_shape=self.out_shape, in_specs=self.in_specs, ou...  161 us
    ppermute x32, starting transfers between devices, moved(): return lax.ppermute(value, 'batch', pairs)  120 us
    ppermute x5, waiting for transfers between devices, inward(): return lax.ppermute(x, 'batch', pairs)  48.1 us
    ppermute x32, waiting for transfers between devices, moved(): return lax.ppermute(value, 'batch', pairs)  43.4 us
    pallas_call x5, Pallas kernels, weight_grad(): pl.pallas_call(functools.partial(weight_grad_kernel, shares, first_column...  31.1 us
    ppermute x5, starting transfers between devices, inward(): return lax.ppermute(x, 'batch', pairs)  28.2 us
    unnamed x76, local copies, waits for them, and re-layouts  27.2 us
    ppermute x6, starting transfers between devices, per_device(): sent = lax.ppermute(output, 'section', onward)  19.9 us
  transfers between devices with their start and end apart: 64, of which 21 were waited for; matrix products, arithmetic and copies ran while one was open for 0% of the time, Pallas kernels for 22%

profile of v2, /device:TPU:0, one launch (start us, length us, event | category | flops | bytes accessed | tf_op | source)
XLA Modules:
  0.0 535.1 jit_solution(2524706291749140394)
XLA Ops:
  0.6 17.2 %shard_map.144 = (s32[8]{0:T(128)S(4)}, f32[32,1024]{1,0:T(8,128)S(1)}, bf16[1024,3072]{1,0:T(8,128)(2,1)S(1)}, bf16[1024,1024]{1,0:T(8,128)(2,1)S(1)}, bf16[102...) custom-call(s32[4]{0:T(128)} %refs_0_.1, ...), custom_call_target="tpu_custom_call" | custom-call | flops 3221225472 | bytes 4194304 | tf_op jit(solution)/shard_map/pallas_call | solution.py:574
  17.9 6.7 %collective-permute-start = (bf16[128,1024]{1,0:T(8,128)(2,1)S(1)}, bf16[128,1024]{1,0:T(8,128)(2,1)S(1)}, u32[]{:S(2)}, u32[]{:S(2)}) collective-permute-start(bf16[128,1024]{1,0:T(8,128)(2,1)S(1)} %get-tuple-element.245), channel_id=1, source_target_pairs={{0,8},{1,9},{2,10},{3,11},{4,12},{5,13},{6,14},{7,15}} | collective-permute-start | bytes 786440 | tf_op jit(solution)/shard_map/ppermute | solution.py:1116
  24.6 5.5 %collective-permute-done.refs_10_ = bf16[128,1024]{1,0:T(8,128)(2,1)S(1)} collective-permute-done((bf16[128,1024]{1,0:T(8,128)(2,1)S(1)}, bf16[128,1024]{1,0:T(8,128)(2,1)S(1)}, u32[]{:S(2)}, u32[]{:S(2)}) %collective-permute-start) | collective-permute-done | bytes 262176 | tf_op jit(solution)/shard_map/ppermute | solution.py:1116
  30.2 9.3 %shard_map.145 = (bf16[3072,1024]{1,0:T(8,128)(2,1)S(1)}, bf16[1024,1024]{1,0:T(8,128)(2,1)S(1)}, bf16[4096,1024]{1,0:T(8,128)(2,1)S(1)}, bf16[1024,4096]{1,0:T(...) custom-call(s32[8]{0:T(128)S(4)} %get-tuple-element.235.refs_0_, ...), custom_call_target="tpu_custom_call", output_to_operand_aliasing={{0}: (6, {}), {1}: (7, {}), {2}: (8, {}), {3}: (9, {}), {4}... | custom-call | flops 3221225472 | bytes 4194304 | tf_op jit(solution)/shard_map/pallas_call | solution.py:574
  42.9 4.7 collective-permute-done.1.refs_10_
  47.6 9.2 %shard_map.146 = (bf16[3072,1024]{1,0:T(8,128)(2,1)S(1)}, bf16[1024,1024]{1,0:T(8,128)(2,1)S(1)}, bf16[4096,1024]{1,0:T(8,128)(2,1)S(1)}, bf16[1024,4096]{1,0:T(...) custom-call(s32[8]{0:T(128)S(4)} %get-tuple-element.235.refs_0_, ...), custom_call_target="tpu_custom_call", output_to_operand_aliasing={{0}: (6, {}), {1}: (7, {}), {2}: (8, {}), {3}: (9, {}), {4}... | custom-call | flops 3221225472 | bytes 4194304 | tf_op jit(solution)/shard_map/pallas_call | solution.py:574
  56.8 3.9 collective-permute-start.2
  60.7 4.7 collective-permute-done.2.refs_10_
  65.4 10.2 %shard_map.147 = (bf16[3072,1024]{1,0:T(8,128)(2,1)S(1)}, bf16[1024,1024]{1,0:T(8,128)(2,1)S(1)}, bf16[4096,1024]{1,0:T(8,128)(2,1)S(1)}, bf16[1024,4096]{1,0:T(...) custom-call(s32[8]{0:T(128)S(4)} %get-tuple-element.235.refs_0_, ...), custom_call_target="tpu_custom_call", output_to_operand_aliasing={{0}: (6, {}), {1}: (7, {}), {2}: (8, {}), {3}: (9, {}), {4}... | custom-call | flops 3221225472 | bytes 4194304 | tf_op jit(solution)/shard_map/pallas_call | solution.py:574
  75.6 4.4 collective-permute-start.3
  83.9 12.6 %shard_map.149 = (bf16[3072,1024]{1,0:T(8,128)(2,1)S(1)}, bf16[1024,1024]{1,0:T(8,128)(2,1)S(1)}, bf16[4096,1024]{1,0:T(8,128)(2,1)S(1)}, bf16[1024,4096]{1,0:T(...) custom-call(s32[8]{0:T(128)S(4)} %get-tuple-element.235.refs_0_, ...), custom_call_target="tpu_custom_call", output_to_operand_aliasing={{0}: (6, {}), {1}: (7, {}), {2}: (8, {}), {3}: (9, {}), {4}... | custom-call | flops 3221225472 | bytes 4194304 | tf_op jit(solution)/shard_map/pallas_call | solution.py:574
  96.5 3.6 collective-permute-start.11
  102.5 16.5 %shard_map.151 = (bf16[3072,1024]{1,0:T(8,128)(2,1)S(1)}, bf16[1024,1024]{1,0:T(8,128)(2,1)S(1)}, bf16[4096,1024]{1,0:T(8,128)(2,1)S(1)}, bf16[1024,4096]{1,0:T(...) custom-call(s32[8]{0:T(128)S(4)} %get-tuple-element.235.refs_0_, ...), custom_call_target="tpu_custom_call", output_to_operand_aliasing={{0}: (6, {}), {1}: (7, {}), {2}: (8, {}), {3}: (9, {}), {4}... | custom-call | flops 3221225472 | bytes 4194304 | tf_op jit(solution)/shard_map/pallas_call | solution.py:574
  121.1 22.0 %collective-permute-done.11.refs_11_.refs_6_ = bf16[2,128,4096]{2,1,0:T(8,128)(2,1)S(1)} collective-permute-done((bf16[2,128,4096]{2,1,0:T(8,128)(2,1)}, bf16[2,128,4096]{2,1,0:T(8,128)(2,1)S(1)}, u32[]{:S(2)}, u32[]{:S(2)}) %collective-permute-start.11) | collective-permute-done | bytes 2097184 | tf_op jit(solution)/shard_map/ppermute | solution.py:965
  143.1 6.1 %shard_map.153 = (bf16[3072,1024]{1,0:T(8,128)(2,1)S(1)}, bf16[1024,1024]{1,0:T(8,128)(2,1)S(1)}, bf16[4096,1024]{1,0:T(8,128)(2,1)S(1)}, bf16[1024,4096]{1,0:T(...) custom-call(s32[8]{0:T(128)S(4)} %get-tuple-element.235.refs_0_, ...), custom_call_target="tpu_custom_call", output_to_operand_aliasing={{0}: (6, {}), {1}: (7, {}), {2}: (8, {}), {3}: (9, {}), {4}... | custom-call | flops 3221225472 | bytes 4194304 | tf_op jit(solution)/shard_map/pallas_call | solution.py:574
  149.7 6.4 %collective-permute-start.9 = (bf16[2,128,4096]{2,1,0:T(8,128)(2,1)}, bf16[2,128,4096]{2,1,0:T(8,128)(2,1)}, u32[]{:S(2)}, u32[]{:S(2)}) collective-permute-start(bf16[2,128,4096]{2,1,0:T(8,128)(2,1)} %get-tuple-element.355.refs_8_.refs_12_), channel_id=1, source_target_pairs={{0,2},{1,3},{6,4},{7,5},{8,10},{9,11},{14,12},{15,13},{16,18},{17,... | collective-permute-start | bytes 6291464 | tf_op jit(solution)/shard_map/ppermute | solution.py:965
  156.1 9.1 %shard_map.154 = (bf16[4,128,1024]{2,1,0:T(8,128)(2,1)}, bf16[4,128,3072]{2,1,0:T(8,128)(2,1)}, bf16[4,2048,128]{2,1,0:T(8,128)(2,1)}, f32[4,128,1024]{2,1,0:T(8...) custom-call(s32[8]{0:T(128)S(4)} %get-tuple-element.235.refs_0_, ...), custom_call_target="tpu_custom_call", output_to_operand_aliasing={{0}: (12, {}), {1}: (13, {}), {2}: (14, {}), {3}: (15, {}),... | custom-call | flops 3221225472 | bytes 4194304 | tf_op jit(solution)/shard_map/pallas_call | solution.py:574
  166.5 8.6 %collective-permute-done.13.refs_12_ = bf16[128,1024]{1,0:T(8,128)(2,1)S(1)} collective-permute-done((bf16[128,1024]{1,0:T(8,128)(2,1)S(1)}, bf16[128,1024]{1,0:T(8,128)(2,1)S(1)}, u32[]{:S(2)}, u32[]{:S(2)}) %collective-permute-start.13) | collective-permute-done | bytes 262176 | tf_op jit(solution)/shard_map/ppermute | solution.py:1124
  176.5 8.6 %shard_map.155 = (bf16[4,128,1024]{2,1,0:T(8,128)(2,1)}, bf16[4,128,3072]{2,1,0:T(8,128)(2,1)}, bf16[4,2048,128]{2,1,0:T(8,128)(2,1)}, f32[4,128,1024]{2,1,0:T(8...) custom-call(s32[8]{0:T(128)S(4)} %get-tuple-element.235.refs_0_, ...), custom_call_target="tpu_custom_call", output_to_operand_aliasing={{0}: (14, {}), {1}: (15, {}), {2}: (16, {}), {3}: (17, {}),... | custom-call | flops 3221225472 | bytes 4194304 | tf_op jit(solution)/shard_map/pallas_call | solution.py:574
  188.5 7.8 %collective-permute-done.14.refs_10_ = bf16[128,1024]{1,0:T(8,128)(2,1)S(1)} collective-permute-done((bf16[128,1024]{1,0:T(8,128)(2,1)S(1)}, bf16[128,1024]{1,0:T(8,128)(2,1)S(1)}, u32[]{:S(2)}, u32[]{:S(2)}) %collective-permute-start.14) | collective-permute-done | bytes 262176 | tf_op jit(solution)/shard_map/ppermute | solution.py:1124
  196.3 14.4 %collective-permute-done.17.refs_2_ = bf16[2,2,128,512]{3,2,1,0:T(8,128)(2,1)} collective-permute-done((bf16[2,2,128,512]{3,2,1,0:T(8,128)(2,1)}, bf16[2,2,128,512]{3,2,1,0:T(8,128)(2,1)}, u32[]{:S(2)}, u32[]{:S(2)}) %collective-permute-start.17) | collective-permute-done | bytes 524320 | tf_op jit(solution)/shard_map/ppermute | solution.py:965
  210.7 8.6 %shard_map.156 = (bf16[4,128,1024]{2,1,0:T(8,128)(2,1)}, bf16[4,128,3072]{2,1,0:T(8,128)(2,1)}, bf16[4,2048,128]{2,1,0:T(8,128)(2,1)}, f32[4,128,1024]{2,1,0:T(8...) custom-call(s32[8]{0:T(128)S(4)} %get-tuple-element.235.refs_0_, ...), custom_call_target="tpu_custom_call", output_to_operand_aliasing={{0}: (12, {}), {1}: (13, {}), {2}: (14, {}), {3}: (15, {}),... | custom-call | flops 3221225472 | bytes 4194304 | tf_op jit(solution)/shard_map/pallas_call | solution.py:574
  225.1 6.3 %shard_map.157._.refs_16_ = bf16[512,4096]{1,0:T(8,128)(2,1)} custom-call(bf16[2,2,128,512]{3,2,1,0:T(8,128)(2,1)S(1)} %copy-done.20, bf16[2,2,128,512]{3,2,1,0:T(8,128)(2,1)} %collective-permute-done.16.refs_1_, bf16[2,2,128,512]{3,2,1,0:T(8,128)(2,1)} %collective-permute-done.17.refs_2_, bf16[2,2,128,512]{3,2,1,0:T(8,128)(2,1)} %collective-permute-done.18.refs_3_, ...), custom_call_target="tpu_custom_call" | custom-call | flops 4294967296 | bytes 4194304 | tf_op jit(solution)/shard_map/pallas_call | solution.py:770
  242.3 10.3 %shard_map.159 = (bf16[4,128,1024]{2,1,0:T(8,128)(2,1)}, bf16[4,128,3072]{2,1,0:T(8,128)(2,1)}, bf16[4,2048,128]{2,1,0:T(8,128)(2,1)}, f32[4,128,1024]{2,1,0:T(8...) custom-call(s32[8]{0:T(128)S(4)} %get-tuple-element.235.refs_0_, ...), custom_call_target="tpu_custom_call", output_to_operand_aliasing={{0}: (11, {}), {1}: (12, {}), {2}: (13, {}), {3}: (14, {}),... | custom-call | flops 3221225472 | bytes 4194304 | tf_op jit(solution)/shard_map/pallas_call | solution.py:574
  253.7 8.5 %collective-permute-start.23 = (bf16[2,1,128,512]{3,2,1,0:T(8,128)(2,1)S(1)}, bf16[2,1,128,512]{3,2,1,0:T(8,128)(2,1)S(1)}, u32[]{:S(2)}, u32[]{:S(2)}) collective-permute-start(bf16[2,1,128,512]{3,2,1,0:T(8,128)(2,1)S(1)} %copy-done.21), channel_id=1, source_target_pairs={{0,2},{1,3},{6,4},{7,5},{8,10},{9,11},{14,12},{15,13},{16,18},{17,... | collective-permute-start | bytes 786440 | tf_op jit(solution)/shard_map/ppermute | solution.py:965
  262.2 5.7 %collective-permute-done.23.refs_2_ = bf16[2,1,128,512]{3,2,1,0:T(8,128)(2,1)S(1)} collective-permute-done((bf16[2,1,128,512]{3,2,1,0:T(8,128)(2,1)S(1)}, bf16[2,1,128,512]{3,2,1,0:T(8,128)(2,1)S(1)}, u32[]{:S(2)}, u32[]{:S(2)}) %collective-permute-start.23) | collective-permute-done | bytes 262176 | tf_op jit(solution)/shard_map/ppermute | solution.py:965
  268.5 5.1 collective-permute-done.24.refs_3_
  273.6 7.6 %collective-permute-start.26 = (bf16[2,1,128,512]{3,2,1,0:T(8,128)(2,1)S(1)}, bf16[2,1,128,512]{3,2,1,0:T(8,128)(2,1)S(1)}, u32[]{:S(2)}, u32[]{:S(2)}) collective-permute-start(bf16[2,1,128,512]{3,2,1,0:T(8,128)(2,1)S(1)} %shard_map.158.refs_8_.refs_4_), channel_id=1, source_target_pairs={{0,2},{1,3},{6,4},{7,5},{8,10},{9,11},{14,12},{15,13},{16,18},{17,... | collective-permute-start | bytes 786440 | tf_op jit(solution)/shard_map/ppermute | solution.py:965
  281.2 6.1 %collective-permute-done.26.refs_6_ = bf16[2,1,128,512]{3,2,1,0:T(8,128)(2,1)S(1)} collective-permute-done((bf16[2,1,128,512]{3,2,1,0:T(8,128)(2,1)S(1)}, bf16[2,1,128,512]{3,2,1,0:T(8,128)(2,1)S(1)}, u32[]{:S(2)}, u32[]{:S(2)}) %collective-permute-start.26) | collective-permute-done | bytes 262176 | tf_op jit(solution)/shard_map/ppermute | solution.py:965
  290.3 7.8 %shard_map.160.refs_0_.refs_1_ = bf16[512,4096]{1,0:T(8,128)(2,1)} custom-call(bf16[2,1,128,512]{3,2,1,0:T(8,128)(2,1)S(1)} %copy-done.21, bf16[2,1,128,512]{3,2,1,0:T(8,128)(2,1)S(1)} %collective-permute-done.22.refs_1_, bf16[2,1,128,512]{3,2,1,0:T(8,128)(2,1)S(1)} %collective-permute-done.23.refs_2_, ...), custom_call_target="tpu_custom_call" | custom-call | flops 4294967296 | bytes 4194304 | tf_op jit(solution)/shard_map/pallas_call | solution.py:770
  304.1 7.9 %shard_map.163.refs_0_.refs_1_ = bf16[512,4096]{1,0:T(8,128)(2,1)} custom-call(bf16[2,4,128,1536]{3,2,1,0:T(8,128)(2,1)S(1)} %copy-done.7, bf16[2,4,128,1536]{3,2,1,0:T(8,128)(2,1)S(1)} %collective-permute-done.20.refs_1_, bf16[4,128,4096]{2,1,0:T(8,128)(2,1)S(1)} %copy-done.9, bf16[4,128,4096]{2,1,0:T(8,128)(2,1)S(1)} %collective-permute-done.33.refs_3_, ...), custom_call_target="tpu_custom_call" | custom-call | flops 4294967296 | bytes 4194304 | tf_op jit(solution)/shard_map/pallas_call | solution.py:770
  313.3 28.2 %collective-permute-start.37 = (bf16[128,2048]{1,0:T(8,128)(2,1)S(1)}, bf16[128,2048]{1,0:T(8,128)(2,1)S(1)}, u32[]{:S(2)}, u32[]{:S(2)}) collective-permute-start(bf16[128,2048]{1,0:T(8,128)(2,1)S(1)} %get-tuple-element.420.refs_1_), channel_id=1, source_target_pairs={{0,2},{1,3},{8,10},{9,11},{16,18},{17,19},{24,26},{25,27}} | collective-permute-start | bytes 1572872 | tf_op jit(solution)/shard_map/ppermute | solution.py:911
  355.8 6.2 %shard_map.168.refs_3_.refs_0_ = bf16[512,3072]{1,0:T(8,128)(2,1)} custom-call(bf16[2,4,128,1536]{3,2,1,0:T(8,128)(2,1)S(1)} %copy-done.7, bf16[2,4,128,1536]{3,2,1,0:T(8,128)(2,1)S(1)} %collective-permute-done.20.refs_1_, bf16[4,128,3072]{2,1,0:T(8,128)(2,1)S(1)} %copy-done.10, bf16[4,128,3072]{2,1,0:T(8,128)(2,1)S(1)} %collective-permute-done.21.refs_3_, ...), custom_call_target="tpu_custom_call" | custom-call | flops 3221225472 | bytes 3145728 | tf_op jit(solution)/shard_map/pallas_call | solution.py:770
  368.6 9.1 %collective-permute-start.42 = (bf16[128,2048]{1,0:T(8,128)(2,1)}, bf16[128,2048]{1,0:T(8,128)(2,1)}, u32[]{:S(2)}, u32[]{:S(2)}) collective-permute-start(bf16[128,2048]{1,0:T(8,128)(2,1)} %get-tuple-element.427.refs_3_), channel_id=1, source_target_pairs={{0,2},{1,3},{2,4},{3,5},{8,10},{9,11},{10,12},{11,13},{16,18},{17,... | collective-permute-start | bytes 1572872 | tf_op jit(solution)/shard_map/ppermute | solution.py:911
  383.0 4.6 collective-permute-start.40
  406.9 3.8 collective-permute-start.54
  415.5 5.2 collective-permute-start.52
  425.8 3.9 collective-permute-start.48
  431.8 4.6 collective-permute-start.50
  439.3 6.8 %collective-permute-done.53.refs_2_ = bf16[128,2048]{1,0:T(8,128)(2,1)S(1)} collective-permute-done((bf16[128,2048]{1,0:T(8,128)(2,1)S(1)}, bf16[128,2048]{1,0:T(8,128)(2,1)S(1)}, u32[]{:S(2)}, u32[]{:S(2)}) %collective-permute-start.53) | collective-permute-done | bytes 524320 | tf_op jit(solution)/shard_map/ppermute | solution.py:911
  448.2 4.9 collective-permute-done.50.refs_1_
  456.1 4.4 collective-permute-start.56
  461.3 14.6 %collective-permute-start.58 = (bf16[128,2048]{1,0:T(8,128)(2,1)S(1)}, bf16[128,2048]{1,0:T(8,128)(2,1)S(1)}, u32[]{:S(2)}, u32[]{:S(2)}) collective-permute-start(bf16[128,2048]{1,0:T(8,128)(2,1)S(1)} %get-tuple-element.448.refs_5_), channel_id=1, source_target_pairs={{0,2},{1,3},{2,4},{3,5},{8,10},{9,11},{10,12},{11,13},{16,18},{17,... | collective-permute-start | bytes 1572872 | tf_op jit(solution)/shard_map/ppermute | solution.py:911
  476.6 9.6 %collective-permute-done.58.refs_1_ = bf16[128,2048]{1,0:T(8,128)(2,1)S(1)} collective-permute-done((bf16[128,2048]{1,0:T(8,128)(2,1)S(1)}, bf16[128,2048]{1,0:T(8,128)(2,1)S(1)}, u32[]{:S(2)}, u32[]{:S(2)}) %collective-permute-start.58) | collective-permute-done | bytes 524320 | tf_op jit(solution)/shard_map/ppermute | solution.py:911
  489.3 15.1 %collective-permute-start.60 = (bf16[128,2176]{1,0:T(8,128)(2,1)S(1)}, bf16[128,2176]{1,0:T(8,128)(2,1)S(1)}, u32[]{:S(2)}, u32[]{:S(2)}) collective-permute-start(bf16[128,2176]{1,0:T(8,128)(2,1)S(1)} %get-tuple-element.453.refs_3_), channel_id=1, source_target_pairs={{0,2},{1,3},{2,4},{3,5},{4,6},{5,7},{8,10},{9,11},{10,12},{11,13},... | collective-permute-start | bytes 1671176 | tf_op jit(solution)/shard_map/ppermute | solution.py:911
  505.6 4.6 collective-permute-start.62
  511.5 14.2 %collective-permute-done.62.refs_1_ = bf16[128,2048]{1,0:T(8,128)(2,1)S(1)} collective-permute-done((bf16[128,2048]{1,0:T(8,128)(2,1)S(1)}, bf16[128,2048]{1,0:T(8,128)(2,1)S(1)}, u32[]{:S(2)}, u32[]{:S(2)}) %collective-permute-start.62) | collective-permute-done | bytes 524320 | tf_op jit(solution)/shard_map/ppermute | solution.py:911
  525.7 4.1 collective-permute-done.63.refs_2_
  (208 shorter events, 123.9 us)
Async XLA Ops:
  17.9 12.3 %collective-permute-start = (bf16[128,1024]{1,0:T(8,128)(2,1)S(1)}, bf16[128,1024]{1,0:T(8,128)(2,1)S(1)}, u32[]{:S(2)}, u32[]{:S(2)}) collective-permute-start(bf16[128,1024]{1,0:T(8,128)(2,1)S(1)} %get-tuple-element.245), channel_id=1, source_target_pairs={{0,8},{1,9},{2,10},{3,11},{4,12},{5,13},{6,14},{7,15}} | collective-permute-start | bytes 786440 | tf_op jit(solution)/shard_map/ppermute | solution.py:1116
  96.5 46.6 %collective-permute-start.11 = (bf16[2,128,4096]{2,1,0:T(8,128)(2,1)}, bf16[2,128,4096]{2,1,0:T(8,128)(2,1)S(1)}, u32[]{:S(2)}, u32[]{:S(2)}) collective-permute-start(bf16[2,128,4096]{2,1,0:T(8,128)(2,1)} %get-tuple-element.356.refs_4_), channel_id=1, source_target_pairs={{0,2},{1,3},{6,4},{7,5},{8,10},{9,11},{14,12},{15,13},{16,18},{17,... | collective-permute-start | bytes 6291464 | tf_op jit(solution)/shard_map/ppermute | solution.py:965
  100.1 75.0 %collective-permute-start.10 = (bf16[2,128,4096]{2,1,0:T(8,128)(2,1)}, bf16[2,128,4096]{2,1,0:T(8,128)(2,1)S(1)}, u32[]{:S(2)}, u32[]{:S(2)}) collective-permute-start(bf16[2,128,4096]{2,1,0:T(8,128)(2,1)} %get-tuple-element.356.refs_4_), channel_id=1, source_target_pairs={{0,1},{1,0},{2,3},{3,2},{4,5},{5,4},{6,7},{7,6},{8,9},{9,8},{10,11... | collective-permute-start | bytes 6291464 | tf_op jit(solution)/shard_map/ppermute | solution.py:957
  101.8 17.9 %collective-permute-start.7 = (bf16[128,1024]{1,0:T(8,128)(2,1)S(1)}, bf16[128,1024]{1,0:T(8,128)(2,1)S(1)}, u32[]{:S(2)}, u32[]{:S(2)}) collective-permute-start(bf16[128,1024]{1,0:T(8,128)(2,1)S(1)} %get-tuple-element.330), channel_id=1, source_target_pairs={{16,8},{24,16},{17,9},{25,17},{18,10},{26,18},{19,11},{27,19},{20,... | collective-permute-start | bytes 786440 | tf_op jit(solution)/shard_map/ppermute | solution.py:1124
  118.9 24.2 %collective-permute-start.6 = (bf16[128,1024]{1,0:T(8,128)(2,1)S(1)}, bf16[128,1024]{1,0:T(8,128)(2,1)S(1)}, u32[]{:S(2)}, u32[]{:S(2)}) collective-permute-start(bf16[128,1024]{1,0:T(8,128)(2,1)S(1)} %get-tuple-element.329), channel_id=1, source_target_pairs={{16,24},{17,25},{18,26},{19,27},{20,28},{21,29},{22,30},{23,31}} | collective-permute-start | bytes 786440 | tf_op jit(solution)/shard_map/ppermute | solution.py:1116
  119.8 36.3 %collective-permute-start.12 = (bf16[128,1024]{1,0:T(8,128)(2,1)S(1)}, bf16[128,1024]{1,0:T(8,128)(2,1)S(1)}, u32[]{:S(2)}, u32[]{:S(2)}) collective-permute-start(bf16[128,1024]{1,0:T(8,128)(2,1)S(1)} %get-tuple-element.357), channel_id=1, source_target_pairs={{8,0},{16,8},{24,16},{9,1},{17,9},{25,17},{10,2},{18,10},{26,18},{... | collective-permute-start | bytes 786440 | tf_op jit(solution)/shard_map/ppermute | solution.py:1124
  143.1 77.5 %collective-permute-start.19 = (bf16[2,128,4096]{2,1,0:T(8,128)(2,1)S(1)}, bf16[2,128,4096]{2,1,0:T(8,128)(2,1)}, u32[]{:S(2)}, u32[]{:S(2)}) collective-permute-start(bf16[2,128,4096]{2,1,0:T(8,128)(2,1)S(1)} %collective-permute-done.11.refs_11_.refs_6_), channel_id=1, source_target_pairs={{0,1},{1,0},{2,3},{3,2},{4,5},{5,4},{6,7},{7,6},{8,9},{9,8},{10,11... | collective-permute-start | bytes 6291464 | tf_op jit(solution)/shard_map/ppermute | solution.py:957
  149.2 82.3 %collective-permute-start.8 = (bf16[2,128,4096]{2,1,0:T(8,128)(2,1)}, bf16[2,128,4096]{2,1,0:T(8,128)(2,1)}, u32[]{:S(2)}, u32[]{:S(2)}) collective-permute-start(bf16[2,128,4096]{2,1,0:T(8,128)(2,1)} %get-tuple-element.355.refs_8_.refs_12_), channel_id=1, source_target_pairs={{0,1},{1,0},{2,3},{3,2},{4,5},{5,4},{6,7},{7,6},{8,9},{9,8},{10,11... | collective-permute-start | bytes 6291464 | tf_op jit(solution)/shard_map/ppermute | solution.py:957
  149.7 81.8 %collective-permute-start.9 = (bf16[2,128,4096]{2,1,0:T(8,128)(2,1)}, bf16[2,128,4096]{2,1,0:T(8,128)(2,1)}, u32[]{:S(2)}, u32[]{:S(2)}) collective-permute-start(bf16[2,128,4096]{2,1,0:T(8,128)(2,1)} %get-tuple-element.355.refs_8_.refs_12_), channel_id=1, source_target_pairs={{0,2},{1,3},{6,4},{7,5},{8,10},{9,11},{14,12},{15,13},{16,18},{17,... | collective-permute-start | bytes 6291464 | tf_op jit(solution)/shard_map/ppermute | solution.py:965
  185.1 25.6 %collective-permute-start.17 = (bf16[2,2,128,512]{3,2,1,0:T(8,128)(2,1)}, bf16[2,2,128,512]{3,2,1,0:T(8,128)(2,1)}, u32[]{:S(2)}, u32[]{:S(2)}) collective-permute-start(bf16[2,2,128,512]{3,2,1,0:T(8,128)(2,1)} %get-tuple-element.399.refs_0_), channel_id=1, source_target_pairs={{0,2},{1,3},{6,4},{7,5},{8,10},{9,11},{14,12},{15,13},{16,18},{17,... | collective-permute-start | bytes 1572872 | tf_op jit(solution)/shard_map/ppermute | solution.py:965
  196.3 23.1 %collective-permute-start.16 = (bf16[2,2,128,512]{3,2,1,0:T(8,128)(2,1)}, bf16[2,2,128,512]{3,2,1,0:T(8,128)(2,1)}, u32[]{:S(2)}, u32[]{:S(2)}) collective-permute-start(bf16[2,2,128,512]{3,2,1,0:T(8,128)(2,1)} %get-tuple-element.399.refs_0_), channel_id=1, source_target_pairs={{0,1},{1,0},{2,3},{3,2},{4,5},{5,4},{6,7},{7,6},{8,9},{9,8},{10,11... | collective-permute-start | bytes 1572872 | tf_op jit(solution)/shard_map/ppermute | solution.py:957
  219.3 12.1 %collective-permute-start.15 = (bf16[128,1024]{1,0:T(8,128)(2,1)S(1)}, bf16[128,1024]{1,0:T(8,128)(2,1)S(1)}, u32[]{:S(2)}, u32[]{:S(2)}) collective-permute-start(bf16[128,1024]{1,0:T(8,128)(2,1)S(1)} %get-tuple-element.397), channel_id=1, source_target_pairs={{8,0},{9,1},{10,2},{11,3},{12,4},{13,5},{14,6},{15,7}} | collective-permute-start | bytes 786440 | tf_op jit(solution)/shard_map/ppermute | solution.py:1124
  252.6 50.8 %collective-permute-start.33 = (bf16[4,128,4096]{2,1,0:T(8,128)(2,1)}, bf16[4,128,4096]{2,1,0:T(8,128)(2,1)S(1)}, u32[]{:S(2)}, u32[]{:S(2)}) collective-permute-start(bf16[4,128,4096]{2,1,0:T(8,128)(2,1)} %get-tuple-element.419.refs_2_), channel_id=1, source_target_pairs={{0,1},{1,0},{2,3},{3,2},{4,5},{5,4},{6,7},{7,6},{8,9},{9,8},{10,11... | collective-permute-start | bytes 12582920 | tf_op jit(solution)/shard_map/ppermute | solution.py:957
  253.1 48.8 %collective-permute-start.20 = (bf16[2,4,128,1536]{3,2,1,0:T(8,128)(2,1)S(1)}, bf16[2,4,128,1536]{3,2,1,0:T(8,128)(2,1)S(1)}, u32[]{:S(2)}, u32[]{:S(2)}) collective-permute-start(bf16[2,4,128,1536]{3,2,1,0:T(8,128)(2,1)S(1)} %copy-done.7), channel_id=1, source_target_pairs={{0,1},{1,0},{2,3},{3,2},{4,5},{5,4},{6,7},{7,6},{8,9},{9,8},{10,11... | collective-permute-start | bytes 9437192 | tf_op jit(solution)/shard_map/ppermute | solution.py:957
  253.2 37.1 %collective-permute-start.28 = (bf16[2,128,4096]{2,1,0:T(8,128)(2,1)}, bf16[2,128,4096]{2,1,0:T(8,128)(2,1)S(1)}, u32[]{:S(2)}, u32[]{:S(2)}) collective-permute-start(bf16[2,128,4096]{2,1,0:T(8,128)(2,1)} %collective-permute-done.9.refs_7_.refs_10_.refs_14_), channel_id=1, source_target_pairs={{0,1},{1,0},{2,3},{3,2},{4,5},{5,4},{6,7},{7,6},{8,9},{9,8},{10,11... | collective-permute-start | bytes 6291464 | tf_op jit(solution)/shard_map/ppermute | solution.py:957
  253.7 14.3 %collective-permute-start.23 = (bf16[2,1,128,512]{3,2,1,0:T(8,128)(2,1)S(1)}, bf16[2,1,128,512]{3,2,1,0:T(8,128)(2,1)S(1)}, u32[]{:S(2)}, u32[]{:S(2)}) collective-permute-start(bf16[2,1,128,512]{3,2,1,0:T(8,128)(2,1)S(1)} %copy-done.21), channel_id=1, source_target_pairs={{0,2},{1,3},{6,4},{7,5},{8,10},{9,11},{14,12},{15,13},{16,18},{17,... | collective-permute-start | bytes 786440 | tf_op jit(solution)/shard_map/ppermute | solution.py:965
  267.9 80.1 %collective-permute-start.21 = (bf16[4,128,3072]{2,1,0:T(8,128)(2,1)}, bf16[4,128,3072]{2,1,0:T(8,128)(2,1)S(1)}, u32[]{:S(2)}, u32[]{:S(2)}) collective-permute-start(bf16[4,128,3072]{2,1,0:T(8,128)(2,1)} %get-tuple-element.412.refs_2_), channel_id=1, source_target_pairs={{0,1},{1,0},{2,3},{3,2},{4,5},{5,4},{6,7},{7,6},{8,9},{9,8},{10,11... | collective-permute-start | bytes 9437192 | tf_op jit(solution)/shard_map/ppermute | solution.py:957
  273.6 13.6 %collective-permute-start.26 = (bf16[2,1,128,512]{3,2,1,0:T(8,128)(2,1)S(1)}, bf16[2,1,128,512]{3,2,1,0:T(8,128)(2,1)S(1)}, u32[]{:S(2)}, u32[]{:S(2)}) collective-permute-start(bf16[2,1,128,512]{3,2,1,0:T(8,128)(2,1)S(1)} %shard_map.158.refs_8_.refs_4_), channel_id=1, source_target_pairs={{0,2},{1,3},{6,4},{7,5},{8,10},{9,11},{14,12},{15,13},{16,18},{17,... | collective-permute-start | bytes 786440 | tf_op jit(solution)/shard_map/ppermute | solution.py:965
  300.3 46.9 %collective-permute-start.34 = (bf16[4,128,1024]{2,1,0:T(8,128)(2,1)S(1)}, bf16[4,128,1024]{2,1,0:T(8,128)(2,1)S(1)}, u32[]{:S(2)}, u32[]{:S(2)}) collective-permute-start(bf16[4,128,1024]{2,1,0:T(8,128)(2,1)S(1)} %copy-done.13), channel_id=1, source_target_pairs={{0,1},{1,0},{2,3},{3,2},{4,5},{5,4},{6,7},{7,6},{8,9},{9,8},{10,11... | collective-permute-start | bytes 3145736 | tf_op jit(solution)/shard_map/ppermute | solution.py:957
  302.7 38.8 %collective-permute-start.29 = (bf16[128,2048]{1,0:T(8,128)(2,1)S(1)}, bf16[128,2048]{1,0:T(8,128)(2,1)S(1)}, u32[]{:S(2)}, u32[]{:S(2)}) collective-permute-start(bf16[128,2048]{1,0:T(8,128)(2,1)S(1)} %get-tuple-element.416.refs_4_), channel_id=1, source_target_pairs={{2,4},{3,5},{10,12},{11,13},{18,20},{19,21},{26,28},{27,29}} | collective-permute-start | bytes 1572872 | tf_op jit(solution)/shard_map/ppermute | solution.py:911
  303.4 40.0 %collective-permute-start.30 = (bf16[128,2048]{1,0:T(8,128)(2,1)S(1)}, bf16[128,2048]{1,0:T(8,128)(2,1)S(1)}, u32[]{:S(2)}, u32[]{:S(2)}) collective-permute-start(bf16[128,2048]{1,0:T(8,128)(2,1)S(1)} %get-tuple-element.417), channel_id=1, source_target_pairs={{4,2},{5,3},{12,10},{13,11},{20,18},{21,19},{28,26},{29,27}} | collective-permute-start | bytes 1572872 | tf_op jit(solution)/shard_map/ppermute | solution.py:911
  313.3 40.5 %collective-permute-start.37 = (bf16[128,2048]{1,0:T(8,128)(2,1)S(1)}, bf16[128,2048]{1,0:T(8,128)(2,1)S(1)}, u32[]{:S(2)}, u32[]{:S(2)}) collective-permute-start(bf16[128,2048]{1,0:T(8,128)(2,1)S(1)} %get-tuple-element.420.refs_1_), channel_id=1, source_target_pairs={{0,2},{1,3},{8,10},{9,11},{16,18},{17,19},{24,26},{25,27}} | collective-permute-start | bytes 1572872 | tf_op jit(solution)/shard_map/ppermute | solution.py:911
  341.5 13.6 %collective-permute-start.38 = (bf16[128,2048]{1,0:T(8,128)(2,1)S(1)}, bf16[128,2048]{1,0:T(8,128)(2,1)S(1)}, u32[]{:S(2)}, u32[]{:S(2)}) collective-permute-start(bf16[128,2048]{1,0:T(8,128)(2,1)S(1)} %get-tuple-element.426), channel_id=1, source_target_pairs={{6,4},{7,5},{14,12},{15,13},{22,20},{23,21},{30,28},{31,29}} | collective-permute-start | bytes 1572872 | tf_op jit(solution)/shard_map/ppermute | solution.py:911
  343.4 19.6 %collective-permute-start.35 = (bf16[128,2048]{1,0:T(8,128)(2,1)S(1)}, bf16[128,2048]{1,0:T(8,128)(2,1)S(1)}, u32[]{:S(2)}, u32[]{:S(2)}) collective-permute-start(bf16[128,2048]{1,0:T(8,128)(2,1)S(1)} %get-tuple-element.421.refs_3_), channel_id=1, source_target_pairs={{0,2},{1,3},{8,10},{9,11},{16,18},{17,19},{24,26},{25,27}} | collective-permute-start | bytes 1572872 | tf_op jit(solution)/shard_map/ppermute | solution.py:911
  347.2 21.3 %collective-permute-start.36 = (bf16[128,2048]{1,0:T(8,128)(2,1)S(1)}, bf16[128,2048]{1,0:T(8,128)(2,1)S(1)}, u32[]{:S(2)}, u32[]{:S(2)}) collective-permute-start(bf16[128,2048]{1,0:T(8,128)(2,1)S(1)} %get-tuple-element.425), channel_id=1, source_target_pairs={{6,4},{7,5},{14,12},{15,13},{22,20},{23,21},{30,28},{31,29}} | collective-permute-start | bytes 1572872 | tf_op jit(solution)/shard_map/ppermute | solution.py:911
  348.1 29.5 %collective-permute-start.46 = (bf16[128,2048]{1,0:T(8,128)(2,1)S(1)}, bf16[128,2048]{1,0:T(8,128)(2,1)S(1)}, u32[]{:S(2)}, u32[]{:S(2)}) collective-permute-start(bf16[128,2048]{1,0:T(8,128)(2,1)S(1)} %get-tuple-element.422.refs_3_), channel_id=1, source_target_pairs={{2,4},{3,5},{4,6},{5,7},{10,12},{11,13},{12,14},{13,15},{18,20},{1... | collective-permute-start | bytes 1572872 | tf_op jit(solution)/shard_map/ppermute | solution.py:911
  353.8 28.4 %collective-permute-start.47 = (bf16[128,2048]{1,0:T(8,128)(2,1)S(1)}, bf16[128,2048]{1,0:T(8,128)(2,1)S(1)}, u32[]{:S(2)}, u32[]{:S(2)}) collective-permute-start(bf16[128,2048]{1,0:T(8,128)(2,1)S(1)} %get-tuple-element.433), channel_id=1, source_target_pairs={{2,0},{3,1},{4,2},{5,3},{10,8},{11,9},{12,10},{13,11},{18,16},{19,... | collective-permute-start | bytes 1572872 | tf_op jit(solution)/shard_map/ppermute | solution.py:911
  355.1 32.5 %collective-permute-start.44 = (bf16[128,2048]{1,0:T(8,128)(2,1)S(1)}, bf16[128,2048]{1,0:T(8,128)(2,1)S(1)}, u32[]{:S(2)}, u32[]{:S(2)}) collective-permute-start(bf16[128,2048]{1,0:T(8,128)(2,1)S(1)} %get-tuple-element.423.refs_4_), channel_id=1, source_target_pairs={{2,4},{3,5},{4,6},{5,7},{10,12},{11,13},{12,14},{13,15},{18,20},{1... | collective-permute-start | bytes 1572872 | tf_op jit(solution)/shard_map/ppermute | solution.py:911
  363.0 37.7 %collective-permute-start.45 = (bf16[128,2048]{1,0:T(8,128)(2,1)}, bf16[128,2048]{1,0:T(8,128)(2,1)}, u32[]{:S(2)}, u32[]{:S(2)}) collective-permute-start(bf16[128,2048]{1,0:T(8,128)(2,1)} %get-tuple-element.432), channel_id=1, source_target_pairs={{2,0},{3,1},{4,2},{5,3},{10,8},{11,9},{12,10},{13,11},{18,16},{19,... | collective-permute-start | bytes 1572872 | tf_op jit(solution)/shard_map/ppermute | solution.py:911
  368.6 35.7 %collective-permute-start.42 = (bf16[128,2048]{1,0:T(8,128)(2,1)}, bf16[128,2048]{1,0:T(8,128)(2,1)}, u32[]{:S(2)}, u32[]{:S(2)}) collective-permute-start(bf16[128,2048]{1,0:T(8,128)(2,1)} %get-tuple-element.427.refs_3_), channel_id=1, source_target_pairs={{0,2},{1,3},{2,4},{3,5},{8,10},{9,11},{10,12},{11,13},{16,18},{17,... | collective-permute-start | bytes 1572872 | tf_op jit(solution)/shard_map/ppermute | solution.py:911
  378.4 25.8 %collective-permute-start.43 = (bf16[128,2048]{1,0:T(8,128)(2,1)}, bf16[128,2048]{1,0:T(8,128)(2,1)}, u32[]{:S(2)}, u32[]{:S(2)}) collective-permute-start(bf16[128,2048]{1,0:T(8,128)(2,1)} %get-tuple-element.431), channel_id=1, source_target_pairs={{4,2},{5,3},{6,4},{7,5},{12,10},{13,11},{14,12},{15,13},{20,18},{2... | collective-permute-start | bytes 1572872 | tf_op jit(solution)/shard_map/ppermute | solution.py:911
  383.0 29.0 %collective-permute-start.40 = (bf16[128,2048]{1,0:T(8,128)(2,1)}, bf16[128,2048]{1,0:T(8,128)(2,1)}, u32[]{:S(2)}, u32[]{:S(2)}) collective-permute-start(bf16[128,2048]{1,0:T(8,128)(2,1)} %get-tuple-element.428.refs_4_), channel_id=1, source_target_pairs={{0,2},{1,3},{2,4},{3,5},{8,10},{9,11},{10,12},{11,13},{16,18},{17,... | collective-permute-start | bytes 1572872 | tf_op jit(solution)/shard_map/ppermute | solution.py:911
  388.4 23.6 %collective-permute-start.41 = (bf16[128,2048]{1,0:T(8,128)(2,1)}, bf16[128,2048]{1,0:T(8,128)(2,1)}, u32[]{:S(2)}, u32[]{:S(2)}) collective-permute-start(bf16[128,2048]{1,0:T(8,128)(2,1)} %get-tuple-element.430), channel_id=1, source_target_pairs={{4,2},{5,3},{6,4},{7,5},{12,10},{13,11},{14,12},{15,13},{20,18},{2... | collective-permute-start | bytes 1572872 | tf_op jit(solution)/shard_map/ppermute | solution.py:911
  406.9 23.5 %collective-permute-start.54 = (bf16[128,2048]{1,0:T(8,128)(2,1)S(1)}, bf16[128,2048]{1,0:T(8,128)(2,1)S(1)}, u32[]{:S(2)}, u32[]{:S(2)}) collective-permute-start(bf16[128,2048]{1,0:T(8,128)(2,1)S(1)} %get-tuple-element.437.refs_3_), channel_id=1, source_target_pairs={{0,2},{1,3},{2,4},{3,5},{4,6},{5,7},{8,10},{9,11},{10,12},{11,13},... | collective-permute-start | bytes 1572872 | tf_op jit(solution)/shard_map/ppermute | solution.py:911
  410.7 21.1 %collective-permute-start.55 = (bf16[128,2048]{1,0:T(8,128)(2,1)S(1)}, bf16[128,2048]{1,0:T(8,128)(2,1)S(1)}, u32[]{:S(2)}, u32[]{:S(2)}) collective-permute-start(bf16[128,2048]{1,0:T(8,128)(2,1)S(1)} %get-tuple-element.444), channel_id=1, source_target_pairs={{2,0},{3,1},{4,2},{5,3},{6,4},{7,5},{10,8},{11,9},{12,10},{13,11},... | collective-permute-start | bytes 1572872 | tf_op jit(solution)/shard_map/ppermute | solution.py:911
  415.5 20.9 %collective-permute-start.52 = (bf16[128,2048]{1,0:T(8,128)(2,1)S(1)}, bf16[128,2048]{1,0:T(8,128)(2,1)S(1)}, u32[]{:S(2)}, u32[]{:S(2)}) collective-permute-start(bf16[128,2048]{1,0:T(8,128)(2,1)S(1)} %get-tuple-element.438.refs_1_), channel_id=1, source_target_pairs={{0,2},{1,3},{2,4},{3,5},{4,6},{5,7},{8,10},{9,11},{10,12},{11,13},... | collective-permute-start | bytes 1572872 | tf_op jit(solution)/shard_map/ppermute | solution.py:911
  425.8 28.8 %collective-permute-start.48 = (bf16[128,2176]{1,0:T(8,128)(2,1)S(1)}, bf16[128,2176]{1,0:T(8,128)(2,1)S(1)}, u32[]{:S(2)}, u32[]{:S(2)}) collective-permute-start(bf16[128,2176]{1,0:T(8,128)(2,1)S(1)} %get-tuple-element.440.refs_3_), channel_id=1, source_target_pairs={{0,2},{1,3},{8,10},{9,11},{16,18},{17,19},{24,26},{25,27}} | collective-permute-start | bytes 1671176 | tf_op jit(solution)/shard_map/ppermute | solution.py:911
  429.7 24.9 %collective-permute-start.49 = (bf16[128,2176]{1,0:T(8,128)(2,1)S(1)}, bf16[128,2176]{1,0:T(8,128)(2,1)S(1)}, u32[]{:S(2)}, u32[]{:S(2)}) collective-permute-start(bf16[128,2176]{1,0:T(8,128)(2,1)S(1)} %get-tuple-element.441), channel_id=1, source_target_pairs={{6,4},{7,5},{14,12},{15,13},{22,20},{23,21},{30,28},{31,29}} | collective-permute-start | bytes 1671176 | tf_op jit(solution)/shard_map/ppermute | solution.py:911
  430.4 15.6 %collective-permute-start.53 = (bf16[128,2048]{1,0:T(8,128)(2,1)S(1)}, bf16[128,2048]{1,0:T(8,128)(2,1)S(1)}, u32[]{:S(2)}, u32[]{:S(2)}) collective-permute-start(bf16[128,2048]{1,0:T(8,128)(2,1)S(1)} %copy-done.35), channel_id=1, source_target_pairs={{2,0},{3,1},{4,2},{5,3},{6,4},{7,5},{10,8},{11,9},{12,10},{13,11},... | collective-permute-start | bytes 1572872 | tf_op jit(solution)/shard_map/ppermute | solution.py:911
  431.8 21.3 %collective-permute-start.50 = (bf16[128,2048]{1,0:T(8,128)(2,1)S(1)}, bf16[128,2048]{1,0:T(8,128)(2,1)S(1)}, u32[]{:S(2)}, u32[]{:S(2)}) collective-permute-start(bf16[128,2048]{1,0:T(8,128)(2,1)S(1)} %get-tuple-element.439.refs_3_), channel_id=1, source_target_pairs={{0,2},{1,3},{8,10},{9,11},{16,18},{17,19},{24,26},{25,27}} | collective-permute-start | bytes 1572872 | tf_op jit(solution)/shard_map/ppermute | solution.py:911
  436.4 16.8 %collective-permute-start.51 = (bf16[128,2048]{1,0:T(8,128)(2,1)S(1)}, bf16[128,2048]{1,0:T(8,128)(2,1)S(1)}, u32[]{:S(2)}, u32[]{:S(2)}) collective-permute-start(bf16[128,2048]{1,0:T(8,128)(2,1)S(1)} %get-tuple-element.442), channel_id=1, source_target_pairs={{6,4},{7,5},{14,12},{15,13},{22,20},{23,21},{30,28},{31,29}} | collective-permute-start | bytes 1572872 | tf_op jit(solution)/shard_map/ppermute | solution.py:911
  456.1 31.6 %collective-permute-start.56 = (bf16[128,2176]{1,0:T(8,128)(2,1)S(1)}, bf16[128,2176]{1,0:T(8,128)(2,1)S(1)}, u32[]{:S(2)}, u32[]{:S(2)}) collective-permute-start(bf16[128,2176]{1,0:T(8,128)(2,1)S(1)} %get-tuple-element.449.refs_3_), channel_id=1, source_target_pairs={{0,2},{1,3},{2,4},{3,5},{8,10},{9,11},{10,12},{11,13},{16,18},{17,... | collective-permute-start | bytes 1671176 | tf_op jit(solution)/shard_map/ppermute | solution.py:911
  460.6 27.1 %collective-permute-start.57 = (bf16[128,2176]{1,0:T(8,128)(2,1)S(1)}, bf16[128,2176]{1,0:T(8,128)(2,1)S(1)}, u32[]{:S(2)}, u32[]{:S(2)}) collective-permute-start(bf16[128,2176]{1,0:T(8,128)(2,1)S(1)} %get-tuple-element.450), channel_id=1, source_target_pairs={{4,2},{5,3},{6,4},{7,5},{12,10},{13,11},{14,12},{15,13},{20,18},{2... | collective-permute-start | bytes 1671176 | tf_op jit(solution)/shard_map/ppermute | solution.py:911
  461.3 24.9 %collective-permute-start.58 = (bf16[128,2048]{1,0:T(8,128)(2,1)S(1)}, bf16[128,2048]{1,0:T(8,128)(2,1)S(1)}, u32[]{:S(2)}, u32[]{:S(2)}) collective-permute-start(bf16[128,2048]{1,0:T(8,128)(2,1)S(1)} %get-tuple-element.448.refs_5_), channel_id=1, source_target_pairs={{0,2},{1,3},{2,4},{3,5},{8,10},{9,11},{10,12},{11,13},{16,18},{17,... | collective-permute-start | bytes 1572872 | tf_op jit(solution)/shard_map/ppermute | solution.py:911
  489.3 42.8 %collective-permute-start.60 = (bf16[128,2176]{1,0:T(8,128)(2,1)S(1)}, bf16[128,2176]{1,0:T(8,128)(2,1)S(1)}, u32[]{:S(2)}, u32[]{:S(2)}) collective-permute-start(bf16[128,2176]{1,0:T(8,128)(2,1)S(1)} %get-tuple-element.453.refs_3_), channel_id=1, source_target_pairs={{0,2},{1,3},{2,4},{3,5},{4,6},{5,7},{8,10},{9,11},{10,12},{11,13},... | collective-permute-start | bytes 1671176 | tf_op jit(solution)/shard_map/ppermute | solution.py:911
  504.3 27.7 %collective-permute-start.61 = (bf16[128,2176]{1,0:T(8,128)(2,1)S(1)}, bf16[128,2176]{1,0:T(8,128)(2,1)S(1)}, u32[]{:S(2)}, u32[]{:S(2)}) collective-permute-start(bf16[128,2176]{1,0:T(8,128)(2,1)S(1)} %get-tuple-element.454), channel_id=1, source_target_pairs={{2,0},{3,1},{4,2},{5,3},{6,4},{7,5},{10,8},{11,9},{12,10},{13,11},... | collective-permute-start | bytes 1671176 | tf_op jit(solution)/shard_map/ppermute | solution.py:911
  505.6 20.1 %collective-permute-start.62 = (bf16[128,2048]{1,0:T(8,128)(2,1)S(1)}, bf16[128,2048]{1,0:T(8,128)(2,1)S(1)}, u32[]{:S(2)}, u32[]{:S(2)}) collective-permute-start(bf16[128,2048]{1,0:T(8,128)(2,1)S(1)} %get-tuple-element.452.refs_5_), channel_id=1, source_target_pairs={{0,2},{1,3},{2,4},{3,5},{4,6},{5,7},{8,10},{9,11},{10,12},{11,13},... | collective-permute-start | bytes 1572872 | tf_op jit(solution)/shard_map/ppermute | solution.py:911
  510.2 19.6 %collective-permute-start.63 = (bf16[128,2048]{1,0:T(8,128)(2,1)S(1)}, bf16[128,2048]{1,0:T(8,128)(2,1)S(1)}, u32[]{:S(2)}, u32[]{:S(2)}) collective-permute-start(bf16[128,2048]{1,0:T(8,128)(2,1)S(1)} %get-tuple-element.455), channel_id=1, source_target_pairs={{2,0},{3,1},{4,2},{5,3},{6,4},{7,5},{10,8},{11,9},{12,10},{13,11},... | collective-permute-start | bytes 1572872 | tf_op jit(solution)/shard_map/ppermute | solution.py:911
  (54 other events, 560.3 us)

commit v3 on v2

--- a/solution.py
+++ b/solution.py
@@ -13,6 +13,8 @@
 BLOCK = 512
 LANES = 128
 CORES = 2
+VMEM_LIMIT = 14 * 2**20
+WHOLE, FIRST, SECOND = 0, 1, 2
 LINE = 4
 
 epsilon = 1e-05
@@ -43,8 +45,8 @@
 class Kept(NamedTuple):
     layer_out: Any
     left: Any
-    act_early: Any
-    act_late: Any
+    second: Any
+    act: Any
 
 
 class Back(NamedTuple):
@@ -52,7 +54,8 @@
     y_early: Any
     y_late: Any
     y_last: Any
-    grad_up: Any
+    up_early: Any
+    up_last: Any
     grad_attn: Any
     grad_packed: Any
     row_grads: Any
@@ -169,28 +172,6 @@
         strip(i).wait()
 
 
-def split_columns(plan, core, source, target):
-    width = plan.rows
-    for b in range(plan.features // width):
-        at = (b // CORES) * width
-        which = jnp.where(core == b % CORES, 0, 1)
-        target[which, :, at : at + width] = source[:, b * width : (b + 1) * width]
-
-
-def last_y_kernel(plan, arriving, stored, _, y_last, sem):
-    at_start = lax.axis_index("section") == 0
-
-    @pl.when(at_start)
-    def split():
-        split_columns(plan, lax.axis_index("batch") % CORES, arriving, y_last.at[:, 0])
-
-    @pl.when(jnp.logical_not(at_start))
-    def fetch():
-        copy = pltpu.make_async_copy(stored, y_last, sem)
-        copy.start()
-        copy.wait()
-
-
 class Plan(NamedTuple):
     sections: int
     micros: int
@@ -205,22 +186,23 @@
     def ticks(self):
         return self.micros + 2 * (self.sections - 1)
 
-    def act_spans(self):
-        half = self.micros // 2
-        return (0, half), (half, self.micros)
-
     def y_spans(self):
         half = self.micros // 2
         return (0, half), (half, self.micros - 1), (self.micros - 1, self.micros)
 
-    def fwd_reaches(self, tick):
-        low, high = tick - (self.sections - 1), tick
-        return tuple(low < end and high >= first for first, end in self.act_spans())
+    def up_spans(self):
+        return (0, self.micros - 1), (self.micros - 1, self.micros)
 
     def bwd_reaches(self, tick):
         low, high = tick - 2 * (self.sections - 1), tick - (self.sections - 1)
-        last = tick == self.ticks() - 1
-        return tuple(low < end and high >= first and not last for first, end in self.y_spans())
+        grad_y = tuple(low < end and high >= first for first, end in self.y_spans())
+        grad_up = tuple(low < end and high >= first for first, end in self.up_spans())
+        return (True,) + grad_y + grad_up + (True,) * 3
+
+    def bwd_uses(self, tick, part):
+        first = (False,) + (True,) * 6 + (False, False)
+        halves = {WHOLE: (True,) * 9, FIRST: first, SECOND: tuple(not f for f in first)}
+        return tuple(r and h for r, h in zip(self.bwd_reaches(tick), halves[part]))
 
     def fwd_id(self, tick, section):
         return tick - section
@@ -241,16 +223,14 @@
         take(4)
     incoming = take(1)[0] if has_incoming else None
     (frames_in,) = take(1)
-    reaches = plan.fwd_reaches(tick)
     if loads_weights:
         info, table = take(2)
         weight = Weights(*take(4))
     else:
-        take(len(Reread._fields) + 2)
-        take(sum(now and had for now, had in zip(reaches, plan.fwd_reaches(tick - 1))))
+        take(len(Reread._fields) + len(Kept._fields))
     turned = Weights(*take(4))
     reread = Reread(*take(5))
-    kept = Kept(*take(2), *[take(1)[0] if on else None for on in reaches])
+    kept = Kept(*take(4))
     (outgoing,) = take(1)
     entry, packed, probs, hidden, slope, normed, left, attended, act, strips, sems = refs
 
@@ -347,6 +327,7 @@
         normal_two, _ = normalize(hidden[...])
         normed[...] = (normal_two * (1.0 + rows[2:3]) + rows[3:4]).astype(BF16)
         share_columns(normed, 2 * share)
+        save(normed, kept.second.at[slot])
         save(left.at[core], kept.left.at[0, slot])
         save(left.at[1 - core], kept.left.at[1, slot])
         ready(3)
@@ -355,7 +336,7 @@
             act[:, j : j + BLOCK] = value.astype(BF16)
             slope[:, j : j + BLOCK] = gradient.astype(BF16)
         save(slope, reread.slope.at[slot])
-        save.spread(act, (kept.act_early, kept.act_late), plan.act_spans(), slot)
+        save(act, kept.act.at[slot])
         ready(4)
         for j in range(0, features, BLOCK):
             outgoing[:, j : j + BLOCK] = (
@@ -386,45 +367,49 @@
                 turn(source, target, r, c, features, strips, sems, base)
 
 
-def backward_kernel(plan, tick, has_arriving, first, unread, *refs):
+def backward_kernel(plan, tick, part, has_arriving, present, unread, *refs):
     refs = list(refs)
     take = lambda n: [refs.pop(0) for _ in range(n)]
     info, table = take(2)
-    turned = Weights(*take(4))
+    turned = Weights(*(take(1) + [None] * 3 if part == SECOND else take(4)))
     take(unread)
     arriving = take(1)[0] if has_arriving else None
     (cotangent,) = take(1)
     take(len(Reread._fields))
-    reaches = plan.bwd_reaches(tick)
-    used = (True,) + reaches + (True,) * 4
-    if not first:
-        had = (True,) + plan.bwd_reaches(tick - 1) + (True,) * 4
-        take(sum(u and h for u, h in zip(used, had)))
+    used = plan.bwd_uses(tick, part)
+    take(sum(u and p for u, p in zip(used, present)))
+    halfway = take(3) if part == SECOND else None
     reread = Reread(*take(5))
     back = Back(*[take(1)[0] if u else None for u in used])
-    (returning,) = take(1)
-    (entry, packed, probs, hidden, slope, grad_y, y_split, grad_up, wide, grad_hidden, grad_attn,
-     mixed, grad_packed, row_grads, sems) = refs
+    if part == FIRST:
+        halfway = take(3)
+    else:
+        (returning,) = take(1)
+    (entry, packed, probs, hidden, slope, grad_y, grad_up, wide, grad_hidden, grad_attn, mixed,
+     grad_packed, row_grads, sems) = refs
 
     micros, frames, features, hidden_units, _ = plan[1:]
     head_size = features // HEADS
     group_width = GROUP * head_size
     section = lax.axis_index("section")
-    core = lax.axis_index("batch") % CORES
     is_nar = section % 2
     micro = plan.bwd_id(tick, section)
     active = (micro >= 0) & (micro < micros)
     slot = jnp.clip(micro, 0, micros - 1)
 
-    @pl.when(active)
-    def backward():
-        length = info[slot]
-        code = info[micros + slot] * is_nar
+    def start_fetches(wanted):
         fetches = []
         for i, target in enumerate((entry, packed, probs, hidden, slope)):
             fetches.append(pltpu.make_async_copy(reread[i].at[slot], target, sems.at[i]))
         for i in (4, 3, 1, 2, 0):
-            fetches[i].start()
+            if i in wanted:
+                fetches[i].start()
+        return fetches
+
+    def first_half():
+        length = info[slot]
+        code = info[micros + slot] * is_nar
+        fetches = start_fetches((3, 4) if part == FIRST else range(5))
         save = Saver(sems, len(fetches))
 
         def own_cotangent():
@@ -442,11 +427,7 @@
         else:
             own_cotangent()
 
-        if any(reaches):
-            split_columns(plan, core, grad_y, y_split)
-            for c in range(CORES):
-                places = [None if b is None else b.at[c] for b in back[1:4]]
-                save.spread(y_split.at[c], places, plan.y_spans(), slot)
+        save.spread(grad_y, back[1:4], plan.y_spans(), slot)
         rows = table_rows(table, code)
         fetches[4].wait()
         for j in range(0, hidden_units, BLOCK):
@@ -454,7 +435,7 @@
             grad_up[:, j : j + BLOCK] = (
                 grad_act * slope[:, j : j + BLOCK].astype(F32)
             ).astype(BF16)
-        save(grad_up, back.grad_up.at[slot])
+        save.spread(grad_up, (back.up_early, back.up_last), plan.up_spans(), slot)
         for j in range(0, features, BLOCK):
             wide[:, j : j + BLOCK] = product(grad_up[...], turned.up[:, j : j + BLOCK])
         fetches[3].wait()
@@ -471,6 +452,11 @@
             mixed[:, j : j + BLOCK] = product(
                 grad_attn[...], turned.out[:, j : j + BLOCK]
             ).astype(BF16)
+        return fetches, save
+
+    def second_half(fetches, save):
+        code = info[micros + slot] * is_nar
+        rows = table_rows(table, code)
         fetches[1].wait()
         fetches[2].wait()
         inv_root = head_size ** (-0.5)
@@ -509,6 +495,24 @@
         save(returning, back.grad_in.at[slot])
         save.wait()
 
+    @pl.when(active)
+    def backward():
+        if part == SECOND:
+            fetches = start_fetches((0, 1, 2))
+            load = Saver(sems, 5)
+            for source, target in zip(halfway, (grad_hidden, mixed, row_grads)):
+                load(source, target)
+            load.wait()
+            second_half(fetches, Saver(sems, 5))
+            return
+        fetches, save = first_half()
+        if part == FIRST:
+            for source, target in zip((grad_hidden, mixed, row_grads), halfway):
+                save(source, target)
+            save.wait()
+        else:
+            second_half(fetches, save)
+
 
 def shapes_of(plan):
     micros, frames, features, hidden_units, _ = plan[1:]
@@ -520,16 +524,16 @@
         hidden=(own + (features,), F32),
         slope=(own + (hidden_units,), BF16),
     )
-    def buffers(spans, before, columns):
-        return [(before + (end - first, frames, columns), BF16) for first, end in spans]
+    def buffers(spans, columns):
+        return [((end - first, frames, columns), BF16) for first, end in spans]
 
     left = ((CORES,) + own + (3 * features // CORES,), BF16)
-    kept = Kept((own + (features,), BF16), left, *buffers(plan.act_spans(), (), hidden_units))
     wide = (own + (features,), BF16)
+    kept = Kept(wide, left, wide, (own + (hidden_units,), BF16))
     back = Back(
         wide,
-        *buffers(plan.y_spans(), (CORES,), features // CORES),
-        grad_up=(own + (hidden_units,), BF16),
+        *buffers(plan.y_spans(), features),
+        *buffers(plan.up_spans(), hidden_units),
         grad_attn=wide,
         grad_packed=(own + (3 * features,), BF16),
         row_grads=((micros, 4, features), F32),
@@ -569,7 +573,7 @@
             elif use:
                 self.give([shape], anywhere, pltpu.HBM)
 
-    def run(self, body, scratch, flops):
+    def run(self, body, scratch, flops, limit=VMEM_LIMIT):
         return list(
             pl.pallas_call(
                 body,
@@ -578,9 +582,9 @@
                 out_specs=self.out_specs,
                 scratch_shapes=scratch,
                 input_output_aliases=self.aliases,
-                compiler_params=pltpu.CompilerParams(vmem_limit_bytes=10 * 2**20),
+                compiler_params=pltpu.CompilerParams(vmem_limit_bytes=limit),
                 cost_estimate=pl.CostEstimate(
-                    flops=flops, bytes_accessed=2**22, transcendentals=0
+                    flops=flops, bytes_accessed=0, transcendentals=0
                 ),
             )(*self.args)
         )
@@ -631,11 +635,9 @@
         call.give(like(state.weights), in_vmem, pltpu.VMEM)
     else:
         at_kept = len(call.args)
-        call.take(state.reread, anywhere, pltpu.HBM)
+        call.take(state.reread + state.kept, anywhere, pltpu.HBM)
     call.give([(w.shape[::-1], BF16) for w in state.weights], anywhere, pltpu.VMEM, at_turned)
-    call.give(reread_shapes, anywhere, pltpu.HBM, at_kept)
-    used = (True, True) + plan.fwd_reaches(tick)
-    call.update(state.kept, kept_shapes, used)
+    call.give(reread_shapes + kept_shapes, anywhere, pltpu.HBM, at_kept)
     call.give([((plan.frames, plan.features), BF16)], in_vmem, pltpu.VMEM)
     scratch = scratch_of(reread_shapes) + [
         pltpu.VMEM((plan.frames, plan.features), BF16),
@@ -645,24 +647,23 @@
         pltpu.VMEM((2, plan.features, 256), BF16),
         pltpu.SemaphoreType.DMA((24,)),
     ]
-    flops = 2 * plan.frames * sum(w.size for w in state.weights)
+    flops = 8 * plan.frames * sum(w.size for w in state.weights)
     body = functools.partial(forward_kernel, plan, tick, incoming is not None, first)
     got = call.run(body, scratch, flops)
     if first:
         state = state._replace(info=got[0], table=got[1], weights=Weights(*got[2:6]))
         got = got[6:]
-    kept = Kept(*updated(state.kept, used, got[9:-1]))
+    kept = Kept(*got[9:13])
     return state._replace(turned=Weights(*got[:4]), reread=Reread(*got[4:9]), kept=kept), got[-1]
 
 
-def run_backward(plan, tick, state, arriving, cotangent, after):
+def run_backward(plan, tick, state, arriving, cotangent, after, part=WHOLE, halfway=()):
     reread_shapes, _, back_shapes = shapes_of(plan)
-    first = state.back is None
     call = Call()
     call.take([state.info], in_smem, pltpu.SMEM)
     call.take([state.table], in_vmem, pltpu.VMEM)
-    call.take(state.turned, in_vmem, pltpu.VMEM)
-    staying = state.weights if tick < plan.ticks() - 1 else ()
+    call.take(state.turned[:1] if part == SECOND else state.turned, in_vmem, pltpu.VMEM)
+    staying = () if part == SECOND else state.weights
     call.take(staying, anywhere, pltpu.VMEM)
     call.take(after, anywhere)
     unread = len(staying) + len(after)
@@ -672,39 +673,37 @@
     at_reread = len(call.args)
     call.take(state.reread, anywhere, pltpu.HBM)
     call.give(reread_shapes, anywhere, pltpu.HBM, at_reread)
-    used = (True,) + plan.bwd_reaches(tick) + (True,) * 4
+    used = plan.bwd_uses(tick, part)
+    present = [b is not None for b in state.back or (None,) * len(used)]
     call.update(state.back, back_shapes, used)
-    call.give([((plan.frames, plan.features), BF16)], in_vmem, pltpu.VMEM)
-    narrow = pltpu.VMEM((plan.frames, plan.features), BF16)
-    full = pltpu.VMEM((plan.frames, plan.features), F32)
+    narrow = ((plan.frames, plan.features), BF16)
+    full = ((plan.frames, plan.features), F32)
+    between = [full, narrow, ((4, plan.features), F32)]
+    call.take(halfway, anywhere, pltpu.HBM)
+    results = between if part == FIRST else [narrow]
+    if part == FIRST:
+        call.give(results, anywhere, pltpu.HBM)
+    else:
+        call.give(results, in_vmem, pltpu.VMEM)
     scratch = scratch_of(reread_shapes) + [
-        narrow,
-        pltpu.VMEM((CORES, plan.frames, plan.features // CORES), BF16),
+        pltpu.VMEM(*narrow),
         pltpu.VMEM((plan.frames, plan.hidden_units), BF16),
-        full,
-        full,
-        narrow,
-        narrow,
+        pltpu.VMEM(*full),
+        pltpu.VMEM(*full),
+        pltpu.VMEM(*narrow),
+        pltpu.VMEM(*narrow),
         pltpu.VMEM((plan.frames, 3 * plan.features), BF16),
         pltpu.VMEM((4, plan.features), F32),
         pltpu.SemaphoreType.DMA((16,)),
     ]
-    flops = 2 * plan.frames * sum(w.size for w in state.turned)
-    body = functools.partial(backward_kernel, plan, tick, arriving is not None, first, unread)
-    got = call.run(body, scratch, flops)
-    back = Back(*updated(state.back, used, got[5:-1]))
-    return state._replace(reread=Reread(*got[:5]), back=back), got[-1]
-
-
-def last_y(plan, state, arriving, before):
-    stored = state.back.y_last
-    return pl.pallas_call(
-        functools.partial(last_y_kernel, plan),
-        out_shape=pltpu.VMEM(stored.shape, BF16),
-        in_specs=[in_vmem, anywhere, anywhere],
-        out_specs=in_vmem,
-        scratch_shapes=[pltpu.SemaphoreType.DMA],
-    )(pltpu.with_memory_space_constraint(arriving, pltpu.VMEM), in_hbm(stored), before)
+    flops = 8 * plan.frames * sum(w.size for w in state.turned)
+    body = functools.partial(
+        backward_kernel, plan, tick, part, arriving is not None, present, unread
+    )
+    got = call.run(body, scratch, flops if part == WHOLE else flops // 2)
+    got, last = got[: -len(results)], got[-len(results) :]
+    back = Back(*updated(state.back, used, got[5:]))
+    return state._replace(reread=Reread(*got[:5]), back=back), last
 
 
 def in_hbm(x):
@@ -713,92 +712,148 @@
 
 class Pair(NamedTuple):
     left: Any
-    share: int
+    share: Any
     right: Any
-    first: int = 0
-
-
-def weight_grad_kernel(shares, first_column, width, has_start, skip_ends, *refs):
-    count = len(shares)
-    lefts, rights = refs[:count], refs[count : 2 * count]
-    start = refs[2 * count] if has_start else None
-    out, stage, turned, sems = refs[-4:]
-    micros, frames, step = rights[0].shape
+    count: int
+    left_first: int = 0
+    right_first: int = 0
+
+
+def weight_grad_kernel(pairs, first_column, rows, step, outputs, remade, *refs):
+    lefts, rights = refs[: len(pairs)], refs[len(pairs) : len(pairs) + len(pairs) - remade]
+    if remade:
+        normed_in, weight_in = refs[2 * len(pairs) - remade : 2 * len(pairs) - remade + 2]
+        normed, weight_slots, refs = refs[-2], refs[-1], refs[:-2]
+    outs = refs[-5 - outputs : -5]
+    stage, turned, right_slots, sems, right_sems = refs[-5:]
+    frames, width = stage.shape[1:]
+    share = width // outputs
+    steps = outs[0].shape[1] // step
+    core = lax.axis_index("batch") % CORES
     chip = lax.axis_index("batch") // CORES
     chips = lax.axis_size("batch") // CORES
-    works = (chip > 0) & (chip < chips - 1) if skip_ends else chip >= 0
-
-    @pl.when(works & (pl.program_id(0) == 0))
-    def turn_lefts():
-        copies = []
-        for i, left in enumerate(lefts):
-            part = left.at[shares[i], :, :, pl.ds(first_column, width)]
-            copies.append(pltpu.make_async_copy(part, stage.at[i], sems.at[i]))
-            copies[i].start()
-        for i in range(count):
-            copies[i].wait()
-            for m in range(micros):
-                turned[i, :, m * frames : (m + 1) * frames] = stage[i, m].T
+    works = (chip > 0) & (chip < chips - 1) if remade else chip >= 0
+    firsts = [sum(p.count for p in pairs[:i]) for i in range(len(pairs))]
+    columns = lambda j: pl.ds(pl.multiple_of(j * step, step), step)
+
+    given = list(enumerate(pairs))[: len(rights)]
+    remade_from = sum(p.count for _, p in given)
+
+    def right_copies(j, slot):
+        copies = [
+            pltpu.make_async_copy(
+                rights[i].at[pl.ds(p.right_first, p.count), :, columns(j)],
+                right_slots.at[slot, pl.ds(firsts[i], p.count)],
+                right_sems.at[slot, i],
+            )
+            for i, p in given
+        ]
+        if remade:
+            copies.append(
+                pltpu.make_async_copy(
+                    weight_in.at[:, columns(j)], weight_slots.at[slot], right_sems.at[slot, len(given)]
+                )
+            )
+        return copies
+
+    def turn_in(m, at):
+        if outputs == 1:
+            turned[0, :, at : at + frames] = stage[m].T
+            return
+        for b in range(width // rows):
+            which = jnp.where(core == b % CORES, 0, 1)
+            place = (b // CORES) * rows
+            block = stage[m, :, b * rows : (b + 1) * rows].T
+            turned[which, place : place + rows, at : at + frames] = block
 
     @pl.when(works)
     def add_up():
-        total = start[...].astype(F32) if has_start else None
-        for i in range(count):
-            term = product(turned[i], rights[i][...].reshape(micros * frames, step))
-            total = term if total is None else total + term
-        out[...] = total.astype(BF16)
-
-    if skip_ends:
+        copies = []
+        for i, p in enumerate(pairs):
+            left = lefts[i] if p.share is None else lefts[i].at[p.share]
+            source = left.at[pl.ds(p.left_first, p.count), :, pl.ds(first_column, width)]
+            copies.append(
+                pltpu.make_async_copy(source, stage.at[pl.ds(firsts[i], p.count)], sems.at[i])
+            )
+            copies[i].start()
+        for copy in right_copies(0, 0):
+            copy.start()
+        if remade:
+            load = pltpu.make_async_copy(normed_in, normed, sems.at[len(pairs)])
+            load.start()
+        for i, p in enumerate(pairs):
+            copies[i].wait()
+            for m in range(firsts[i], firsts[i] + p.count):
+                turn_in(m, m * frames)
+        if remade:
+            load.wait()
+
+        def one_step(j, carry):
+            slot = j % 2
+
+            @pl.when(j + 1 < steps)
+            def next_block():
+                for copy in right_copies(j + 1, 1 - slot):
+                    copy.start()
+
+            for copy in right_copies(j, slot):
+                copy.wait()
+            if remade:
+                frames_all = normed.shape[0] * frames
+                upward = product(normed[...].reshape(frames_all, -1), weight_slots[slot])
+                act = gelu_and_slope(upward)[0].astype(BF16)
+                right_slots[slot, remade_from:] = act.reshape(-1, frames, step)
+
+            right = right_slots[slot].reshape(-1, step)
+            for i in range(outputs):
+                outs[i][:, columns(j)] = product(turned[i], right).astype(BF16)
+            return carry
+
+        lax.fori_loop(0, steps, one_step, 0)
+
+    if remade:
 
         @pl.when(jnp.logical_not(works))
         def nothing():
-            out[...] = jnp.zeros(out.shape, BF16)
-
-
-def weight_grad(pairs, first_column, width, start=None, skip_ends=False, after=()):
-    count = len(pairs)
-    _, micros, frames, _ = pairs[0].left.shape
+            for out in outs:
+                out[...] = jnp.zeros(out.shape, BF16)
+
+
+def weight_grad(
+    pairs, first_column, width, rows, after=(), outputs=1, staying=(), remade=(), sources=()
+):
     columns = pairs[0].right.shape[2]
-    step = min(columns, BLOCK)
-    right_specs = [
-        pl.BlockSpec((micros, frames, step), lambda j, at=p.first // micros: (at, 0, j))
-        for p in pairs
+    frames = pairs[0].right.shape[1]
+    step = min(columns, 2 * BLOCK // outputs)
+    every = [*pairs, *remade]
+    micros = sum(p.count for p in every)
+    call = Call()
+    call.take([p.left for p in every], anywhere)
+    call.take([p.right for p in pairs], anywhere)
+    call.take(sources, anywhere)
+    call.take(after, anywhere)
+    call.take(staying, anywhere, pltpu.VMEM)
+    call.give([((width // outputs, columns), BF16)] * outputs, in_vmem, pltpu.VMEM)
+    scratch = [
+        pltpu.VMEM((micros, frames, width), BF16),
+        pltpu.VMEM((outputs, width // outputs, micros * frames), BF16),
+        pltpu.VMEM((2, micros, frames, step), BF16),
+        pltpu.SemaphoreType.DMA((len(every) + 1,)),
+        pltpu.SemaphoreType.DMA((2, len(pairs) + 1)),
     ]
-    block = pl.BlockSpec((width, step), lambda j: (0, j))
-    starts = [] if start is None else [start]
-    shares = [p.share for p in pairs]
-    return pl.pallas_call(
-        functools.partial(
-            weight_grad_kernel, shares, first_column, width, start is not None, skip_ends
-        ),
-        grid=(columns // step,),
-        out_shape=pltpu.HBM((width, columns), BF16),
-        in_specs=[anywhere] * count
-        + right_specs
-        + [block] * len(starts)
-        + [anywhere] * len(after),
-        out_specs=block,
-        scratch_shapes=[
-            pltpu.VMEM((count, micros, frames, width), BF16),
-            pltpu.VMEM((count, width, micros * frames), BF16),
-            pltpu.SemaphoreType.DMA((count,)),
-        ],
-        compiler_params=pltpu.CompilerParams(vmem_limit_bytes=10 * 2**20),
-        cost_estimate=pl.CostEstimate(
-            flops=2 * count * micros * frames * width * columns,
-            bytes_accessed=2 * width * columns,
-            transcendentals=0,
-        ),
-    )(
-        *[p.left for p in pairs],
-        *[p.right for p in pairs],
-        *[in_hbm(x) for x in starts],
-        *after,
+    if remade:
+        normed, weight = sources
+        scratch.append(pltpu.VMEM(normed.shape, BF16))
+        scratch.append(pltpu.VMEM((2, weight.shape[0], step), BF16))
+    bare = [p._replace(left=None, right=None) for p in every]
+    body = functools.partial(
+        weight_grad_kernel, bare, first_column, rows, step, outputs, len(remade)
     )
+    return call.run(body, scratch, 0, limit=(24 if remade else 14) * 2**20)
 
 
 class Part(NamedTuple):
-    grad: Any
+    grads: Any
     column: int
     width: int
     result: int
@@ -806,52 +861,52 @@
     tall: bool
 
 
-def fetch_parts(parts, grads, rows, index, target, sems):
-    copies, at = [], 0
-    first_row = pl.multiple_of(index * rows, rows)
-    for i, part in enumerate(parts):
-        source = grads[i].at[pl.ds(first_row, rows), pl.ds(part.column, part.width)]
-        copies.append(
-            pltpu.make_async_copy(source, target.at[:, pl.ds(at, part.width)], sems.at[i])
-        )
-        copies[i].start()
-        at += part.width
-    return copies
+def added_terms(part, grads, rows, index):
+    block = pl.ds(pl.multiple_of(index * rows, rows), rows)
+    total = None
+    for grad in grads:
+        term = grad[block, part.column : part.column + part.width].astype(F32)
+        total = term if total is None else total + term
+    return total
 
 
 def send_kernel(parts, rows, hop, adds, *refs):
-    grads, refs = refs[: len(parts)], refs[len(parts) :]
+    refs = list(refs)
+    grads = [[refs.pop(0) for _ in range(p.grads)] for p in parts]
     came = refs[:2] if adds else None
-    up, down, here, sems = refs[-4:]
+    sends = refs[-2:]
     chip = lax.axis_index("batch") // CORES
     last = lax.axis_size("batch") // CORES - 1
     places = (jnp.minimum(chip + last - (hop - 1), last), jnp.maximum(chip - last + (hop - 1), 0))
-    targets = (here.at[0], here.at[1]) if adds else (up, down)
-    copies = []
     for d in range(2):
-        copies += fetch_parts(parts, grads, rows, places[d], targets[d], sems.at[d])
-    for copy in copies:
-        copy.wait()
-    if adds:
-        up[...] = (here[0].astype(F32) + came[0][...].astype(F32)).astype(BF16)
-        down[...] = (here[1].astype(F32) + came[1][...].astype(F32)).astype(BF16)
+        at = 0
+        for part, terms in zip(parts, grads):
+            total = added_terms(part, terms, rows, places[d])
+            if adds:
+                total = total + came[d][:, at : at + part.width].astype(F32)
+            sends[d][:, at : at + part.width] = total.astype(BF16)
+            at += part.width
 
 
 def finish_kernel(parts, rows, result_count, *refs):
-    grads, refs = refs[: len(parts)], refs[len(parts) :]
+    refs = list(refs)
+    grads = [[refs.pop(0) for _ in range(p.grads)] for p in parts]
     came = refs[:2]
-    here, total, turned, sems = refs[-4:]
-    results = refs[-5 - result_count : -5]
-    refs[-5][...] = jnp.zeros(refs[-5].shape, F32)
+    total, turned, sems = refs[-3:]
+    results = refs[-4 - result_count : -4]
+    refs[-4][...] = jnp.zeros(refs[-4].shape, F32)
     chip = lax.axis_index("batch") // CORES
-    for copy in fetch_parts(parts, grads, rows, chip, here, sems):
-        copy.wait()
-    total[...] = here[...].astype(F32) + came[0][...].astype(F32) + came[1][...].astype(F32)
     copies, at = [], 0
-    for i, part in enumerate(parts):
+    for i, (part, terms) in enumerate(zip(parts, grads)):
+        own = slice(at, at + part.width)
+        total[:, own] = (
+            added_terms(part, terms, rows, chip)
+            + came[0][:, own].astype(F32)
+            + came[1][:, own].astype(F32)
+        )
         result = results[part.result]
         if part.tall:
-            turned[...] = total[:, at : at + part.width].T
+            turned[...] = total[:, own].T
             source, target = turned, result.at[pl.ds(part.place, part.width), :]
         else:
             source = total.at[pl.ds(0, result.shape[0]), pl.ds(at, part.width)]
@@ -876,27 +931,25 @@
         self.results = {}
         self.shapes = results
 
-    def step(self, piece):
-        if piece.hop == self.chips - 1:
-            self.finish(piece)
-        else:
-            self.send(piece)
-
-    def send(self, piece):
+    def bare(self, piece, names=None):
+        parts = [p._replace(grads=len(p.grads)) for p in piece.parts]
+        return parts if names is None else [
+            p._replace(result=names.index(p.result)) for p in parts
+        ]
+
+    def send(self, piece, after=()):
         adds = piece.came is not None
         piece.hop += 1
         shape = (self.rows, piece.width)
         call = Call()
-        call.take([p.grad for p in piece.parts], anywhere, pltpu.HBM)
+        call.take([g for p in piece.parts for g in p.grads], in_vmem, pltpu.VMEM)
         if adds:
             call.take(piece.came, in_vmem, pltpu.VMEM)
-        call.take([self.before], anywhere)
+        call.take([self.before, *after], anywhere)
         call.give([(shape, BF16)] * 2, in_vmem, pltpu.VMEM)
-        count = len(piece.parts)
-        scratch = [pltpu.VMEM((2,) + shape, BF16), pltpu.SemaphoreType.DMA((2, count))]
-        parts = [p._replace(grad=None) for p in piece.parts]
+        parts = self.bare(piece)
         up, down = call.run(
-            functools.partial(send_kernel, parts, self.rows, piece.hop, adds), scratch, 2**20
+            functools.partial(send_kernel, parts, self.rows, piece.hop, adds), [], 0
         )
         self.before = up
         edge = piece.first_hop - 1
@@ -912,30 +965,24 @@
 
     def finish(self, piece):
         names = sorted({p.result for p in piece.parts})
-        parts = [p._replace(grad=None, result=names.index(p.result)) for p in piece.parts]
+        parts = self.bare(piece, names)
         call = Call()
-        call.take([p.grad for p in piece.parts], anywhere, pltpu.HBM)
+        call.take([g for p in piece.parts for g in p.grads], in_vmem, pltpu.VMEM)
         call.take(piece.came, in_vmem, pltpu.VMEM)
-        call.update(
-            [self.results.get(n) for n in names],
-            [(self.shapes[n], F32) for n in names],
-            [True] * len(names),
-        )
         call.take([self.before], anywhere)
+        call.give([(self.shapes[n], F32) for n in names], anywhere, pltpu.HBM)
         call.give([((8, LANES), F32)], in_vmem, pltpu.VMEM)
         shape = (self.rows, piece.width)
         tall = max([p.width for p in parts if p.tall], default=8)
         scratch = [
-            pltpu.VMEM(shape, BF16),
             pltpu.VMEM(shape, F32),
             pltpu.VMEM((tall, self.rows), F32),
             pltpu.SemaphoreType.DMA((len(parts),)),
         ]
         done = call.run(
-            functools.partial(finish_kernel, parts, self.rows, len(names)), scratch, 2**20
+            functools.partial(finish_kernel, parts, self.rows, len(names)), scratch, 0
         )
         self.results.update(zip(names, done))
-        piece.hop = self.chips
         self.before = done[-1]
 
 
@@ -955,6 +1002,9 @@
         if not self.by_hops:
             return None
         return lax.ppermute(x, "batch", [(b, b ^ 1) for b in range(self.batch)])
+
+    def both(self, x):
+        return [in_hbm(x), self.swap(x)]
 
     def inward(self, x):
         if not self.ends_hand_over:
@@ -965,13 +1015,10 @@
         return lax.ppermute(x, "batch", pairs)
 
     def sources(self, x):
-        if not self.ends_hand_over:
-            return [x, self.swap(x)]
-        came = self.inward(x)
-        return [x, self.swap(x), came, self.swap(came)]
-
-
-def sums_by_hops(plan, exchange, kept, back, grad_down, lefts, table_grad, before):
+        return [in_hbm(x), self.inward(x)] if self.ends_hand_over else [in_hbm(x)]
+
+
+def sums_by_hops(plan, exchange, back, downs, grad_up, lefts, table_grad, before):
     chips, rows = exchange.chips, plan.rows
     features, hidden_units = plan.features, plan.hidden_units
     core = lax.axis_index("batch") % CORES
@@ -988,48 +1035,47 @@
     line = Line(exchange, rows, results, before)
 
     def of(right, first_column):
-        pairs = [Pair(left, i, r) for i, (left, r) in enumerate(zip(lefts, (right, swap(right))))]
-        grad = weight_grad(pairs, first_column, share, after=[line.before])
+        rights = exchange.both(right)
+        pairs = [Pair(left, i, rights[i], plan.micros) for i, left in enumerate(lefts)]
+        (grad,) = weight_grad(pairs, first_column, share, rows, [line.before])
         line.before = grad
         return grad
 
-    half = hidden_units // 2
-    down = grad_down(before)
-    line.before = down
+    up = line.before = grad_up(before)
+    ups = Piece([Part([up], 0, hidden_units, 2, 0, False)], 1)
+    line.send(ups)
+    down, down_given = downs
     first = 2 if exchange.ends_hand_over else 1
-    downs = [Piece([Part(down, c, half, 3, c, True)], first) for c in (0, half)]
-    for piece in downs:
-        line.step(piece)
-    up = of(back.grad_up, 2 * share)
-    ups = [Piece([Part(up, c, half, 2, c, False)], 1) for c in (0, half)]
-    for piece in ups + downs:
-        line.step(piece)
+    downs = Piece([Part([down, swap(down_given)], 0, hidden_units, 3, 0, True)], first)
+    line.send(downs)
     qkv = of(back.grad_packed, 0)
-    for piece in ups:
-        line.step(piece)
     out = of(back.grad_attn, share)
     norms = table_grad + swap(table_grad)
     norms = norms.reshape(table_size, chips, CORES, rows)
     norms = lax.dynamic_index_in_dim(norms, core, 2, keepdims=False).transpose(1, 0, 2)
     norms = jnp.pad(norms.astype(BF16), ((0, 0), (0, rows - table_size), (0, 0)))
     norms = norms.reshape(chips * rows, rows)
-    cut = 2 * features
-    others = [
-        Piece([Part(qkv, 0, cut, 0, 0, False)], 1),
-        Piece(
-            [
-                Part(qkv, cut, features, 0, cut, False),
-                Part(out, 0, features, 1, 0, False),
-                Part(norms, 0, rows, 4, 0, False),
-            ],
-            1,
-        ),
-    ]
-    order = [downs, ups, others, ups, others, others, others]
-    for pieces in order:
-        for piece in pieces:
-            if piece.hop < chips:
-                line.step(piece)
+    others = Piece(
+        [
+            Part([qkv], 0, 3 * features, 0, 0, False),
+            Part([out], 0, features, 1, 0, False),
+            Part([norms], 0, rows, 4, 0, False),
+        ],
+        1,
+    )
+    order = [downs, others, ups, others, ups, others]
+    gone = [ups.came, downs.came]
+    pieces = [ups, downs, others]
+    for piece in order:
+        if piece.hop < chips - 1:
+            line.send(piece, gone.pop(0))
+            gone.append(piece.came)
+        for done in pieces[:]:
+            if done.hop == chips - 1 and done is not piece:
+                line.finish(done)
+                pieces.remove(done)
+    for piece in pieces:
+        line.finish(piece)
     return [line.results[i] for i in range(len(results))]
 
 
@@ -1039,11 +1085,17 @@
     core = lax.axis_index("batch") % CORES
 
     def local(lefts, rights, column):
-        start = [None, None]
-        for left, right in zip(lefts, rights):
-            for i in range(CORES):
-                start[i] = weight_grad([Pair(left, i, right)], column, share, start[i])
-        mine, other = start
+        pairs = [Pair(left, None, right, left.shape[0]) for left, right in zip(lefts, rights)]
+        if column is None:
+            mine, other = weight_grad(pairs, 0, features, plan.rows, outputs=2)
+        else:
+            (left,), (right,) = lefts, rights
+            mine, other = [
+                weight_grad(
+                    [Pair(left, i, right, left.shape[1])], column, share, plan.rows
+                )[0]
+                for i in range(CORES)
+            ]
         even, odd = jnp.where(core == 0, mine, other), jnp.where(core == 0, other, mine)
         blocks = [x.reshape(-1, 1, plan.rows, x.shape[1]) for x in (even, odd)]
         return jnp.concatenate(blocks, axis=1).reshape(features, -1)
@@ -1053,12 +1105,13 @@
             x, "batch", scatter_dimension=dimension, tiled=True
         ).astype(F32)
 
-    grad_y = [back.y_early, jnp.concatenate([back.y_late, back.y_last], axis=1)]
-    down = local(grad_y, [kept.act_early, kept.act_late], 0)
+    grad_y = [back.y_early, back.y_late, back.y_last]
+    down = local([jnp.concatenate(grad_y, axis=0)], [kept.act], None)
+    grad_up = jnp.concatenate([back.up_early, back.up_last], axis=0)
     return (
         scattered(local([kept.left], [back.grad_packed], 0), 0),
         scattered(local([kept.left], [back.grad_attn], share), 0),
-        scattered(local([kept.left], [back.grad_up], 2 * share), 0),
+        scattered(local([kept.left], [grad_up], 2 * share), 0),
         scattered(down, 0).T,
         scattered(table_grad, 1),
     )
@@ -1088,25 +1141,23 @@
     )
     exchange = Exchange(batch)
 
-    def down_pairs(grad_y, act, first=0):
-        return [Pair(y, i % CORES, a, first) for i, (y, a) in enumerate(zip(grad_y, act))]
-
-    def down_grad(pairs, start, before):
-        share = features // CORES
-        return weight_grad(pairs, 0, share, start, exchange.ends_hand_over, [before])
-
-    after = ()
+    share = features // CORES
+
+    def down_pairs(grad_ys, act):
+        firsts = [span[0] for span in plan.y_spans()]
+        return [Pair(y, None, act, y.shape[0], 0, at) for y, at in zip(grad_ys, firsts)]
+
+    def up_pairs(grad_up, first):
+        count = grad_up[0].shape[0]
+        return [
+            Pair(left, i, g, count, first, 0) for i, (left, g) in enumerate(zip(lefts, grad_up))
+        ]
+
+    before_bwd = [[] for _ in range(plan.ticks())]
     incoming = arriving = None
     working = lambda micro: 0 <= micro < micros
     for tick in range(plan.ticks()):
         sent = returned = None
-        if tick == plan.ticks() - 1 and exchange.by_hops:
-            down = down_grad(down_pairs(y_early, act_early), None, state.back.grad_in)
-            y_last = exchange.sources(last_y(plan, state, arriving, down))
-            after = act_late[1:3] + y_last[:1]
-        elif tick == plan.ticks() - 1:
-            y_last = last_y(plan, state, arriving, state.back.grad_in)
-            state = state._replace(back=state.back._replace(y_last=y_last))
         if tick < plan.fwd_ticks():
             state, output = run_forward(plan, tick, state, incoming, frames_all)
             onward = [
@@ -1115,8 +1166,30 @@
             if onward:
                 sent = lax.ppermute(output, "section", onward)
         if tick >= sections - 1:
-            state, output = run_backward(plan, tick, state, arriving, cot_all, after)
-            after = ()
+            late = tick == plan.ticks() - 1
+            state, output = run_backward(
+                plan, tick, state, arriving, cot_all, before_bwd[tick], FIRST if late else WHOLE
+            )
+            if late:
+                after = []
+                if exchange.by_hops:
+                    y_last = exchange.sources(state.back.y_last)
+                    up_last = exchange.both(state.back.up_last)
+                    sides = list(zip(y_early, y_late, y_last))
+                    pairs = down_pairs(sides[0], in_hbm(state.kept.act))
+                    remade, sources = (), ()
+                    if exchange.ends_hand_over:
+                        remade = down_pairs(sides[1], None)
+                        sources = (second[1], up_weight[0])
+                    down = weight_grad(
+                        pairs, 0, features, plan.rows, output[:1], 2, state.turned[:1],
+                        remade, sources,
+                    )
+                    after = up_early[1:] + down
+                state, output = run_backward(
+                    plan, tick, state, arriving, cot_all, after, SECOND, output
+                )
+            output = output[0]
             backward = [
                 (s, s - 1) for s in range(1, sections) if working(plan.bwd_id(tick, s))
             ]
@@ -1124,25 +1197,28 @@
                 returned = lax.ppermute(output, "section", backward)
         incoming, arriving = sent, returned
         if exchange.by_hops:
-            if tick == plan.act_spans()[0][1] + sections - 2:
-                act_early = exchange.sources(state.kept.act_early)
             if tick == plan.fwd_ticks() - 1:
-                act_late = exchange.sources(state.kept.act_late)
-                lefts = [state.kept.left, exchange.swap(state.kept.left)]
-                after = act_early[1:3]
+                lefts = exchange.both(state.kept.left)
+                before_bwd[tick + 1] += lefts[1:]
+                second = exchange.sources(state.kept.second)
+                before_bwd[tick + 2] += second[1:]
             if tick == plan.y_spans()[0][1] + 2 * sections - 3:
                 y_early = exchange.sources(state.back.y_early)
+                before_bwd[plan.ticks() - 1] += y_early[1:]
             if tick == plan.ticks() - 2:
                 y_late = exchange.sources(state.back.y_late)
+                up_early = exchange.both(state.back.up_early)
 
     blocks = norm_table.shape[1] // 4
     codes = codebooks * (section % 2)
     table_grad = table_gradient(state.back.row_grads, codes, blocks).reshape(norm_table.shape[1:])
     if exchange.by_hops:
-        late_pairs = down_pairs(y_late, act_late) + down_pairs(y_last, act_late, micros // 2 - 1)
+        def grad_up(before):
+            pairs = up_pairs(up_early, 0) + up_pairs(up_last, micros - 1)
+            return weight_grad(pairs, 2 * share, share, plan.rows, [before])[0]
+
         sums = sums_by_hops(
-            plan, exchange, state.kept, state.back,
-            lambda before: down_grad(late_pairs, down, before), lefts, table_grad, output,
+            plan, exchange, state.back, down, grad_up, lefts, table_grad, output
         )
     else:
         sums = sums_by_scatter(plan, state.kept, state.back, table_grad)

time: 545 us -> 476 us (0.87)
  starting transfers between devices: 177 us -> 102 us
  waiting for transfers between devices: 136 us -> 187 us
  Pallas kernels: 192 us -> 158 us
  local copies, waits for them, and re-layouts: 28.1 us -> 15.8 us
    ppermute x32 -> x16, waiting for transfers between devices: 43.4 us -> 109 us  [moved(): return lax.ppermute(value, 'batch', pairs)]
    ppermute x32 -> x16, starting transfers between devices: 120 us -> 61.4 us  [moved(): return lax.ppermute(value, 'batch', pairs)]
    pallas_call x6 -> x0, Pallas kernels: 31.2 us -> none  [the longest x5 31.1 us: weight_grad(): pl.pallas_call(functools.partial(weight_grad_kernel, shares, first_column...]
    ppermute x5 -> x4, waiting for transfers between devices: 48.1 us -> 19 us  [inward(): return lax.ppermute(x, 'batch', pairs)]
    ppermute x6, waiting for transfers between devices: 16.4 us -> 35.3 us  [per_device(): returned = lax.ppermute(output, 'section', backward)]
    ppermute x5 -> x4, starting transfers between devices: 28.2 us -> 13.4 us  [inward(): return lax.ppermute(x, 'batch', pairs)]
    unnamed x76 -> x42, local copies, waits for them, and re-layouts: 27.2 us -> 15.5 us
    pallas_call x36 -> x30, Pallas kernels: 161 us -> 158 us  [run(): pl.pallas_call(body, out_shape=self.out_shape, in_specs=self.in_specs, ou...]
  transfers between devices with their start and end apart: 64 -> 39, of which waited for: 21 -> 16; matrix products, arithmetic and copies ran while one was open for 0% -> 0% of each run, Pallas kernels for 22% -> 20%
where the time goes in v3:
time: 476 us; the launch traced here: 468 us
  waiting for transfers between devices  187 us (39%)
  Pallas kernels  158 us (33%)
  starting transfers between devices  102 us (21%)
  local copies, waits for them, and re-layouts  15.8 us (3%)
    pallas_call x30, Pallas kernels, run(): pl.pallas_call(body, out_shape=self.out_shape, in_specs=self.in_specs, ou...  158 us
    ppermute x16, waiting for transfers between devices, moved(): return lax.ppermute(value, 'batch', pairs)  109 us
    ppermute x16, starting transfers between devices, moved(): return lax.ppermute(value, 'batch', pairs)  61.4 us
    ppermute x6, waiting for transfers between devices, per_device(): returned = lax.ppermute(output, 'section', backward)  35.3 us
    ppermute x6, starting transfers between devices, per_device(): sent = lax.ppermute(output, 'section', onward)  19.8 us
    ppermute x4, waiting for transfers between devices, inward(): return lax.ppermute(x, 'batch', pairs)  19 us
    ppermute x6, waiting for transfers between devices, per_device(): sent = lax.ppermute(output, 'section', onward)  17.7 us
    unnamed x42, local copies, waits for them, and re-layouts  15.5 us
  transfers between devices with their start and end apart: 39, of which 16 were waited for; matrix products, arithmetic and copies ran while one was open for 0% of the time, Pallas kernels for 20%

profile of v3, /device:TPU:0, one launch (start us, length us, event | category | flops | bytes accessed | tf_op | source)
XLA Modules:
  0.0 467.5 jit_solution(2956315406541877414)
XLA Ops:
  0.6 17.3 %shard_map.144 = (s32[8]{0:T(128)S(4)}, f32[32,1024]{1,0:T(8,128)S(1)}, bf16[1024,3072]{1,0:T(8,128)(2,1)S(1)}, bf16[1024,1024]{1,0:T(8,128)(2,1)S(1)}, bf16[102...) custom-call(s32[4]{0:T(128)} %refs_0_.1, ...), custom_call_target="tpu_custom_call" | custom-call | flops 12884901888 | tf_op jit(solution)/shard_map/pallas_call | solution.py:578
  17.9 6.7 %collective-permute-start = (bf16[128,1024]{1,0:T(8,128)(2,1)S(1)}, bf16[128,1024]{1,0:T(8,128)(2,1)S(1)}, u32[]{:S(2)}, u32[]{:S(2)}) collective-permute-start(bf16[128,1024]{1,0:T(8,128)(2,1)S(1)} %get-tuple-element.241), channel_id=1, source_target_pairs={{0,8},{1,9},{2,10},{3,11},{4,12},{5,13},{6,14},{7,15}} | collective-permute-start | bytes 786440 | tf_op jit(solution)/shard_map/ppermute | solution.py:1167
  24.6 5.5 %collective-permute-done.refs_10_ = bf16[128,1024]{1,0:T(8,128)(2,1)S(1)} collective-permute-done((bf16[128,1024]{1,0:T(8,128)(2,1)S(1)}, bf16[128,1024]{1,0:T(8,128)(2,1)S(1)}, u32[]{:S(2)}, u32[]{:S(2)}) %collective-permute-start) | collective-permute-done | bytes 262176 | tf_op jit(solution)/shard_map/ppermute | solution.py:1167
  30.2 9.3 %shard_map.145 = (bf16[3072,1024]{1,0:T(8,128)(2,1)S(1)}, bf16[1024,1024]{1,0:T(8,128)(2,1)S(1)}, bf16[4096,1024]{1,0:T(8,128)(2,1)S(1)}, bf16[1024,4096]{1,0:T(...) custom-call(s32[8]{0:T(128)S(4)} %get-tuple-element.231.refs_0_, ...), custom_call_target="tpu_custom_call", output_to_operand_aliasing={{0}: (6, {}), {1}: (7, {}), {2}: (8, {}), {3}: (9, {}), {4}... | custom-call | flops 12884901888 | tf_op jit(solution)/shard_map/pallas_call | solution.py:578
  39.5 3.5 collective-permute-start.1
  43.0 4.7 collective-permute-done.1.refs_10_
  47.6 9.2 %shard_map.146 = (bf16[3072,1024]{1,0:T(8,128)(2,1)S(1)}, bf16[1024,1024]{1,0:T(8,128)(2,1)S(1)}, bf16[4096,1024]{1,0:T(8,128)(2,1)S(1)}, bf16[1024,4096]{1,0:T(...) custom-call(s32[8]{0:T(128)S(4)} %get-tuple-element.231.refs_0_, ...), custom_call_target="tpu_custom_call", output_to_operand_aliasing={{0}: (6, {}), {1}: (7, {}), {2}: (8, {}), {3}: (9, {}), {4}... | custom-call | flops 12884901888 | tf_op jit(solution)/shard_map/pallas_call | solution.py:578
  56.8 3.9 collective-permute-start.2
  60.7 4.7 collective-permute-done.2.refs_10_
  65.4 10.3 %shard_map.147 = (bf16[3072,1024]{1,0:T(8,128)(2,1)S(1)}, bf16[1024,1024]{1,0:T(8,128)(2,1)S(1)}, bf16[4096,1024]{1,0:T(8,128)(2,1)S(1)}, bf16[1024,4096]{1,0:T(...) custom-call(s32[8]{0:T(128)S(4)} %get-tuple-element.231.refs_0_, ...), custom_call_target="tpu_custom_call", output_to_operand_aliasing={{0}: (6, {}), {1}: (7, {}), {2}: (8, {}), {3}: (9, {}), {4}... | custom-call | flops 12884901888 | tf_op jit(solution)/shard_map/pallas_call | solution.py:578
  75.7 4.4 collective-permute-start.3
  81.1 2.8 collective-permute-done.3.refs_10_
  83.9 12.3 %shard_map.149 = (bf16[3072,1024]{1,0:T(8,128)(2,1)S(1)}, bf16[1024,1024]{1,0:T(8,128)(2,1)S(1)}, bf16[4096,1024]{1,0:T(8,128)(2,1)S(1)}, bf16[1024,4096]{1,0:T(...) custom-call(s32[8]{0:T(128)S(4)} %get-tuple-element.231.refs_0_, ...), custom_call_target="tpu_custom_call", output_to_operand_aliasing={{0}: (6, {}), {1}: (7, {}), {2}: (8, {}), {3}: (9, {}), {4}... | custom-call | flops 12884901888 | tf_op jit(solution)/shard_map/pallas_call | solution.py:578
  97.9 16.3 %shard_map.151 = (bf16[3072,1024]{1,0:T(8,128)(2,1)S(1)}, bf16[1024,1024]{1,0:T(8,128)(2,1)S(1)}, bf16[4096,1024]{1,0:T(8,128)(2,1)S(1)}, bf16[1024,4096]{1,0:T(...) custom-call(s32[8]{0:T(128)S(4)} %get-tuple-element.231.refs_0_, ...), custom_call_target="tpu_custom_call", output_to_operand_aliasing={{0}: (6, {}), {1}: (7, {}), {2}: (8, {}), {3}: (9, {}), {4}... | custom-call | flops 12884901888 | tf_op jit(solution)/shard_map/pallas_call | solution.py:578
  115.1 6.1 %shard_map.153 = (bf16[3072,1024]{1,0:T(8,128)(2,1)S(1)}, bf16[1024,1024]{1,0:T(8,128)(2,1)S(1)}, bf16[4096,1024]{1,0:T(8,128)(2,1)S(1)}, bf16[1024,4096]{1,0:T(...) custom-call(s32[8]{0:T(128)S(4)} %get-tuple-element.231.refs_0_, ...), custom_call_target="tpu_custom_call", output_to_operand_aliasing={{0}: (6, {}), {1}: (7, {}), {2}: (8, {}), {3}: (9, {}), {4}... | custom-call | flops 12884901888 | tf_op jit(solution)/shard_map/pallas_call | solution.py:578
  122.6 22.5 %collective-permute-done.10.refs_10_ = bf16[128,1024]{1,0:T(8,128)(2,1)S(1)} collective-permute-done((bf16[128,1024]{1,0:T(8,128)(2,1)S(1)}, bf16[128,1024]{1,0:T(8,128)(2,1)S(1)}, u32[]{:S(2)}, u32[]{:S(2)}) %collective-permute-start.10) | collective-permute-done | bytes 262176 | tf_op jit(solution)/shard_map/ppermute | solution.py:1197
  145.1 8.5 %shard_map.154 = (bf16[4,128,1024]{2,1,0:T(8,128)(2,1)}, bf16[4,128,3072]{2,1,0:T(8,128)(2,1)}, bf16[4,2048,128]{2,1,0:T(8,128)(2,1)}, f32[4,128,1024]{2,1,0:T(8...) custom-call(s32[8]{0:T(128)S(4)} %get-tuple-element.231.refs_0_, ...), custom_call_target="tpu_custom_call", output_to_operand_aliasing={{0}: (12, {}), {1}: (13, {}), {2}: (14, {}), {3}: (15, {}),... | custom-call | flops 12884901888 | tf_op jit(solution)/shard_map/pallas_call | solution.py:578
  154.9 3.6 collective-permute-start.8
  158.4 7.8 %collective-permute-done.11.refs_11_ = bf16[128,1024]{1,0:T(8,128)(2,1)S(1)} collective-permute-done((bf16[128,1024]{1,0:T(8,128)(2,1)S(1)}, bf16[128,1024]{1,0:T(8,128)(2,1)S(1)}, u32[]{:S(2)}, u32[]{:S(2)}) %collective-permute-start.11) | collective-permute-done | bytes 262176 | tf_op jit(solution)/shard_map/ppermute | solution.py:1197
  166.2 9.2 %shard_map.155 = (bf16[4,128,1024]{2,1,0:T(8,128)(2,1)}, bf16[4,128,3072]{2,1,0:T(8,128)(2,1)}, bf16[4,2048,128]{2,1,0:T(8,128)(2,1)}, f32[4,128,1024]{2,1,0:T(8...) custom-call(s32[8]{0:T(128)S(4)} %get-tuple-element.231.refs_0_, ...), custom_call_target="tpu_custom_call", output_to_operand_aliasing={{0}: (13, {}), {1}: (14, {}), {2}: (15, {}), {3}: (16, {}),... | custom-call | flops 12884901888 | tf_op jit(solution)/shard_map/pallas_call | solution.py:578
  176.7 4.5 collective-permute-done.8.refs_10_.refs_9_
  181.2 5.1 %collective-permute-done.12.refs_11_ = bf16[128,1024]{1,0:T(8,128)(2,1)S(1)} collective-permute-done((bf16[128,1024]{1,0:T(8,128)(2,1)S(1)}, bf16[128,1024]{1,0:T(8,128)(2,1)S(1)}, u32[]{:S(2)}, u32[]{:S(2)}) %collective-permute-start.12) | collective-permute-done | bytes 262176 | tf_op jit(solution)/shard_map/ppermute | solution.py:1197
  186.2 8.5 %shard_map.156 = (bf16[4,128,1024]{2,1,0:T(8,128)(2,1)}, bf16[4,128,3072]{2,1,0:T(8,128)(2,1)}, bf16[4,2048,128]{2,1,0:T(8,128)(2,1)}, f32[4,128,1024]{2,1,0:T(8...) custom-call(s32[8]{0:T(128)S(4)} %get-tuple-element.231.refs_0_, ...), custom_call_target="tpu_custom_call", output_to_operand_aliasing={{0}: (13, {}), {1}: (14, {}), {2}: (15, {}), {3}: (16, {}),... | custom-call | flops 12884901888 | tf_op jit(solution)/shard_map/pallas_call | solution.py:578
  195.4 3.5 collective-permute-start.14
  202.2 9.2 %collective-permute-done.14.refs_10_.refs_3_ = bf16[2,128,1024]{2,1,0:T(8,128)(2,1)S(1)} collective-permute-done((bf16[2,128,1024]{2,1,0:T(8,128)(2,1)}, bf16[2,128,1024]{2,1,0:T(8,128)(2,1)S(1)}, u32[]{:S(2)}, u32[]{:S(2)}) %collective-permute-start.14) | collective-permute-done | bytes 524320 | tf_op jit(solution)/shard_map/ppermute | solution.py:1015
  213.3 5.5 %shard_map.157 = (bf16[4,128,1024]{2,1,0:T(8,128)(2,1)}, bf16[4,128,3072]{2,1,0:T(8,128)(2,1)}, bf16[4,2048,128]{2,1,0:T(8,128)(2,1)}, f32[4,128,1024]{2,1,0:T(8...) custom-call(s32[8]{0:T(128)S(4)} %get-tuple-element.231.refs_0_, ...), custom_call_target="tpu_custom_call", output_to_operand_aliasing={{0}: (13, {}), {1}: (14, {}), {2}: (15, {}), {3}: (16, {}),... | custom-call | flops 6442450944 | tf_op jit(solution)/shard_map/pallas_call | solution.py:578
  218.8 4.3 collective-permute-start.17
  223.1 5.3 %collective-permute-done.17.refs_5_ = bf16[1,128,1024]{2,1,0:T(8,128)(2,1)S(1)} collective-permute-done((bf16[1,128,1024]{2,1,0:T(8,128)(2,1)}, bf16[1,128,1024]{2,1,0:T(8,128)(2,1)S(1)}, u32[]{:S(2)}, u32[]{:S(2)}) %collective-permute-start.17) | collective-permute-done | bytes 262176 | tf_op jit(solution)/shard_map/ppermute | solution.py:1015
  228.5 2.8 copy-done.1
  231.3 3.4 copy-done.9
  236.7 3.0 shard_map.158
  242.8 5.6 %shard_map.159 = (bf16[4,128,1024]{2,1,0:T(8,128)(2,1)}, bf16[4,128,3072]{2,1,0:T(8,128)(2,1)}, bf16[4,2048,128]{2,1,0:T(8,128)(2,1)}, f32[4,128,1024]{2,1,0:T(8...) custom-call(s32[8]{0:T(128)S(4)} %get-tuple-element.231.refs_0_, ...), custom_call_target="tpu_custom_call", output_to_operand_aliasing={{0}: (8, {}), {1}: (9, {}), {2}: (10, {}), {3}: (11, {}), {... | custom-call | flops 6442450944 | tf_op jit(solution)/shard_map/pallas_call | solution.py:578
  250.8 6.0 %collective-permute-done.20.refs_7_ = bf16[1,128,4096]{2,1,0:T(8,128)(2,1)S(1)} collective-permute-done((bf16[1,128,4096]{2,1,0:T(8,128)(2,1)S(1)}, bf16[1,128,4096]{2,1,0:T(8,128)(2,1)S(1)}, u32[]{:S(2)}, u32[]{:S(2)}) %collective-permute-start.20) | collective-permute-done | bytes 1048608 | tf_op jit(solution)/shard_map/ppermute | solution.py:1004
  256.8 7.3 %shard_map.160.refs_0_.refs_1_ = bf16[512,4096]{1,0:T(8,128)(2,1)S(1)} custom-call(bf16[2,4,128,1536]{3,2,1,0:T(8,128)(2,1)} %get-tuple-element.356.refs_0_.refs_2_, bf16[2,4,128,1536]{3,2,1,0:T(8,128)(2,1)} %collective-permute-done.9.refs_10_.refs_1_.refs_3_, bf16[2,4,128,1536]{3,2,1,0:T(8,128)(2,1)} %get-tuple-element.356.refs_0_.refs_2_, ...), custom_call_target="tpu_custom_call" | custom-call | tf_op jit(solution)/shard_map/pallas_call | solution.py:578
  267.2 21.6 %collective-permute-start.25 = (bf16[128,4096]{1,0:T(8,128)(2,1)}, bf16[128,4096]{1,0:T(8,128)(2,1)S(1)}, u32[]{:S(2)}, u32[]{:S(2)}) collective-permute-start(bf16[128,4096]{1,0:T(8,128)(2,1)} %get-tuple-element.430.refs_2_), channel_id=1, source_target_pairs={{0,2},{1,3},{8,10},{9,11},{16,18},{17,19},{24,26},{25,27}} | collective-permute-start | bytes 3145736 | tf_op jit(solution)/shard_map/ppermute | solution.py:964
  290.5 3.9 shard_map.162
  297.0 6.1 %shard_map.163.refs_4_.refs_0_ = bf16[512,3072]{1,0:T(8,128)(2,1)S(1)} custom-call(bf16[2,4,128,1536]{3,2,1,0:T(8,128)(2,1)} %get-tuple-element.356.refs_0_.refs_2_, bf16[2,4,128,1536]{3,2,1,0:T(8,128)(2,1)} %collective-permute-done.9.refs_10_.refs_1_.refs_3_, bf16[4,128,3072]{2,1,0:T(8,128)(2,1)} %get-tuple-element.427.refs_2_, ...), custom_call_target="tpu_custom_call" | custom-call | tf_op jit(solution)/shard_map/pallas_call | solution.py:578
  303.1 3.4 shard_map.164.refs_4_.refs_1_
  306.5 5.5 %collective-permute-done.25.refs_5_.refs_1_ = bf16[128,4096]{1,0:T(8,128)(2,1)S(1)} collective-permute-done((bf16[128,4096]{1,0:T(8,128)(2,1)}, bf16[128,4096]{1,0:T(8,128)(2,1)S(1)}, u32[]{:S(2)}, u32[]{:S(2)}) %collective-permute-start.25) | collective-permute-done | bytes 1048608 | tf_op jit(solution)/shard_map/ppermute | solution.py:964
  312.0 3.0 shard_map.165
  315.1 13.6 %collective-permute-start.27 = (bf16[128,4224]{1,0:T(8,128)(2,1)S(1)}, bf16[128,4224]{1,0:T(8,128)(2,1)S(1)}, u32[]{:S(2)}, u32[]{:S(2)}) collective-permute-start(bf16[128,4224]{1,0:T(8,128)(2,1)S(1)} %get-tuple-element.437.refs_4_), channel_id=1, source_target_pairs={{0,2},{1,3},{8,10},{9,11},{16,18},{17,19},{24,26},{25,27}} | collective-permute-start | bytes 3244040 | tf_op jit(solution)/shard_map/ppermute | solution.py:964
  332.0 24.4 %collective-permute-done.30.refs_3_.refs_5_ = bf16[128,4096]{1,0:T(8,128)(2,1)S(1)} collective-permute-done((bf16[128,4096]{1,0:T(8,128)(2,1)S(1)}, bf16[128,4096]{1,0:T(8,128)(2,1)S(1)}, u32[]{:S(2)}, u32[]{:S(2)}) %collective-permute-start.30) | collective-permute-done | bytes 1048608 | tf_op jit(solution)/shard_map/ppermute | solution.py:964
  356.4 4.1 shard_map.167
  369.2 39.8 %collective-permute-done.33.refs_1_.refs_4_ = bf16[128,4096]{1,0:T(8,128)(2,1)S(1)} collective-permute-done((bf16[128,4096]{1,0:T(8,128)(2,1)S(1)}, bf16[128,4096]{1,0:T(8,128)(2,1)S(1)}, u32[]{:S(2)}, u32[]{:S(2)}) %collective-permute-start.33) | collective-permute-done | bytes 1048608 | tf_op jit(solution)/shard_map/ppermute | solution.py:964
  410.0 6.4 %collective-permute-start.35 = (bf16[128,4224]{1,0:T(8,128)(2,1)S(1)}, bf16[128,4224]{1,0:T(8,128)(2,1)S(1)}, u32[]{:S(2)}, u32[]{:S(2)}) collective-permute-start(bf16[128,4224]{1,0:T(8,128)(2,1)S(1)} %get-tuple-element.446.refs_3_), channel_id=1, source_target_pairs={{0,2},{1,3},{2,4},{3,5},{4,6},{5,7},{8,10},{9,11},{10,12},{11,13},... | collective-permute-start | bytes 3244040 | tf_op jit(solution)/shard_map/ppermute | solution.py:964
  417.7 4.6 collective-permute-start.37
  423.6 35.6 %collective-permute-done.37.refs_1_ = bf16[128,4096]{1,0:T(8,128)(2,1)S(1)} collective-permute-done((bf16[128,4096]{1,0:T(8,128)(2,1)S(1)}, bf16[128,4096]{1,0:T(8,128)(2,1)S(1)}, u32[]{:S(2)}, u32[]{:S(2)}) %collective-permute-start.37) | collective-permute-done | bytes 1048608 | tf_op jit(solution)/shard_map/ppermute | solution.py:964
  459.2 4.2 collective-permute-done.38.refs_2_
  (112 shorter events, 47.6 us)
Async XLA Ops:
  17.9 12.2 %collective-permute-start = (bf16[128,1024]{1,0:T(8,128)(2,1)S(1)}, bf16[128,1024]{1,0:T(8,128)(2,1)S(1)}, u32[]{:S(2)}, u32[]{:S(2)}) collective-permute-start(bf16[128,1024]{1,0:T(8,128)(2,1)S(1)} %get-tuple-element.241), channel_id=1, source_target_pairs={{0,8},{1,9},{2,10},{3,11},{4,12},{5,13},{6,14},{7,15}} | collective-permute-start | bytes 786440 | tf_op jit(solution)/shard_map/ppermute | solution.py:1167
  39.5 8.2 %collective-permute-start.1 = (bf16[128,1024]{1,0:T(8,128)(2,1)S(1)}, bf16[128,1024]{1,0:T(8,128)(2,1)S(1)}, u32[]{:S(2)}, u32[]{:S(2)}) collective-permute-start(bf16[128,1024]{1,0:T(8,128)(2,1)S(1)} %get-tuple-element.255), channel_id=1, source_target_pairs={{0,8},{8,16},{1,9},{9,17},{2,10},{10,18},{3,11},{11,19},{4,12},{12... | collective-permute-start | bytes 786440 | tf_op jit(solution)/shard_map/ppermute | solution.py:1167
  56.8 8.6 %collective-permute-start.2 = (bf16[128,1024]{1,0:T(8,128)(2,1)S(1)}, bf16[128,1024]{1,0:T(8,128)(2,1)S(1)}, u32[]{:S(2)}, u32[]{:S(2)}) collective-permute-start(bf16[128,1024]{1,0:T(8,128)(2,1)S(1)} %get-tuple-element.269), channel_id=1, source_target_pairs={{0,8},{8,16},{16,24},{1,9},{9,17},{17,25},{2,10},{10,18},{18,26},{... | collective-permute-start | bytes 786440 | tf_op jit(solution)/shard_map/ppermute | solution.py:1167
  75.7 8.2 %collective-permute-start.3 = (bf16[128,1024]{1,0:T(8,128)(2,1)S(1)}, bf16[128,1024]{1,0:T(8,128)(2,1)S(1)}, u32[]{:S(2)}, u32[]{:S(2)}) collective-permute-start(bf16[128,1024]{1,0:T(8,128)(2,1)S(1)} %get-tuple-element.283), channel_id=1, source_target_pairs={{0,8},{8,16},{16,24},{1,9},{9,17},{17,25},{2,10},{10,18},{18,26},{... | collective-permute-start | bytes 786440 | tf_op jit(solution)/shard_map/ppermute | solution.py:1167
  80.4 16.5 %collective-permute-start.5 = (bf16[128,1024]{1,0:T(8,128)(2,1)S(1)}, bf16[128,1024]{1,0:T(8,128)(2,1)S(1)}, u32[]{:S(2)}, u32[]{:S(2)}) collective-permute-start(bf16[128,1024]{1,0:T(8,128)(2,1)S(1)} %get-tuple-element.303), channel_id=1, source_target_pairs={{24,16},{25,17},{26,18},{27,19},{28,20},{29,21},{30,22},{31,23}} | collective-permute-start | bytes 786440 | tf_op jit(solution)/shard_map/ppermute | solution.py:1197
  96.3 1.6 collective-permute-start.4
  97.2 17.7 %collective-permute-start.7 = (bf16[128,1024]{1,0:T(8,128)(2,1)S(1)}, bf16[128,1024]{1,0:T(8,128)(2,1)S(1)}, u32[]{:S(2)}, u32[]{:S(2)}) collective-permute-start(bf16[128,1024]{1,0:T(8,128)(2,1)S(1)} %get-tuple-element.329), channel_id=1, source_target_pairs={{16,8},{24,16},{17,9},{25,17},{18,10},{26,18},{19,11},{27,19},{20,... | collective-permute-start | bytes 786440 | tf_op jit(solution)/shard_map/ppermute | solution.py:1197
  114.2 0.9 collective-permute-start.6
  121.2 91.1 %copy-start = (bf16[3072,1024]{1,0:T(8,128)(2,1)}, bf16[3072,1024]{1,0:T(8,128)(2,1)S(1)}, u32[]{:S(2)}) copy-start(bf16[3072,1024]{1,0:T(8,128)(2,1)S(1)} %get-tuple-element.351.refs_2_.refs_12_) | copy-start | bytes 18874372
  121.2 45.0 %collective-permute-start.9 = (bf16[2,4,128,1536]{3,2,1,0:T(8,128)(2,1)}, bf16[2,4,128,1536]{3,2,1,0:T(8,128)(2,1)}, u32[]{:S(2)}, u32[]{:S(2)}) collective-permute-start(bf16[2,4,128,1536]{3,2,1,0:T(8,128)(2,1)} %get-tuple-element.356.refs_0_.refs_2_), channel_id=1, source_target_pairs={{0,1},{1,0},{2,3},{3,2},{4,5},{5,4},{6,7},{7,6},{8,9},{9,8},{10,11... | collective-permute-start | bytes 9437192 | tf_op jit(solution)/shard_map/ppermute | solution.py:1004
  121.3 23.8 %collective-permute-start.10 = (bf16[128,1024]{1,0:T(8,128)(2,1)S(1)}, bf16[128,1024]{1,0:T(8,128)(2,1)S(1)}, u32[]{:S(2)}, u32[]{:S(2)}) collective-permute-start(bf16[128,1024]{1,0:T(8,128)(2,1)S(1)} %get-tuple-element.357), channel_id=1, source_target_pairs={{8,0},{16,8},{24,16},{9,1},{17,9},{25,17},{10,2},{18,10},{26,18},{... | collective-permute-start | bytes 786440 | tf_op jit(solution)/shard_map/ppermute | solution.py:1197
  153.6 12.6 %collective-permute-start.11 = (bf16[128,1024]{1,0:T(8,128)(2,1)S(1)}, bf16[128,1024]{1,0:T(8,128)(2,1)S(1)}, u32[]{:S(2)}, u32[]{:S(2)}) collective-permute-start(bf16[128,1024]{1,0:T(8,128)(2,1)S(1)} %get-tuple-element.370), channel_id=1, source_target_pairs={{8,0},{16,8},{24,16},{9,1},{17,9},{25,17},{10,2},{18,10},{26,18},{... | collective-permute-start | bytes 786440 | tf_op jit(solution)/shard_map/ppermute | solution.py:1197
  154.9 26.3 %collective-permute-start.8 = (bf16[4,128,1024]{2,1,0:T(8,128)(2,1)}, bf16[4,128,1024]{2,1,0:T(8,128)(2,1)S(1)}, u32[]{:S(2)}, u32[]{:S(2)}) collective-permute-start(bf16[4,128,1024]{2,1,0:T(8,128)(2,1)} %get-tuple-element.355), channel_id=1, source_target_pairs={{0,2},{1,3},{6,4},{7,5},{8,10},{9,11},{14,12},{15,13},{16,18},{17,... | collective-permute-start | bytes 3145736 | tf_op jit(solution)/shard_map/ppermute | solution.py:1015
  175.4 10.8 %collective-permute-start.12 = (bf16[128,1024]{1,0:T(8,128)(2,1)S(1)}, bf16[128,1024]{1,0:T(8,128)(2,1)S(1)}, u32[]{:S(2)}, u32[]{:S(2)}) collective-permute-start(bf16[128,1024]{1,0:T(8,128)(2,1)S(1)} %get-tuple-element.385), channel_id=1, source_target_pairs={{8,0},{16,8},{9,1},{17,9},{10,2},{18,10},{11,3},{19,11},{12,4},{20... | collective-permute-start | bytes 786440 | tf_op jit(solution)/shard_map/ppermute | solution.py:1197
  195.4 44.4 %collective-permute-start.13 = (bf16[3,128,4096]{2,1,0:T(8,128)(2,1)}, bf16[3,128,4096]{2,1,0:T(8,128)(2,1)}, u32[]{:S(2)}, u32[]{:S(2)}) collective-permute-start(bf16[3,128,4096]{2,1,0:T(8,128)(2,1)} %get-tuple-element.399.refs_4_), channel_id=1, source_target_pairs={{0,1},{1,0},{2,3},{3,2},{4,5},{5,4},{6,7},{7,6},{8,9},{9,8},{10,11... | collective-permute-start | bytes 9437192 | tf_op jit(solution)/shard_map/ppermute | solution.py:1004
  195.4 16.0 %collective-permute-start.14 = (bf16[2,128,1024]{2,1,0:T(8,128)(2,1)}, bf16[2,128,1024]{2,1,0:T(8,128)(2,1)S(1)}, u32[]{:S(2)}, u32[]{:S(2)}) collective-permute-start(bf16[2,128,1024]{2,1,0:T(8,128)(2,1)} %get-tuple-element.400.refs_0_), channel_id=1, source_target_pairs={{0,2},{1,3},{6,4},{7,5},{8,10},{9,11},{14,12},{15,13},{16,18},{17,... | collective-permute-start | bytes 1572872 | tf_op jit(solution)/shard_map/ppermute | solution.py:1015
  198.9 12.5 %collective-permute-start.15 = (bf16[128,1024]{1,0:T(8,128)(2,1)}, bf16[128,1024]{1,0:T(8,128)(2,1)S(1)}, u32[]{:S(2)}, u32[]{:S(2)}) collective-permute-start(bf16[128,1024]{1,0:T(8,128)(2,1)} %copy-done.17), channel_id=1, source_target_pairs={{8,0},{9,1},{10,2},{11,3},{12,4},{13,5},{14,6},{15,7}} | collective-permute-start | bytes 786440 | tf_op jit(solution)/shard_map/ppermute | solution.py:1197
  200.2 22.9 %collective-permute-start.16 = (bf16[1,128,1024]{2,1,0:T(8,128)(2,1)}, bf16[1,128,1024]{2,1,0:T(8,128)(2,1)}, u32[]{:S(2)}, u32[]{:S(2)}) collective-permute-start(bf16[1,128,1024]{2,1,0:T(8,128)(2,1)} %get-tuple-element.401.refs_1_), channel_id=1, source_target_pairs={{0,2},{1,3},{6,4},{7,5},{8,10},{9,11},{14,12},{15,13},{16,18},{17,... | collective-permute-start | bytes 786440 | tf_op jit(solution)/shard_map/ppermute | solution.py:1015
  213.3 15.2 %copy-start.11 = (bf16[4,128,1024]{2,1,0:T(8,128)(2,1)S(1)}, bf16[4,128,1024]{2,1,0:T(8,128)(2,1)}, u32[]{:S(2)}) copy-start(bf16[4,128,1024]{2,1,0:T(8,128)(2,1)} %copy-done.10) | copy-start | bytes 3145732
  218.8 9.7 %collective-permute-start.17 = (bf16[1,128,1024]{2,1,0:T(8,128)(2,1)}, bf16[1,128,1024]{2,1,0:T(8,128)(2,1)S(1)}, u32[]{:S(2)}, u32[]{:S(2)}) collective-permute-start(bf16[1,128,1024]{2,1,0:T(8,128)(2,1)} %get-tuple-element.411.refs_2_), channel_id=1, source_target_pairs={{0,2},{1,3},{6,4},{7,5},{8,10},{9,11},{14,12},{15,13},{16,18},{17,... | collective-permute-start | bytes 786440 | tf_op jit(solution)/shard_map/ppermute | solution.py:1015
  236.7 6.1 %copy-start.5 = (bf16[512,1024]{1,0:T(8,128)(2,1)S(1)}, bf16[512,1024]{1,0:T(8,128)(2,1)}, u32[]{:S(2)}) copy-start(bf16[512,1024]{1,0:T(8,128)(2,1)} %param.10) | copy-start | bytes 3145732
  239.7 8.7 %copy-start.6 = (bf16[512,4096]{1,0:T(8,128)(2,1)}, bf16[512,4096]{1,0:T(8,128)(2,1)S(1)}, u32[]{:S(2)}) copy-start(bf16[512,4096]{1,0:T(8,128)(2,1)S(1)} %get-tuple-element.414.refs_4_.refs_0_) | copy-start | bytes 12582916
  239.7 49.1 %collective-permute-start.19 = (bf16[512,4096]{1,0:T(8,128)(2,1)}, bf16[512,4096]{1,0:T(8,128)(2,1)}, u32[]{:S(2)}, u32[]{:S(2)}) collective-permute-start(bf16[512,4096]{1,0:T(8,128)(2,1)} %get-tuple-element.415.refs_5_), channel_id=1, source_target_pairs={{0,1},{1,0},{2,3},{3,2},{4,5},{5,4},{6,7},{7,6},{8,9},{9,8},{10,11... | collective-permute-start | bytes 12582920 | tf_op jit(solution)/shard_map/ppermute | solution.py:1004
  242.8 5.7 %copy-start.18 = (bf16[1,128,4096]{2,1,0:T(8,128)(2,1)S(1)}, bf16[1,128,4096]{2,1,0:T(8,128)(2,1)}, u32[]{:S(2)}) copy-start(bf16[1,128,4096]{2,1,0:T(8,128)(2,1)} %get-tuple-element.428.refs_6_) | copy-start | bytes 3145732
  242.8 6.2 %copy-start.20 = (s32[4]{0:T(128)S(1)}, s32[4]{0:T(128)}, u32[]{:S(2)}) copy-start(s32[4]{0:T(128)} %refs_1_.1) | copy-start | bytes 52
  248.4 46.8 %collective-permute-start.18 = (bf16[4,128,3072]{2,1,0:T(8,128)(2,1)}, bf16[4,128,3072]{2,1,0:T(8,128)(2,1)}, u32[]{:S(2)}, u32[]{:S(2)}) collective-permute-start(bf16[4,128,3072]{2,1,0:T(8,128)(2,1)} %get-tuple-element.427.refs_2_), channel_id=1, source_target_pairs={{0,1},{1,0},{2,3},{3,2},{4,5},{5,4},{6,7},{7,6},{8,9},{9,8},{10,11... | collective-permute-start | bytes 9437192 | tf_op jit(solution)/shard_map/ppermute | solution.py:1004
  248.5 8.3 %collective-permute-start.20 = (bf16[1,128,4096]{2,1,0:T(8,128)(2,1)S(1)}, bf16[1,128,4096]{2,1,0:T(8,128)(2,1)S(1)}, u32[]{:S(2)}, u32[]{:S(2)}) collective-permute-start(bf16[1,128,4096]{2,1,0:T(8,128)(2,1)S(1)} %copy-done.18), channel_id=1, source_target_pairs={{0,1},{1,0},{2,3},{3,2},{4,5},{5,4},{6,7},{7,6},{8,9},{9,8},{10,11... | collective-permute-start | bytes 3145736 | tf_op jit(solution)/shard_map/ppermute | solution.py:1004
  250.2 44.3 %collective-permute-start.22 = (f32[32,1024]{1,0:T(8,128)S(1)}, f32[32,1024]{1,0:T(8,128)S(1)}, u32[]{:S(2)}, u32[]{:S(2)}) collective-permute-start(f32[32,1024]{1,0:T(8,128)S(1)} %reshape.56), channel_id=1, source_target_pairs={{0,1},{1,0},{2,3},{3,2},{4,5},{5,4},{6,7},{7,6},{8,9},{9,8},{10,11... | collective-permute-start | bytes 393224 | tf_op jit(solution)/shard_map/ppermute | solution.py:1004
  250.3 52.8 %collective-permute-start.21 = (bf16[4,128,1024]{2,1,0:T(8,128)(2,1)}, bf16[4,128,1024]{2,1,0:T(8,128)(2,1)}, u32[]{:S(2)}, u32[]{:S(2)}) collective-permute-start(bf16[4,128,1024]{2,1,0:T(8,128)(2,1)} %get-tuple-element.432.refs_2_), channel_id=1, source_target_pairs={{0,1},{1,0},{2,3},{3,2},{4,5},{5,4},{6,7},{7,6},{8,9},{9,8},{10,11... | collective-permute-start | bytes 3145736 | tf_op jit(solution)/shard_map/ppermute | solution.py:1004
  264.1 26.4 %copy-start.7 = (bf16[512,4096]{1,0:T(8,128)(2,1)S(1)}, bf16[512,4096]{1,0:T(8,128)(2,1)}, u32[]{:S(2)}) copy-start(bf16[512,4096]{1,0:T(8,128)(2,1)} %copy-done.6) | copy-start | bytes 12582916
  267.2 44.8 %collective-permute-start.25 = (bf16[128,4096]{1,0:T(8,128)(2,1)}, bf16[128,4096]{1,0:T(8,128)(2,1)S(1)}, u32[]{:S(2)}, u32[]{:S(2)}) collective-permute-start(bf16[128,4096]{1,0:T(8,128)(2,1)} %get-tuple-element.430.refs_2_), channel_id=1, source_target_pairs={{0,2},{1,3},{8,10},{9,11},{16,18},{17,19},{24,26},{25,27}} | collective-permute-start | bytes 3145736 | tf_op jit(solution)/shard_map/ppermute | solution.py:964
  288.8 23.2 %collective-permute-start.26 = (bf16[128,4096]{1,0:T(8,128)(2,1)}, bf16[128,4096]{1,0:T(8,128)(2,1)}, u32[]{:S(2)}, u32[]{:S(2)}) collective-permute-start(bf16[128,4096]{1,0:T(8,128)(2,1)} %get-tuple-element.435), channel_id=1, source_target_pairs={{6,4},{7,5},{14,12},{15,13},{22,20},{23,21},{30,28},{31,29}} | collective-permute-start | bytes 3145736 | tf_op jit(solution)/shard_map/ppermute | solution.py:964
  294.4 17.5 %collective-permute-start.23 = (bf16[128,4096]{1,0:T(8,128)(2,1)}, bf16[128,4096]{1,0:T(8,128)(2,1)S(1)}, u32[]{:S(2)}, u32[]{:S(2)}) collective-permute-start(bf16[128,4096]{1,0:T(8,128)(2,1)} %get-tuple-element.431.refs_4_), channel_id=1, source_target_pairs={{2,4},{3,5},{10,12},{11,13},{18,20},{19,21},{26,28},{27,29}} | collective-permute-start | bytes 3145736 | tf_op jit(solution)/shard_map/ppermute | solution.py:964
  295.2 16.8 %collective-permute-start.24 = (bf16[128,4096]{1,0:T(8,128)(2,1)}, bf16[128,4096]{1,0:T(8,128)(2,1)S(1)}, u32[]{:S(2)}, u32[]{:S(2)}) collective-permute-start(bf16[128,4096]{1,0:T(8,128)(2,1)} %get-tuple-element.434), channel_id=1, source_target_pairs={{4,2},{5,3},{12,10},{13,11},{20,18},{21,19},{28,26},{29,27}} | collective-permute-start | bytes 3145736 | tf_op jit(solution)/shard_map/ppermute | solution.py:964
  303.1 8.9 %copy-start.8 = (bf16[512,4096]{1,0:T(8,128)(2,1)S(1)}, bf16[512,4096]{1,0:T(8,128)(2,1)}, u32[]{:S(2)}) copy-start(bf16[512,4096]{1,0:T(8,128)(2,1)} %copy-done.6) | copy-start | bytes 12582916
  315.1 47.2 %collective-permute-start.27 = (bf16[128,4224]{1,0:T(8,128)(2,1)S(1)}, bf16[128,4224]{1,0:T(8,128)(2,1)S(1)}, u32[]{:S(2)}, u32[]{:S(2)}) collective-permute-start(bf16[128,4224]{1,0:T(8,128)(2,1)S(1)} %get-tuple-element.437.refs_4_), channel_id=1, source_target_pairs={{0,2},{1,3},{8,10},{9,11},{16,18},{17,19},{24,26},{25,27}} | collective-permute-start | bytes 3244040 | tf_op jit(solution)/shard_map/ppermute | solution.py:964
  328.7 33.6 %collective-permute-start.28 = (bf16[128,4224]{1,0:T(8,128)(2,1)S(1)}, bf16[128,4224]{1,0:T(8,128)(2,1)S(1)}, u32[]{:S(2)}, u32[]{:S(2)}) collective-permute-start(bf16[128,4224]{1,0:T(8,128)(2,1)S(1)} %get-tuple-element.438), channel_id=1, source_target_pairs={{6,4},{7,5},{14,12},{15,13},{22,20},{23,21},{30,28},{31,29}} | collective-permute-start | bytes 3244040 | tf_op jit(solution)/shard_map/ppermute | solution.py:964
  329.5 2.5 collective-permute-start.29
  330.2 30.3 %copy-start.4 = (bf16[512,4096]{1,0:T(8,128)(2,1)S(1)}, bf16[512,4096]{1,0:T(8,128)(2,1)}, u32[]{:S(2)}) copy-start(bf16[512,4096]{1,0:T(8,128)(2,1)} %copy-done.3) | copy-start | bytes 12582916
  330.2 26.2 %collective-permute-start.30 = (bf16[128,4096]{1,0:T(8,128)(2,1)S(1)}, bf16[128,4096]{1,0:T(8,128)(2,1)S(1)}, u32[]{:S(2)}, u32[]{:S(2)}) collective-permute-start(bf16[128,4096]{1,0:T(8,128)(2,1)S(1)} %get-tuple-element.439), channel_id=1, source_target_pairs={{2,0},{3,1},{4,2},{5,3},{10,8},{11,9},{12,10},{13,11},{18,16},{19,... | collective-permute-start | bytes 3145736 | tf_op jit(solution)/shard_map/ppermute | solution.py:964
  362.9 46.6 %collective-permute-start.31 = (bf16[128,4224]{1,0:T(8,128)(2,1)S(1)}, bf16[128,4224]{1,0:T(8,128)(2,1)S(1)}, u32[]{:S(2)}, u32[]{:S(2)}) collective-permute-start(bf16[128,4224]{1,0:T(8,128)(2,1)S(1)} %get-tuple-element.442.refs_3_), channel_id=1, source_target_pairs={{0,2},{1,3},{2,4},{3,5},{8,10},{9,11},{10,12},{11,13},{16,18},{17,... | collective-permute-start | bytes 3244040 | tf_op jit(solution)/shard_map/ppermute | solution.py:964
  365.2 44.2 %collective-permute-start.32 = (bf16[128,4224]{1,0:T(8,128)(2,1)S(1)}, bf16[128,4224]{1,0:T(8,128)(2,1)S(1)}, u32[]{:S(2)}, u32[]{:S(2)}) collective-permute-start(bf16[128,4224]{1,0:T(8,128)(2,1)S(1)} %get-tuple-element.443), channel_id=1, source_target_pairs={{4,2},{5,3},{6,4},{7,5},{12,10},{13,11},{14,12},{15,13},{20,18},{2... | collective-permute-start | bytes 3244040 | tf_op jit(solution)/shard_map/ppermute | solution.py:964
  365.9 43.0 %collective-permute-start.33 = (bf16[128,4096]{1,0:T(8,128)(2,1)S(1)}, bf16[128,4096]{1,0:T(8,128)(2,1)S(1)}, u32[]{:S(2)}, u32[]{:S(2)}) collective-permute-start(bf16[128,4096]{1,0:T(8,128)(2,1)S(1)} %get-tuple-element.441.refs_5_), channel_id=1, source_target_pairs={{0,2},{1,3},{2,4},{3,5},{8,10},{9,11},{10,12},{11,13},{16,18},{17,... | collective-permute-start | bytes 3145736 | tf_op jit(solution)/shard_map/ppermute | solution.py:964
  368.4 40.5 %collective-permute-start.34 = (bf16[128,4096]{1,0:T(8,128)(2,1)S(1)}, bf16[128,4096]{1,0:T(8,128)(2,1)S(1)}, u32[]{:S(2)}, u32[]{:S(2)}) collective-permute-start(bf16[128,4096]{1,0:T(8,128)(2,1)S(1)} %get-tuple-element.444), channel_id=1, source_target_pairs={{4,2},{5,3},{6,4},{7,5},{12,10},{13,11},{14,12},{15,13},{20,18},{2... | collective-permute-start | bytes 3145736 | tf_op jit(solution)/shard_map/ppermute | solution.py:964
  410.0 55.1 %collective-permute-start.35 = (bf16[128,4224]{1,0:T(8,128)(2,1)S(1)}, bf16[128,4224]{1,0:T(8,128)(2,1)S(1)}, u32[]{:S(2)}, u32[]{:S(2)}) collective-permute-start(bf16[128,4224]{1,0:T(8,128)(2,1)S(1)} %get-tuple-element.446.refs_3_), channel_id=1, source_target_pairs={{0,2},{1,3},{2,4},{3,5},{4,6},{5,7},{8,10},{9,11},{10,12},{11,13},... | collective-permute-start | bytes 3244040 | tf_op jit(solution)/shard_map/ppermute | solution.py:964
  416.4 48.7 %collective-permute-start.36 = (bf16[128,4224]{1,0:T(8,128)(2,1)S(1)}, bf16[128,4224]{1,0:T(8,128)(2,1)S(1)}, u32[]{:S(2)}, u32[]{:S(2)}) collective-permute-start(bf16[128,4224]{1,0:T(8,128)(2,1)S(1)} %get-tuple-element.447), channel_id=1, source_target_pairs={{2,0},{3,1},{4,2},{5,3},{6,4},{7,5},{10,8},{11,9},{12,10},{13,11},... | collective-permute-start | bytes 3244040 | tf_op jit(solution)/shard_map/ppermute | solution.py:964
  417.7 41.5 %collective-permute-start.37 = (bf16[128,4096]{1,0:T(8,128)(2,1)S(1)}, bf16[128,4096]{1,0:T(8,128)(2,1)S(1)}, u32[]{:S(2)}, u32[]{:S(2)}) collective-permute-start(bf16[128,4096]{1,0:T(8,128)(2,1)S(1)} %get-tuple-element.445.refs_5_), channel_id=1, source_target_pairs={{0,2},{1,3},{2,4},{3,5},{4,6},{5,7},{8,10},{9,11},{10,12},{11,13},... | collective-permute-start | bytes 3145736 | tf_op jit(solution)/shard_map/ppermute | solution.py:964
  422.3 41.1 %collective-permute-start.38 = (bf16[128,4096]{1,0:T(8,128)(2,1)S(1)}, bf16[128,4096]{1,0:T(8,128)(2,1)S(1)}, u32[]{:S(2)}, u32[]{:S(2)}) collective-permute-start(bf16[128,4096]{1,0:T(8,128)(2,1)S(1)} %get-tuple-element.448), channel_id=1, source_target_pairs={{2,0},{3,1},{4,2},{5,3},{6,4},{7,5},{10,8},{11,9},{12,10},{13,11},... | collective-permute-start | bytes 3145736 | tf_op jit(solution)/shard_map/ppermute | solution.py:964
  (12 other events, 25.7 us)

commit v4 on v3

--- a/solution.py
+++ b/solution.py
@@ -137,20 +137,14 @@
 
 
 def turn(source, target, row0, col0, side_by, strips, sems, base):
-    side = 256
-    ones = (
-        lax.broadcasted_iota(jnp.int32, (side, side), 0)
-        == lax.broadcasted_iota(jnp.int32, (side, side), 1)
-    ).astype(BF16)
-
-    slots = strips.shape[0]
+    slots, side, _ = strips.shape
     count = side_by // side
 
     def strip(i):
-        r = pl.multiple_of(row0 + i * side, side)
+        c = pl.multiple_of(col0 + i * side, side)
         return pltpu.make_async_copy(
             strips.at[i % slots],
-            target.at[pl.ds(col0, side_by), pl.ds(r, side)],
+            target.at[pl.ds(c, side), pl.ds(row0, side_by)],
             sems.at[base + i % slots],
         )
 
@@ -159,11 +153,8 @@
         def slot_is_free():
             strip(i - slots).wait()
 
-        r = pl.multiple_of(row0 + i * side, side)
-        for c in range(0, side_by, side):
-            strips[i % slots, c : c + side, :] = product_last(
-                ones, source[pl.ds(r, side), col0 + c : col0 + c + side]
-            ).astype(BF16)
+        c = pl.multiple_of(col0 + i * side, side)
+        strips[i % slots] = source[row0 : row0 + side_by, pl.ds(c, side)].T
         strip(i).start()
         return carry
 
@@ -252,12 +243,28 @@
         pairs = [(given_table, table)] + list(zip(given, weight))
         for i, (source, target) in enumerate(pairs):
             loads.append(pltpu.make_async_copy(source, target, sems.at[i]))
-            loads[i].start()
+        loads[0].start()
+
+        @pl.when(core == 1)
+        def later():
+            loads[4].start()
+            loads[4].wait()
+
+        loads[1].start()
     base = len(loads)
 
     def ready(i):
-        if loads_weights:
-            loads[i].wait()
+        if not loads_weights:
+            return
+        if i == 4:
+            pl.when(core != 1)(loads[4].wait)
+            return
+        loads[i].wait()
+        if i == 1:
+            loads[2].start()
+            loads[3].start()
+        if i == 2:
+            pl.when(core != 1)(loads[4].start)
 
     @pl.when(active)
     def forward():
@@ -313,7 +320,7 @@
             scores = jnp.where(allowed, product_last(queries, keys) * inv_root, masked_score)
             exp_scores = jnp.exp(scores - jnp.max(scores, axis=-1, keepdims=True))
             total = jnp.sum(exp_scores, axis=-1, keepdims=True)
-            group_probs = (exp_scores / total).astype(BF16)
+            group_probs = (exp_scores * (1.0 / total)).astype(BF16)
             probs[g * GROUP * frames : (g + 1) * GROUP * frames, :] = group_probs
             attended[:, lo:hi] = product(beside(group_probs, frames), values).astype(BF16)
         save(probs, reread.probs.at[slot])
@@ -335,8 +342,10 @@
             value, gradient = gelu_and_slope(product(normed[...], weight.up[:, j : j + BLOCK]))
             act[:, j : j + BLOCK] = value.astype(BF16)
             slope[:, j : j + BLOCK] = gradient.astype(BF16)
-        save(slope, reread.slope.at[slot])
-        save(act, kept.act.at[slot])
+            if (j + BLOCK) % (hidden_units // 2) == 0:
+                done = pl.ds(j + BLOCK - hidden_units // 2, hidden_units // 2)
+                save(slope.at[:, done], reread.slope.at[slot, :, done])
+                save(act.at[:, done], kept.act.at[slot, :, done])
         ready(4)
         for j in range(0, features, BLOCK):
             outgoing[:, j : j + BLOCK] = (
@@ -351,7 +360,8 @@
         for r in range(0, total_rows, features):
             for c in range(0, total_cols, features):
                 units.append((source, target, r, c))
-    pieces = 2
+    cut = len(units) // 3
+    pieces = (units[:cut], units[cut:])
     piece = jnp.where(micro < 0, tick, micro - micros + section)
 
     @pl.when(jnp.logical_not(active))
@@ -359,11 +369,11 @@
         for i in range(base):
             ready(i)
 
-    for k in range(pieces):
+    for k in range(len(pieces)):
 
         @pl.when(jnp.logical_not(active) & (piece == k))
         def one_piece(k=k):
-            for source, target, r, c in units[k::pieces]:
+            for source, target, r, c in pieces[k]:
                 turn(source, target, r, c, features, strips, sems, base)
 
 
@@ -644,7 +654,7 @@
         pltpu.VMEM((CORES, plan.frames, 3 * plan.features // CORES), BF16),
         pltpu.VMEM((plan.frames, plan.features), BF16),
         pltpu.VMEM((plan.frames, plan.hidden_units), BF16),
-        pltpu.VMEM((2, plan.features, 256), BF16),
+        pltpu.VMEM((2, 256, plan.features), BF16),
         pltpu.SemaphoreType.DMA((24,)),
     ]
     flops = 8 * plan.frames * sum(w.size for w in state.weights)
@@ -788,28 +798,53 @@
         if remade:
             load.wait()
 
-        def one_step(j, carry):
-            slot = j % 2
-
-            @pl.when(j + 1 < steps)
-            def next_block():
-                for copy in right_copies(j + 1, 1 - slot):
-                    copy.start()
-
+        def fill(j, slot):
             for copy in right_copies(j, slot):
                 copy.wait()
             if remade:
-                frames_all = normed.shape[0] * frames
-                upward = product(normed[...].reshape(frames_all, -1), weight_slots[slot])
-                act = gelu_and_slope(upward)[0].astype(BF16)
+                rows = normed[...].reshape(normed.shape[0] * frames, -1)
+                act = gelu_and_slope(product(rows, weight_slots[slot]))[0].astype(BF16)
                 right_slots[slot, remade_from:] = act.reshape(-1, frames, step)
 
+        def add(j, slot):
             right = right_slots[slot].reshape(-1, step)
             for i in range(outputs):
                 outs[i][:, columns(j)] = product(turned[i], right).astype(BF16)
+
+        def start(j, slot):
+            for copy in right_copies(j, slot):
+                copy.start()
+
+        def two_steps(i, carry):
+            j = 2 * i
+            fill(j + 1, 1)
+            add(j, 0)
+
+            @pl.when(j + 2 < steps)
+            def next_block():
+                start(j + 2, 0)
+
+            @pl.when(j + 3 < steps)
+            def block_after():
+                fill(j + 2, 0)
+                add(j + 1, 1)
+                start(j + 3, 1)
+
+            @pl.when(j + 3 >= steps)
+            def last_block():
+                add(j + 1, 1)
+
             return carry
 
-        lax.fori_loop(0, steps, one_step, 0)
+        fill(0, 0)
+        if steps == 1:
+            add(0, 0)
+        else:
+            start(1, 1)
+            lax.fori_loop(0, steps // 2, two_steps, 0)
+            if steps % 2:
+                fill(steps - 1, 0)
+                add(steps - 1, 0)
 
     if remade:
 
@@ -870,10 +905,17 @@
     return total
 
 
-def send_kernel(parts, rows, hop, adds, *refs):
+def arrived(came, side, at, width):
+    for pair in came:
+        if at < pair[side].shape[1]:
+            return pair[side][:, at : at + width].astype(F32)
+        at -= pair[side].shape[1]
+
+
+def send_kernel(parts, rows, hop, joined, *refs):
     refs = list(refs)
     grads = [[refs.pop(0) for _ in range(p.grads)] for p in parts]
-    came = refs[:2] if adds else None
+    came = [(refs.pop(0), refs.pop(0)) for _ in range(joined)]
     sends = refs[-2:]
     chip = lax.axis_index("batch") // CORES
     last = lax.axis_size("batch") // CORES - 1
@@ -882,16 +924,16 @@
         at = 0
         for part, terms in zip(parts, grads):
             total = added_terms(part, terms, rows, places[d])
-            if adds:
-                total = total + came[d][:, at : at + part.width].astype(F32)
+            if joined:
+                total = total + arrived(came, d, at, part.width)
             sends[d][:, at : at + part.width] = total.astype(BF16)
             at += part.width
 
 
-def finish_kernel(parts, rows, result_count, *refs):
+def finish_kernel(parts, rows, result_count, joined, *refs):
     refs = list(refs)
     grads = [[refs.pop(0) for _ in range(p.grads)] for p in parts]
-    came = refs[:2]
+    came = [(refs.pop(0), refs.pop(0)) for _ in range(joined)]
     total, turned, sems = refs[-3:]
     results = refs[-4 - result_count : -4]
     refs[-4][...] = jnp.zeros(refs[-4].shape, F32)
@@ -901,8 +943,8 @@
         own = slice(at, at + part.width)
         total[:, own] = (
             added_terms(part, terms, rows, chip)
-            + came[0][:, own].astype(F32)
-            + came[1][:, own].astype(F32)
+            + arrived(came, 0, at, part.width)
+            + arrived(came, 1, at, part.width)
         )
         result = results[part.result]
         if part.tall:
@@ -921,8 +963,16 @@
 class Piece:
     def __init__(self, parts, first_hop):
         self.parts, self.hop, self.first_hop = parts, first_hop - 1, first_hop
-        self.came = None
+        self.came = []
         self.width = sum(p.width for p in parts)
+
+    def arrivals(self):
+        return [x for pair in self.came for x in pair]
+
+    def joined(self, other):
+        piece = Piece(self.parts + other.parts, self.first_hop)
+        piece.hop, piece.came = self.hop, self.came + other.came
+        return piece
 
 
 class Line:
@@ -938,26 +988,24 @@
         ]
 
     def send(self, piece, after=()):
-        adds = piece.came is not None
         piece.hop += 1
         shape = (self.rows, piece.width)
         call = Call()
         call.take([g for p in piece.parts for g in p.grads], in_vmem, pltpu.VMEM)
-        if adds:
-            call.take(piece.came, in_vmem, pltpu.VMEM)
+        call.take(piece.arrivals(), in_vmem, pltpu.VMEM)
         call.take([self.before, *after], anywhere)
         call.give([(shape, BF16)] * 2, in_vmem, pltpu.VMEM)
         parts = self.bare(piece)
         up, down = call.run(
-            functools.partial(send_kernel, parts, self.rows, piece.hop, adds), [], 0
+            functools.partial(send_kernel, parts, self.rows, piece.hop, len(piece.came)), [], 0
         )
         self.before = up
         edge = piece.first_hop - 1
         last = self.chips - 1
-        piece.came = [
+        piece.came = [(
             self.moved(up, [z for z in range(last) if edge <= z < piece.hop], 1),
             self.moved(down, [z for z in range(1, last + 1) if edge <= last - z < piece.hop], -1),
-        ]
+        )]
 
     def moved(self, value, senders, by):
         pairs = [(CORES * z + c, CORES * (z + by) + c) for z in senders for c in range(CORES)]
@@ -968,7 +1016,7 @@
         parts = self.bare(piece, names)
         call = Call()
         call.take([g for p in piece.parts for g in p.grads], in_vmem, pltpu.VMEM)
-        call.take(piece.came, in_vmem, pltpu.VMEM)
+        call.take(piece.arrivals(), in_vmem, pltpu.VMEM)
         call.take([self.before], anywhere)
         call.give([(self.shapes[n], F32) for n in names], anywhere, pltpu.HBM)
         call.give([((8, LANES), F32)], in_vmem, pltpu.VMEM)
@@ -980,7 +1028,9 @@
             pltpu.SemaphoreType.DMA((len(parts),)),
         ]
         done = call.run(
-            functools.partial(finish_kernel, parts, self.rows, len(names)), scratch, 0
+            functools.partial(finish_kernel, parts, self.rows, len(names), len(piece.came)),
+            scratch,
+            0,
         )
         self.results.update(zip(names, done))
         self.before = done[-1]
@@ -1018,7 +1068,7 @@
         return [in_hbm(x), self.inward(x)] if self.ends_hand_over else [in_hbm(x)]
 
 
-def sums_by_hops(plan, exchange, back, downs, grad_up, lefts, table_grad, before):
+def sums_by_hops(plan, exchange, back, down, up, lefts, table_grad):
     chips, rows = exchange.chips, plan.rows
     features, hidden_units = plan.features, plan.hidden_units
     core = lax.axis_index("batch") % CORES
@@ -1032,7 +1082,7 @@
         (hidden_units, rows),
         (table_size, rows),
     ]
-    line = Line(exchange, rows, results, before)
+    line = Line(exchange, rows, results, up)
 
     def of(right, first_column):
         rights = exchange.both(right)
@@ -1041,12 +1091,10 @@
         line.before = grad
         return grad
 
-    up = line.before = grad_up(before)
     ups = Piece([Part([up], 0, hidden_units, 2, 0, False)], 1)
     line.send(ups)
-    down, down_given = downs
     first = 2 if exchange.ends_hand_over else 1
-    downs = Piece([Part([down, swap(down_given)], 0, hidden_units, 3, 0, True)], first)
+    downs = Piece([Part([down[0], swap(down[1])], 0, hidden_units, 3, 0, True)], first)
     line.send(downs)
     qkv = of(back.grad_packed, 0)
     out = of(back.grad_attn, share)
@@ -1063,19 +1111,17 @@
         ],
         1,
     )
-    order = [downs, others, ups, others, ups, others]
-    gone = [ups.came, downs.came]
-    pieces = [ups, downs, others]
-    for piece in order:
-        if piece.hop < chips - 1:
-            line.send(piece, gone.pop(0))
-            gone.append(piece.came)
-        for done in pieces[:]:
-            if done.hop == chips - 1 and done is not piece:
-                line.finish(done)
-                pieces.remove(done)
-    for piece in pieces:
-        line.finish(piece)
+    last = chips - 1
+    while downs.hop < last:
+        line.send(downs)
+    line.send(others, ups.arrivals())
+    rest = ups.joined(others)
+    if rest.hop < last:
+        line.send(rest, downs.arrivals())
+    line.finish(downs)
+    while rest.hop < last:
+        line.send(rest)
+    line.finish(rest)
     return [line.results[i] for i in range(len(results))]
 
 
@@ -1175,17 +1221,7 @@
                 if exchange.by_hops:
                     y_last = exchange.sources(state.back.y_last)
                     up_last = exchange.both(state.back.up_last)
-                    sides = list(zip(y_early, y_late, y_last))
-                    pairs = down_pairs(sides[0], in_hbm(state.kept.act))
-                    remade, sources = (), ()
-                    if exchange.ends_hand_over:
-                        remade = down_pairs(sides[1], None)
-                        sources = (second[1], up_weight[0])
-                    down = weight_grad(
-                        pairs, 0, features, plan.rows, output[:1], 2, state.turned[:1],
-                        remade, sources,
-                    )
-                    after = up_early[1:] + down
+                    after = up_early[1:]
                 state, output = run_backward(
                     plan, tick, state, arriving, cot_all, after, SECOND, output
                 )
@@ -1213,13 +1249,17 @@
     codes = codebooks * (section % 2)
     table_grad = table_gradient(state.back.row_grads, codes, blocks).reshape(norm_table.shape[1:])
     if exchange.by_hops:
-        def grad_up(before):
-            pairs = up_pairs(up_early, 0) + up_pairs(up_last, micros - 1)
-            return weight_grad(pairs, 2 * share, share, plan.rows, [before])[0]
-
-        sums = sums_by_hops(
-            plan, exchange, state.back, down, grad_up, lefts, table_grad, output
-        )
+        sides = list(zip(y_early, y_late, y_last))
+        pairs = down_pairs(sides[0], in_hbm(state.kept.act))
+        remade, sources = (), ()
+        if exchange.ends_hand_over:
+            remade = down_pairs(sides[1], None)
+            sources = (second[1], in_hbm(up_weight[0]))
+        ready = [output, up_last[1], up_early[1]]
+        down = weight_grad(pairs, 0, features, plan.rows, ready, 2, (), remade, sources)
+        pairs = up_pairs(up_early, 0) + up_pairs(up_last, micros - 1)
+        (up,) = weight_grad(pairs, 2 * share, share, plan.rows, down[:1])
+        sums = sums_by_hops(plan, exchange, state.back, down, up, lefts, table_grad)
     else:
         sums = sums_by_scatter(plan, state.kept, state.back, table_grad)
     return (

time: 476 us -> 457 us (0.960)
  local copies, waits for them, and re-layouts: 15.8 us -> 6.79 us
  Pallas kernels: 158 us -> 151 us
    unnamed x42 -> x24, local copies, waits for them, and re-layouts: 15.5 us -> 6.52 us
    pallas_call x30 -> x27, Pallas kernels: 158 us -> 151 us  [run(): pl.pallas_call(body, out_shape=self.out_shape, in_specs=self.in_specs, ou...]
    ppermute x7, waiting for transfers between devices: 6.02 us -> 0.02 us  [swap(): return lax.ppermute(x, 'batch', [(b, b ^ 1) for b in range(self.batch)])]
    ppermute x16 -> x12, starting transfers between devices: 61.4 us -> 66.6 us  [moved(): return lax.ppermute(value, 'batch', pairs)]
    ppermute x16 -> x12, waiting for transfers between devices: 109 us -> 107 us  [moved(): return lax.ppermute(value, 'batch', pairs)]
  transfers between devices with their start and end apart: 39 -> 35, of which waited for: 16 -> 15; matrix products, arithmetic and copies ran while one was open for 0% -> 0% of each run, Pallas kernels for 20% -> 19%
where the time goes in v4:
time: 457 us; the launch traced here: 449 us
  waiting for transfers between devices  185 us (40%)
  Pallas kernels  151 us (33%)
  starting transfers between devices  105 us (23%)
  local copies, waits for them, and re-layouts  6.79 us (1%)
    pallas_call x27, Pallas kernels, run(): pl.pallas_call(body, out_shape=self.out_shape, in_specs=self.in_specs, ou...  151 us
    ppermute x12, waiting for transfers between devices, moved(): return lax.ppermute(value, 'batch', pairs)  107 us
    ppermute x12, starting transfers between devices, moved(): return lax.ppermute(value, 'batch', pairs)  66.6 us
    ppermute x6, waiting for transfers between devices, per_device(): returned = lax.ppermute(output, 'section', backward)  39 us
    ppermute x6, waiting for transfers between devices, per_device(): sent = lax.ppermute(output, 'section', onward)  19.5 us
    ppermute x4, waiting for transfers between devices, inward(): return lax.ppermute(x, 'batch', pairs)  18.6 us
    ppermute x6, starting transfers between devices, per_device(): sent = lax.ppermute(output, 'section', onward)  17 us
    ppermute x4, starting transfers between devices, inward(): return lax.ppermute(x, 'batch', pairs)  13.6 us
  transfers between devices with their start and end apart: 35, of which 15 were waited for; matrix products, arithmetic and copies ran while one was open for 0% of the time, Pallas kernels for 19%

profile of v4, /device:TPU:0, one launch (start us, length us, event | category | flops | bytes accessed | tf_op | source)
XLA Modules:
  0.0 449.3 jit_solution(4502357068927119665)
XLA Ops:
  0.6 14.1 %shard_map.144 = (s32[8]{0:T(128)S(4)}, f32[32,1024]{1,0:T(8,128)S(1)}, bf16[1024,3072]{1,0:T(8,128)(2,1)S(1)}, bf16[1024,1024]{1,0:T(8,128)(2,1)S(1)}, bf16[102...) custom-call(s32[4]{0:T(128)} %refs_0_.1, ...), custom_call_target="tpu_custom_call" | custom-call | flops 12884901888 | tf_op jit(solution)/shard_map/pallas_call | solution.py:588
  14.7 5.2 %collective-permute-start = (bf16[128,1024]{1,0:T(8,128)(2,1)S(1)}, bf16[128,1024]{1,0:T(8,128)(2,1)S(1)}, u32[]{:S(2)}, u32[]{:S(2)}) collective-permute-start(bf16[128,1024]{1,0:T(8,128)(2,1)S(1)} %get-tuple-element.236), channel_id=1, source_target_pairs={{0,8},{1,9},{2,10},{3,11},{4,12},{5,13},{6,14},{7,15}} | collective-permute-start | bytes 786440 | tf_op jit(solution)/shard_map/ppermute | solution.py:1213
  19.9 6.3 %collective-permute-done.refs_10_ = bf16[128,1024]{1,0:T(8,128)(2,1)S(1)} collective-permute-done((bf16[128,1024]{1,0:T(8,128)(2,1)S(1)}, bf16[128,1024]{1,0:T(8,128)(2,1)S(1)}, u32[]{:S(2)}, u32[]{:S(2)}) %collective-permute-start) | collective-permute-done | bytes 262176 | tf_op jit(solution)/shard_map/ppermute | solution.py:1213
  26.2 9.5 %shard_map.145 = (bf16[3072,1024]{1,0:T(8,128)(2,1)S(1)}, bf16[1024,1024]{1,0:T(8,128)(2,1)S(1)}, bf16[4096,1024]{1,0:T(8,128)(2,1)S(1)}, bf16[1024,4096]{1,0:T(...) custom-call(s32[8]{0:T(128)S(4)} %get-tuple-element.226.refs_0_, ...), custom_call_target="tpu_custom_call", output_to_operand_aliasing={{0}: (6, {}), {1}: (7, {}), {2}: (8, {}), {3}: (9, {}), {4}... | custom-call | flops 12884901888 | tf_op jit(solution)/shard_map/pallas_call | solution.py:588
  35.7 3.5 collective-permute-start.1
  39.2 5.5 %collective-permute-done.1.refs_10_ = bf16[128,1024]{1,0:T(8,128)(2,1)S(1)} collective-permute-done((bf16[128,1024]{1,0:T(8,128)(2,1)S(1)}, bf16[128,1024]{1,0:T(8,128)(2,1)S(1)}, u32[]{:S(2)}, u32[]{:S(2)}) %collective-permute-start.1) | collective-permute-done | bytes 262176 | tf_op jit(solution)/shard_map/ppermute | solution.py:1213
  44.7 8.9 %shard_map.146 = (bf16[3072,1024]{1,0:T(8,128)(2,1)S(1)}, bf16[1024,1024]{1,0:T(8,128)(2,1)S(1)}, bf16[4096,1024]{1,0:T(8,128)(2,1)S(1)}, bf16[1024,4096]{1,0:T(...) custom-call(s32[8]{0:T(128)S(4)} %get-tuple-element.226.refs_0_, ...), custom_call_target="tpu_custom_call", output_to_operand_aliasing={{0}: (6, {}), {1}: (7, {}), {2}: (8, {}), {3}: (9, {}), {4}... | custom-call | flops 12884901888 | tf_op jit(solution)/shard_map/pallas_call | solution.py:588
  53.6 3.5 collective-permute-start.2
  57.1 4.6 %collective-permute-done.2.refs_10_ = bf16[128,1024]{1,0:T(8,128)(2,1)S(1)} collective-permute-done((bf16[128,1024]{1,0:T(8,128)(2,1)S(1)}, bf16[128,1024]{1,0:T(8,128)(2,1)S(1)}, u32[]{:S(2)}, u32[]{:S(2)}) %collective-permute-start.2) | collective-permute-done | bytes 262176 | tf_op jit(solution)/shard_map/ppermute | solution.py:1213
  61.7 9.3 %shard_map.147 = (bf16[3072,1024]{1,0:T(8,128)(2,1)S(1)}, bf16[1024,1024]{1,0:T(8,128)(2,1)S(1)}, bf16[4096,1024]{1,0:T(8,128)(2,1)S(1)}, bf16[1024,4096]{1,0:T(...) custom-call(s32[8]{0:T(128)S(4)} %get-tuple-element.226.refs_0_, ...), custom_call_target="tpu_custom_call", output_to_operand_aliasing={{0}: (6, {}), {1}: (7, {}), {2}: (8, {}), {3}: (9, {}), {4}... | custom-call | flops 12884901888 | tf_op jit(solution)/shard_map/pallas_call | solution.py:588
  71.0 3.5 collective-permute-start.3
  75.4 3.0 collective-permute-done.3.refs_10_
  78.4 9.8 %shard_map.149 = (bf16[3072,1024]{1,0:T(8,128)(2,1)S(1)}, bf16[1024,1024]{1,0:T(8,128)(2,1)S(1)}, bf16[4096,1024]{1,0:T(8,128)(2,1)S(1)}, bf16[1024,4096]{1,0:T(...) custom-call(s32[8]{0:T(128)S(4)} %get-tuple-element.226.refs_0_, ...), custom_call_target="tpu_custom_call", output_to_operand_aliasing={{0}: (6, {}), {1}: (7, {}), {2}: (8, {}), {3}: (9, {}), {4}... | custom-call | flops 12884901888 | tf_op jit(solution)/shard_map/pallas_call | solution.py:588
  89.7 14.1 %shard_map.151 = (bf16[3072,1024]{1,0:T(8,128)(2,1)S(1)}, bf16[1024,1024]{1,0:T(8,128)(2,1)S(1)}, bf16[4096,1024]{1,0:T(8,128)(2,1)S(1)}, bf16[1024,4096]{1,0:T(...) custom-call(s32[8]{0:T(128)S(4)} %get-tuple-element.226.refs_0_, ...), custom_call_target="tpu_custom_call", output_to_operand_aliasing={{0}: (6, {}), {1}: (7, {}), {2}: (8, {}), {3}: (9, {}), {4}... | custom-call | flops 12884901888 | tf_op jit(solution)/shard_map/pallas_call | solution.py:588
  104.7 6.4 %shard_map.153 = (bf16[3072,1024]{1,0:T(8,128)(2,1)S(1)}, bf16[1024,1024]{1,0:T(8,128)(2,1)S(1)}, bf16[4096,1024]{1,0:T(8,128)(2,1)S(1)}, bf16[1024,4096]{1,0:T(...) custom-call(s32[8]{0:T(128)S(4)} %get-tuple-element.226.refs_0_, ...), custom_call_target="tpu_custom_call", output_to_operand_aliasing={{0}: (6, {}), {1}: (7, {}), {2}: (8, {}), {3}: (9, {}), {4}... | custom-call | flops 12884901888 | tf_op jit(solution)/shard_map/pallas_call | solution.py:588
  112.5 24.7 %collective-permute-done.10.refs_10_ = bf16[128,1024]{1,0:T(8,128)(2,1)S(1)} collective-permute-done((bf16[128,1024]{1,0:T(8,128)(2,1)S(1)}, bf16[128,1024]{1,0:T(8,128)(2,1)S(1)}, u32[]{:S(2)}, u32[]{:S(2)}) %collective-permute-start.10) | collective-permute-done | bytes 262176 | tf_op jit(solution)/shard_map/ppermute | solution.py:1233
  137.2 8.5 %shard_map.154 = (bf16[4,128,1024]{2,1,0:T(8,128)(2,1)}, bf16[4,128,3072]{2,1,0:T(8,128)(2,1)}, bf16[4,2048,128]{2,1,0:T(8,128)(2,1)}, f32[4,128,1024]{2,1,0:T(8...) custom-call(s32[8]{0:T(128)S(4)} %get-tuple-element.226.refs_0_, ...), custom_call_target="tpu_custom_call", output_to_operand_aliasing={{0}: (12, {}), {1}: (13, {}), {2}: (14, {}), {3}: (15, {}),... | custom-call | flops 12884901888 | tf_op jit(solution)/shard_map/pallas_call | solution.py:588
  147.0 4.4 collective-permute-start.8
  151.5 8.7 %collective-permute-done.11.refs_11_ = bf16[128,1024]{1,0:T(8,128)(2,1)S(1)} collective-permute-done((bf16[128,1024]{1,0:T(8,128)(2,1)S(1)}, bf16[128,1024]{1,0:T(8,128)(2,1)S(1)}, u32[]{:S(2)}, u32[]{:S(2)}) %collective-permute-start.11) | collective-permute-done | bytes 262176 | tf_op jit(solution)/shard_map/ppermute | solution.py:1233
  160.2 8.7 %shard_map.155 = (bf16[4,128,1024]{2,1,0:T(8,128)(2,1)}, bf16[4,128,3072]{2,1,0:T(8,128)(2,1)}, bf16[4,2048,128]{2,1,0:T(8,128)(2,1)}, f32[4,128,1024]{2,1,0:T(8...) custom-call(s32[8]{0:T(128)S(4)} %get-tuple-element.226.refs_0_, ...), custom_call_target="tpu_custom_call", output_to_operand_aliasing={{0}: (13, {}), {1}: (14, {}), {2}: (15, {}), {3}: (16, {}),... | custom-call | flops 12884901888 | tf_op jit(solution)/shard_map/pallas_call | solution.py:588
  170.1 3.2 collective-permute-done.8.refs_10_.refs_9_
  173.3 5.6 %collective-permute-done.12.refs_11_ = bf16[128,1024]{1,0:T(8,128)(2,1)S(1)} collective-permute-done((bf16[128,1024]{1,0:T(8,128)(2,1)S(1)}, bf16[128,1024]{1,0:T(8,128)(2,1)S(1)}, u32[]{:S(2)}, u32[]{:S(2)}) %collective-permute-start.12) | collective-permute-done | bytes 262176 | tf_op jit(solution)/shard_map/ppermute | solution.py:1233
  178.9 8.5 %shard_map.156 = (bf16[4,128,1024]{2,1,0:T(8,128)(2,1)}, bf16[4,128,3072]{2,1,0:T(8,128)(2,1)}, bf16[4,2048,128]{2,1,0:T(8,128)(2,1)}, f32[4,128,1024]{2,1,0:T(8...) custom-call(s32[8]{0:T(128)S(4)} %get-tuple-element.226.refs_0_, ...), custom_call_target="tpu_custom_call", output_to_operand_aliasing={{0}: (13, {}), {1}: (14, {}), {2}: (15, {}), {3}: (16, {}),... | custom-call | flops 12884901888 | tf_op jit(solution)/shard_map/pallas_call | solution.py:588
  187.4 3.5 collective-permute-start.15
  192.2 10.8 %collective-permute-done.15.refs_10_.refs_3_ = bf16[2,128,1024]{2,1,0:T(8,128)(2,1)S(1)} collective-permute-done((bf16[2,128,1024]{2,1,0:T(8,128)(2,1)}, bf16[2,128,1024]{2,1,0:T(8,128)(2,1)S(1)}, u32[]{:S(2)}, u32[]{:S(2)}) %collective-permute-start.15) | collective-permute-done | bytes 524320 | tf_op jit(solution)/shard_map/ppermute | solution.py:1065
  203.8 5.5 %shard_map.157 = (bf16[4,128,1024]{2,1,0:T(8,128)(2,1)}, bf16[4,128,3072]{2,1,0:T(8,128)(2,1)}, bf16[4,2048,128]{2,1,0:T(8,128)(2,1)}, f32[4,128,1024]{2,1,0:T(8...) custom-call(s32[8]{0:T(128)S(4)} %get-tuple-element.226.refs_0_, ...), custom_call_target="tpu_custom_call", output_to_operand_aliasing={{0}: (13, {}), {1}: (14, {}), {2}: (15, {}), {3}: (16, {}),... | custom-call | flops 6442450944 | tf_op jit(solution)/shard_map/pallas_call | solution.py:588
  209.5 4.3 collective-permute-start.17
  215.1 5.9 %shard_map.158 = (bf16[4,128,1024]{2,1,0:T(8,128)(2,1)}, bf16[4,128,3072]{2,1,0:T(8,128)(2,1)}, bf16[4,2048,128]{2,1,0:T(8,128)(2,1)}, f32[4,128,1024]{2,1,0:T(8...) custom-call(s32[8]{0:T(128)S(4)} %get-tuple-element.226.refs_0_, ...), custom_call_target="tpu_custom_call", output_to_operand_aliasing={{0}: (6, {}), {1}: (7, {}), {2}: (8, {}), {3}: (9, {}), {4}... | custom-call | flops 6442450944 | tf_op jit(solution)/shard_map/pallas_call | solution.py:588
  221.1 4.6 %collective-permute-done.18.refs_5_ = bf16[1,128,1024]{2,1,0:T(8,128)(2,1)S(1)} collective-permute-done((bf16[1,128,1024]{2,1,0:T(8,128)(2,1)}, bf16[1,128,1024]{2,1,0:T(8,128)(2,1)S(1)}, u32[]{:S(2)}, u32[]{:S(2)}) %collective-permute-start.18) | collective-permute-done | bytes 262176 | tf_op jit(solution)/shard_map/ppermute | solution.py:1065
  225.7 2.8 shard_map.159
  228.5 2.0 copy-done.3
  231.9 2.2 copy-done.4
  234.1 10.5 %shard_map.160.refs_0_.refs_1_ = bf16[512,4096]{1,0:T(8,128)(2,1)S(1)} custom-call(bf16[2,4,128,1536]{3,2,1,0:T(8,128)(2,1)} %get-tuple-element.351.refs_0_.refs_2_, bf16[2,4,128,1536]{3,2,1,0:T(8,128)(2,1)} %collective-permute-done.9.refs_10_.refs_1_.refs_3_, bf16[2,4,128,1536]{3,2,1,0:T(8,128)(2,1)} %get-tuple-element.351.refs_0_.refs_2_, ...), custom_call_target="tpu_custom_call" | custom-call | tf_op jit(solution)/shard_map/pallas_call | solution.py:588
  247.2 30.1 %collective-permute-start.23 = (bf16[128,4096]{1,0:T(8,128)(2,1)S(1)}, bf16[128,4096]{1,0:T(8,128)(2,1)S(1)}, u32[]{:S(2)}, u32[]{:S(2)}) collective-permute-start(bf16[128,4096]{1,0:T(8,128)(2,1)S(1)} %get-tuple-element.425.refs_2_), channel_id=1, source_target_pairs={{0,2},{1,3},{8,10},{9,11},{16,18},{17,19},{24,26},{25,27}} | collective-permute-start | bytes 3145736 | tf_op jit(solution)/shard_map/ppermute | solution.py:1012
  277.4 3.9 shard_map.162
  282.9 1.6 collective-permute-start.26
  285.5 7.2 %shard_map.163.refs_4_.refs_0_.refs_1_ = bf16[512,3072]{1,0:T(8,128)(2,1)S(1)} custom-call(bf16[2,4,128,1536]{3,2,1,0:T(8,128)(2,1)} %get-tuple-element.351.refs_0_.refs_2_, bf16[2,4,128,1536]{3,2,1,0:T(8,128)(2,1)} %collective-permute-done.9.refs_10_.refs_1_.refs_3_, bf16[4,128,3072]{2,1,0:T(8,128)(2,1)} %get-tuple-element.423.refs_2_, ...), custom_call_target="tpu_custom_call" | custom-call | tf_op jit(solution)/shard_map/pallas_call | solution.py:588
  292.7 3.4 shard_map.164.refs_4_.refs_1_.refs_2_
  296.1 3.5 shard_map.165
  299.9 18.0 %collective-permute-start.27 = (bf16[128,4224]{1,0:T(8,128)(2,1)S(1)}, bf16[128,4224]{1,0:T(8,128)(2,1)S(1)}, u32[]{:S(2)}, u32[]{:S(2)}) collective-permute-start(bf16[128,4224]{1,0:T(8,128)(2,1)S(1)} %get-tuple-element.432.refs_8_), channel_id=1, source_target_pairs={{0,2},{1,3},{8,10},{9,11},{16,18},{17,19},{24,26},{25,27}} | collective-permute-start | bytes 3244040 | tf_op jit(solution)/shard_map/ppermute | solution.py:1012
  320.7 24.3 %collective-permute-done.30.refs_10_.refs_3_ = bf16[128,4096]{1,0:T(8,128)(2,1)S(1)} collective-permute-done((bf16[128,4096]{1,0:T(8,128)(2,1)S(1)}, bf16[128,4096]{1,0:T(8,128)(2,1)S(1)}, u32[]{:S(2)}, u32[]{:S(2)}) %collective-permute-start.30) | collective-permute-done | bytes 1048608 | tf_op jit(solution)/shard_map/ppermute | solution.py:1012
  346.0 3.2 collective-permute-start.31
  350.0 4.1 shard_map.168
  354.2 38.1 %collective-permute-done.31.refs_4_ = bf16[128,8320]{1,0:T(8,128)(2,1)S(1)} collective-permute-done((bf16[128,8320]{1,0:T(8,128)(2,1)S(1)}, bf16[128,8320]{1,0:T(8,128)(2,1)S(1)}, u32[]{:S(2)}, u32[]{:S(2)}) %collective-permute-start.31) | collective-permute-done | bytes 2129952 | tf_op jit(solution)/shard_map/ppermute | solution.py:1012
  393.3 6.4 %collective-permute-start.33 = (bf16[128,8320]{1,0:T(8,128)(2,1)S(1)}, bf16[128,8320]{1,0:T(8,128)(2,1)S(1)}, u32[]{:S(2)}, u32[]{:S(2)}) collective-permute-start(bf16[128,8320]{1,0:T(8,128)(2,1)S(1)} %get-tuple-element.438.refs_6_), channel_id=1, source_target_pairs={{0,2},{1,3},{2,4},{3,5},{4,6},{5,7},{8,10},{9,11},{10,12},{11,13},... | collective-permute-start | bytes 6389768 | tf_op jit(solution)/shard_map/ppermute | solution.py:1012
  401.0 40.8 %collective-permute-done.33.refs_4_ = bf16[128,8320]{1,0:T(8,128)(2,1)S(1)} collective-permute-done((bf16[128,8320]{1,0:T(8,128)(2,1)S(1)}, bf16[128,8320]{1,0:T(8,128)(2,1)S(1)}, u32[]{:S(2)}, u32[]{:S(2)}) %collective-permute-start.33) | collective-permute-done | bytes 2129952 | tf_op jit(solution)/shard_map/ppermute | solution.py:1012
  441.8 4.2 collective-permute-done.34.refs_5_
  446.1 3.0 shard_map.170
  (83 shorter events, 24.5 us)
Async XLA Ops:
  14.7 11.5 %collective-permute-start = (bf16[128,1024]{1,0:T(8,128)(2,1)S(1)}, bf16[128,1024]{1,0:T(8,128)(2,1)S(1)}, u32[]{:S(2)}, u32[]{:S(2)}) collective-permute-start(bf16[128,1024]{1,0:T(8,128)(2,1)S(1)} %get-tuple-element.236), channel_id=1, source_target_pairs={{0,8},{1,9},{2,10},{3,11},{4,12},{5,13},{6,14},{7,15}} | collective-permute-start | bytes 786440 | tf_op jit(solution)/shard_map/ppermute | solution.py:1213
  35.7 9.0 %collective-permute-start.1 = (bf16[128,1024]{1,0:T(8,128)(2,1)S(1)}, bf16[128,1024]{1,0:T(8,128)(2,1)S(1)}, u32[]{:S(2)}, u32[]{:S(2)}) collective-permute-start(bf16[128,1024]{1,0:T(8,128)(2,1)S(1)} %get-tuple-element.250), channel_id=1, source_target_pairs={{0,8},{8,16},{1,9},{9,17},{2,10},{10,18},{3,11},{11,19},{4,12},{12... | collective-permute-start | bytes 786440 | tf_op jit(solution)/shard_map/ppermute | solution.py:1213
  53.6 8.1 %collective-permute-start.2 = (bf16[128,1024]{1,0:T(8,128)(2,1)S(1)}, bf16[128,1024]{1,0:T(8,128)(2,1)S(1)}, u32[]{:S(2)}, u32[]{:S(2)}) collective-permute-start(bf16[128,1024]{1,0:T(8,128)(2,1)S(1)} %get-tuple-element.264), channel_id=1, source_target_pairs={{0,8},{8,16},{16,24},{1,9},{9,17},{17,25},{2,10},{10,18},{18,26},{... | collective-permute-start | bytes 786440 | tf_op jit(solution)/shard_map/ppermute | solution.py:1213
  71.0 7.3 %collective-permute-start.3 = (bf16[128,1024]{1,0:T(8,128)(2,1)S(1)}, bf16[128,1024]{1,0:T(8,128)(2,1)S(1)}, u32[]{:S(2)}, u32[]{:S(2)}) collective-permute-start(bf16[128,1024]{1,0:T(8,128)(2,1)S(1)} %get-tuple-element.278), channel_id=1, source_target_pairs={{0,8},{8,16},{16,24},{1,9},{9,17},{17,25},{2,10},{10,18},{18,26},{... | collective-permute-start | bytes 786440 | tf_op jit(solution)/shard_map/ppermute | solution.py:1213
  74.7 14.2 %collective-permute-start.5 = (bf16[128,1024]{1,0:T(8,128)(2,1)S(1)}, bf16[128,1024]{1,0:T(8,128)(2,1)S(1)}, u32[]{:S(2)}, u32[]{:S(2)}) collective-permute-start(bf16[128,1024]{1,0:T(8,128)(2,1)S(1)} %get-tuple-element.298), channel_id=1, source_target_pairs={{24,16},{25,17},{26,18},{27,19},{28,20},{29,21},{30,22},{31,23}} | collective-permute-start | bytes 786440 | tf_op jit(solution)/shard_map/ppermute | solution.py:1233
  88.2 1.6 collective-permute-start.4
  89.0 15.5 %collective-permute-start.7 = (bf16[128,1024]{1,0:T(8,128)(2,1)S(1)}, bf16[128,1024]{1,0:T(8,128)(2,1)S(1)}, u32[]{:S(2)}, u32[]{:S(2)}) collective-permute-start(bf16[128,1024]{1,0:T(8,128)(2,1)S(1)} %get-tuple-element.324), channel_id=1, source_target_pairs={{16,8},{24,16},{17,9},{25,17},{18,10},{26,18},{19,11},{27,19},{20,... | collective-permute-start | bytes 786440 | tf_op jit(solution)/shard_map/ppermute | solution.py:1233
  103.8 0.9 collective-permute-start.6
  111.1 49.0 %collective-permute-start.9 = (bf16[2,4,128,1536]{3,2,1,0:T(8,128)(2,1)}, bf16[2,4,128,1536]{3,2,1,0:T(8,128)(2,1)}, u32[]{:S(2)}, u32[]{:S(2)}) collective-permute-start(bf16[2,4,128,1536]{3,2,1,0:T(8,128)(2,1)} %get-tuple-element.351.refs_0_.refs_2_), channel_id=1, source_target_pairs={{0,1},{1,0},{2,3},{3,2},{4,5},{5,4},{6,7},{7,6},{8,9},{9,8},{10,11... | collective-permute-start | bytes 9437192 | tf_op jit(solution)/shard_map/ppermute | solution.py:1054
  111.2 26.0 %collective-permute-start.10 = (bf16[128,1024]{1,0:T(8,128)(2,1)S(1)}, bf16[128,1024]{1,0:T(8,128)(2,1)S(1)}, u32[]{:S(2)}, u32[]{:S(2)}) collective-permute-start(bf16[128,1024]{1,0:T(8,128)(2,1)S(1)} %get-tuple-element.352), channel_id=1, source_target_pairs={{8,0},{16,8},{24,16},{9,1},{17,9},{25,17},{10,2},{18,10},{26,18},{... | collective-permute-start | bytes 786440 | tf_op jit(solution)/shard_map/ppermute | solution.py:1233
  145.7 14.4 %collective-permute-start.11 = (bf16[128,1024]{1,0:T(8,128)(2,1)S(1)}, bf16[128,1024]{1,0:T(8,128)(2,1)S(1)}, u32[]{:S(2)}, u32[]{:S(2)}) collective-permute-start(bf16[128,1024]{1,0:T(8,128)(2,1)S(1)} %get-tuple-element.365), channel_id=1, source_target_pairs={{8,0},{16,8},{24,16},{9,1},{17,9},{25,17},{10,2},{18,10},{26,18},{... | collective-permute-start | bytes 786440 | tf_op jit(solution)/shard_map/ppermute | solution.py:1233
  147.0 26.3 %collective-permute-start.8 = (bf16[4,128,1024]{2,1,0:T(8,128)(2,1)}, bf16[4,128,1024]{2,1,0:T(8,128)(2,1)}, u32[]{:S(2)}, u32[]{:S(2)}) collective-permute-start(bf16[4,128,1024]{2,1,0:T(8,128)(2,1)} %get-tuple-element.350), channel_id=1, source_target_pairs={{0,2},{1,3},{6,4},{7,5},{8,10},{9,11},{14,12},{15,13},{16,18},{17,... | collective-permute-start | bytes 3145736 | tf_op jit(solution)/shard_map/ppermute | solution.py:1065
  168.8 10.0 %collective-permute-start.12 = (bf16[128,1024]{1,0:T(8,128)(2,1)S(1)}, bf16[128,1024]{1,0:T(8,128)(2,1)S(1)}, u32[]{:S(2)}, u32[]{:S(2)}) collective-permute-start(bf16[128,1024]{1,0:T(8,128)(2,1)S(1)} %get-tuple-element.380), channel_id=1, source_target_pairs={{8,0},{16,8},{9,1},{17,9},{10,2},{18,10},{11,3},{19,11},{12,4},{20... | collective-permute-start | bytes 786440 | tf_op jit(solution)/shard_map/ppermute | solution.py:1233
  187.3 27.8 %collective-permute-start.13 = (bf16[3,128,4096]{2,1,0:T(8,128)(2,1)}, bf16[3,128,4096]{2,1,0:T(8,128)(2,1)}, u32[]{:S(2)}, u32[]{:S(2)}) collective-permute-start(bf16[3,128,4096]{2,1,0:T(8,128)(2,1)} %get-tuple-element.394.refs_4_), channel_id=1, source_target_pairs={{0,1},{1,0},{2,3},{3,2},{4,5},{5,4},{6,7},{7,6},{8,9},{9,8},{10,11... | collective-permute-start | bytes 9437192 | tf_op jit(solution)/shard_map/ppermute | solution.py:1054
  187.4 15.6 %collective-permute-start.15 = (bf16[2,128,1024]{2,1,0:T(8,128)(2,1)}, bf16[2,128,1024]{2,1,0:T(8,128)(2,1)S(1)}, u32[]{:S(2)}, u32[]{:S(2)}) collective-permute-start(bf16[2,128,1024]{2,1,0:T(8,128)(2,1)} %get-tuple-element.396.refs_0_), channel_id=1, source_target_pairs={{0,2},{1,3},{6,4},{7,5},{8,10},{9,11},{14,12},{15,13},{16,18},{17,... | collective-permute-start | bytes 1572872 | tf_op jit(solution)/shard_map/ppermute | solution.py:1065
  190.9 12.1 %collective-permute-start.14 = (bf16[128,1024]{1,0:T(8,128)(2,1)S(1)}, bf16[128,1024]{1,0:T(8,128)(2,1)S(1)}, u32[]{:S(2)}, u32[]{:S(2)}) collective-permute-start(bf16[128,1024]{1,0:T(8,128)(2,1)S(1)} %get-tuple-element.395), channel_id=1, source_target_pairs={{8,0},{9,1},{10,2},{11,3},{12,4},{13,5},{14,6},{15,7}} | collective-permute-start | bytes 786440 | tf_op jit(solution)/shard_map/ppermute | solution.py:1233
  203.0 0.8 copy-start.7
  203.8 5.6 %copy-start.9 = (bf16[1,128,1024]{2,1,0:T(8,128)(2,1)S(1)}, bf16[1,128,1024]{2,1,0:T(8,128)(2,1)}, u32[]{:S(2)}) copy-start(bf16[1,128,1024]{2,1,0:T(8,128)(2,1)} %get-tuple-element.418.refs_1_) | copy-start | bytes 786436
  203.8 11.3 %copy-start.2 = (bf16[512,1024]{1,0:T(8,128)(2,1)S(1)}, bf16[512,1024]{1,0:T(8,128)(2,1)}, u32[]{:S(2)}) copy-start(bf16[512,1024]{1,0:T(8,128)(2,1)} %param.10) | copy-start | bytes 3145732
  209.4 16.3 %collective-permute-start.16 = (bf16[1,128,4096]{2,1,0:T(8,128)(2,1)}, bf16[1,128,4096]{2,1,0:T(8,128)(2,1)S(1)}, u32[]{:S(2)}, u32[]{:S(2)}) collective-permute-start(bf16[1,128,4096]{2,1,0:T(8,128)(2,1)} %get-tuple-element.417.refs_6_), channel_id=1, source_target_pairs={{0,1},{1,0},{2,3},{3,2},{4,5},{5,4},{6,7},{7,6},{8,9},{9,8},{10,11... | collective-permute-start | bytes 3145736 | tf_op jit(solution)/shard_map/ppermute | solution.py:1054
  209.5 11.6 %collective-permute-start.17 = (bf16[1,128,1024]{2,1,0:T(8,128)(2,1)S(1)}, bf16[1,128,1024]{2,1,0:T(8,128)(2,1)S(1)}, u32[]{:S(2)}, u32[]{:S(2)}) collective-permute-start(bf16[1,128,1024]{2,1,0:T(8,128)(2,1)S(1)} %copy-done.9), channel_id=1, source_target_pairs={{0,2},{1,3},{6,4},{7,5},{8,10},{9,11},{14,12},{15,13},{16,18},{17,... | collective-permute-start | bytes 786440 | tf_op jit(solution)/shard_map/ppermute | solution.py:1065
  213.8 11.9 %collective-permute-start.18 = (bf16[1,128,1024]{2,1,0:T(8,128)(2,1)}, bf16[1,128,1024]{2,1,0:T(8,128)(2,1)S(1)}, u32[]{:S(2)}, u32[]{:S(2)}) collective-permute-start(bf16[1,128,1024]{2,1,0:T(8,128)(2,1)} %get-tuple-element.419.refs_2_), channel_id=1, source_target_pairs={{0,2},{1,3},{6,4},{7,5},{8,10},{9,11},{14,12},{15,13},{16,18},{17,... | collective-permute-start | bytes 786440 | tf_op jit(solution)/shard_map/ppermute | solution.py:1065
  215.1 10.6 %copy-start.8 = (bf16[2,128,1024]{2,1,0:T(8,128)(2,1)S(1)}, bf16[2,128,1024]{2,1,0:T(8,128)(2,1)}, u32[]{:S(2)}) copy-start(bf16[2,128,1024]{2,1,0:T(8,128)(2,1)} %copy-done.7) | copy-start | bytes 1572868
  225.7 5.3 %copy-start.11 = (s32[4]{0:T(128)S(1)}, s32[4]{0:T(128)}, u32[]{:S(2)}) copy-start(s32[4]{0:T(128)} %refs_1_.1) | copy-start | bytes 52
  225.7 5.4 %copy-start.10 = (f32[4,4,1024]{2,1,0:T(4,128)S(1)}, f32[4,4,1024]{2,1,0:T(4,128)}, u32[]{:S(2)}) copy-start(f32[4,4,1024]{2,1,0:T(4,128)} %get-tuple-element.428) | copy-start | bytes 196612
  228.5 2.0 copy-start.3
  230.5 46.9 %collective-permute-start.20 = (bf16[512,4096]{1,0:T(8,128)(2,1)}, bf16[512,4096]{1,0:T(8,128)(2,1)}, u32[]{:S(2)}, u32[]{:S(2)}) collective-permute-start(bf16[512,4096]{1,0:T(8,128)(2,1)} %get-tuple-element.424), channel_id=1, source_target_pairs={{0,1},{1,0},{2,3},{3,2},{4,5},{5,4},{6,7},{7,6},{8,9},{9,8},{10,11... | collective-permute-start | bytes 12582920 | tf_op jit(solution)/shard_map/ppermute | solution.py:1054
  230.5 54.1 %collective-permute-start.19 = (bf16[4,128,3072]{2,1,0:T(8,128)(2,1)}, bf16[4,128,3072]{2,1,0:T(8,128)(2,1)}, u32[]{:S(2)}, u32[]{:S(2)}) collective-permute-start(bf16[4,128,3072]{2,1,0:T(8,128)(2,1)} %get-tuple-element.423.refs_2_), channel_id=1, source_target_pairs={{0,1},{1,0},{2,3},{3,2},{4,5},{5,4},{6,7},{7,6},{8,9},{9,8},{10,11... | collective-permute-start | bytes 9437192 | tf_op jit(solution)/shard_map/ppermute | solution.py:1054
  231.3 51.6 %collective-permute-start.22 = (f32[32,1024]{1,0:T(8,128)S(1)}, f32[32,1024]{1,0:T(8,128)S(1)}, u32[]{:S(2)}, u32[]{:S(2)}) collective-permute-start(f32[32,1024]{1,0:T(8,128)S(1)} %reshape.56), channel_id=1, source_target_pairs={{0,1},{1,0},{2,3},{3,2},{4,5},{5,4},{6,7},{7,6},{8,9},{9,8},{10,11... | collective-permute-start | bytes 393224 | tf_op jit(solution)/shard_map/ppermute | solution.py:1054
  231.4 61.3 %collective-permute-start.21 = (bf16[4,128,1024]{2,1,0:T(8,128)(2,1)}, bf16[4,128,1024]{2,1,0:T(8,128)(2,1)}, u32[]{:S(2)}, u32[]{:S(2)}) collective-permute-start(bf16[4,128,1024]{2,1,0:T(8,128)(2,1)} %get-tuple-element.427.refs_2_), channel_id=1, source_target_pairs={{0,1},{1,0},{2,3},{3,2},{4,5},{5,4},{6,7},{7,6},{8,9},{9,8},{10,11... | collective-permute-start | bytes 3145736 | tf_op jit(solution)/shard_map/ppermute | solution.py:1054
  231.9 2.2 copy-start.4
  244.6 2.6 copy-start
  244.6 32.8 %copy-start.5 = (bf16[512,4096]{1,0:T(8,128)(2,1)S(1)}, bf16[512,4096]{1,0:T(8,128)(2,1)}, u32[]{:S(2)}) copy-start(bf16[512,4096]{1,0:T(8,128)(2,1)} %copy-done.3) | copy-start | bytes 12582916
  247.2 52.5 %collective-permute-start.23 = (bf16[128,4096]{1,0:T(8,128)(2,1)S(1)}, bf16[128,4096]{1,0:T(8,128)(2,1)S(1)}, u32[]{:S(2)}, u32[]{:S(2)}) collective-permute-start(bf16[128,4096]{1,0:T(8,128)(2,1)S(1)} %get-tuple-element.425.refs_2_), channel_id=1, source_target_pairs={{0,2},{1,3},{8,10},{9,11},{16,18},{17,19},{24,26},{25,27}} | collective-permute-start | bytes 3145736 | tf_op jit(solution)/shard_map/ppermute | solution.py:1012
  281.3 14.8 %collective-permute-start.25 = (bf16[128,4096]{1,0:T(8,128)(2,1)}, bf16[128,4096]{1,0:T(8,128)(2,1)}, u32[]{:S(2)}, u32[]{:S(2)}) collective-permute-start(bf16[128,4096]{1,0:T(8,128)(2,1)} %get-tuple-element.426.refs_4_), channel_id=1, source_target_pairs={{2,4},{3,5},{10,12},{11,13},{18,20},{19,21},{26,28},{27,29}} | collective-permute-start | bytes 3145736 | tf_op jit(solution)/shard_map/ppermute | solution.py:1012
  282.9 13.2 %collective-permute-start.26 = (bf16[128,4096]{1,0:T(8,128)(2,1)}, bf16[128,4096]{1,0:T(8,128)(2,1)}, u32[]{:S(2)}, u32[]{:S(2)}) collective-permute-start(bf16[128,4096]{1,0:T(8,128)(2,1)} %get-tuple-element.430), channel_id=1, source_target_pairs={{4,2},{5,3},{12,10},{13,11},{20,18},{21,19},{28,26},{29,27}} | collective-permute-start | bytes 3145736 | tf_op jit(solution)/shard_map/ppermute | solution.py:1012
  284.6 15.2 %collective-permute-start.24 = (bf16[128,4096]{1,0:T(8,128)(2,1)}, bf16[128,4096]{1,0:T(8,128)(2,1)S(1)}, u32[]{:S(2)}, u32[]{:S(2)}) collective-permute-start(bf16[128,4096]{1,0:T(8,128)(2,1)} %get-tuple-element.429), channel_id=1, source_target_pairs={{6,4},{7,5},{14,12},{15,13},{22,20},{23,21},{30,28},{31,29}} | collective-permute-start | bytes 3145736 | tf_op jit(solution)/shard_map/ppermute | solution.py:1012
  292.7 3.4 copy-start.6
  299.7 45.3 %copy-start.1 = (bf16[512,4096]{1,0:T(8,128)(2,1)S(1)}, bf16[512,4096]{1,0:T(8,128)(2,1)}, u32[]{:S(2)}) copy-start(bf16[512,4096]{1,0:T(8,128)(2,1)} %copy-done) | copy-start | bytes 12582916
  299.9 45.1 %collective-permute-start.27 = (bf16[128,4224]{1,0:T(8,128)(2,1)S(1)}, bf16[128,4224]{1,0:T(8,128)(2,1)S(1)}, u32[]{:S(2)}, u32[]{:S(2)}) collective-permute-start(bf16[128,4224]{1,0:T(8,128)(2,1)S(1)} %get-tuple-element.432.refs_8_), channel_id=1, source_target_pairs={{0,2},{1,3},{8,10},{9,11},{16,18},{17,19},{24,26},{25,27}} | collective-permute-start | bytes 3244040 | tf_op jit(solution)/shard_map/ppermute | solution.py:1012
  317.9 27.1 %collective-permute-start.28 = (bf16[128,4224]{1,0:T(8,128)(2,1)S(1)}, bf16[128,4224]{1,0:T(8,128)(2,1)S(1)}, u32[]{:S(2)}, u32[]{:S(2)}) collective-permute-start(bf16[128,4224]{1,0:T(8,128)(2,1)S(1)} %get-tuple-element.433), channel_id=1, source_target_pairs={{6,4},{7,5},{14,12},{15,13},{22,20},{23,21},{30,28},{31,29}} | collective-permute-start | bytes 3244040 | tf_op jit(solution)/shard_map/ppermute | solution.py:1012
  318.7 2.0 collective-permute-start.29
  319.4 25.6 %collective-permute-start.30 = (bf16[128,4096]{1,0:T(8,128)(2,1)S(1)}, bf16[128,4096]{1,0:T(8,128)(2,1)S(1)}, u32[]{:S(2)}, u32[]{:S(2)}) collective-permute-start(bf16[128,4096]{1,0:T(8,128)(2,1)S(1)} %get-tuple-element.434), channel_id=1, source_target_pairs={{2,0},{3,1},{4,2},{5,3},{10,8},{11,9},{12,10},{13,11},{18,16},{19,... | collective-permute-start | bytes 3145736 | tf_op jit(solution)/shard_map/ppermute | solution.py:1012
  346.0 46.2 %collective-permute-start.31 = (bf16[128,8320]{1,0:T(8,128)(2,1)S(1)}, bf16[128,8320]{1,0:T(8,128)(2,1)S(1)}, u32[]{:S(2)}, u32[]{:S(2)}) collective-permute-start(bf16[128,8320]{1,0:T(8,128)(2,1)S(1)} %get-tuple-element.435.refs_4_), channel_id=1, source_target_pairs={{0,2},{1,3},{2,4},{3,5},{8,10},{9,11},{10,12},{11,13},{16,18},{17,... | collective-permute-start | bytes 6389768 | tf_op jit(solution)/shard_map/ppermute | solution.py:1012
  349.2 43.0 %collective-permute-start.32 = (bf16[128,8320]{1,0:T(8,128)(2,1)S(1)}, bf16[128,8320]{1,0:T(8,128)(2,1)S(1)}, u32[]{:S(2)}, u32[]{:S(2)}) collective-permute-start(bf16[128,8320]{1,0:T(8,128)(2,1)S(1)} %get-tuple-element.436), channel_id=1, source_target_pairs={{4,2},{5,3},{6,4},{7,5},{12,10},{13,11},{14,12},{15,13},{20,18},{2... | collective-permute-start | bytes 6389768 | tf_op jit(solution)/shard_map/ppermute | solution.py:1012
  393.3 48.5 %collective-permute-start.33 = (bf16[128,8320]{1,0:T(8,128)(2,1)S(1)}, bf16[128,8320]{1,0:T(8,128)(2,1)S(1)}, u32[]{:S(2)}, u32[]{:S(2)}) collective-permute-start(bf16[128,8320]{1,0:T(8,128)(2,1)S(1)} %get-tuple-element.438.refs_6_), channel_id=1, source_target_pairs={{0,2},{1,3},{2,4},{3,5},{4,6},{5,7},{8,10},{9,11},{10,12},{11,13},... | collective-permute-start | bytes 6389768 | tf_op jit(solution)/shard_map/ppermute | solution.py:1012
  399.7 46.3 %collective-permute-start.34 = (bf16[128,8320]{1,0:T(8,128)(2,1)S(1)}, bf16[128,8320]{1,0:T(8,128)(2,1)S(1)}, u32[]{:S(2)}, u32[]{:S(2)}) collective-permute-start(bf16[128,8320]{1,0:T(8,128)(2,1)S(1)} %get-tuple-element.439), channel_id=1, source_target_pairs={{2,0},{3,1},{4,2},{5,3},{6,4},{7,5},{10,8},{11,9},{12,10},{13,11},... | collective-permute-start | bytes 6389768 | tf_op jit(solution)/shard_map/ppermute | solution.py:1012

commit v5 on v4

--- a/solution.py
+++ b/solution.py
@@ -52,7 +52,6 @@
 class Back(NamedTuple):
     grad_in: Any
     y_early: Any
-    y_late: Any
     y_last: Any
     up_early: Any
     up_last: Any
@@ -163,6 +162,56 @@
         strip(i).wait()
 
 
+def redo_activated(normed_in, weight, act_out, normed, act_slots, sems, base):
+    micros, frames, _ = normed.shape
+    step = act_slots.shape[3]
+    load = pltpu.make_async_copy(normed_in, normed, sems.at[base])
+    load.start()
+    load.wait()
+    copies = []
+    for j in range(0, weight.shape[1], step):
+        slot = (j // step) % 2
+        if len(copies) >= 2:
+            copies[-2].wait()
+        rows = normed[...].reshape(micros * frames, -1)
+        act = gelu_and_slope(product(rows, weight[:, j : j + step]))[0].astype(BF16)
+        act_slots[slot] = act.reshape(micros, frames, step)
+        target = act_out.at[:, :, pl.ds(j, step)]
+        copies.append(pltpu.make_async_copy(act_slots.at[slot], target, sems.at[base + slot]))
+        copies[-1].start()
+    for copy in copies[-2:]:
+        copy.wait()
+
+
+def copy_kernel(source, target, held, sem):
+    @pl.when(lax.axis_index("section") == 0)
+    def copy():
+        for start, end in ((source, held), (held, target)):
+            moving = pltpu.make_async_copy(start, end, sem)
+            moving.start()
+            moving.wait()
+
+
+def first_sections(x):
+    call = Call()
+    call.take([x], anywhere, pltpu.HBM)
+    call.give(like([x]), anywhere, pltpu.HBM)
+    return call.run(copy_kernel, [pltpu.VMEM(x.shape, x.dtype), pltpu.SemaphoreType.DMA], 0)[0]
+
+
+def redo_scratch(plan):
+    lead = (plan.micros, plan.frames)
+    return [
+        pltpu.VMEM(lead + (plan.features,), BF16),
+        pltpu.VMEM((2,) + lead + (2 * BLOCK,), BF16),
+    ]
+
+
+def beside_an_end():
+    chip = lax.axis_index("batch") // CORES
+    return (chip == 1) | (chip == lax.axis_size("batch") // CORES - 2)
+
+
 class Plan(NamedTuple):
     sections: int
     micros: int
@@ -177,22 +226,17 @@
     def ticks(self):
         return self.micros + 2 * (self.sections - 1)
 
-    def y_spans(self):
-        half = self.micros // 2
-        return (0, half), (half, self.micros - 1), (self.micros - 1, self.micros)
-
     def up_spans(self):
         return (0, self.micros - 1), (self.micros - 1, self.micros)
 
     def bwd_reaches(self, tick):
         low, high = tick - 2 * (self.sections - 1), tick - (self.sections - 1)
-        grad_y = tuple(low < end and high >= first for first, end in self.y_spans())
-        grad_up = tuple(low < end and high >= first for first, end in self.up_spans())
-        return (True,) + grad_y + grad_up + (True,) * 3
+        spread = tuple(low < end and high >= first for first, end in self.up_spans())
+        return (True,) + spread + spread + (True,) * 3
 
     def bwd_uses(self, tick, part):
-        first = (False,) + (True,) * 6 + (False, False)
-        halves = {WHOLE: (True,) * 9, FIRST: first, SECOND: tuple(not f for f in first)}
+        first = (False,) + (True,) * 5 + (False, False)
+        halves = {WHOLE: (True,) * 8, FIRST: first, SECOND: tuple(not f for f in first)}
         return tuple(r and h for r, h in zip(self.bwd_reaches(tick), halves[part]))
 
     def fwd_id(self, tick, section):
@@ -202,7 +246,7 @@
         return tick - 2 * (self.sections - 1) + section
 
 
-def forward_kernel(plan, tick, has_incoming, loads_weights, *refs):
+def forward_kernel(plan, tick, has_incoming, loads_weights, redoes, *refs):
     refs = list(refs)
     take = lambda n: [refs.pop(0) for _ in range(n)]
     if loads_weights:
@@ -214,6 +258,8 @@
         take(4)
     incoming = take(1)[0] if has_incoming else None
     (frames_in,) = take(1)
+    if redoes:
+        (second_in,) = take(1)
     if loads_weights:
         info, table = take(2)
         weight = Weights(*take(4))
@@ -223,6 +269,9 @@
     reread = Reread(*take(5))
     kept = Kept(*take(4))
     (outgoing,) = take(1)
+    if redoes:
+        (act_in,) = take(1)
+        redo = (refs.pop(), refs.pop())[::-1]
     entry, packed, probs, hidden, slope, normed, left, attended, act, strips, sems = refs
 
     micros, frames, features, hidden_units, rows_kept = plan[1:]
@@ -354,6 +403,12 @@
         save(outgoing, kept.layer_out.at[slot])
         save.wait()
 
+    if redoes:
+
+        @pl.when((section == 0) & beside_an_end())
+        def redo_early():
+            redo_activated(second_in, weight.up, act_in, *redo, sems, base)
+
     units = []
     for source, target in zip(weight, turned):
         total_rows, total_cols = source.shape
@@ -377,12 +432,14 @@
                 turn(source, target, r, c, features, strips, sems, base)
 
 
-def backward_kernel(plan, tick, part, has_arriving, present, unread, *refs):
+def backward_kernel(plan, tick, part, has_arriving, present, unread, redoes, *refs):
     refs = list(refs)
     take = lambda n: [refs.pop(0) for _ in range(n)]
     info, table = take(2)
     turned = Weights(*(take(1) + [None] * 3 if part == SECOND else take(4)))
     take(unread)
+    if redoes:
+        second_in, up_weight, _ = take(3)
     arriving = take(1)[0] if has_arriving else None
     (cotangent,) = take(1)
     take(len(Reread._fields))
@@ -395,6 +452,9 @@
         halfway = take(3)
     else:
         (returning,) = take(1)
+    if redoes:
+        (act_in,) = take(1)
+        redo = (refs.pop(), refs.pop())[::-1]
     (entry, packed, probs, hidden, slope, grad_y, grad_up, wide, grad_hidden, grad_attn, mixed,
      grad_packed, row_grads, sems) = refs
 
@@ -407,6 +467,13 @@
     active = (micro >= 0) & (micro < micros)
     slot = jnp.clip(micro, 0, micros - 1)
 
+    if redoes:
+        through = micro >= micros if part == WHOLE else micro == micros
+
+        @pl.when(through & beside_an_end())
+        def redo_late():
+            redo_activated(second_in, up_weight, act_in, *redo, sems, 0)
+
     def start_fetches(wanted):
         fetches = []
         for i, target in enumerate((entry, packed, probs, hidden, slope)):
@@ -437,7 +504,7 @@
         else:
             own_cotangent()
 
-        save.spread(grad_y, back[1:4], plan.y_spans(), slot)
+        save.spread(grad_y, back[1:3], plan.up_spans(), slot)
         rows = table_rows(table, code)
         fetches[4].wait()
         for j in range(0, hidden_units, BLOCK):
@@ -542,7 +609,7 @@
     kept = Kept(wide, left, wide, (own + (hidden_units,), BF16))
     back = Back(
         wide,
-        *buffers(plan.y_spans(), features),
+        *buffers(plan.up_spans(), features),
         *buffers(plan.up_spans(), hidden_units),
         grad_attn=wide,
         grad_packed=(own + (3 * features,), BF16),
@@ -621,7 +688,7 @@
     back: Any = None
 
 
-def run_forward(plan, tick, state, incoming, frames_in):
+def run_forward(plan, tick, state, incoming, frames_in, second_in=None):
     reread_shapes, kept_shapes, _ = shapes_of(plan)
     first = state.turned is None
     at_turned = at_kept = None
@@ -639,6 +706,8 @@
     if incoming is not None:
         call.take([incoming], in_vmem, pltpu.VMEM)
     call.take([frames_in], anywhere)
+    if second_in is not None:
+        call.take([second_in], anywhere)
     if first:
         call.give([((2 * plan.micros,), jnp.int32)], in_smem, pltpu.SMEM)
         call.give(like([state.table]), in_vmem, pltpu.VMEM)
@@ -649,6 +718,8 @@
     call.give([(w.shape[::-1], BF16) for w in state.weights], anywhere, pltpu.VMEM, at_turned)
     call.give(reread_shapes + kept_shapes, anywhere, pltpu.HBM, at_kept)
     call.give([((plan.frames, plan.features), BF16)], in_vmem, pltpu.VMEM)
+    if second_in is not None:
+        call.give([kept_shapes.act], anywhere, pltpu.HBM)
     scratch = scratch_of(reread_shapes) + [
         pltpu.VMEM((plan.frames, plan.features), BF16),
         pltpu.VMEM((CORES, plan.frames, 3 * plan.features // CORES), BF16),
@@ -658,16 +729,23 @@
         pltpu.SemaphoreType.DMA((24,)),
     ]
     flops = 8 * plan.frames * sum(w.size for w in state.weights)
-    body = functools.partial(forward_kernel, plan, tick, incoming is not None, first)
+    if second_in is not None:
+        scratch += redo_scratch(plan)
+    body = functools.partial(
+        forward_kernel, plan, tick, incoming is not None, first, second_in is not None
+    )
     got = call.run(body, scratch, flops)
     if first:
         state = state._replace(info=got[0], table=got[1], weights=Weights(*got[2:6]))
         got = got[6:]
     kept = Kept(*got[9:13])
-    return state._replace(turned=Weights(*got[:4]), reread=Reread(*got[4:9]), kept=kept), got[-1]
-
-
-def run_backward(plan, tick, state, arriving, cotangent, after, part=WHOLE, halfway=()):
+    state = state._replace(turned=Weights(*got[:4]), reread=Reread(*got[4:9]), kept=kept)
+    return state, got[13], got[14:]
+
+
+def run_backward(
+    plan, tick, state, arriving, cotangent, after, part=WHOLE, halfway=(), redo=None
+):
     reread_shapes, _, back_shapes = shapes_of(plan)
     call = Call()
     call.take([state.info], in_smem, pltpu.SMEM)
@@ -677,6 +755,12 @@
     call.take(staying, anywhere, pltpu.VMEM)
     call.take(after, anywhere)
     unread = len(staying) + len(after)
+    if redo is not None:
+        second_in, act_in = redo
+        call.take([second_in], anywhere)
+        call.take([state.weights.up], in_vmem, pltpu.VMEM)
+        at_act = len(call.args)
+        call.take([act_in], anywhere, pltpu.HBM)
     if arriving is not None:
         call.take([arriving], in_vmem, pltpu.VMEM)
     call.take([cotangent], anywhere)
@@ -695,6 +779,8 @@
         call.give(results, anywhere, pltpu.HBM)
     else:
         call.give(results, in_vmem, pltpu.VMEM)
+    if redo is not None:
+        call.give(like([act_in]), anywhere, pltpu.HBM, at_act)
     scratch = scratch_of(reread_shapes) + [
         pltpu.VMEM(*narrow),
         pltpu.VMEM((plan.frames, plan.hidden_units), BF16),
@@ -707,13 +793,16 @@
         pltpu.SemaphoreType.DMA((16,)),
     ]
     flops = 8 * plan.frames * sum(w.size for w in state.turned)
+    if redo is not None:
+        scratch += redo_scratch(plan)
     body = functools.partial(
-        backward_kernel, plan, tick, part, arriving is not None, present, unread
+        backward_kernel, plan, tick, part, arriving is not None, present, unread, redo is not None
     )
     got = call.run(body, scratch, flops if part == WHOLE else flops // 2)
+    act_in = got.pop() if redo is not None else None
     got, last = got[: -len(results)], got[-len(results) :]
     back = Back(*updated(state.back, used, got[5:]))
-    return state._replace(reread=Reread(*got[:5]), back=back), last
+    return state._replace(reread=Reread(*got[:5]), back=back), last, act_in
 
 
 def in_hbm(x):
@@ -729,11 +818,8 @@
     right_first: int = 0
 
 
-def weight_grad_kernel(pairs, first_column, rows, step, outputs, remade, *refs):
-    lefts, rights = refs[: len(pairs)], refs[len(pairs) : len(pairs) + len(pairs) - remade]
-    if remade:
-        normed_in, weight_in = refs[2 * len(pairs) - remade : 2 * len(pairs) - remade + 2]
-        normed, weight_slots, refs = refs[-2], refs[-1], refs[:-2]
+def weight_grad_kernel(pairs, first_column, rows, step, outputs, skip_ends, *refs):
+    lefts, rights = refs[: len(pairs)], refs[len(pairs) : 2 * len(pairs)]
     outs = refs[-5 - outputs : -5]
     stage, turned, right_slots, sems, right_sems = refs[-5:]
     frames, width = stage.shape[1:]
@@ -742,29 +828,19 @@
     core = lax.axis_index("batch") % CORES
     chip = lax.axis_index("batch") // CORES
     chips = lax.axis_size("batch") // CORES
-    works = (chip > 0) & (chip < chips - 1) if remade else chip >= 0
+    works = (chip > 0) & (chip < chips - 1) if skip_ends else chip >= 0
     firsts = [sum(p.count for p in pairs[:i]) for i in range(len(pairs))]
     columns = lambda j: pl.ds(pl.multiple_of(j * step, step), step)
 
-    given = list(enumerate(pairs))[: len(rights)]
-    remade_from = sum(p.count for _, p in given)
-
     def right_copies(j, slot):
-        copies = [
+        return [
             pltpu.make_async_copy(
                 rights[i].at[pl.ds(p.right_first, p.count), :, columns(j)],
                 right_slots.at[slot, pl.ds(firsts[i], p.count)],
                 right_sems.at[slot, i],
             )
-            for i, p in given
+            for i, p in enumerate(pairs)
         ]
-        if remade:
-            copies.append(
-                pltpu.make_async_copy(
-                    weight_in.at[:, columns(j)], weight_slots.at[slot], right_sems.at[slot, len(given)]
-                )
-            )
-        return copies
 
     def turn_in(m, at):
         if outputs == 1:
@@ -788,23 +864,14 @@
             copies[i].start()
         for copy in right_copies(0, 0):
             copy.start()
-        if remade:
-            load = pltpu.make_async_copy(normed_in, normed, sems.at[len(pairs)])
-            load.start()
         for i, p in enumerate(pairs):
             copies[i].wait()
             for m in range(firsts[i], firsts[i] + p.count):
                 turn_in(m, m * frames)
-        if remade:
-            load.wait()
 
         def fill(j, slot):
             for copy in right_copies(j, slot):
                 copy.wait()
-            if remade:
-                rows = normed[...].reshape(normed.shape[0] * frames, -1)
-                act = gelu_and_slope(product(rows, weight_slots[slot]))[0].astype(BF16)
-                right_slots[slot, remade_from:] = act.reshape(-1, frames, step)
 
         def add(j, slot):
             right = right_slots[slot].reshape(-1, step)
@@ -846,7 +913,7 @@
                 fill(steps - 1, 0)
                 add(steps - 1, 0)
 
-    if remade:
+    if skip_ends:
 
         @pl.when(jnp.logical_not(works))
         def nothing():
@@ -854,37 +921,28 @@
                 out[...] = jnp.zeros(out.shape, BF16)
 
 
-def weight_grad(
-    pairs, first_column, width, rows, after=(), outputs=1, staying=(), remade=(), sources=()
-):
+def weight_grad(pairs, first_column, width, rows, after=(), outputs=1, skip_ends=False):
     columns = pairs[0].right.shape[2]
     frames = pairs[0].right.shape[1]
     step = min(columns, 2 * BLOCK // outputs)
-    every = [*pairs, *remade]
-    micros = sum(p.count for p in every)
+    micros = sum(p.count for p in pairs)
     call = Call()
-    call.take([p.left for p in every], anywhere)
+    call.take([p.left for p in pairs], anywhere)
     call.take([p.right for p in pairs], anywhere)
-    call.take(sources, anywhere)
     call.take(after, anywhere)
-    call.take(staying, anywhere, pltpu.VMEM)
     call.give([((width // outputs, columns), BF16)] * outputs, in_vmem, pltpu.VMEM)
     scratch = [
         pltpu.VMEM((micros, frames, width), BF16),
         pltpu.VMEM((outputs, width // outputs, micros * frames), BF16),
         pltpu.VMEM((2, micros, frames, step), BF16),
-        pltpu.SemaphoreType.DMA((len(every) + 1,)),
-        pltpu.SemaphoreType.DMA((2, len(pairs) + 1)),
+        pltpu.SemaphoreType.DMA((len(pairs),)),
+        pltpu.SemaphoreType.DMA((2, len(pairs))),
     ]
-    if remade:
-        normed, weight = sources
-        scratch.append(pltpu.VMEM(normed.shape, BF16))
-        scratch.append(pltpu.VMEM((2, weight.shape[0], step), BF16))
-    bare = [p._replace(left=None, right=None) for p in every]
+    bare = [p._replace(left=None, right=None) for p in pairs]
     body = functools.partial(
-        weight_grad_kernel, bare, first_column, rows, step, outputs, len(remade)
+        weight_grad_kernel, bare, first_column, rows, step, outputs, skip_ends
     )
-    return call.run(body, scratch, 0, limit=(24 if remade else 14) * 2**20)
+    return call.run(body, scratch, 0, limit=20 * 2**20)
 
 
 class Part(NamedTuple):
@@ -1056,13 +1114,14 @@
     def both(self, x):
         return [in_hbm(x), self.swap(x)]
 
-    def inward(self, x):
-        if not self.ends_hand_over:
-            return None
+    def inward(self, x, sections=None):
         top = self.batch - CORES
         pairs = [(c, CORES + c) for c in range(CORES)]
         pairs += [(top + c, top - CORES + c) for c in range(CORES)]
-        return lax.ppermute(x, "batch", pairs)
+        if sections is None:
+            return lax.ppermute(x, "batch", pairs)
+        pairs = [(s * self.batch + a, s * self.batch + b) for s in sections for a, b in pairs]
+        return lax.ppermute(x, ("section", "batch"), pairs)
 
     def sources(self, x):
         return [in_hbm(x), self.inward(x)] if self.ends_hand_over else [in_hbm(x)]
@@ -1151,7 +1210,7 @@
             x, "batch", scatter_dimension=dimension, tiled=True
         ).astype(F32)
 
-    grad_y = [back.y_early, back.y_late, back.y_last]
+    grad_y = [back.y_early, back.y_last]
     down = local([jnp.concatenate(grad_y, axis=0)], [kept.act], None)
     grad_up = jnp.concatenate([back.up_early, back.up_last], axis=0)
     return (
@@ -1190,7 +1249,7 @@
     share = features // CORES
 
     def down_pairs(grad_ys, act):
-        firsts = [span[0] for span in plan.y_spans()]
+        firsts = [span[0] for span in plan.up_spans()]
         return [Pair(y, None, act, y.shape[0], 0, at) for y, at in zip(grad_ys, firsts)]
 
     def up_pairs(grad_up, first):
@@ -1205,7 +1264,12 @@
     for tick in range(plan.ticks()):
         sent = returned = None
         if tick < plan.fwd_ticks():
-            state, output = run_forward(plan, tick, state, incoming, frames_all)
+            last_fwd = tick == plan.fwd_ticks() - 1 and exchange.ends_hand_over
+            state, output, act_in = run_forward(
+                plan, tick, state, incoming, frames_all, second_first if last_fwd else None
+            )
+            if tick == micros - 1 and exchange.ends_hand_over:
+                second_first = exchange.inward(first_sections(state.kept.second), [0])
             onward = [
                 (s, s + 1) for s in range(sections - 1) if working(plan.fwd_id(tick, s))
             ]
@@ -1213,16 +1277,21 @@
                 sent = lax.ppermute(output, "section", onward)
         if tick >= sections - 1:
             late = tick == plan.ticks() - 1
-            state, output = run_backward(
-                plan, tick, state, arriving, cot_all, before_bwd[tick], FIRST if late else WHOLE
+            redo = None
+            if tick >= plan.ticks() - 2 and exchange.ends_hand_over:
+                redo = (second_rest, act_in)
+            state, output, redone = run_backward(
+                plan, tick, state, arriving, cot_all, before_bwd[tick], FIRST if late else WHOLE,
+                (), redo,
             )
+            act_in = act_in if redone is None else redone
             if late:
                 after = []
                 if exchange.by_hops:
                     y_last = exchange.sources(state.back.y_last)
                     up_last = exchange.both(state.back.up_last)
-                    after = up_early[1:]
-                state, output = run_backward(
+                    after = up_early[1:] + y_early[1:]
+                state, output, _ = run_backward(
                     plan, tick, state, arriving, cot_all, after, SECOND, output
                 )
             output = output[0]
@@ -1236,27 +1305,25 @@
             if tick == plan.fwd_ticks() - 1:
                 lefts = exchange.both(state.kept.left)
                 before_bwd[tick + 1] += lefts[1:]
-                second = exchange.sources(state.kept.second)
-                before_bwd[tick + 2] += second[1:]
-            if tick == plan.y_spans()[0][1] + 2 * sections - 3:
+                if exchange.ends_hand_over:
+                    (act_in,) = act_in
+                    second_rest = exchange.inward(state.kept.second, range(1, sections))
+            if tick == plan.ticks() - 2:
                 y_early = exchange.sources(state.back.y_early)
-                before_bwd[plan.ticks() - 1] += y_early[1:]
-            if tick == plan.ticks() - 2:
-                y_late = exchange.sources(state.back.y_late)
                 up_early = exchange.both(state.back.up_early)
 
     blocks = norm_table.shape[1] // 4
     codes = codebooks * (section % 2)
     table_grad = table_gradient(state.back.row_grads, codes, blocks).reshape(norm_table.shape[1:])
     if exchange.by_hops:
-        sides = list(zip(y_early, y_late, y_last))
+        sides = list(zip(y_early, y_last))
         pairs = down_pairs(sides[0], in_hbm(state.kept.act))
-        remade, sources = (), ()
         if exchange.ends_hand_over:
-            remade = down_pairs(sides[1], None)
-            sources = (second[1], in_hbm(up_weight[0]))
+            pairs += down_pairs(sides[1], act_in)
         ready = [output, up_last[1], up_early[1]]
-        down = weight_grad(pairs, 0, features, plan.rows, ready, 2, (), remade, sources)
+        down = weight_grad(
+            pairs, 0, features, plan.rows, ready, 2, exchange.ends_hand_over
+        )
         pairs = up_pairs(up_early, 0) + up_pairs(up_last, micros - 1)
         (up,) = weight_grad(pairs, 2 * share, share, plan.rows, down[:1])
         sums = sums_by_hops(plan, exchange, state.back, down, up, lefts, table_grad)

time: 457 us -> 443 us (0.969)
  waiting for transfers between devices: 185 us -> 175 us
  starting transfers between devices: 105 us -> 95.7 us
  Pallas kernels: 151 us -> 157 us
    ppermute x4 -> x2, waiting for transfers between devices: 18.6 us -> 2.92 us  [inward(): return lax.ppermute(x, 'batch', pairs)]
    ppermute x12, starting transfers between devices: 66.6 us -> 56.8 us  [moved(): return lax.ppermute(value, 'batch', pairs)]
    ppermute x6, waiting for transfers between devices: 39 us -> 48.1 us  [per_device(): returned = lax.ppermute(output, 'section', backward)]
    ppermute x0 -> x2, starting transfers between devices: none -> 6.21 us  [inward(): return lax.ppermute(x, ('section', 'batch'), pairs)]
    ppermute x4 -> x2, starting transfers between devices: 13.6 us -> 7.85 us  [inward(): return lax.ppermute(x, 'batch', pairs)]
    pallas_call x27 -> x28, Pallas kernels: 151 us -> 157 us  [run(): pl.pallas_call(body, out_shape=self.out_shape, in_specs=self.in_specs, ou...]
  transfers between devices with their start and end apart: 35 -> 35, of which waited for: 15 -> 13; matrix products, arithmetic and copies ran while one was open for 0% -> 0% of each run, Pallas kernels for 19% -> 21%
where the time goes in v5:
time: 443 us; the launch traced here: 435 us
  waiting for transfers between devices  175 us (40%)
  Pallas kernels  157 us (35%)
  starting transfers between devices  95.7 us (22%)
  local copies, waits for them, and re-layouts  5.47 us (1%)
    pallas_call x28, Pallas kernels, run(): pl.pallas_call(body, out_shape=self.out_shape, in_specs=self.in_specs, ou...  157 us
    ppermute x12, waiting for transfers between devices, moved(): return lax.ppermute(value, 'batch', pairs)  107 us
    ppermute x12, starting transfers between devices, moved(): return lax.ppermute(value, 'batch', pairs)  56.8 us
    ppermute x6, waiting for transfers between devices, per_device(): returned = lax.ppermute(output, 'section', backward)  48.1 us
    ppermute x6, starting transfers between devices, per_device(): sent = lax.ppermute(output, 'section', onward)  17.1 us
    ppermute x6, waiting for transfers between devices, per_device(): sent = lax.ppermute(output, 'section', onward)  16.5 us
  transfers between devices with their start and end apart: 35, of which 13 were waited for; matrix products, arithmetic and copies ran while one was open for 0% of the time, Pallas kernels for 21%

profile of v5, /device:TPU:0, one launch (start us, length us, event | category | flops | bytes accessed | tf_op | source)
XLA Modules:
  0.0 435.0 jit_solution(15374600239531715248)
XLA Ops:
  0.6 14.0 %shard_map.144 = (s32[8]{0:T(128)S(4)}, f32[32,1024]{1,0:T(8,128)S(1)}, bf16[1024,3072]{1,0:T(8,128)(2,1)S(1)}, bf16[1024,1024]{1,0:T(8,128)(2,1)S(1)}, bf16[102...) custom-call(s32[4]{0:T(128)} %refs_0_.1, ...), custom_call_target="tpu_custom_call" | custom-call | flops 12884901888 | tf_op jit(solution)/shard_map/pallas_call | solution.py:655
  14.7 5.2 %collective-permute-start = (bf16[128,1024]{1,0:T(8,128)(2,1)S(1)}, bf16[128,1024]{1,0:T(8,128)(2,1)S(1)}, u32[]{:S(2)}, u32[]{:S(2)}) collective-permute-start(bf16[128,1024]{1,0:T(8,128)(2,1)S(1)} %get-tuple-element.236), channel_id=1, source_target_pairs={{0,8},{1,9},{2,10},{3,11},{4,12},{5,13},{6,14},{7,15}} | collective-permute-start | bytes 786440 | tf_op jit(solution)/shard_map/ppermute | solution.py:1277
  19.9 6.3 %collective-permute-done.refs_10_ = bf16[128,1024]{1,0:T(8,128)(2,1)S(1)} collective-permute-done((bf16[128,1024]{1,0:T(8,128)(2,1)S(1)}, bf16[128,1024]{1,0:T(8,128)(2,1)S(1)}, u32[]{:S(2)}, u32[]{:S(2)}) %collective-permute-start) | collective-permute-done | bytes 262176 | tf_op jit(solution)/shard_map/ppermute | solution.py:1277
  26.2 9.3 %shard_map.145 = (bf16[3072,1024]{1,0:T(8,128)(2,1)S(1)}, bf16[1024,1024]{1,0:T(8,128)(2,1)S(1)}, bf16[4096,1024]{1,0:T(8,128)(2,1)S(1)}, bf16[1024,4096]{1,0:T(...) custom-call(s32[8]{0:T(128)S(4)} %get-tuple-element.226.refs_0_, ...), custom_call_target="tpu_custom_call", output_to_operand_aliasing={{0}: (6, {}), {1}: (7, {}), {2}: (8, {}), {3}: (9, {}), {4}... | custom-call | flops 12884901888 | tf_op jit(solution)/shard_map/pallas_call | solution.py:655
  35.5 3.5 collective-permute-start.1
  39.0 5.5 %collective-permute-done.1.refs_10_ = bf16[128,1024]{1,0:T(8,128)(2,1)S(1)} collective-permute-done((bf16[128,1024]{1,0:T(8,128)(2,1)S(1)}, bf16[128,1024]{1,0:T(8,128)(2,1)S(1)}, u32[]{:S(2)}, u32[]{:S(2)}) %collective-permute-start.1) | collective-permute-done | bytes 262176 | tf_op jit(solution)/shard_map/ppermute | solution.py:1277
  44.6 8.9 %shard_map.146 = (bf16[3072,1024]{1,0:T(8,128)(2,1)S(1)}, bf16[1024,1024]{1,0:T(8,128)(2,1)S(1)}, bf16[4096,1024]{1,0:T(8,128)(2,1)S(1)}, bf16[1024,4096]{1,0:T(...) custom-call(s32[8]{0:T(128)S(4)} %get-tuple-element.226.refs_0_, ...), custom_call_target="tpu_custom_call", output_to_operand_aliasing={{0}: (6, {}), {1}: (7, {}), {2}: (8, {}), {3}: (9, {}), {4}... | custom-call | flops 12884901888 | tf_op jit(solution)/shard_map/pallas_call | solution.py:655
  53.4 3.5 collective-permute-start.2
  56.9 4.6 %collective-permute-done.2.refs_10_ = bf16[128,1024]{1,0:T(8,128)(2,1)S(1)} collective-permute-done((bf16[128,1024]{1,0:T(8,128)(2,1)S(1)}, bf16[128,1024]{1,0:T(8,128)(2,1)S(1)}, u32[]{:S(2)}, u32[]{:S(2)}) %collective-permute-start.2) | collective-permute-done | bytes 262176 | tf_op jit(solution)/shard_map/ppermute | solution.py:1277
  61.6 9.5 %shard_map.147 = (bf16[3072,1024]{1,0:T(8,128)(2,1)S(1)}, bf16[1024,1024]{1,0:T(8,128)(2,1)S(1)}, bf16[4096,1024]{1,0:T(8,128)(2,1)S(1)}, bf16[1024,4096]{1,0:T(...) custom-call(s32[8]{0:T(128)S(4)} %get-tuple-element.226.refs_0_, ...), custom_call_target="tpu_custom_call", output_to_operand_aliasing={{0}: (6, {}), {1}: (7, {}), {2}: (8, {}), {3}: (9, {}), {4}... | custom-call | flops 12884901888 | tf_op jit(solution)/shard_map/pallas_call | solution.py:655
  71.0 3.5 collective-permute-start.3
  74.7 2.2 shard_map.152
  77.6 4.5 %collective-permute-start.7 = (bf16[4,128,1024]{2,1,0:T(8,128)(2,1)}, bf16[4,128,1024]{2,1,0:T(8,128)(2,1)}, u32[]{:S(2)}, u32[]{:S(2)}) collective-permute-start(bf16[4,128,1024]{2,1,0:T(8,128)(2,1)} %shard_map.152), channel_id=1, source_target_pairs={{0,2},{1,3},{6,4},{7,5}} | collective-permute-start | bytes 3145736 | tf_op jit(solution)/shard_map/ppermute | solution.py:1124
  82.1 9.6 %shard_map.149 = (bf16[3072,1024]{1,0:T(8,128)(2,1)S(1)}, bf16[1024,1024]{1,0:T(8,128)(2,1)S(1)}, bf16[4096,1024]{1,0:T(8,128)(2,1)S(1)}, bf16[1024,4096]{1,0:T(...) custom-call(s32[8]{0:T(128)S(4)} %get-tuple-element.226.refs_0_, ...), custom_call_target="tpu_custom_call", output_to_operand_aliasing={{0}: (6, {}), {1}: (7, {}), {2}: (8, {}), {3}: (9, {}), {4}... | custom-call | flops 12884901888 | tf_op jit(solution)/shard_map/pallas_call | solution.py:655
  93.3 14.4 %shard_map.151 = (bf16[3072,1024]{1,0:T(8,128)(2,1)S(1)}, bf16[1024,1024]{1,0:T(8,128)(2,1)S(1)}, bf16[4096,1024]{1,0:T(8,128)(2,1)S(1)}, bf16[1024,4096]{1,0:T(...) custom-call(s32[8]{0:T(128)S(4)} %get-tuple-element.226.refs_0_, ...), custom_call_target="tpu_custom_call", output_to_operand_aliasing={{0}: (6, {}), {1}: (7, {}), {2}: (8, {}), {3}: (9, {}), {4}... | custom-call | flops 12884901888 | tf_op jit(solution)/shard_map/pallas_call | solution.py:655
  108.6 9.3 %shard_map.154 = (bf16[3072,1024]{1,0:T(8,128)(2,1)S(1)}, bf16[1024,1024]{1,0:T(8,128)(2,1)S(1)}, bf16[4096,1024]{1,0:T(8,128)(2,1)S(1)}, bf16[1024,4096]{1,0:T(...) custom-call(s32[8]{0:T(128)S(4)} %get-tuple-element.226.refs_0_, ...), custom_call_target="tpu_custom_call", output_to_operand_aliasing={{0}: (6, {}), {1}: (7, {}), {2}: (8, {}), {3}: (9, {}), {4}... | custom-call | flops 12884901888 | tf_op jit(solution)/shard_map/pallas_call | solution.py:655
  119.3 21.1 %collective-permute-done.11.refs_10_ = bf16[128,1024]{1,0:T(8,128)(2,1)S(1)} collective-permute-done((bf16[128,1024]{1,0:T(8,128)(2,1)S(1)}, bf16[128,1024]{1,0:T(8,128)(2,1)S(1)}, u32[]{:S(2)}, u32[]{:S(2)}) %collective-permute-start.11) | collective-permute-done | bytes 262176 | tf_op jit(solution)/shard_map/ppermute | solution.py:1302
  140.3 8.5 %shard_map.155 = (bf16[4,128,1024]{2,1,0:T(8,128)(2,1)}, bf16[4,128,3072]{2,1,0:T(8,128)(2,1)}, bf16[4,2048,128]{2,1,0:T(8,128)(2,1)}, f32[4,128,1024]{2,1,0:T(8...) custom-call(s32[8]{0:T(128)S(4)} %get-tuple-element.226.refs_0_, ...), custom_call_target="tpu_custom_call", output_to_operand_aliasing={{0}: (12, {}), {1}: (13, {}), {2}: (14, {}), {3}: (15, {}),... | custom-call | flops 12884901888 | tf_op jit(solution)/shard_map/pallas_call | solution.py:655
  150.1 1.7 collective-permute-start.9
  151.8 13.1 %collective-permute-done.12.refs_11_ = bf16[128,1024]{1,0:T(8,128)(2,1)S(1)} collective-permute-done((bf16[128,1024]{1,0:T(8,128)(2,1)S(1)}, bf16[128,1024]{1,0:T(8,128)(2,1)S(1)}, u32[]{:S(2)}, u32[]{:S(2)}) %collective-permute-start.12) | collective-permute-done | bytes 262176 | tf_op jit(solution)/shard_map/ppermute | solution.py:1302
  164.9 8.9 %shard_map.156 = (bf16[4,128,1024]{2,1,0:T(8,128)(2,1)}, bf16[4,128,3072]{2,1,0:T(8,128)(2,1)}, bf16[4,2048,128]{2,1,0:T(8,128)(2,1)}, f32[4,128,1024]{2,1,0:T(8...) custom-call(s32[8]{0:T(128)S(4)} %get-tuple-element.226.refs_0_, ...), custom_call_target="tpu_custom_call", output_to_operand_aliasing={{0}: (13, {}), {1}: (14, {}), {2}: (15, {}), {3}: (16, {}),... | custom-call | flops 12884901888 | tf_op jit(solution)/shard_map/pallas_call | solution.py:655
  175.1 8.7 %collective-permute-done.13.refs_13_ = bf16[128,1024]{1,0:T(8,128)(2,1)S(1)} collective-permute-done((bf16[128,1024]{1,0:T(8,128)(2,1)S(1)}, bf16[128,1024]{1,0:T(8,128)(2,1)S(1)}, u32[]{:S(2)}, u32[]{:S(2)}) %collective-permute-start.13) | collective-permute-done | bytes 262176 | tf_op jit(solution)/shard_map/ppermute | solution.py:1302
  183.9 8.5 %shard_map.157 = (bf16[4,128,1024]{2,1,0:T(8,128)(2,1)}, bf16[4,128,3072]{2,1,0:T(8,128)(2,1)}, bf16[4,2048,128]{2,1,0:T(8,128)(2,1)}, f32[4,128,1024]{2,1,0:T(8...) custom-call(s32[8]{0:T(128)S(4)} %get-tuple-element.226.refs_0_, ...), custom_call_target="tpu_custom_call", output_to_operand_aliasing={{0}: (15, {}), {1}: (16, {}), {2}: (17, {}), {3}: (18, {}),... | custom-call | flops 12884901888 | tf_op jit(solution)/shard_map/pallas_call | solution.py:655
  193.7 4.4 %collective-permute-start.15 = (bf16[3,128,1024]{2,1,0:T(8,128)(2,1)}, bf16[3,128,1024]{2,1,0:T(8,128)(2,1)}, u32[]{:S(2)}, u32[]{:S(2)}) collective-permute-start(bf16[3,128,1024]{2,1,0:T(8,128)(2,1)} %get-tuple-element.394.refs_0_), channel_id=1, source_target_pairs={{0,2},{1,3},{6,4},{7,5},{8,10},{9,11},{14,12},{15,13},{16,18},{17,... | collective-permute-start | bytes 2359304 | tf_op jit(solution)/shard_map/ppermute | solution.py:1122
  198.1 5.2 %collective-permute-done.16.refs_13_.refs_5_ = bf16[128,1024]{1,0:T(8,128)(2,1)S(1)} collective-permute-done((bf16[128,1024]{1,0:T(8,128)(2,1)S(1)}, bf16[128,1024]{1,0:T(8,128)(2,1)S(1)}, u32[]{:S(2)}, u32[]{:S(2)}) %collective-permute-start.16) | collective-permute-done | bytes 262176 | tf_op jit(solution)/shard_map/ppermute | solution.py:1302
  203.3 5.6 %shard_map.158 = (bf16[4,128,1024]{2,1,0:T(8,128)(2,1)}, bf16[4,128,3072]{2,1,0:T(8,128)(2,1)}, bf16[4,2048,128]{2,1,0:T(8,128)(2,1)}, f32[4,128,1024]{2,1,0:T(8...) custom-call(s32[8]{0:T(128)S(4)} %get-tuple-element.226.refs_0_, ...), custom_call_target="tpu_custom_call", output_to_operand_aliasing={{0}: (15, {}), {1}: (16, {}), {2}: (17, {}), {3}: (18, {}),... | custom-call | flops 6442450944 | tf_op jit(solution)/shard_map/pallas_call | solution.py:655
  208.9 3.5 collective-permute-start.18
  212.4 2.9 collective-permute-done.15.refs_4_.refs_2_
  215.4 5.6 %shard_map.159 = (bf16[4,128,1024]{2,1,0:T(8,128)(2,1)}, bf16[4,128,3072]{2,1,0:T(8,128)(2,1)}, bf16[4,2048,128]{2,1,0:T(8,128)(2,1)}, f32[4,128,1024]{2,1,0:T(8...) custom-call(s32[8]{0:T(128)S(4)} %get-tuple-element.226.refs_0_, ...), custom_call_target="tpu_custom_call", output_to_operand_aliasing={{0}: (7, {}), {1}: (8, {}), {2}: (9, {}), {3}: (10, {}), {4... | custom-call | flops 6442450944 | tf_op jit(solution)/shard_map/pallas_call | solution.py:655
  221.1 2.9 shard_map.160
  224.0 2.0 copy-done.3
  227.5 2.2 copy-done.4
  229.6 10.4 %shard_map.161.refs_0_.refs_1_ = bf16[512,4096]{1,0:T(8,128)(2,1)S(1)} custom-call(bf16[2,4,128,1536]{3,2,1,0:T(8,128)(2,1)} %get-tuple-element.352.refs_0_.refs_2_, bf16[2,4,128,1536]{3,2,1,0:T(8,128)(2,1)} %collective-permute-done.10.refs_10_.refs_1_.refs_3_, bf16[2,4,128,1536]{3,2,1,0:T(8,128)(2,1)} %get-tuple-element.352.refs_0_.refs_2_, ...), custom_call_target="tpu_custom_call" | custom-call | tf_op jit(solution)/shard_map/pallas_call | solution.py:655
  242.3 20.9 %collective-permute-start.23 = (bf16[128,4096]{1,0:T(8,128)(2,1)S(1)}, bf16[128,4096]{1,0:T(8,128)(2,1)S(1)}, u32[]{:S(2)}, u32[]{:S(2)}) collective-permute-start(bf16[128,4096]{1,0:T(8,128)(2,1)S(1)} %get-tuple-element.425.refs_2_), channel_id=1, source_target_pairs={{0,2},{1,3},{8,10},{9,11},{16,18},{17,19},{24,26},{25,27}} | collective-permute-start | bytes 3145736 | tf_op jit(solution)/shard_map/ppermute | solution.py:1070
  263.2 3.9 shard_map.163
  267.1 1.6 collective-permute-start.25
  271.3 7.2 %shard_map.164.refs_4_.refs_0_.refs_1_ = bf16[512,3072]{1,0:T(8,128)(2,1)S(1)} custom-call(bf16[2,4,128,1536]{3,2,1,0:T(8,128)(2,1)} %get-tuple-element.352.refs_0_.refs_2_, bf16[2,4,128,1536]{3,2,1,0:T(8,128)(2,1)} %collective-permute-done.10.refs_10_.refs_1_.refs_3_, bf16[4,128,3072]{2,1,0:T(8,128)(2,1)} %get-tuple-element.423.refs_2_, ...), custom_call_target="tpu_custom_call" | custom-call | tf_op jit(solution)/shard_map/pallas_call | solution.py:655
  278.5 3.6 shard_map.165.refs_4_.refs_1_.refs_2_
  282.2 3.5 shard_map.166
  286.0 17.5 %collective-permute-start.27 = (bf16[128,4224]{1,0:T(8,128)(2,1)S(1)}, bf16[128,4224]{1,0:T(8,128)(2,1)S(1)}, u32[]{:S(2)}, u32[]{:S(2)}) collective-permute-start(bf16[128,4224]{1,0:T(8,128)(2,1)S(1)} %get-tuple-element.432.refs_8_), channel_id=1, source_target_pairs={{0,2},{1,3},{8,10},{9,11},{16,18},{17,19},{24,26},{25,27}} | collective-permute-start | bytes 3244040 | tf_op jit(solution)/shard_map/ppermute | solution.py:1070
  306.2 24.3 %collective-permute-done.30.refs_10_.refs_3_ = bf16[128,4096]{1,0:T(8,128)(2,1)S(1)} collective-permute-done((bf16[128,4096]{1,0:T(8,128)(2,1)S(1)}, bf16[128,4096]{1,0:T(8,128)(2,1)S(1)}, u32[]{:S(2)}, u32[]{:S(2)}) %collective-permute-start.30) | collective-permute-done | bytes 1048608 | tf_op jit(solution)/shard_map/ppermute | solution.py:1070
  331.5 3.2 collective-permute-start.31
  335.5 4.1 shard_map.169
  339.7 38.1 %collective-permute-done.31.refs_4_ = bf16[128,8320]{1,0:T(8,128)(2,1)S(1)} collective-permute-done((bf16[128,8320]{1,0:T(8,128)(2,1)S(1)}, bf16[128,8320]{1,0:T(8,128)(2,1)S(1)}, u32[]{:S(2)}, u32[]{:S(2)}) %collective-permute-start.31) | collective-permute-done | bytes 2129952 | tf_op jit(solution)/shard_map/ppermute | solution.py:1070
  378.8 6.4 %collective-permute-start.33 = (bf16[128,8320]{1,0:T(8,128)(2,1)S(1)}, bf16[128,8320]{1,0:T(8,128)(2,1)S(1)}, u32[]{:S(2)}, u32[]{:S(2)}) collective-permute-start(bf16[128,8320]{1,0:T(8,128)(2,1)S(1)} %get-tuple-element.438.refs_6_), channel_id=1, source_target_pairs={{0,2},{1,3},{2,4},{3,5},{4,6},{5,7},{8,10},{9,11},{10,12},{11,13},... | collective-permute-start | bytes 6389768 | tf_op jit(solution)/shard_map/ppermute | solution.py:1070
  386.5 40.8 %collective-permute-done.33.refs_4_ = bf16[128,8320]{1,0:T(8,128)(2,1)S(1)} collective-permute-done((bf16[128,8320]{1,0:T(8,128)(2,1)S(1)}, bf16[128,8320]{1,0:T(8,128)(2,1)S(1)}, u32[]{:S(2)}, u32[]{:S(2)}) %collective-permute-start.33) | collective-permute-done | bytes 2129952 | tf_op jit(solution)/shard_map/ppermute | solution.py:1070
  427.3 4.2 collective-permute-done.34.refs_5_
  431.6 3.0 shard_map.171
  (78 shorter events, 22.0 us)
Async XLA Ops:
  14.7 11.5 %collective-permute-start = (bf16[128,1024]{1,0:T(8,128)(2,1)S(1)}, bf16[128,1024]{1,0:T(8,128)(2,1)S(1)}, u32[]{:S(2)}, u32[]{:S(2)}) collective-permute-start(bf16[128,1024]{1,0:T(8,128)(2,1)S(1)} %get-tuple-element.236), channel_id=1, source_target_pairs={{0,8},{1,9},{2,10},{3,11},{4,12},{5,13},{6,14},{7,15}} | collective-permute-start | bytes 786440 | tf_op jit(solution)/shard_map/ppermute | solution.py:1277
  35.5 9.0 %collective-permute-start.1 = (bf16[128,1024]{1,0:T(8,128)(2,1)S(1)}, bf16[128,1024]{1,0:T(8,128)(2,1)S(1)}, u32[]{:S(2)}, u32[]{:S(2)}) collective-permute-start(bf16[128,1024]{1,0:T(8,128)(2,1)S(1)} %get-tuple-element.250), channel_id=1, source_target_pairs={{0,8},{8,16},{1,9},{9,17},{2,10},{10,18},{3,11},{11,19},{4,12},{12... | collective-permute-start | bytes 786440 | tf_op jit(solution)/shard_map/ppermute | solution.py:1277
  53.4 8.1 %collective-permute-start.2 = (bf16[128,1024]{1,0:T(8,128)(2,1)S(1)}, bf16[128,1024]{1,0:T(8,128)(2,1)S(1)}, u32[]{:S(2)}, u32[]{:S(2)}) collective-permute-start(bf16[128,1024]{1,0:T(8,128)(2,1)S(1)} %get-tuple-element.264), channel_id=1, source_target_pairs={{0,8},{8,16},{16,24},{1,9},{9,17},{17,25},{2,10},{10,18},{18,26},{... | collective-permute-start | bytes 786440 | tf_op jit(solution)/shard_map/ppermute | solution.py:1277
  71.0 11.1 %collective-permute-start.3 = (bf16[128,1024]{1,0:T(8,128)(2,1)S(1)}, bf16[128,1024]{1,0:T(8,128)(2,1)S(1)}, u32[]{:S(2)}, u32[]{:S(2)}) collective-permute-start(bf16[128,1024]{1,0:T(8,128)(2,1)S(1)} %get-tuple-element.278), channel_id=1, source_target_pairs={{0,8},{8,16},{16,24},{1,9},{9,17},{17,25},{2,10},{10,18},{18,26},{... | collective-permute-start | bytes 786440 | tf_op jit(solution)/shard_map/ppermute | solution.py:1277
  76.9 15.5 %collective-permute-start.5 = (bf16[128,1024]{1,0:T(8,128)(2,1)S(1)}, bf16[128,1024]{1,0:T(8,128)(2,1)S(1)}, u32[]{:S(2)}, u32[]{:S(2)}) collective-permute-start(bf16[128,1024]{1,0:T(8,128)(2,1)S(1)} %get-tuple-element.298), channel_id=1, source_target_pairs={{24,16},{25,17},{26,18},{27,19},{28,20},{29,21},{30,22},{31,23}} | collective-permute-start | bytes 786440 | tf_op jit(solution)/shard_map/ppermute | solution.py:1302
  77.6 31.0 %collective-permute-start.7 = (bf16[4,128,1024]{2,1,0:T(8,128)(2,1)}, bf16[4,128,1024]{2,1,0:T(8,128)(2,1)}, u32[]{:S(2)}, u32[]{:S(2)}) collective-permute-start(bf16[4,128,1024]{2,1,0:T(8,128)(2,1)} %shard_map.152), channel_id=1, source_target_pairs={{0,2},{1,3},{6,4},{7,5}} | collective-permute-start | bytes 3145736 | tf_op jit(solution)/shard_map/ppermute | solution.py:1124
  91.7 1.6 collective-permute-start.4
  92.6 15.8 %collective-permute-start.8 = (bf16[128,1024]{1,0:T(8,128)(2,1)S(1)}, bf16[128,1024]{1,0:T(8,128)(2,1)S(1)}, u32[]{:S(2)}, u32[]{:S(2)}) collective-permute-start(bf16[128,1024]{1,0:T(8,128)(2,1)S(1)} %get-tuple-element.324), channel_id=1, source_target_pairs={{16,8},{24,16},{17,9},{25,17},{18,10},{26,18},{19,11},{27,19},{20,... | collective-permute-start | bytes 786440 | tf_op jit(solution)/shard_map/ppermute | solution.py:1302
  107.7 0.9 collective-permute-start.6
  117.9 47.0 %collective-permute-start.10 = (bf16[2,4,128,1536]{3,2,1,0:T(8,128)(2,1)}, bf16[2,4,128,1536]{3,2,1,0:T(8,128)(2,1)}, u32[]{:S(2)}, u32[]{:S(2)}) collective-permute-start(bf16[2,4,128,1536]{3,2,1,0:T(8,128)(2,1)} %get-tuple-element.352.refs_0_.refs_2_), channel_id=1, source_target_pairs={{0,1},{1,0},{2,3},{3,2},{4,5},{5,4},{6,7},{7,6},{8,9},{9,8},{10,11... | collective-permute-start | bytes 9437192 | tf_op jit(solution)/shard_map/ppermute | solution.py:1112
  118.0 22.4 %collective-permute-start.11 = (bf16[128,1024]{1,0:T(8,128)(2,1)S(1)}, bf16[128,1024]{1,0:T(8,128)(2,1)S(1)}, u32[]{:S(2)}, u32[]{:S(2)}) collective-permute-start(bf16[128,1024]{1,0:T(8,128)(2,1)S(1)} %get-tuple-element.353), channel_id=1, source_target_pairs={{8,0},{16,8},{24,16},{9,1},{17,9},{25,17},{10,2},{18,10},{26,18},{... | collective-permute-start | bytes 786440 | tf_op jit(solution)/shard_map/ppermute | solution.py:1302
  148.8 16.1 %collective-permute-start.12 = (bf16[128,1024]{1,0:T(8,128)(2,1)S(1)}, bf16[128,1024]{1,0:T(8,128)(2,1)S(1)}, u32[]{:S(2)}, u32[]{:S(2)}) collective-permute-start(bf16[128,1024]{1,0:T(8,128)(2,1)S(1)} %get-tuple-element.365), channel_id=1, source_target_pairs={{8,0},{16,8},{24,16},{9,1},{17,9},{25,17},{10,2},{18,10},{26,18},{... | collective-permute-start | bytes 786440 | tf_op jit(solution)/shard_map/ppermute | solution.py:1302
  150.1 25.0 %collective-permute-start.9 = (bf16[4,128,1024]{2,1,0:T(8,128)(2,1)}, bf16[4,128,1024]{2,1,0:T(8,128)(2,1)}, u32[]{:S(2)}, u32[]{:S(2)}) collective-permute-start(bf16[4,128,1024]{2,1,0:T(8,128)(2,1)} %get-tuple-element.350), channel_id=1, source_target_pairs={{8,10},{9,11},{14,12},{15,13},{16,18},{17,19},{22,20},{23,21},{24,... | collective-permute-start | bytes 3145736 | tf_op jit(solution)/shard_map/ppermute | solution.py:1124
  173.8 10.1 %collective-permute-start.13 = (bf16[128,1024]{1,0:T(8,128)(2,1)S(1)}, bf16[128,1024]{1,0:T(8,128)(2,1)S(1)}, u32[]{:S(2)}, u32[]{:S(2)}) collective-permute-start(bf16[128,1024]{1,0:T(8,128)(2,1)S(1)} %get-tuple-element.379), channel_id=1, source_target_pairs={{8,0},{16,8},{9,1},{17,9},{10,2},{18,10},{11,3},{19,11},{12,4},{20... | collective-permute-start | bytes 786440 | tf_op jit(solution)/shard_map/ppermute | solution.py:1302
  192.3 23.0 %collective-permute-start.14 = (bf16[3,128,4096]{2,1,0:T(8,128)(2,1)}, bf16[3,128,4096]{2,1,0:T(8,128)(2,1)}, u32[]{:S(2)}, u32[]{:S(2)}) collective-permute-start(bf16[3,128,4096]{2,1,0:T(8,128)(2,1)} %get-tuple-element.393.refs_4_), channel_id=1, source_target_pairs={{0,1},{1,0},{2,3},{3,2},{4,5},{5,4},{6,7},{7,6},{8,9},{9,8},{10,11... | collective-permute-start | bytes 9437192 | tf_op jit(solution)/shard_map/ppermute | solution.py:1112
  192.4 10.9 %collective-permute-start.16 = (bf16[128,1024]{1,0:T(8,128)(2,1)S(1)}, bf16[128,1024]{1,0:T(8,128)(2,1)S(1)}, u32[]{:S(2)}, u32[]{:S(2)}) collective-permute-start(bf16[128,1024]{1,0:T(8,128)(2,1)S(1)} %get-tuple-element.395), channel_id=1, source_target_pairs={{8,0},{9,1},{10,2},{11,3},{12,4},{13,5},{14,6},{15,7}} | collective-permute-start | bytes 786440 | tf_op jit(solution)/shard_map/ppermute | solution.py:1302
  193.7 21.6 %collective-permute-start.15 = (bf16[3,128,1024]{2,1,0:T(8,128)(2,1)}, bf16[3,128,1024]{2,1,0:T(8,128)(2,1)}, u32[]{:S(2)}, u32[]{:S(2)}) collective-permute-start(bf16[3,128,1024]{2,1,0:T(8,128)(2,1)} %get-tuple-element.394.refs_0_), channel_id=1, source_target_pairs={{0,2},{1,3},{6,4},{7,5},{8,10},{9,11},{14,12},{15,13},{16,18},{17,... | collective-permute-start | bytes 2359304 | tf_op jit(solution)/shard_map/ppermute | solution.py:1122
  203.3 12.1 %copy-start.2 = (bf16[512,1024]{1,0:T(8,128)(2,1)S(1)}, bf16[512,1024]{1,0:T(8,128)(2,1)}, u32[]{:S(2)}) copy-start(bf16[512,1024]{1,0:T(8,128)(2,1)} %param.10) | copy-start | bytes 3145732
  208.9 12.2 %collective-permute-start.17 = (bf16[1,128,4096]{2,1,0:T(8,128)(2,1)}, bf16[1,128,4096]{2,1,0:T(8,128)(2,1)S(1)}, u32[]{:S(2)}, u32[]{:S(2)}) collective-permute-start(bf16[1,128,4096]{2,1,0:T(8,128)(2,1)} %get-tuple-element.417.refs_6_), channel_id=1, source_target_pairs={{0,1},{1,0},{2,3},{3,2},{4,5},{5,4},{6,7},{7,6},{8,9},{9,8},{10,11... | collective-permute-start | bytes 3145736 | tf_op jit(solution)/shard_map/ppermute | solution.py:1112
  208.9 12.1 %collective-permute-start.18 = (bf16[1,128,1024]{2,1,0:T(8,128)(2,1)}, bf16[1,128,1024]{2,1,0:T(8,128)(2,1)S(1)}, u32[]{:S(2)}, u32[]{:S(2)}) collective-permute-start(bf16[1,128,1024]{2,1,0:T(8,128)(2,1)} %get-tuple-element.418.refs_1_), channel_id=1, source_target_pairs={{0,2},{1,3},{6,4},{7,5},{8,10},{9,11},{14,12},{15,13},{16,18},{17,... | collective-permute-start | bytes 786440 | tf_op jit(solution)/shard_map/ppermute | solution.py:1122
  215.4 5.7 %copy-start.6 = (bf16[4,128,4096]{2,1,0:T(8,128)(2,1)S(1)}, bf16[4,128,4096]{2,1,0:T(8,128)(2,1)}, u32[]{:S(2)}) copy-start(bf16[4,128,4096]{2,1,0:T(8,128)(2,1)} %get-tuple-element.420.refs_6_.refs_7_) | copy-start | bytes 12582916
  221.0 5.5 %copy-start.8 = (s32[4]{0:T(128)S(1)}, s32[4]{0:T(128)}, u32[]{:S(2)}) copy-start(s32[4]{0:T(128)} %refs_1_.1) | copy-start | bytes 52
  221.1 5.6 %copy-start.7 = (f32[4,4,1024]{2,1,0:T(4,128)S(1)}, f32[4,4,1024]{2,1,0:T(4,128)}, u32[]{:S(2)}) copy-start(f32[4,4,1024]{2,1,0:T(4,128)} %get-tuple-element.428) | copy-start | bytes 196612
  224.0 2.0 copy-start.3
  226.0 37.2 %collective-permute-start.20 = (bf16[512,4096]{1,0:T(8,128)(2,1)}, bf16[512,4096]{1,0:T(8,128)(2,1)}, u32[]{:S(2)}, u32[]{:S(2)}) collective-permute-start(bf16[512,4096]{1,0:T(8,128)(2,1)} %get-tuple-element.424), channel_id=1, source_target_pairs={{0,1},{1,0},{2,3},{3,2},{4,5},{5,4},{6,7},{7,6},{8,9},{9,8},{10,11... | collective-permute-start | bytes 12582920 | tf_op jit(solution)/shard_map/ppermute | solution.py:1112
  226.0 44.4 %collective-permute-start.19 = (bf16[4,128,3072]{2,1,0:T(8,128)(2,1)}, bf16[4,128,3072]{2,1,0:T(8,128)(2,1)}, u32[]{:S(2)}, u32[]{:S(2)}) collective-permute-start(bf16[4,128,3072]{2,1,0:T(8,128)(2,1)} %get-tuple-element.423.refs_2_), channel_id=1, source_target_pairs={{0,1},{1,0},{2,3},{3,2},{4,5},{5,4},{6,7},{7,6},{8,9},{9,8},{10,11... | collective-permute-start | bytes 9437192 | tf_op jit(solution)/shard_map/ppermute | solution.py:1112
  226.9 41.9 %collective-permute-start.22 = (f32[32,1024]{1,0:T(8,128)S(1)}, f32[32,1024]{1,0:T(8,128)S(1)}, u32[]{:S(2)}, u32[]{:S(2)}) collective-permute-start(f32[32,1024]{1,0:T(8,128)S(1)} %reshape.56), channel_id=1, source_target_pairs={{0,1},{1,0},{2,3},{3,2},{4,5},{5,4},{6,7},{7,6},{8,9},{9,8},{10,11... | collective-permute-start | bytes 393224 | tf_op jit(solution)/shard_map/ppermute | solution.py:1112
  227.0 51.6 %collective-permute-start.21 = (bf16[4,128,1024]{2,1,0:T(8,128)(2,1)}, bf16[4,128,1024]{2,1,0:T(8,128)(2,1)}, u32[]{:S(2)}, u32[]{:S(2)}) collective-permute-start(bf16[4,128,1024]{2,1,0:T(8,128)(2,1)} %get-tuple-element.427.refs_2_), channel_id=1, source_target_pairs={{0,1},{1,0},{2,3},{3,2},{4,5},{5,4},{6,7},{7,6},{8,9},{9,8},{10,11... | collective-permute-start | bytes 3145736 | tf_op jit(solution)/shard_map/ppermute | solution.py:1112
  227.5 2.2 copy-start.4
  240.1 2.2 copy-start
  242.3 43.5 %collective-permute-start.23 = (bf16[128,4096]{1,0:T(8,128)(2,1)S(1)}, bf16[128,4096]{1,0:T(8,128)(2,1)S(1)}, u32[]{:S(2)}, u32[]{:S(2)}) collective-permute-start(bf16[128,4096]{1,0:T(8,128)(2,1)S(1)} %get-tuple-element.425.refs_2_), channel_id=1, source_target_pairs={{0,2},{1,3},{8,10},{9,11},{16,18},{17,19},{24,26},{25,27}} | collective-permute-start | bytes 3145736 | tf_op jit(solution)/shard_map/ppermute | solution.py:1070
  267.1 15.0 %collective-permute-start.25 = (bf16[128,4096]{1,0:T(8,128)(2,1)}, bf16[128,4096]{1,0:T(8,128)(2,1)}, u32[]{:S(2)}, u32[]{:S(2)}) collective-permute-start(bf16[128,4096]{1,0:T(8,128)(2,1)} %get-tuple-element.426.refs_4_), channel_id=1, source_target_pairs={{2,4},{3,5},{10,12},{11,13},{18,20},{19,21},{26,28},{27,29}} | collective-permute-start | bytes 3145736 | tf_op jit(solution)/shard_map/ppermute | solution.py:1070
  268.8 13.4 %collective-permute-start.26 = (bf16[128,4096]{1,0:T(8,128)(2,1)}, bf16[128,4096]{1,0:T(8,128)(2,1)}, u32[]{:S(2)}, u32[]{:S(2)}) collective-permute-start(bf16[128,4096]{1,0:T(8,128)(2,1)} %get-tuple-element.430), channel_id=1, source_target_pairs={{4,2},{5,3},{12,10},{13,11},{20,18},{21,19},{28,26},{29,27}} | collective-permute-start | bytes 3145736 | tf_op jit(solution)/shard_map/ppermute | solution.py:1070
  270.4 15.4 %collective-permute-start.24 = (bf16[128,4096]{1,0:T(8,128)(2,1)}, bf16[128,4096]{1,0:T(8,128)(2,1)S(1)}, u32[]{:S(2)}, u32[]{:S(2)}) collective-permute-start(bf16[128,4096]{1,0:T(8,128)(2,1)} %get-tuple-element.429), channel_id=1, source_target_pairs={{6,4},{7,5},{14,12},{15,13},{22,20},{23,21},{30,28},{31,29}} | collective-permute-start | bytes 3145736 | tf_op jit(solution)/shard_map/ppermute | solution.py:1070
  278.5 3.6 copy-start.5
  285.8 44.7 %copy-start.1 = (bf16[512,4096]{1,0:T(8,128)(2,1)S(1)}, bf16[512,4096]{1,0:T(8,128)(2,1)}, u32[]{:S(2)}) copy-start(bf16[512,4096]{1,0:T(8,128)(2,1)} %copy-done) | copy-start | bytes 12582916
  286.0 44.6 %collective-permute-start.27 = (bf16[128,4224]{1,0:T(8,128)(2,1)S(1)}, bf16[128,4224]{1,0:T(8,128)(2,1)S(1)}, u32[]{:S(2)}, u32[]{:S(2)}) collective-permute-start(bf16[128,4224]{1,0:T(8,128)(2,1)S(1)} %get-tuple-element.432.refs_8_), channel_id=1, source_target_pairs={{0,2},{1,3},{8,10},{9,11},{16,18},{17,19},{24,26},{25,27}} | collective-permute-start | bytes 3244040 | tf_op jit(solution)/shard_map/ppermute | solution.py:1070
  303.4 27.1 %collective-permute-start.28 = (bf16[128,4224]{1,0:T(8,128)(2,1)S(1)}, bf16[128,4224]{1,0:T(8,128)(2,1)S(1)}, u32[]{:S(2)}, u32[]{:S(2)}) collective-permute-start(bf16[128,4224]{1,0:T(8,128)(2,1)S(1)} %get-tuple-element.433), channel_id=1, source_target_pairs={{6,4},{7,5},{14,12},{15,13},{22,20},{23,21},{30,28},{31,29}} | collective-permute-start | bytes 3244040 | tf_op jit(solution)/shard_map/ppermute | solution.py:1070
  304.2 2.0 collective-permute-start.29
  304.9 25.6 %collective-permute-start.30 = (bf16[128,4096]{1,0:T(8,128)(2,1)S(1)}, bf16[128,4096]{1,0:T(8,128)(2,1)S(1)}, u32[]{:S(2)}, u32[]{:S(2)}) collective-permute-start(bf16[128,4096]{1,0:T(8,128)(2,1)S(1)} %get-tuple-element.434), channel_id=1, source_target_pairs={{2,0},{3,1},{4,2},{5,3},{10,8},{11,9},{12,10},{13,11},{18,16},{19,... | collective-permute-start | bytes 3145736 | tf_op jit(solution)/shard_map/ppermute | solution.py:1070
  331.5 46.2 %collective-permute-start.31 = (bf16[128,8320]{1,0:T(8,128)(2,1)S(1)}, bf16[128,8320]{1,0:T(8,128)(2,1)S(1)}, u32[]{:S(2)}, u32[]{:S(2)}) collective-permute-start(bf16[128,8320]{1,0:T(8,128)(2,1)S(1)} %get-tuple-element.435.refs_4_), channel_id=1, source_target_pairs={{0,2},{1,3},{2,4},{3,5},{8,10},{9,11},{10,12},{11,13},{16,18},{17,... | collective-permute-start | bytes 6389768 | tf_op jit(solution)/shard_map/ppermute | solution.py:1070
  334.7 43.0 %collective-permute-start.32 = (bf16[128,8320]{1,0:T(8,128)(2,1)S(1)}, bf16[128,8320]{1,0:T(8,128)(2,1)S(1)}, u32[]{:S(2)}, u32[]{:S(2)}) collective-permute-start(bf16[128,8320]{1,0:T(8,128)(2,1)S(1)} %get-tuple-element.436), channel_id=1, source_target_pairs={{4,2},{5,3},{6,4},{7,5},{12,10},{13,11},{14,12},{15,13},{20,18},{2... | collective-permute-start | bytes 6389768 | tf_op jit(solution)/shard_map/ppermute | solution.py:1070
  378.8 48.5 %collective-permute-start.33 = (bf16[128,8320]{1,0:T(8,128)(2,1)S(1)}, bf16[128,8320]{1,0:T(8,128)(2,1)S(1)}, u32[]{:S(2)}, u32[]{:S(2)}) collective-permute-start(bf16[128,8320]{1,0:T(8,128)(2,1)S(1)} %get-tuple-element.438.refs_6_), channel_id=1, source_target_pairs={{0,2},{1,3},{2,4},{3,5},{4,6},{5,7},{8,10},{9,11},{10,12},{11,13},... | collective-permute-start | bytes 6389768 | tf_op jit(solution)/shard_map/ppermute | solution.py:1070
  385.2 46.3 %collective-permute-start.34 = (bf16[128,8320]{1,0:T(8,128)(2,1)S(1)}, bf16[128,8320]{1,0:T(8,128)(2,1)S(1)}, u32[]{:S(2)}, u32[]{:S(2)}) collective-permute-start(bf16[128,8320]{1,0:T(8,128)(2,1)S(1)} %get-tuple-element.439), channel_id=1, source_target_pairs={{2,0},{3,1},{4,2},{5,3},{6,4},{7,5},{10,8},{11,9},{12,10},{13,11},... | collective-permute-start | bytes 6389768 | tf_op jit(solution)/shard_map/ppermute | solution.py:1070

commit v6 on v5

--- a/solution.py
+++ b/solution.py
@@ -293,27 +293,18 @@
         for i, (source, target) in enumerate(pairs):
             loads.append(pltpu.make_async_copy(source, target, sems.at[i]))
         loads[0].start()
-
-        @pl.when(core == 1)
-        def later():
-            loads[4].start()
-            loads[4].wait()
-
         loads[1].start()
     base = len(loads)
 
     def ready(i):
         if not loads_weights:
-            return
-        if i == 4:
-            pl.when(core != 1)(loads[4].wait)
             return
         loads[i].wait()
         if i == 1:
             loads[2].start()
             loads[3].start()
         if i == 2:
-            pl.when(core != 1)(loads[4].start)
+            loads[4].start()
 
     @pl.when(active)
     def forward():
@@ -942,7 +933,7 @@
     body = functools.partial(
         weight_grad_kernel, bare, first_column, rows, step, outputs, skip_ends
     )
-    return call.run(body, scratch, 0, limit=20 * 2**20)
+    return call.run(body, scratch, 0, limit=(20 if outputs == 2 else 14) * 2**20)
 
 
 class Part(NamedTuple):
@@ -1303,7 +1294,7 @@
         incoming, arriving = sent, returned
         if exchange.by_hops:
             if tick == plan.fwd_ticks() - 1:
-                lefts = exchange.both(state.kept.left)
+                lefts = [in_hbm(x) for x in exchange.both(state.kept.left)]
                 before_bwd[tick + 1] += lefts[1:]
                 if exchange.ends_hand_over:
                     (act_in,) = act_in

time: 443 us -> 442 us (level)
  no operation moved by 1% of the time
where the time goes in v6:
time: 442 us; the launch traced here: 435 us
  waiting for transfers between devices  174 us (39%)
  Pallas kernels  157 us (36%)
  starting transfers between devices  96.5 us (22%)
  local copies, waits for them, and re-layouts  5.99 us (1%)
    pallas_call x28, Pallas kernels, run(): pl.pallas_call(body, out_shape=self.out_shape, in_specs=self.in_specs, ou...  157 us
    ppermute x12, waiting for transfers between devices, moved(): return lax.ppermute(value, 'batch', pairs)  107 us
    ppermute x12, starting transfers between devices, moved(): return lax.ppermute(value, 'batch', pairs)  57.4 us
    ppermute x6, waiting for transfers between devices, per_device(): returned = lax.ppermute(output, 'section', backward)  49.1 us
    ppermute x6, starting transfers between devices, per_device(): sent = lax.ppermute(output, 'section', onward)  17.2 us
    ppermute x6, waiting for transfers between devices, per_device(): sent = lax.ppermute(output, 'section', onward)  14.1 us
  transfers between devices with their start and end apart: 35, of which 13 were waited for; matrix products, arithmetic and copies ran while one was open for 0% of the time, Pallas kernels for 21%

profile of v6, /device:TPU:0, one launch (start us, length us, event | category | flops | bytes accessed | tf_op | source)
XLA Modules:
  0.0 434.7 jit_solution(15158157175436381905)
XLA Ops:
  0.6 14.0 %shard_map.144 = (s32[8]{0:T(128)S(4)}, f32[32,1024]{1,0:T(8,128)S(1)}, bf16[1024,3072]{1,0:T(8,128)(2,1)S(1)}, bf16[1024,1024]{1,0:T(8,128)(2,1)S(1)}, bf16[102...) custom-call(s32[4]{0:T(128)} %refs_0_.1, ...), custom_call_target="tpu_custom_call" | custom-call | flops 12884901888 | tf_op jit(solution)/shard_map/pallas_call | solution.py:646
  14.6 5.3 %collective-permute-start = (bf16[128,1024]{1,0:T(8,128)(2,1)S(1)}, bf16[128,1024]{1,0:T(8,128)(2,1)S(1)}, u32[]{:S(2)}, u32[]{:S(2)}) collective-permute-start(bf16[128,1024]{1,0:T(8,128)(2,1)S(1)} %get-tuple-element.236), channel_id=1, source_target_pairs={{0,8},{1,9},{2,10},{3,11},{4,12},{5,13},{6,14},{7,15}} | collective-permute-start | bytes 786440 | tf_op jit(solution)/shard_map/ppermute | solution.py:1268
  19.9 5.5 %collective-permute-done.refs_10_ = bf16[128,1024]{1,0:T(8,128)(2,1)S(1)} collective-permute-done((bf16[128,1024]{1,0:T(8,128)(2,1)S(1)}, bf16[128,1024]{1,0:T(8,128)(2,1)S(1)}, u32[]{:S(2)}, u32[]{:S(2)}) %collective-permute-start) | collective-permute-done | bytes 262176 | tf_op jit(solution)/shard_map/ppermute | solution.py:1268
  25.5 9.3 %shard_map.145 = (bf16[3072,1024]{1,0:T(8,128)(2,1)S(1)}, bf16[1024,1024]{1,0:T(8,128)(2,1)S(1)}, bf16[4096,1024]{1,0:T(8,128)(2,1)S(1)}, bf16[1024,4096]{1,0:T(...) custom-call(s32[8]{0:T(128)S(4)} %get-tuple-element.226.refs_0_, ...), custom_call_target="tpu_custom_call", output_to_operand_aliasing={{0}: (6, {}), {1}: (7, {}), {2}: (8, {}), {3}: (9, {}), {4}... | custom-call | flops 12884901888 | tf_op jit(solution)/shard_map/pallas_call | solution.py:646
  34.8 3.5 collective-permute-start.1
  38.3 4.7 %collective-permute-done.1.refs_10_ = bf16[128,1024]{1,0:T(8,128)(2,1)S(1)} collective-permute-done((bf16[128,1024]{1,0:T(8,128)(2,1)S(1)}, bf16[128,1024]{1,0:T(8,128)(2,1)S(1)}, u32[]{:S(2)}, u32[]{:S(2)}) %collective-permute-start.1) | collective-permute-done | bytes 262176 | tf_op jit(solution)/shard_map/ppermute | solution.py:1268
  42.9 8.9 %shard_map.146 = (bf16[3072,1024]{1,0:T(8,128)(2,1)S(1)}, bf16[1024,1024]{1,0:T(8,128)(2,1)S(1)}, bf16[4096,1024]{1,0:T(8,128)(2,1)S(1)}, bf16[1024,4096]{1,0:T(...) custom-call(s32[8]{0:T(128)S(4)} %get-tuple-element.226.refs_0_, ...), custom_call_target="tpu_custom_call", output_to_operand_aliasing={{0}: (6, {}), {1}: (7, {}), {2}: (8, {}), {3}: (9, {}), {4}... | custom-call | flops 12884901888 | tf_op jit(solution)/shard_map/pallas_call | solution.py:646
  51.8 3.5 collective-permute-start.2
  55.3 3.9 collective-permute-done.2.refs_10_
  59.1 9.5 %shard_map.147 = (bf16[3072,1024]{1,0:T(8,128)(2,1)S(1)}, bf16[1024,1024]{1,0:T(8,128)(2,1)S(1)}, bf16[4096,1024]{1,0:T(8,128)(2,1)S(1)}, bf16[1024,4096]{1,0:T(...) custom-call(s32[8]{0:T(128)S(4)} %get-tuple-element.226.refs_0_, ...), custom_call_target="tpu_custom_call", output_to_operand_aliasing={{0}: (6, {}), {1}: (7, {}), {2}: (8, {}), {3}: (9, {}), {4}... | custom-call | flops 12884901888 | tf_op jit(solution)/shard_map/pallas_call | solution.py:646
  68.6 3.6 collective-permute-start.3
  72.4 2.2 shard_map.152
  75.3 4.5 %collective-permute-start.7 = (bf16[4,128,1024]{2,1,0:T(8,128)(2,1)}, bf16[4,128,1024]{2,1,0:T(8,128)(2,1)}, u32[]{:S(2)}, u32[]{:S(2)}) collective-permute-start(bf16[4,128,1024]{2,1,0:T(8,128)(2,1)} %shard_map.152), channel_id=1, source_target_pairs={{0,2},{1,3},{6,4},{7,5}} | collective-permute-start | bytes 3145736 | tf_op jit(solution)/shard_map/ppermute | solution.py:1115
  79.8 9.6 %shard_map.149 = (bf16[3072,1024]{1,0:T(8,128)(2,1)S(1)}, bf16[1024,1024]{1,0:T(8,128)(2,1)S(1)}, bf16[4096,1024]{1,0:T(8,128)(2,1)S(1)}, bf16[1024,4096]{1,0:T(...) custom-call(s32[8]{0:T(128)S(4)} %get-tuple-element.226.refs_0_, ...), custom_call_target="tpu_custom_call", output_to_operand_aliasing={{0}: (6, {}), {1}: (7, {}), {2}: (8, {}), {3}: (9, {}), {4}... | custom-call | flops 12884901888 | tf_op jit(solution)/shard_map/pallas_call | solution.py:646
  91.0 14.4 %shard_map.151 = (bf16[3072,1024]{1,0:T(8,128)(2,1)S(1)}, bf16[1024,1024]{1,0:T(8,128)(2,1)S(1)}, bf16[4096,1024]{1,0:T(8,128)(2,1)S(1)}, bf16[1024,4096]{1,0:T(...) custom-call(s32[8]{0:T(128)S(4)} %get-tuple-element.226.refs_0_, ...), custom_call_target="tpu_custom_call", output_to_operand_aliasing={{0}: (6, {}), {1}: (7, {}), {2}: (8, {}), {3}: (9, {}), {4}... | custom-call | flops 12884901888 | tf_op jit(solution)/shard_map/pallas_call | solution.py:646
  106.3 9.3 %shard_map.154 = (bf16[3072,1024]{1,0:T(8,128)(2,1)S(1)}, bf16[1024,1024]{1,0:T(8,128)(2,1)S(1)}, bf16[4096,1024]{1,0:T(8,128)(2,1)S(1)}, bf16[1024,4096]{1,0:T(...) custom-call(s32[8]{0:T(128)S(4)} %get-tuple-element.226.refs_0_, ...), custom_call_target="tpu_custom_call", output_to_operand_aliasing={{0}: (6, {}), {1}: (7, {}), {2}: (8, {}), {3}: (9, {}), {4}... | custom-call | flops 12884901888 | tf_op jit(solution)/shard_map/pallas_call | solution.py:646
  117.0 21.8 %collective-permute-done.11.refs_10_ = bf16[128,1024]{1,0:T(8,128)(2,1)S(1)} collective-permute-done((bf16[128,1024]{1,0:T(8,128)(2,1)S(1)}, bf16[128,1024]{1,0:T(8,128)(2,1)S(1)}, u32[]{:S(2)}, u32[]{:S(2)}) %collective-permute-start.11) | collective-permute-done | bytes 262176 | tf_op jit(solution)/shard_map/ppermute | solution.py:1293
  138.8 8.5 %shard_map.155 = (bf16[4,128,1024]{2,1,0:T(8,128)(2,1)}, bf16[4,128,3072]{2,1,0:T(8,128)(2,1)}, bf16[4,2048,128]{2,1,0:T(8,128)(2,1)}, f32[4,128,1024]{2,1,0:T(8...) custom-call(s32[8]{0:T(128)S(4)} %get-tuple-element.226.refs_0_, ...), custom_call_target="tpu_custom_call", output_to_operand_aliasing={{0}: (12, {}), {1}: (13, {}), {2}: (14, {}), {3}: (15, {}),... | custom-call | flops 12884901888 | tf_op jit(solution)/shard_map/pallas_call | solution.py:646
  148.5 1.7 collective-permute-start.9
  150.2 13.3 %collective-permute-done.12.refs_11_ = bf16[128,1024]{1,0:T(8,128)(2,1)S(1)} collective-permute-done((bf16[128,1024]{1,0:T(8,128)(2,1)S(1)}, bf16[128,1024]{1,0:T(8,128)(2,1)S(1)}, u32[]{:S(2)}, u32[]{:S(2)}) %collective-permute-start.12) | collective-permute-done | bytes 262176 | tf_op jit(solution)/shard_map/ppermute | solution.py:1293
  163.6 8.9 %shard_map.156 = (bf16[4,128,1024]{2,1,0:T(8,128)(2,1)}, bf16[4,128,3072]{2,1,0:T(8,128)(2,1)}, bf16[4,2048,128]{2,1,0:T(8,128)(2,1)}, f32[4,128,1024]{2,1,0:T(8...) custom-call(s32[8]{0:T(128)S(4)} %get-tuple-element.226.refs_0_, ...), custom_call_target="tpu_custom_call", output_to_operand_aliasing={{0}: (13, {}), {1}: (14, {}), {2}: (15, {}), {3}: (16, {}),... | custom-call | flops 12884901888 | tf_op jit(solution)/shard_map/pallas_call | solution.py:646
  173.8 8.7 %collective-permute-done.13.refs_13_ = bf16[128,1024]{1,0:T(8,128)(2,1)S(1)} collective-permute-done((bf16[128,1024]{1,0:T(8,128)(2,1)S(1)}, bf16[128,1024]{1,0:T(8,128)(2,1)S(1)}, u32[]{:S(2)}, u32[]{:S(2)}) %collective-permute-start.13) | collective-permute-done | bytes 262176 | tf_op jit(solution)/shard_map/ppermute | solution.py:1293
  182.5 8.5 %shard_map.157 = (bf16[4,128,1024]{2,1,0:T(8,128)(2,1)}, bf16[4,128,3072]{2,1,0:T(8,128)(2,1)}, bf16[4,2048,128]{2,1,0:T(8,128)(2,1)}, f32[4,128,1024]{2,1,0:T(8...) custom-call(s32[8]{0:T(128)S(4)} %get-tuple-element.226.refs_0_, ...), custom_call_target="tpu_custom_call", output_to_operand_aliasing={{0}: (15, {}), {1}: (16, {}), {2}: (17, {}), {3}: (18, {}),... | custom-call | flops 12884901888 | tf_op jit(solution)/shard_map/pallas_call | solution.py:646
  192.4 4.4 %collective-permute-start.15 = (bf16[3,128,1024]{2,1,0:T(8,128)(2,1)}, bf16[3,128,1024]{2,1,0:T(8,128)(2,1)}, u32[]{:S(2)}, u32[]{:S(2)}) collective-permute-start(bf16[3,128,1024]{2,1,0:T(8,128)(2,1)} %get-tuple-element.394.refs_0_), channel_id=1, source_target_pairs={{0,2},{1,3},{6,4},{7,5},{8,10},{9,11},{14,12},{15,13},{16,18},{17,... | collective-permute-start | bytes 2359304 | tf_op jit(solution)/shard_map/ppermute | solution.py:1113
  196.7 5.2 %collective-permute-done.16.refs_13_.refs_5_ = bf16[128,1024]{1,0:T(8,128)(2,1)S(1)} collective-permute-done((bf16[128,1024]{1,0:T(8,128)(2,1)S(1)}, bf16[128,1024]{1,0:T(8,128)(2,1)S(1)}, u32[]{:S(2)}, u32[]{:S(2)}) %collective-permute-start.16) | collective-permute-done | bytes 262176 | tf_op jit(solution)/shard_map/ppermute | solution.py:1293
  201.9 5.6 %shard_map.158 = (bf16[4,128,1024]{2,1,0:T(8,128)(2,1)}, bf16[4,128,3072]{2,1,0:T(8,128)(2,1)}, bf16[4,2048,128]{2,1,0:T(8,128)(2,1)}, f32[4,128,1024]{2,1,0:T(8...) custom-call(s32[8]{0:T(128)S(4)} %get-tuple-element.226.refs_0_, ...), custom_call_target="tpu_custom_call", output_to_operand_aliasing={{0}: (15, {}), {1}: (16, {}), {2}: (17, {}), {3}: (18, {}),... | custom-call | flops 6442450944 | tf_op jit(solution)/shard_map/pallas_call | solution.py:646
  207.6 3.5 collective-permute-start.18
  211.1 2.9 collective-permute-done.15.refs_4_.refs_2_
  214.0 5.6 %shard_map.159 = (bf16[4,128,1024]{2,1,0:T(8,128)(2,1)}, bf16[4,128,3072]{2,1,0:T(8,128)(2,1)}, bf16[4,2048,128]{2,1,0:T(8,128)(2,1)}, f32[4,128,1024]{2,1,0:T(8...) custom-call(s32[8]{0:T(128)S(4)} %get-tuple-element.226.refs_0_, ...), custom_call_target="tpu_custom_call", output_to_operand_aliasing={{0}: (7, {}), {1}: (8, {}), {2}: (9, {}), {3}: (10, {}), {4... | custom-call | flops 6442450944 | tf_op jit(solution)/shard_map/pallas_call | solution.py:646
  219.7 2.9 shard_map.160
  222.6 2.0 copy-done.3
  226.1 2.2 copy-done.4
  228.3 10.4 %shard_map.161.refs_0_.refs_1_ = bf16[512,4096]{1,0:T(8,128)(2,1)S(1)} custom-call(bf16[2,4,128,1536]{3,2,1,0:T(8,128)(2,1)} %get-tuple-element.352.refs_0_.refs_2_, bf16[2,4,128,1536]{3,2,1,0:T(8,128)(2,1)} %collective-permute-done.10.refs_10_.refs_1_.refs_3_, bf16[2,4,128,1536]{3,2,1,0:T(8,128)(2,1)} %get-tuple-element.352.refs_0_.refs_2_, ...), custom_call_target="tpu_custom_call" | custom-call | tf_op jit(solution)/shard_map/pallas_call | solution.py:646
  241.4 21.0 %collective-permute-start.23 = (bf16[128,4096]{1,0:T(8,128)(2,1)S(1)}, bf16[128,4096]{1,0:T(8,128)(2,1)S(1)}, u32[]{:S(2)}, u32[]{:S(2)}) collective-permute-start(bf16[128,4096]{1,0:T(8,128)(2,1)S(1)} %get-tuple-element.425.refs_2_), channel_id=1, source_target_pairs={{0,2},{1,3},{8,10},{9,11},{16,18},{17,19},{24,26},{25,27}} | collective-permute-start | bytes 3145736 | tf_op jit(solution)/shard_map/ppermute | solution.py:1061
  262.4 3.9 shard_map.163
  266.3 1.6 collective-permute-start.25
  270.5 7.2 %shard_map.164.refs_4_.refs_0_.refs_1_ = bf16[512,3072]{1,0:T(8,128)(2,1)S(1)} custom-call(bf16[2,4,128,1536]{3,2,1,0:T(8,128)(2,1)} %get-tuple-element.352.refs_0_.refs_2_, bf16[2,4,128,1536]{3,2,1,0:T(8,128)(2,1)} %collective-permute-done.10.refs_10_.refs_1_.refs_3_, bf16[4,128,3072]{2,1,0:T(8,128)(2,1)} %get-tuple-element.423.refs_2_, ...), custom_call_target="tpu_custom_call" | custom-call | tf_op jit(solution)/shard_map/pallas_call | solution.py:646
  277.7 3.6 shard_map.165.refs_4_.refs_1_.refs_2_
  281.3 3.5 shard_map.166
  285.1 18.0 %collective-permute-start.27 = (bf16[128,4224]{1,0:T(8,128)(2,1)S(1)}, bf16[128,4224]{1,0:T(8,128)(2,1)S(1)}, u32[]{:S(2)}, u32[]{:S(2)}) collective-permute-start(bf16[128,4224]{1,0:T(8,128)(2,1)S(1)} %get-tuple-element.432.refs_8_), channel_id=1, source_target_pairs={{0,2},{1,3},{8,10},{9,11},{16,18},{17,19},{24,26},{25,27}} | collective-permute-start | bytes 3244040 | tf_op jit(solution)/shard_map/ppermute | solution.py:1061
  305.9 24.3 %collective-permute-done.30.refs_10_.refs_3_ = bf16[128,4096]{1,0:T(8,128)(2,1)S(1)} collective-permute-done((bf16[128,4096]{1,0:T(8,128)(2,1)S(1)}, bf16[128,4096]{1,0:T(8,128)(2,1)S(1)}, u32[]{:S(2)}, u32[]{:S(2)}) %collective-permute-start.30) | collective-permute-done | bytes 1048608 | tf_op jit(solution)/shard_map/ppermute | solution.py:1061
  331.2 3.2 collective-permute-start.31
  335.2 4.1 shard_map.169
  339.3 38.1 %collective-permute-done.31.refs_4_ = bf16[128,8320]{1,0:T(8,128)(2,1)S(1)} collective-permute-done((bf16[128,8320]{1,0:T(8,128)(2,1)S(1)}, bf16[128,8320]{1,0:T(8,128)(2,1)S(1)}, u32[]{:S(2)}, u32[]{:S(2)}) %collective-permute-start.31) | collective-permute-done | bytes 2129952 | tf_op jit(solution)/shard_map/ppermute | solution.py:1061
  378.4 6.4 %collective-permute-start.33 = (bf16[128,8320]{1,0:T(8,128)(2,1)S(1)}, bf16[128,8320]{1,0:T(8,128)(2,1)S(1)}, u32[]{:S(2)}, u32[]{:S(2)}) collective-permute-start(bf16[128,8320]{1,0:T(8,128)(2,1)S(1)} %get-tuple-element.438.refs_6_), channel_id=1, source_target_pairs={{0,2},{1,3},{2,4},{3,5},{4,6},{5,7},{8,10},{9,11},{10,12},{11,13},... | collective-permute-start | bytes 6389768 | tf_op jit(solution)/shard_map/ppermute | solution.py:1061
  386.2 40.8 %collective-permute-done.33.refs_4_ = bf16[128,8320]{1,0:T(8,128)(2,1)S(1)} collective-permute-done((bf16[128,8320]{1,0:T(8,128)(2,1)S(1)}, bf16[128,8320]{1,0:T(8,128)(2,1)S(1)}, u32[]{:S(2)}, u32[]{:S(2)}) %collective-permute-start.33) | collective-permute-done | bytes 2129952 | tf_op jit(solution)/shard_map/ppermute | solution.py:1061
  427.0 4.2 collective-permute-done.34.refs_5_
  431.2 3.0 shard_map.171
  (80 shorter events, 22.4 us)
Async XLA Ops:
  14.6 10.8 %collective-permute-start = (bf16[128,1024]{1,0:T(8,128)(2,1)S(1)}, bf16[128,1024]{1,0:T(8,128)(2,1)S(1)}, u32[]{:S(2)}, u32[]{:S(2)}) collective-permute-start(bf16[128,1024]{1,0:T(8,128)(2,1)S(1)} %get-tuple-element.236), channel_id=1, source_target_pairs={{0,8},{1,9},{2,10},{3,11},{4,12},{5,13},{6,14},{7,15}} | collective-permute-start | bytes 786440 | tf_op jit(solution)/shard_map/ppermute | solution.py:1268
  34.8 8.2 %collective-permute-start.1 = (bf16[128,1024]{1,0:T(8,128)(2,1)S(1)}, bf16[128,1024]{1,0:T(8,128)(2,1)S(1)}, u32[]{:S(2)}, u32[]{:S(2)}) collective-permute-start(bf16[128,1024]{1,0:T(8,128)(2,1)S(1)} %get-tuple-element.250), channel_id=1, source_target_pairs={{0,8},{8,16},{1,9},{9,17},{2,10},{10,18},{3,11},{11,19},{4,12},{12... | collective-permute-start | bytes 786440 | tf_op jit(solution)/shard_map/ppermute | solution.py:1268
  51.8 7.3 %collective-permute-start.2 = (bf16[128,1024]{1,0:T(8,128)(2,1)S(1)}, bf16[128,1024]{1,0:T(8,128)(2,1)S(1)}, u32[]{:S(2)}, u32[]{:S(2)}) collective-permute-start(bf16[128,1024]{1,0:T(8,128)(2,1)S(1)} %get-tuple-element.264), channel_id=1, source_target_pairs={{0,8},{8,16},{16,24},{1,9},{9,17},{17,25},{2,10},{10,18},{18,26},{... | collective-permute-start | bytes 786440 | tf_op jit(solution)/shard_map/ppermute | solution.py:1268
  68.6 11.2 %collective-permute-start.3 = (bf16[128,1024]{1,0:T(8,128)(2,1)S(1)}, bf16[128,1024]{1,0:T(8,128)(2,1)S(1)}, u32[]{:S(2)}, u32[]{:S(2)}) collective-permute-start(bf16[128,1024]{1,0:T(8,128)(2,1)S(1)} %get-tuple-element.278), channel_id=1, source_target_pairs={{0,8},{8,16},{16,24},{1,9},{9,17},{17,25},{2,10},{10,18},{18,26},{... | collective-permute-start | bytes 786440 | tf_op jit(solution)/shard_map/ppermute | solution.py:1268
  74.6 15.5 %collective-permute-start.5 = (bf16[128,1024]{1,0:T(8,128)(2,1)S(1)}, bf16[128,1024]{1,0:T(8,128)(2,1)S(1)}, u32[]{:S(2)}, u32[]{:S(2)}) collective-permute-start(bf16[128,1024]{1,0:T(8,128)(2,1)S(1)} %get-tuple-element.298), channel_id=1, source_target_pairs={{24,16},{25,17},{26,18},{27,19},{28,20},{29,21},{30,22},{31,23}} | collective-permute-start | bytes 786440 | tf_op jit(solution)/shard_map/ppermute | solution.py:1293
  75.3 31.0 %collective-permute-start.7 = (bf16[4,128,1024]{2,1,0:T(8,128)(2,1)}, bf16[4,128,1024]{2,1,0:T(8,128)(2,1)}, u32[]{:S(2)}, u32[]{:S(2)}) collective-permute-start(bf16[4,128,1024]{2,1,0:T(8,128)(2,1)} %shard_map.152), channel_id=1, source_target_pairs={{0,2},{1,3},{6,4},{7,5}} | collective-permute-start | bytes 3145736 | tf_op jit(solution)/shard_map/ppermute | solution.py:1115
  89.4 1.6 collective-permute-start.4
  90.3 15.8 %collective-permute-start.8 = (bf16[128,1024]{1,0:T(8,128)(2,1)S(1)}, bf16[128,1024]{1,0:T(8,128)(2,1)S(1)}, u32[]{:S(2)}, u32[]{:S(2)}) collective-permute-start(bf16[128,1024]{1,0:T(8,128)(2,1)S(1)} %get-tuple-element.324), channel_id=1, source_target_pairs={{16,8},{24,16},{17,9},{25,17},{18,10},{26,18},{19,11},{27,19},{20,... | collective-permute-start | bytes 786440 | tf_op jit(solution)/shard_map/ppermute | solution.py:1293
  105.3 0.9 collective-permute-start.6
  115.6 48.0 %collective-permute-start.10 = (bf16[2,4,128,1536]{3,2,1,0:T(8,128)(2,1)}, bf16[2,4,128,1536]{3,2,1,0:T(8,128)(2,1)}, u32[]{:S(2)}, u32[]{:S(2)}) collective-permute-start(bf16[2,4,128,1536]{3,2,1,0:T(8,128)(2,1)} %get-tuple-element.352.refs_0_.refs_2_), channel_id=1, source_target_pairs={{0,1},{1,0},{2,3},{3,2},{4,5},{5,4},{6,7},{7,6},{8,9},{9,8},{10,11... | collective-permute-start | bytes 9437192 | tf_op jit(solution)/shard_map/ppermute | solution.py:1103
  115.7 23.1 %collective-permute-start.11 = (bf16[128,1024]{1,0:T(8,128)(2,1)S(1)}, bf16[128,1024]{1,0:T(8,128)(2,1)S(1)}, u32[]{:S(2)}, u32[]{:S(2)}) collective-permute-start(bf16[128,1024]{1,0:T(8,128)(2,1)S(1)} %get-tuple-element.353), channel_id=1, source_target_pairs={{8,0},{16,8},{24,16},{9,1},{17,9},{25,17},{10,2},{18,10},{26,18},{... | collective-permute-start | bytes 786440 | tf_op jit(solution)/shard_map/ppermute | solution.py:1293
  147.2 16.3 %collective-permute-start.12 = (bf16[128,1024]{1,0:T(8,128)(2,1)S(1)}, bf16[128,1024]{1,0:T(8,128)(2,1)S(1)}, u32[]{:S(2)}, u32[]{:S(2)}) collective-permute-start(bf16[128,1024]{1,0:T(8,128)(2,1)S(1)} %get-tuple-element.365), channel_id=1, source_target_pairs={{8,0},{16,8},{24,16},{9,1},{17,9},{25,17},{10,2},{18,10},{26,18},{... | collective-permute-start | bytes 786440 | tf_op jit(solution)/shard_map/ppermute | solution.py:1293
  148.5 25.2 %collective-permute-start.9 = (bf16[4,128,1024]{2,1,0:T(8,128)(2,1)}, bf16[4,128,1024]{2,1,0:T(8,128)(2,1)}, u32[]{:S(2)}, u32[]{:S(2)}) collective-permute-start(bf16[4,128,1024]{2,1,0:T(8,128)(2,1)} %get-tuple-element.350), channel_id=1, source_target_pairs={{8,10},{9,11},{14,12},{15,13},{16,18},{17,19},{22,20},{23,21},{24,... | collective-permute-start | bytes 3145736 | tf_op jit(solution)/shard_map/ppermute | solution.py:1115
  172.5 10.1 %collective-permute-start.13 = (bf16[128,1024]{1,0:T(8,128)(2,1)S(1)}, bf16[128,1024]{1,0:T(8,128)(2,1)S(1)}, u32[]{:S(2)}, u32[]{:S(2)}) collective-permute-start(bf16[128,1024]{1,0:T(8,128)(2,1)S(1)} %get-tuple-element.379), channel_id=1, source_target_pairs={{8,0},{16,8},{9,1},{17,9},{10,2},{18,10},{11,3},{19,11},{12,4},{20... | collective-permute-start | bytes 786440 | tf_op jit(solution)/shard_map/ppermute | solution.py:1293
  191.0 23.0 %collective-permute-start.14 = (bf16[3,128,4096]{2,1,0:T(8,128)(2,1)}, bf16[3,128,4096]{2,1,0:T(8,128)(2,1)}, u32[]{:S(2)}, u32[]{:S(2)}) collective-permute-start(bf16[3,128,4096]{2,1,0:T(8,128)(2,1)} %get-tuple-element.393.refs_4_), channel_id=1, source_target_pairs={{0,1},{1,0},{2,3},{3,2},{4,5},{5,4},{6,7},{7,6},{8,9},{9,8},{10,11... | collective-permute-start | bytes 9437192 | tf_op jit(solution)/shard_map/ppermute | solution.py:1103
  191.1 10.9 %collective-permute-start.16 = (bf16[128,1024]{1,0:T(8,128)(2,1)S(1)}, bf16[128,1024]{1,0:T(8,128)(2,1)S(1)}, u32[]{:S(2)}, u32[]{:S(2)}) collective-permute-start(bf16[128,1024]{1,0:T(8,128)(2,1)S(1)} %get-tuple-element.395), channel_id=1, source_target_pairs={{8,0},{9,1},{10,2},{11,3},{12,4},{13,5},{14,6},{15,7}} | collective-permute-start | bytes 786440 | tf_op jit(solution)/shard_map/ppermute | solution.py:1293
  192.4 21.6 %collective-permute-start.15 = (bf16[3,128,1024]{2,1,0:T(8,128)(2,1)}, bf16[3,128,1024]{2,1,0:T(8,128)(2,1)}, u32[]{:S(2)}, u32[]{:S(2)}) collective-permute-start(bf16[3,128,1024]{2,1,0:T(8,128)(2,1)} %get-tuple-element.394.refs_0_), channel_id=1, source_target_pairs={{0,2},{1,3},{6,4},{7,5},{8,10},{9,11},{14,12},{15,13},{16,18},{17,... | collective-permute-start | bytes 2359304 | tf_op jit(solution)/shard_map/ppermute | solution.py:1113
  201.9 12.1 %copy-start.2 = (bf16[512,1024]{1,0:T(8,128)(2,1)S(1)}, bf16[512,1024]{1,0:T(8,128)(2,1)}, u32[]{:S(2)}) copy-start(bf16[512,1024]{1,0:T(8,128)(2,1)} %param.10) | copy-start | bytes 3145732
  207.5 12.2 %collective-permute-start.17 = (bf16[1,128,4096]{2,1,0:T(8,128)(2,1)}, bf16[1,128,4096]{2,1,0:T(8,128)(2,1)S(1)}, u32[]{:S(2)}, u32[]{:S(2)}) collective-permute-start(bf16[1,128,4096]{2,1,0:T(8,128)(2,1)} %get-tuple-element.417.refs_6_), channel_id=1, source_target_pairs={{0,1},{1,0},{2,3},{3,2},{4,5},{5,4},{6,7},{7,6},{8,9},{9,8},{10,11... | collective-permute-start | bytes 3145736 | tf_op jit(solution)/shard_map/ppermute | solution.py:1103
  207.6 12.1 %collective-permute-start.18 = (bf16[1,128,1024]{2,1,0:T(8,128)(2,1)}, bf16[1,128,1024]{2,1,0:T(8,128)(2,1)S(1)}, u32[]{:S(2)}, u32[]{:S(2)}) collective-permute-start(bf16[1,128,1024]{2,1,0:T(8,128)(2,1)} %get-tuple-element.418.refs_1_), channel_id=1, source_target_pairs={{0,2},{1,3},{6,4},{7,5},{8,10},{9,11},{14,12},{15,13},{16,18},{17,... | collective-permute-start | bytes 786440 | tf_op jit(solution)/shard_map/ppermute | solution.py:1113
  214.0 5.7 %copy-start.7 = (bf16[4,128,4096]{2,1,0:T(8,128)(2,1)S(1)}, bf16[4,128,4096]{2,1,0:T(8,128)(2,1)}, u32[]{:S(2)}) copy-start(bf16[4,128,4096]{2,1,0:T(8,128)(2,1)} %get-tuple-element.420.refs_6_.refs_7_) | copy-start | bytes 12582916
  219.7 5.5 %copy-start.9 = (s32[4]{0:T(128)S(1)}, s32[4]{0:T(128)}, u32[]{:S(2)}) copy-start(s32[4]{0:T(128)} %refs_1_.1) | copy-start | bytes 52
  219.7 5.6 %copy-start.8 = (f32[4,4,1024]{2,1,0:T(4,128)S(1)}, f32[4,4,1024]{2,1,0:T(4,128)}, u32[]{:S(2)}) copy-start(f32[4,4,1024]{2,1,0:T(4,128)} %get-tuple-element.428) | copy-start | bytes 196612
  222.6 2.0 copy-start.3
  224.7 37.7 %collective-permute-start.20 = (bf16[512,4096]{1,0:T(8,128)(2,1)}, bf16[512,4096]{1,0:T(8,128)(2,1)}, u32[]{:S(2)}, u32[]{:S(2)}) collective-permute-start(bf16[512,4096]{1,0:T(8,128)(2,1)} %get-tuple-element.424), channel_id=1, source_target_pairs={{0,1},{1,0},{2,3},{3,2},{4,5},{5,4},{6,7},{7,6},{8,9},{9,8},{10,11... | collective-permute-start | bytes 12582920 | tf_op jit(solution)/shard_map/ppermute | solution.py:1103
  224.7 44.9 %collective-permute-start.19 = (bf16[4,128,3072]{2,1,0:T(8,128)(2,1)}, bf16[4,128,3072]{2,1,0:T(8,128)(2,1)}, u32[]{:S(2)}, u32[]{:S(2)}) collective-permute-start(bf16[4,128,3072]{2,1,0:T(8,128)(2,1)} %get-tuple-element.423.refs_2_), channel_id=1, source_target_pairs={{0,1},{1,0},{2,3},{3,2},{4,5},{5,4},{6,7},{7,6},{8,9},{9,8},{10,11... | collective-permute-start | bytes 9437192 | tf_op jit(solution)/shard_map/ppermute | solution.py:1103
  225.5 42.4 %collective-permute-start.22 = (f32[32,1024]{1,0:T(8,128)S(1)}, f32[32,1024]{1,0:T(8,128)S(1)}, u32[]{:S(2)}, u32[]{:S(2)}) collective-permute-start(f32[32,1024]{1,0:T(8,128)S(1)} %reshape.56), channel_id=1, source_target_pairs={{0,1},{1,0},{2,3},{3,2},{4,5},{5,4},{6,7},{7,6},{8,9},{9,8},{10,11... | collective-permute-start | bytes 393224 | tf_op jit(solution)/shard_map/ppermute | solution.py:1103
  225.6 52.1 %collective-permute-start.21 = (bf16[4,128,1024]{2,1,0:T(8,128)(2,1)}, bf16[4,128,1024]{2,1,0:T(8,128)(2,1)}, u32[]{:S(2)}, u32[]{:S(2)}) collective-permute-start(bf16[4,128,1024]{2,1,0:T(8,128)(2,1)} %get-tuple-element.427.refs_2_), channel_id=1, source_target_pairs={{0,1},{1,0},{2,3},{3,2},{4,5},{5,4},{6,7},{7,6},{8,9},{9,8},{10,11... | collective-permute-start | bytes 3145736 | tf_op jit(solution)/shard_map/ppermute | solution.py:1103
  226.1 2.2 copy-start.4
  238.7 2.6 copy-start
  238.7 23.7 %copy-start.5 = (bf16[512,4096]{1,0:T(8,128)(2,1)S(1)}, bf16[512,4096]{1,0:T(8,128)(2,1)}, u32[]{:S(2)}) copy-start(bf16[512,4096]{1,0:T(8,128)(2,1)} %copy-done.3) | copy-start | bytes 12582916
  241.4 43.6 %collective-permute-start.23 = (bf16[128,4096]{1,0:T(8,128)(2,1)S(1)}, bf16[128,4096]{1,0:T(8,128)(2,1)S(1)}, u32[]{:S(2)}, u32[]{:S(2)}) collective-permute-start(bf16[128,4096]{1,0:T(8,128)(2,1)S(1)} %get-tuple-element.425.refs_2_), channel_id=1, source_target_pairs={{0,2},{1,3},{8,10},{9,11},{16,18},{17,19},{24,26},{25,27}} | collective-permute-start | bytes 3145736 | tf_op jit(solution)/shard_map/ppermute | solution.py:1061
  266.3 15.0 %collective-permute-start.25 = (bf16[128,4096]{1,0:T(8,128)(2,1)}, bf16[128,4096]{1,0:T(8,128)(2,1)}, u32[]{:S(2)}, u32[]{:S(2)}) collective-permute-start(bf16[128,4096]{1,0:T(8,128)(2,1)} %get-tuple-element.426.refs_4_), channel_id=1, source_target_pairs={{2,4},{3,5},{10,12},{11,13},{18,20},{19,21},{26,28},{27,29}} | collective-permute-start | bytes 3145736 | tf_op jit(solution)/shard_map/ppermute | solution.py:1061
  267.9 13.4 %collective-permute-start.26 = (bf16[128,4096]{1,0:T(8,128)(2,1)}, bf16[128,4096]{1,0:T(8,128)(2,1)}, u32[]{:S(2)}, u32[]{:S(2)}) collective-permute-start(bf16[128,4096]{1,0:T(8,128)(2,1)} %get-tuple-element.430), channel_id=1, source_target_pairs={{4,2},{5,3},{12,10},{13,11},{20,18},{21,19},{28,26},{29,27}} | collective-permute-start | bytes 3145736 | tf_op jit(solution)/shard_map/ppermute | solution.py:1061
  269.6 15.4 %collective-permute-start.24 = (bf16[128,4096]{1,0:T(8,128)(2,1)}, bf16[128,4096]{1,0:T(8,128)(2,1)S(1)}, u32[]{:S(2)}, u32[]{:S(2)}) collective-permute-start(bf16[128,4096]{1,0:T(8,128)(2,1)} %get-tuple-element.429), channel_id=1, source_target_pairs={{6,4},{7,5},{14,12},{15,13},{22,20},{23,21},{30,28},{31,29}} | collective-permute-start | bytes 3145736 | tf_op jit(solution)/shard_map/ppermute | solution.py:1061
  277.7 3.6 copy-start.6
  285.0 45.2 %copy-start.1 = (bf16[512,4096]{1,0:T(8,128)(2,1)S(1)}, bf16[512,4096]{1,0:T(8,128)(2,1)}, u32[]{:S(2)}) copy-start(bf16[512,4096]{1,0:T(8,128)(2,1)} %copy-done) | copy-start | bytes 12582916
  285.1 45.1 %collective-permute-start.27 = (bf16[128,4224]{1,0:T(8,128)(2,1)S(1)}, bf16[128,4224]{1,0:T(8,128)(2,1)S(1)}, u32[]{:S(2)}, u32[]{:S(2)}) collective-permute-start(bf16[128,4224]{1,0:T(8,128)(2,1)S(1)} %get-tuple-element.432.refs_8_), channel_id=1, source_target_pairs={{0,2},{1,3},{8,10},{9,11},{16,18},{17,19},{24,26},{25,27}} | collective-permute-start | bytes 3244040 | tf_op jit(solution)/shard_map/ppermute | solution.py:1061
  303.1 27.1 %collective-permute-start.28 = (bf16[128,4224]{1,0:T(8,128)(2,1)S(1)}, bf16[128,4224]{1,0:T(8,128)(2,1)S(1)}, u32[]{:S(2)}, u32[]{:S(2)}) collective-permute-start(bf16[128,4224]{1,0:T(8,128)(2,1)S(1)} %get-tuple-element.433), channel_id=1, source_target_pairs={{6,4},{7,5},{14,12},{15,13},{22,20},{23,21},{30,28},{31,29}} | collective-permute-start | bytes 3244040 | tf_op jit(solution)/shard_map/ppermute | solution.py:1061
  303.9 2.0 collective-permute-start.29
  304.6 25.6 %collective-permute-start.30 = (bf16[128,4096]{1,0:T(8,128)(2,1)S(1)}, bf16[128,4096]{1,0:T(8,128)(2,1)S(1)}, u32[]{:S(2)}, u32[]{:S(2)}) collective-permute-start(bf16[128,4096]{1,0:T(8,128)(2,1)S(1)} %get-tuple-element.434), channel_id=1, source_target_pairs={{2,0},{3,1},{4,2},{5,3},{10,8},{11,9},{12,10},{13,11},{18,16},{19,... | collective-permute-start | bytes 3145736 | tf_op jit(solution)/shard_map/ppermute | solution.py:1061
  331.2 46.2 %collective-permute-start.31 = (bf16[128,8320]{1,0:T(8,128)(2,1)S(1)}, bf16[128,8320]{1,0:T(8,128)(2,1)S(1)}, u32[]{:S(2)}, u32[]{:S(2)}) collective-permute-start(bf16[128,8320]{1,0:T(8,128)(2,1)S(1)} %get-tuple-element.435.refs_4_), channel_id=1, source_target_pairs={{0,2},{1,3},{2,4},{3,5},{8,10},{9,11},{10,12},{11,13},{16,18},{17,... | collective-permute-start | bytes 6389768 | tf_op jit(solution)/shard_map/ppermute | solution.py:1061
  334.4 43.0 %collective-permute-start.32 = (bf16[128,8320]{1,0:T(8,128)(2,1)S(1)}, bf16[128,8320]{1,0:T(8,128)(2,1)S(1)}, u32[]{:S(2)}, u32[]{:S(2)}) collective-permute-start(bf16[128,8320]{1,0:T(8,128)(2,1)S(1)} %get-tuple-element.436), channel_id=1, source_target_pairs={{4,2},{5,3},{6,4},{7,5},{12,10},{13,11},{14,12},{15,13},{20,18},{2... | collective-permute-start | bytes 6389768 | tf_op jit(solution)/shard_map/ppermute | solution.py:1061
  378.4 48.5 %collective-permute-start.33 = (bf16[128,8320]{1,0:T(8,128)(2,1)S(1)}, bf16[128,8320]{1,0:T(8,128)(2,1)S(1)}, u32[]{:S(2)}, u32[]{:S(2)}) collective-permute-start(bf16[128,8320]{1,0:T(8,128)(2,1)S(1)} %get-tuple-element.438.refs_6_), channel_id=1, source_target_pairs={{0,2},{1,3},{2,4},{3,5},{4,6},{5,7},{8,10},{9,11},{10,12},{11,13},... | collective-permute-start | bytes 6389768 | tf_op jit(solution)/shard_map/ppermute | solution.py:1061
  384.9 46.3 %collective-permute-start.34 = (bf16[128,8320]{1,0:T(8,128)(2,1)S(1)}, bf16[128,8320]{1,0:T(8,128)(2,1)S(1)}, u32[]{:S(2)}, u32[]{:S(2)}) collective-permute-start(bf16[128,8320]{1,0:T(8,128)(2,1)S(1)} %get-tuple-element.439), channel_id=1, source_target_pairs={{2,0},{3,1},{4,2},{5,3},{6,4},{7,5},{10,8},{11,9},{12,10},{13,11},... | collective-permute-start | bytes 6389768 | tf_op jit(solution)/shard_map/ppermute | solution.py:1061
